TPU v7x, 32 devices: a whole 2x2x4 slice. The times are simulated.
32 devices in a mesh: gx: 8 (over y, x, core), gy: 4 (over z).
Axes of the slice: x: 2, y: 2, z: 4, core: 2. Of those that a mesh axis runs over, the one named last changes fastest.
Arguments:
- forces: float32 [3, 24, 16, 32, 128], P(None, None, 'gx', 'gy'), may hold values from -6 to 6
- levels: int32 [16, 32, 128], P('gx', 'gy'), may hold values from 0 to 15
- supports: int32 [16, 32, 128], P('gx', 'gy'), may hold values 0 or 1
Outputs:
- filtered: float32 [16, 32, 128], P('gx', 'gy')
All inputs are finite; a program needn't handle non-finite values. No bound on the sum of `supports` on one device may be relied on, other than what follows from the above.
Results may differ from a plain program's by a relative error of at most 0.0001.
Values sent between devices are 32-bit elements; how exact they have to be, the bound alone decides.
No kernel may reach another device: no remote copies, remote signals or barrier semaphores. Data moves between devices by JAX's collectives and lax.ppermute only.
A program may use at most 128 MiB of HBM per device.

v0:
```python
import functools
import math

import jax
import jax.numpy as jnp
from jax import lax
from jax.experimental import pallas as pl
from jax.experimental.pallas import tpu as pltpu
from jax.sharding import PartitionSpec as P

LEVELS = 16
LOAD = 0.2
LANES = 128
POISSON = 0.3
LAME = POISSON / ((1.0 + POISSON) * (1.0 - 2.0 * POISSON))
SHEAR = 1.0 / (2.0 * (1.0 + POISSON))
DIAGONAL = (LAME + 2.0 * SHEAR) / 9.0 + 2.0 * SHEAR / 9.0
VMEM = pl.BlockSpec(memory_space=pltpu.VMEM)
PARAMS = pltpu.CompilerParams(vmem_limit_bytes=50 * 2**20)
f32 = jnp.float32
bf16 = jnp.bfloat16


def up8(count):
    return -(-count // 8) * 8


def shift_down(value):
    lane = lax.broadcasted_iota(jnp.int32, value.shape, value.ndim - 1)
    rolled = pltpu.roll(value, LANES - 1, value.ndim - 1)
    return jnp.where(lane == LANES - 1, 0.0, rolled)


def shift_up(value):
    lane = lax.broadcasted_iota(jnp.int32, value.shape, value.ndim - 1)
    return jnp.where(lane == 0, 0.0, pltpu.roll(value, 1, value.ndim - 1))


def split(value):
    high = value.astype(bf16)
    return high, (value - high.astype(f32)).astype(bf16)


def modes_of(lower, upper):
    out = [[[[None] * 3 for _ in range(2)] for _ in range(2)] for _ in range(2)]
    for a in range(2):
        for c in range(2):
            for k in range(3):
                if a or c:
                    out[a][0][c][k] = lower[a][c][k] + upper[a][c][k]
                out[a][1][c][k] = upper[a][c][k] - lower[a][c][k]
    return out


PAIRS = (((1, 1, 0, 0), (0, 1, 1, 2)), ((1, 0, 1, 0), (0, 1, 1, 1)), ((1, 1, 0, 1), (1, 0, 1, 2)))
TRIPLE = ((0, 1, 1, 0), (1, 0, 1, 1), (1, 1, 0, 2))
SHEARS = (((0, 1, 0, 0), (1, 0, 0, 1)), ((0, 0, 1, 0), (1, 0, 0, 2)), ((0, 0, 1, 1), (0, 1, 0, 2)))
AXIAL = ((1, 0, 0, 0), (0, 1, 0, 1), (0, 0, 1, 2))


def at(modes, place):
    a, b, c, k = place
    return modes[a][b][c][k]


def mode_forces(modes, stiff):
    out = [[[[None] * 3 for _ in range(2)] for _ in range(2)] for _ in range(2)]

    def put(place, value):
        a, b, c, k = place
        out[a][b][c][k] = value

    shear = stiff * (SHEAR / 16)
    for first, second in SHEARS:
        force = shear * (at(modes, first) + at(modes, second))
        put(first, force)
        put(second, force)
    one, two, three = (at(modes, place) for place in AXIAL)
    volume = (stiff * (LAME / 16)) * (one + two + three)
    axial = stiff * (SHEAR / 8)
    for place in AXIAL:
        put(place, volume + axial * at(modes, place))
    own, cross = stiff * ((LAME + 3 * SHEAR) / 48), stiff * (LAME / 48)
    for first, second in PAIRS:
        one, two = at(modes, first), at(modes, second)
        put(first, own * one + cross * two)
        put(second, own * two + cross * one)
    twist = stiff * (SHEAR / 48)
    one, two, three = (at(modes, place) for place in TRIPLE)
    total = one + two + three
    for place in TRIPLE:
        put(place, twist * (total + at(modes, place)))
    last = stiff * ((LAME + 4 * SHEAR) / 144)
    for k in range(3):
        put((1, 1, 1, k), last * modes[1][1][1][k])
    return out


def mode_energy(modes):
    def square(value):
        return value * value

    shear = None
    for first, second in SHEARS:
        term = square(at(modes, first) + at(modes, second))
        shear = term if shear is None else shear + term
    one, two, three = (at(modes, place) for place in AXIAL)
    energy = (SHEAR / 16) * shear + (LAME / 16) * square(one + two + three)
    energy = energy + (SHEAR / 8) * (square(one) + square(two) + square(three))
    squares, products = None, None
    for first, second in PAIRS:
        one, two = at(modes, first), at(modes, second)
        term, product = square(one) + square(two), one * two
        squares = term if squares is None else squares + term
        products = product if products is None else products + product
    energy = energy + ((LAME + 3 * SHEAR) / 48) * squares + (LAME / 24) * products
    one, two, three = (at(modes, place) for place in TRIPLE)
    twist = square(one + two + three) + square(one) + square(two) + square(three)
    energy = energy + (SHEAR / 48) * twist
    last = square(modes[1][1][1][0]) + square(modes[1][1][1][1]) + square(modes[1][1][1][2])
    return energy + ((LAME + 4 * SHEAR) / 144) * last


def x_modes(sums, diffs, plane, row, tile, cases, columns):
    out = [[[None] * 3 for _ in range(2)] for _ in range(2)]
    for c, ref in enumerate((sums, diffs)):
        for k in range(3):
            rows = pl.ds(pl.multiple_of(k * cases + tile * 8, 8), 8)
            one = ref[plane * columns + row, rows, :]
            two = ref[(plane + 1) * columns + row, rows, :]
            out[0][c][k] = one + two
            out[1][c][k] = two - one
    return out


def apply_elements(
    sums, diffs, stiff_ref, acc_s, acc_d, planes, rows, skip, stiff_x, stiff_y, cases
):
    columns = rows + 1
    acc_columns = columns - 2 * skip
    tiles = cases // 8

    def step(index, _):
        plane, tile = index // tiles, index % tiles

        def emit(row, total):
            if not skip <= row < columns - skip:
                return
            for c, acc in enumerate((acc_s, acc_d)):
                for k in range(3):
                    lines = pl.ds(pl.multiple_of(k * cases + tile * 8, 8), 8)
                    low = plane * acc_columns + row - skip
                    acc[low, lines, :] += total[0][c][k] - total[1][c][k]
                    acc[low + acc_columns, lines, :] = total[0][c][k] + total[1][c][k]

        lower = x_modes(sums, diffs, plane, 0, tile, cases, columns)
        carry = None
        for row in range(rows):
            upper = x_modes(sums, diffs, plane, row + 1, tile, cases, columns)
            stiff = jnp.broadcast_to(
                stiff_ref[plane + stiff_x, pl.ds(row + stiff_y, 1), :], (8, LANES)
            )
            forces = mode_forces(modes_of(lower, upper), stiff)
            here = [[[None] * 3 for _ in range(2)] for _ in range(2)]
            following = [[[None] * 3 for _ in range(2)] for _ in range(2)]
            for a in range(2):
                for c in range(2):
                    for k in range(3):
                        one, two = forces[a][0][c][k], forces[a][1][c][k]
                        low = -two if one is None else one - two
                        high = two if one is None else one + two
                        here[a][c][k] = low if carry is None else carry[a][c][k] + low
                        following[a][c][k] = high
            emit(row, here)
            carry, lower = following, upper
        emit(rows, carry)
        return 0

    lax.fori_loop(0, planes * tiles, step, 0)


def pack_kernel(sizes, forces, levels, supports, own, up, *rest):
    planes, rows, cases = sizes
    block = 3 * cases
    base = planes * rows * block
    *down, ym, yp, mm, mp, pm, pp = rest
    for x in range(planes):
        density = 0.3 + 0.7 * levels[x].astype(f32) / (LEVELS - 1)
        stiff = density * density * density
        free = supports[x] == 0
        own[base + x * rows : base + (x + 1) * rows, :] = jnp.where(free, stiff, -stiff)
        scale = jnp.where(free, LOAD, 0.0)
        for k in range(3):
            for c in range(cases):
                start = x * rows * block + k * cases + c
                own[pl.ds(start, rows, stride=block), :] = forces[k, c, x] * scale

    def fill(ref, xs, ys, code_xs, code_ys):
        line = 0
        for x in xs:
            for y in ys:
                start = (x * rows + y) * block
                ref[line : line + block, :] = own[start : start + block, :]
                line += block
        for x in code_xs:
            for y in code_ys:
                start = base + x * rows + y
                ref[line : line + 1, :] = own[start : start + 1, :]
                line += 1
        if line < ref.shape[0]:
            ref[line:, :] = jnp.zeros((ref.shape[0] - line, LANES), f32)

    every_x, every_y = range(planes), range(rows)
    first_x, last_x = range(2), range(planes - 2, planes)
    first_y, last_y = range(2), range(rows - 2, rows)
    fill(up, last_x[1:], every_y, last_x, every_y)
    for ref in down:
        fill(ref, first_x, every_y, first_x, every_y)
    fill(ym, every_x, first_y, every_x, first_y)
    fill(yp, every_x, last_y[1:], every_x, last_y)
    fill(mm, first_x, first_y, first_x, first_y)
    fill(mp, first_x, last_y[1:], first_x, last_y)
    fill(pm, last_x[1:], first_y, last_x, first_y)
    fill(pp, last_x[1:], last_y[1:], last_x, last_y)


def main_kernel(
    sizes, own, xm, xp, ym, yp, mm, mp, pm, pp, both_out, system_out, stiff_ref, inverse,
    start, sums, diffs, acc_s, acc_d, w_sums, w_diffs, acc2_s, acc2_d, right, second,
):
    planes, rows, cases = sizes
    block = 3 * cases
    xs, ys = planes + 3, rows + 3
    every_x, every_y = range(planes), range(rows)
    low, high_x, high_y = (-1,), (planes, planes + 1), (rows, rows + 1)
    low2 = (-2, -1)
    regions = (
        (own, every_x, every_y, every_x, every_y),
        (xm, low, every_y, low2, every_y),
        (xp, high_x, every_y, high_x, every_y),
        (ym, every_x, low, every_x, low2),
        (yp, every_x, high_y, every_x, high_y),
        (mm, low, low, low2, low2),
        (mp, low, high_y, low2, high_y),
        (pm, high_x, low, high_x, low2),
        (pp, high_x, high_y, high_x, high_y),
    )
    for ref, bx, by, cx, cy in regions:
        base = len(bx) * len(by) * block
        for i, x in enumerate(cx):
            line = base + i * len(cy)
            stiff_ref[x + 2, cy[0] + 2 : cy[0] + 2 + len(cy), :] = ref[line : line + len(cy), :]
    for x in range(-1, planes + 2):
        codes = stiff_ref[x + 2, 0 : ys + 1, :]
        total = jnp.abs(stiff_ref[x + 1, 0 : ys + 1, :]) + jnp.abs(codes)
        total = total[:-1] + total[1:]
        total = total + shift_up(total)
        free = codes[1:] > 0.0
        value = 1.0 / (DIAGONAL * jnp.where(free, total, 1.0))
        inverse[x + 1, 0:ys, :] = jnp.where(free, value, 0.0)
    for x in range(planes + 4):
        stiff_ref[x] = jnp.abs(stiff_ref[x])

    for ref, bx, by, _, _ in regions:
        for i, x in enumerate(bx):

            def place(j, _, ref=ref, i=i, x=x, by=by):
                y = j + by[0] + 1
                load = ref[pl.ds(pl.multiple_of((i * len(by) + j) * block, 8), block), :]
                value = load * inverse[x + 1, pl.ds(y, 1), :]
                column = (x + 1) * ys + y
                start[column] = value
                moved = shift_down(value)
                sums[column] = value + moved
                diffs[column] = moved - value
                return 0

            lax.fori_loop(0, len(by), place, 0)

    nodes_y = rows + 1
    apply_elements(
        sums, diffs, stiff_ref, acc_s, acc_d, planes + 2, rows + 2, 1, 1, 1, cases
    )

    def image(x, y, place):
        column = (x + 1) * nodes_y + y
        s, d = acc_s[column], acc_d[column]
        force = s - d + shift_up(s + d)
        scaled = force * inverse[x + 1, pl.ds(y + 1, 1), :]
        moved = shift_down(scaled)
        w_sums[x * nodes_y + y] = scaled + moved
        w_diffs[x * nodes_y + y] = moved - scaled
        value = start[(x + 1) * ys + y + 1]
        for k in range(3):
            lines = slice(k * cases, (k + 1) * cases)
            pair = jnp.concatenate([value[lines], scaled[lines]], 0)
            lane = pl.ds(pl.multiple_of((place * 3 + k) * LANES, LANES), LANES)
            high, rest = split(pair)
            both_out[0 : 2 * cases, lane] = high
            both_out[2 * cases : 4 * cases, lane] = rest
        return force

    def inside(index, _):
        x, y = index // rows, index % rows
        force = image(x, y, index)
        load = own[pl.ds(pl.multiple_of(index * block, 8), block), :]
        for k in range(3):
            lines = slice(k * cases, (k + 1) * cases)
            pair = jnp.concatenate([load[lines], force[lines]], 0)
            lane = pl.ds(pl.multiple_of((index * 3 + k) * LANES, LANES), LANES)
            high, rest = split(pair)
            right[0 : 2 * cases, lane] = high
            right[2 * cases : 4 * cases, lane] = rest
        return 0

    count = planes * rows
    lax.fori_loop(0, count, inside, 0)

    def beyond_y(x, _):
        image(x, rows, count + x)
        return 0

    lax.fori_loop(0, planes, beyond_y, 0)

    def beyond_x(y, _):
        image(planes, y, count + planes + y)
        return 0

    lax.fori_loop(0, nodes_y, beyond_x, 0)

    for column in range(nodes_y):
        acc2_s[column] = jnp.zeros((block, LANES), f32)
        acc2_d[column] = jnp.zeros((block, LANES), f32)
    apply_elements(w_sums, w_diffs, stiff_ref, acc2_s, acc2_d, planes, rows, 0, 2, 2, cases)

    def second_force(x, y, place):
        column = x * nodes_y + y
        s, d = acc2_s[column], acc2_d[column]
        force = s - d + shift_up(s + d)
        for k in range(3):
            value = force[k * cases : (k + 1) * cases]
            high = value.astype(bf16).astype(f32)
            lane = pl.ds(pl.multiple_of((place * 3 + k) * LANES, LANES), LANES)
            second[:, lane] = jnp.concatenate([high, value - high], 0).astype(bf16)

    def second_inside(index, _):
        second_force(index // rows, index % rows, index)
        return 0

    def second_y(x, _):
        second_force(x, rows, count + x)
        return 0

    def second_x(y, _):
        second_force(planes, y, count + planes + y)
        return 0

    lax.fori_loop(0, count, second_inside, 0)
    lax.fori_loop(0, planes, second_y, 0)
    lax.fori_loop(0, nodes_y, second_x, 0)

    contract = (((1,), (1,)), ((), ()))
    width = count * 3 * LANES
    two = 2 * cases
    gram = lax.dot_general(both_out[:, :width], right[...], contract, preferred_element_type=f32)
    gram = gram[:two] + gram[two:]
    gram = gram[:, :two] + gram[:, two:]
    other = lax.dot_general(both_out[...], second[...], contract, preferred_element_type=f32)
    other = other[:two] + other[two:]
    other = other[:, :cases] + other[:, cases:]
    system_out[...] = jnp.zeros(system_out.shape, f32)
    system_out[0:cases, 0:cases] = gram[:cases, cases:]
    system_out[0:cases, cases:two] = other[:cases]
    system_out[cases:two, 0:cases] = gram[cases:, cases:]
    system_out[cases:two, cases:two] = other[cases:]
    system_out[two : two + cases, 0:two] = gram[:cases]


def solve_kernel(sizes, system, both, levels, out, mixing, sums, diffs, energy):
    planes, rows, cases = sizes
    two = 2 * cases
    nodes_y = rows + 1
    count = planes * rows
    table = system[...]
    lane = lax.broadcasted_iota(jnp.int32, (1, LANES), 1)
    gone = 0
    for pivot in range(two):
        drop = pivot // 8 * 8 - gone
        table = table[drop:]
        gone += drop
        line = pivot - gone
        row = table[line : line + 1, :]
        inverse = 1.0 / row[:, pivot : pivot + 1]
        row = jnp.where(lane == pivot, -inverse, row * inverse)
        column = table[:, pivot : pivot + 1]
        table = jnp.where(lane == pivot, 0.0, table) - column * row
    answer = table[two - gone :, :two]
    high = answer.astype(bf16).astype(f32)
    mixing[...] = jnp.zeros(mixing.shape, f32)
    mixing[0:cases, 0:two] = high
    mixing[0:cases, two : 2 * two] = high
    mixing[cases:two, 0:two] = answer - high
    mix = mixing[...][:, : 2 * two].astype(bf16)

    def combined(place, width):
        lanes = pl.ds(pl.multiple_of(place * 3 * LANES, LANES), width * 3 * LANES)
        value = jnp.dot(mix, both[:, lanes], preferred_element_type=f32)
        return value[:cases] + value[cases:]

    def keep(value, index, column):
        for k in range(3):
            part = value[:, (index * 3 + k) * LANES : (index * 3 + k + 1) * LANES]
            moved = shift_down(part)
            sums[column, k * cases : (k + 1) * cases, :] = part + moved
            diffs[column, k * cases : (k + 1) * cases, :] = moved - part

    def inside(x, _):
        value = combined(x * rows, rows)
        for y in range(rows):
            keep(value, y, x * nodes_y + y)
        return 0

    lax.fori_loop(0, planes, inside, 0)
    value = combined(count, planes + nodes_y)
    for x in range(planes):
        keep(value, x, x * nodes_y + rows)
    for y in range(nodes_y):
        keep(value, planes + y, planes * nodes_y + y)

    tiles = cases // 8

    def step(plane, _):
        for tile in range(tiles):
            lower = x_modes(sums, diffs, plane, 0, tile, cases, nodes_y)
            for row in range(rows):
                upper = x_modes(sums, diffs, plane, row + 1, tile, cases, nodes_y)
                part = mode_energy(modes_of(lower, upper))
                if tile == 0:
                    energy[row] = part
                else:
                    energy[row] += part
                lower = upper
        total = jnp.sum(energy[...], axis=1)
        density = 0.3 + 0.7 * levels[plane].astype(f32) / (LEVELS - 1)
        out[plane] = (-3.0 / cases) * (density * density * density) * total
        return 0

    lax.fori_loop(0, planes, step, 0)


def filter_kernel(sizes, totals, start, below, above, own, left, right, levels, out, wide, there):
    planes, rows, _ = sizes
    weight = [2.5 - math.sqrt(q) for q in range(7)]
    wide[0:2, 2 : 2 + rows, :] = below[...]
    wide[2 : 2 + planes, 2 : 2 + rows, :] = own[...]
    wide[2 + planes :, 2 : 2 + rows, :] = above[...]
    wide[:, 0:2, :] = left[...]
    wide[:, 2 + rows : 4 + rows, :] = right[...]
    y = lax.broadcasted_iota(jnp.int32, (rows + 4, LANES), 0) + (start[1] - 2)
    in_y = jnp.logical_and(y >= 0, y < totals[1])
    for x in range(planes + 4):
        global_x = start[0] + (x - 2)
        in_x = jnp.logical_and(global_x >= 0, global_x < totals[0])
        there[x] = jnp.where(jnp.logical_and(in_y, in_x), 1.0, 0.0)

    def smooth(ref, x):
        near = {}
        for dx in range(-2, 3):
            for dy in range(-2, 3):
                q = dx * dx + dy * dy
                if q <= 5:
                    value = ref[x + 2 + dx, 2 + dy : 2 + dy + rows, :]
                    near[q] = value if q not in near else near[q] + value
        result = 0.0
        for dz in range(3):
            part = None
            for q, value in near.items():
                if q + dz * dz <= 6:
                    term = weight[q + dz * dz] * value
                    part = term if part is None else part + term
            if dz == 0:
                result = part
            else:
                place = lax.broadcasted_iota(jnp.int32, part.shape, 1)
                forward = jnp.where(place >= LANES - dz, 0.0, pltpu.roll(part, LANES - dz, 1))
                backward = jnp.where(place < dz, 0.0, pltpu.roll(part, dz, 1))
                result = result + (forward + backward)
        return result

    for x in range(planes):
        density = 0.3 + 0.7 * levels[x].astype(f32) / (LEVELS - 1)
        out[x] = smooth(wide, x) / (density * smooth(there, x))


def local(forces, levels, supports):
    _, cases, planes, rows, _ = forces.shape
    sizes = (planes, rows, cases)
    block = 3 * cases
    count_x, count_y = lax.axis_size("gx"), lax.axis_size("gy")

    def shape(blocks, codes):
        return jax.ShapeDtypeStruct((blocks * block + up8(codes), LANES), f32)

    whole = shape(planes * rows, planes * rows)
    down = [] if planes == 2 else [shape(2 * rows, 2 * rows)]
    packed = pl.pallas_call(
        functools.partial(pack_kernel, sizes),
        out_shape=[
            whole, shape(rows, 2 * rows), *down, shape(2 * planes, 2 * planes),
            shape(planes, 2 * planes), shape(4, 4), shape(2, 4), shape(2, 4), shape(1, 4),
        ],
        in_specs=[VMEM] * 3,
        out_specs=[VMEM] * (8 + len(down)),
        compiler_params=PARAMS,
        name="pack",
    )(forces, levels, supports)
    own, up, *rest = packed
    down = own if planes == 2 else rest.pop(0)
    ym, yp, mm, mp, pm, pp = rest

    def moved(value, step_x, step_y):
        pairs = []
        for x in range(count_x):
            for y in range(count_y):
                if 0 <= x + step_x < count_x and 0 <= y + step_y < count_y:
                    pairs.append((x * count_y + y, (x + step_x) * count_y + y + step_y))
        return lax.ppermute(value, ("gx", "gy"), pairs)

    from_xp, from_xm = moved(down, -1, 0), moved(up, 1, 0)
    from_yp, from_ym = moved(ym, 0, -1), moved(yp, 0, 1)
    from_pp, from_pm = moved(mm, -1, -1), moved(mp, -1, 1)
    from_mp, from_mm = moved(pm, 1, -1), moved(pp, 1, 1)

    nodes = (planes + 1) * (rows + 1)
    wide = (planes + 3) * (rows + 3)
    acc = pltpu.VMEM(((planes + 3) * (rows + 1), block, LANES), f32)
    field = pltpu.VMEM((nodes, block, LANES), f32)
    both, system = pl.pallas_call(
        functools.partial(main_kernel, sizes),
        out_shape=[
            jax.ShapeDtypeStruct((4 * cases, nodes * 3 * LANES), bf16),
            jax.ShapeDtypeStruct((3 * cases, LANES), f32),
        ],
        in_specs=[VMEM] * 9,
        out_specs=[VMEM] * 2,
        scratch_shapes=[
            pltpu.VMEM((planes + 4, up8(rows + 4), LANES), f32),
            pltpu.VMEM((planes + 3, up8(rows + 3), LANES), f32),
            pltpu.VMEM((wide, block, LANES), f32),
            pltpu.VMEM((wide, block, LANES), f32),
            pltpu.VMEM((wide, block, LANES), f32),
            acc, acc, field, field, field, field,
            pltpu.VMEM((4 * cases, planes * rows * 3 * LANES), bf16),
            pltpu.VMEM((2 * cases, nodes * 3 * LANES), bf16),
        ],
        compiler_params=PARAMS,
        name="operator",
    )(own, from_xm, from_xp, from_ym, from_yp, from_mm, from_mp, from_pm, from_pp)

    system = lax.psum(system, ("gx", "gy"))

    weighted = pl.pallas_call(
        functools.partial(solve_kernel, sizes),
        out_shape=jax.ShapeDtypeStruct((planes, rows, LANES), f32),
        in_specs=[VMEM] * 3,
        out_specs=VMEM,
        scratch_shapes=[
            pltpu.VMEM((2 * cases, LANES), f32),
            field,
            field,
            pltpu.VMEM((rows, 8, LANES), f32),
        ],
        compiler_params=PARAMS,
        name="solve",
    )(system, both, levels)

    below = moved(weighted[planes - 2 :], 1, 0)
    above = moved(weighted[:2], -1, 0)
    column = jnp.concatenate([below, weighted, above], 0)
    left = moved(column[:, rows - 2 :], 0, 1)
    right = moved(column[:, :2], 0, -1)
    start = jnp.stack([lax.axis_index("gx") * planes, lax.axis_index("gy") * rows])
    totals = (count_x * planes, count_y * rows)
    return pl.pallas_call(
        functools.partial(filter_kernel, sizes, totals),
        out_shape=jax.ShapeDtypeStruct((planes, rows, LANES), f32),
        in_specs=[pl.BlockSpec(memory_space=pltpu.SMEM)] + [VMEM] * 6,
        out_specs=VMEM,
        scratch_shapes=[pltpu.VMEM((planes + 4, rows + 4, LANES), f32)] * 2,
        compiler_params=PARAMS,
        name="cone",
    )(start.astype(jnp.int32), below, above, weighted, left, right, levels)


def solution(mesh):
    return jax.shard_map(
        local,
        mesh=mesh,
        in_specs=(P(None, None, "gx", "gy", None), P("gx", "gy", None), P("gx", "gy", None)),
        out_specs=P("gx", "gy", None),
        check_vma=False,
    )
```

profile of v0, /device:TPU:0, one launch (start us, length us, event | category | flops | bytes accessed | tf_op | source)
XLA Modules:
  0.0 109.1 jit_solution(5643414764638224110)
XLA Ops:
  0.0 0.0 copy-start
  0.0 1.1 copy-done
  1.1 0.0 copy-start.1
  1.1 0.7 copy-done.1
  1.8 0.0 copy-start.3
  1.8 0.7 copy-done.3
  2.5 0.0 copy-start.2
  2.5 0.2 pack.1
  2.6 1.3 %collective-permute-start.1 = (f32[1168,128]{1,0:T(8,128)S(1)}, f32[1168,128]{1,0:T(8,128)S(1)}, u32[]{:S(2)}, u32[]{:S(2)}) collective-permute-start(f32[1168,128]{1,0:T(8,128)S(1)} %get-tuple-element.15.own), channel_id=1, source_target_pairs={{4,0},{5,1},{6,2},{7,3},{8,4},{9,5},{10,6},{11,7},{12,8},{13,9},{1... | collective-permute-start | bytes 1794056 | tf_op jit(solution)/shard_map/ppermute | solution.py:527
  3.9 3.0 %collective-permute-start = (f32[592,128]{1,0:T(8,128)S(1)}, f32[592,128]{1,0:T(8,128)S(1)}, u32[]{:S(2)}, u32[]{:S(2)}) collective-permute-start(f32[592,128]{1,0:T(8,128)S(1)} %get-tuple-element.16), channel_id=1, source_target_pairs={{0,4},{1,5},{2,6},{3,7},{4,8},{5,9},{6,10},{7,11},{8,12},{9,13},{1... | collective-permute-start | bytes 909320 | tf_op jit(solution)/shard_map/ppermute | solution.py:527
  7.0 4.9 %collective-permute-start.2 = (f32[152,128]{1,0:T(8,128)S(1)}, f32[152,128]{1,0:T(8,128)S(1)}, u32[]{:S(2)}, u32[]{:S(2)}) collective-permute-start(f32[152,128]{1,0:T(8,128)S(1)} %get-tuple-element.17), channel_id=1, source_target_pairs={{0,1},{1,2},{2,3},{4,5},{5,6},{6,7},{8,9},{9,10},{10,11},{12,13},{... | collective-permute-start | bytes 233480 | tf_op jit(solution)/shard_map/ppermute | solution.py:527
  11.9 3.9 %collective-permute-start.4 = (f32[80,128]{1,0:T(8,128)S(1)}, f32[80,128]{1,0:T(8,128)S(1)}, u32[]{:S(2)}, u32[]{:S(2)}) collective-permute-start(f32[80,128]{1,0:T(8,128)S(1)} %get-tuple-element.19), channel_id=1, source_target_pairs={{0,5},{1,6},{2,7},{4,9},{5,10},{6,11},{8,13},{9,14},{10,15},{12,17... | collective-permute-start | bytes 122888 | tf_op jit(solution)/shard_map/ppermute | solution.py:527
  15.8 0.7 collective-permute-start.5
  16.5 1.2 %collective-permute-done.4.mm = f32[80,128]{1,0:T(8,128)S(1)} collective-permute-done((f32[80,128]{1,0:T(8,128)S(1)}, f32[80,128]{1,0:T(8,128)S(1)}, u32[]{:S(2)}, u32[]{:S(2)}) %collective-permute-start.4) | collective-permute-done | bytes 40992 | tf_op jit(solution)/shard_map/ppermute | solution.py:527
  17.7 1.3 %collective-permute-start.3 = (f32[296,128]{1,0:T(8,128)S(1)}, f32[296,128]{1,0:T(8,128)S(1)}, u32[]{:S(2)}, u32[]{:S(2)}) collective-permute-start(f32[296,128]{1,0:T(8,128)S(1)} %get-tuple-element.18), channel_id=1, source_target_pairs={{1,0},{2,1},{3,2},{5,4},{6,5},{7,6},{9,8},{10,9},{11,10},{13,12},{... | collective-permute-start | bytes 454664 | tf_op jit(solution)/shard_map/ppermute | solution.py:527
  19.0 0.0 collective-permute-done.2.ym
  19.0 1.3 %collective-permute-start.7 = (f32[296,128]{1,0:T(8,128)S(1)}, f32[296,128]{1,0:T(8,128)S(1)}, u32[]{:S(2)}, u32[]{:S(2)}) collective-permute-start(f32[296,128]{1,0:T(8,128)S(1)} %get-tuple-element.22), channel_id=1, source_target_pairs={{5,0},{6,1},{7,2},{9,4},{10,5},{11,6},{13,8},{14,9},{15,10},{17,12... | collective-permute-start | bytes 454664 | tf_op jit(solution)/shard_map/ppermute | solution.py:527
  20.3 0.0 collective-permute-done.5.mp
  20.3 0.7 collective-permute-start.6
  21.0 0.0 collective-permute-done.6.pm
  21.0 4.7 %collective-permute-done.3.yp = f32[296,128]{1,0:T(8,128)S(1)} collective-permute-done((f32[296,128]{1,0:T(8,128)S(1)}, f32[296,128]{1,0:T(8,128)S(1)}, u32[]{:S(2)}, u32[]{:S(2)}) %collective-permute-start.3) | collective-permute-done | bytes 151584 | tf_op jit(solution)/shard_map/ppermute | solution.py:527
  25.7 2.6 %collective-permute-done.7.pp = f32[296,128]{1,0:T(8,128)S(1)} collective-permute-done((f32[296,128]{1,0:T(8,128)S(1)}, f32[296,128]{1,0:T(8,128)S(1)}, u32[]{:S(2)}, u32[]{:S(2)}) %collective-permute-start.7) | collective-permute-done | bytes 151584 | tf_op jit(solution)/shard_map/ppermute | solution.py:527
  28.3 0.0 collective-permute-done.xm
  28.3 0.0 collective-permute-done.1.xp
  28.3 15.6 %operator.1 = (bf16[96,10368]{1,0:T(8,128)(2,1)S(1)}, f32[72,128]{1,0:T(8,128)S(1)}) custom-call(f32[1168,128]{1,0:T(8,128)S(1)} %get-tuple-element.15.own, f32[592,128]{1,0:T(8,128)S(1)} %collective-permute-done.xm, f32[1168,128]{1,0:T(8,128)S(1)} %collective-permute-done.1.xp, f32[152,128]{1,0:T(8,128)S(1)} %collective-permute-done.2.ym, ...), custom_call_target="tpu_custom_call" | custom-call | tf_op jit(solution)/shard_map/operator/pallas_call | solution.py:538
  43.9 42.4 %psum.7.system = f32[72,128]{1,0:T(8,128)S(1)} all-reduce(f32[72,128]{1,0:T(8,128)S(1)} %get-tuple-element.23), channel_id=1, replica_groups=mesh['gx'=8,'gy'=4] {'gx','gy'}, use_global_device_ids=true, to_apply=%region_0.0 | all-reduce | flops 9216 | bytes 73728 | tf_op jit(solution)/shard_map/psum | solution.py:560
  86.3 0.0 copy-done.2
  86.3 5.7 %solve.1.own = f32[2,8,128]{2,1,0:T(8,128)S(1)} custom-call(f32[72,128]{1,0:T(8,128)S(1)} %psum.7.system, bf16[96,10368]{1,0:T(8,128)(2,1)S(1)} %get-tuple-element.24.both, s32[2,8,128]{2,1,0:T(8,128)S(1)} %copy-done.2), custom_call_target="tpu_custom_call" | custom-call | tf_op jit(solution)/shard_map/solve/pallas_call | solution.py:562
  92.0 1.3 %collective-permute-start.8 = (f32[2,8,128]{2,1,0:T(8,128)S(1)}, f32[2,8,128]{2,1,0:T(8,128)S(1)}, u32[]{:S(2)}, u32[]{:S(2)}) collective-permute-start(f32[2,8,128]{2,1,0:T(8,128)S(1)} %solve.1.own), channel_id=1, source_target_pairs={{0,4},{1,5},{2,6},{3,7},{4,8},{5,9},{6,10},{7,11},{8,12},{9,13},{1... | collective-permute-start | bytes 24584 | tf_op jit(solution)/shard_map/ppermute | solution.py:527
  93.3 1.3 %collective-permute-start.9 = (f32[2,8,128]{2,1,0:T(8,128)S(1)}, f32[2,8,128]{2,1,0:T(8,128)S(1)}, u32[]{:S(2)}, u32[]{:S(2)}) collective-permute-start(f32[2,8,128]{2,1,0:T(8,128)S(1)} %solve.1.own), channel_id=1, source_target_pairs={{4,0},{5,1},{6,2},{7,3},{8,4},{9,5},{10,6},{11,7},{12,8},{13,9},{1... | collective-permute-start | bytes 24584 | tf_op jit(solution)/shard_map/ppermute | solution.py:527
  94.6 0.0 collective-permute-done.8.below
  94.6 4.2 %collective-permute-done.9.above = f32[2,8,128]{2,1,0:T(8,128)S(1)} collective-permute-done((f32[2,8,128]{2,1,0:T(8,128)S(1)}, f32[2,8,128]{2,1,0:T(8,128)S(1)}, u32[]{:S(2)}, u32[]{:S(2)}) %collective-permute-start.9) | collective-permute-done | bytes 8224 | tf_op jit(solution)/shard_map/ppermute | solution.py:527
  98.8 3.5 %collective-permute-start.10 = (f32[6,2,128]{2,1,0:T(2,128)S(1)}, f32[6,2,128]{2,1,0:T(2,128)S(1)}, u32[]{:S(2)}, u32[]{:S(2)}) collective-permute-start(f32[6,2,128]{2,1,0:T(2,128)S(1)} %get-tuple-element.26), channel_id=1, source_target_pairs={{0,1},{1,2},{2,3},{4,5},{5,6},{6,7},{8,9},{9,10},{10,11},{12,13},{... | collective-permute-start | bytes 18440 | tf_op jit(solution)/shard_map/ppermute | solution.py:527
  102.3 1.3 %collective-permute-start.11 = (f32[6,2,128]{2,1,0:T(2,128)S(1)}, f32[6,2,128]{2,1,0:T(2,128)S(1)}, u32[]{:S(2)}, u32[]{:S(2)}) collective-permute-start(f32[6,2,128]{2,1,0:T(2,128)S(1)} %get-tuple-element.25), channel_id=1, source_target_pairs={{1,0},{2,1},{3,2},{5,4},{6,5},{7,6},{9,8},{10,9},{11,10},{13,12},{... | collective-permute-start | bytes 18440 | tf_op jit(solution)/shard_map/ppermute | solution.py:527
  103.6 0.1 pad_add_fusion.start
  103.7 0.0 collective-permute-done.10.left
  103.7 4.1 %collective-permute-done.11.right = f32[6,2,128]{2,1,0:T(2,128)S(1)} collective-permute-done((f32[6,2,128]{2,1,0:T(2,128)S(1)}, f32[6,2,128]{2,1,0:T(2,128)S(1)}, u32[]{:S(2)}, u32[]{:S(2)}) %collective-permute-start.11) | collective-permute-done | bytes 6176 | tf_op jit(solution)/shard_map/ppermute | solution.py:527
  107.9 1.3 %cone.1 = f32[2,8,128]{2,1,0:T(8,128)} custom-call(s32[2]{0:T(128)S(1)} %pad_add_fusion.start, f32[2,8,128]{2,1,0:T(8,128)S(1)} %collective-permute-done.8.below, f32[2,8,128]{2,1,0:T(8,128)S(1)} %collective-permute-done.9.above, f32[2,8,128]{2,1,0:T(8,128)S(1)} %solve.1.own, f32[6,2,128]{2,1,0:T(2,128)S(1)} %collective-permute-done.10.left, ...), custom_call_target="tpu_custom_call" | custom-call | tf_op jit(solution)/shard_map/cone/pallas_call | solution.py:584
  (1 shorter events, 0.0 us)
Async XLA Ops:
  0.0 1.1 copy-start
  1.1 0.7 copy-start.1
  1.8 0.7 copy-start.3
  2.5 83.8 %copy-start.2 = (s32[2,8,128]{2,1,0:T(8,128)S(1)}, s32[2,8,128]{2,1,0:T(8,128)}, u32[]{:S(2)}) copy-start(s32[2,8,128]{2,1,0:T(8,128)} %levels.5) | copy-start | bytes 24580
  2.6 25.7 %collective-permute-start.1 = (f32[1168,128]{1,0:T(8,128)S(1)}, f32[1168,128]{1,0:T(8,128)S(1)}, u32[]{:S(2)}, u32[]{:S(2)}) collective-permute-start(f32[1168,128]{1,0:T(8,128)S(1)} %get-tuple-element.15.own), channel_id=1, source_target_pairs={{4,0},{5,1},{6,2},{7,3},{8,4},{9,5},{10,6},{11,7},{12,8},{13,9},{1... | collective-permute-start | bytes 1794056 | tf_op jit(solution)/shard_map/ppermute | solution.py:527
  3.9 24.4 %collective-permute-start = (f32[592,128]{1,0:T(8,128)S(1)}, f32[592,128]{1,0:T(8,128)S(1)}, u32[]{:S(2)}, u32[]{:S(2)}) collective-permute-start(f32[592,128]{1,0:T(8,128)S(1)} %get-tuple-element.16), channel_id=1, source_target_pairs={{0,4},{1,5},{2,6},{3,7},{4,8},{5,9},{6,10},{7,11},{8,12},{9,13},{1... | collective-permute-start | bytes 909320 | tf_op jit(solution)/shard_map/ppermute | solution.py:527
  7.0 12.0 %collective-permute-start.2 = (f32[152,128]{1,0:T(8,128)S(1)}, f32[152,128]{1,0:T(8,128)S(1)}, u32[]{:S(2)}, u32[]{:S(2)}) collective-permute-start(f32[152,128]{1,0:T(8,128)S(1)} %get-tuple-element.17), channel_id=1, source_target_pairs={{0,1},{1,2},{2,3},{4,5},{5,6},{6,7},{8,9},{9,10},{10,11},{12,13},{... | collective-permute-start | bytes 233480 | tf_op jit(solution)/shard_map/ppermute | solution.py:527
  11.9 5.8 %collective-permute-start.4 = (f32[80,128]{1,0:T(8,128)S(1)}, f32[80,128]{1,0:T(8,128)S(1)}, u32[]{:S(2)}, u32[]{:S(2)}) collective-permute-start(f32[80,128]{1,0:T(8,128)S(1)} %get-tuple-element.19), channel_id=1, source_target_pairs={{0,5},{1,6},{2,7},{4,9},{5,10},{6,11},{8,13},{9,14},{10,15},{12,17... | collective-permute-start | bytes 122888 | tf_op jit(solution)/shard_map/ppermute | solution.py:527
  15.8 4.5 %collective-permute-start.5 = (f32[152,128]{1,0:T(8,128)S(1)}, f32[152,128]{1,0:T(8,128)S(1)}, u32[]{:S(2)}, u32[]{:S(2)}) collective-permute-start(f32[152,128]{1,0:T(8,128)S(1)} %get-tuple-element.20), channel_id=1, source_target_pairs={{1,4},{2,5},{3,6},{5,8},{6,9},{7,10},{9,12},{10,13},{11,14},{13,16... | collective-permute-start | bytes 233480 | tf_op jit(solution)/shard_map/ppermute | solution.py:527
  17.7 8.0 %collective-permute-start.3 = (f32[296,128]{1,0:T(8,128)S(1)}, f32[296,128]{1,0:T(8,128)S(1)}, u32[]{:S(2)}, u32[]{:S(2)}) collective-permute-start(f32[296,128]{1,0:T(8,128)S(1)} %get-tuple-element.18), channel_id=1, source_target_pairs={{1,0},{2,1},{3,2},{5,4},{6,5},{7,6},{9,8},{10,9},{11,10},{13,12},{... | collective-permute-start | bytes 454664 | tf_op jit(solution)/shard_map/ppermute | solution.py:527
  19.0 9.3 %collective-permute-start.7 = (f32[296,128]{1,0:T(8,128)S(1)}, f32[296,128]{1,0:T(8,128)S(1)}, u32[]{:S(2)}, u32[]{:S(2)}) collective-permute-start(f32[296,128]{1,0:T(8,128)S(1)} %get-tuple-element.22), channel_id=1, source_target_pairs={{5,0},{6,1},{7,2},{9,4},{10,5},{11,6},{13,8},{14,9},{15,10},{17,12... | collective-permute-start | bytes 454664 | tf_op jit(solution)/shard_map/ppermute | solution.py:527
  20.3 0.7 collective-permute-start.6
  92.0 2.6 %collective-permute-start.8 = (f32[2,8,128]{2,1,0:T(8,128)S(1)}, f32[2,8,128]{2,1,0:T(8,128)S(1)}, u32[]{:S(2)}, u32[]{:S(2)}) collective-permute-start(f32[2,8,128]{2,1,0:T(8,128)S(1)} %solve.1.own), channel_id=1, source_target_pairs={{0,4},{1,5},{2,6},{3,7},{4,8},{5,9},{6,10},{7,11},{8,12},{9,13},{1... | collective-permute-start | bytes 24584 | tf_op jit(solution)/shard_map/ppermute | solution.py:527
  93.3 5.5 %collective-permute-start.9 = (f32[2,8,128]{2,1,0:T(8,128)S(1)}, f32[2,8,128]{2,1,0:T(8,128)S(1)}, u32[]{:S(2)}, u32[]{:S(2)}) collective-permute-start(f32[2,8,128]{2,1,0:T(8,128)S(1)} %solve.1.own), channel_id=1, source_target_pairs={{4,0},{5,1},{6,2},{7,3},{8,4},{9,5},{10,6},{11,7},{12,8},{13,9},{1... | collective-permute-start | bytes 24584 | tf_op jit(solution)/shard_map/ppermute | solution.py:527
  98.8 4.9 %collective-permute-start.10 = (f32[6,2,128]{2,1,0:T(2,128)S(1)}, f32[6,2,128]{2,1,0:T(2,128)S(1)}, u32[]{:S(2)}, u32[]{:S(2)}) collective-permute-start(f32[6,2,128]{2,1,0:T(2,128)S(1)} %get-tuple-element.26), channel_id=1, source_target_pairs={{0,1},{1,2},{2,3},{4,5},{5,6},{6,7},{8,9},{9,10},{10,11},{12,13},{... | collective-permute-start | bytes 18440 | tf_op jit(solution)/shard_map/ppermute | solution.py:527
  102.3 5.5 %collective-permute-start.11 = (f32[6,2,128]{2,1,0:T(2,128)S(1)}, f32[6,2,128]{2,1,0:T(2,128)S(1)}, u32[]{:S(2)}, u32[]{:S(2)}) collective-permute-start(f32[6,2,128]{2,1,0:T(2,128)S(1)} %get-tuple-element.25), channel_id=1, source_target_pairs={{1,0},{2,1},{3,2},{5,4},{6,5},{7,6},{9,8},{10,9},{11,10},{13,12},{... | collective-permute-start | bytes 18440 | tf_op jit(solution)/shard_map/ppermute | solution.py:527
where the time goes:
time: 110 us; the launch traced here: 109 us
  blocking collectives  42.4 us (39%)
  starting transfers between devices  24.5 us (22%)
  Pallas kernels  22.7 us (21%)
  waiting for transfers between devices  16.8 us (15%)
  local copies, waits for them, and re-layouts  2.46 us (2%)
    psum x1, blocking collectives, local(): system = lax.psum(system, ('gx', 'gy'))  42.4 us
    ppermute x12, starting transfers between devices, moved(): return lax.ppermute(value, ('gx', 'gy'), pairs)  24.5 us
    ppermute x12, waiting for transfers between devices, moved(): return lax.ppermute(value, ('gx', 'gy'), pairs)  16.8 us
    pallas_call x1, Pallas kernels, local(): pl.pallas_call(functools.partial(main_kernel, sizes), out_shape=[jax.Shap...  15.6 us
    pallas_call x1, Pallas kernels, local(): pl.pallas_call(functools.partial(solve_kernel, sizes), out_shape=jax.Shap...  5.71 us
    unnamed x8, local copies, waits for them, and re-layouts  2.46 us
  transfers between devices with their start and end apart: 12, of which 5 were waited for; matrix products, arithmetic and copies ran while one was open for 0% of the time, Pallas kernels for 0%

commit v1 on v0

--- a/solution.py
+++ b/solution.py
@@ -183,7 +183,6 @@
     planes, rows, cases = sizes
     block = 3 * cases
     base = planes * rows * block
-    *down, ym, yp, mm, mp, pm, pp = rest
     for x in range(planes):
         density = 0.3 + 0.7 * levels[x].astype(f32) / (LEVELS - 1)
         stiff = density * density * density
@@ -195,37 +194,43 @@
                 start = x * rows * block + k * cases + c
                 own[pl.ds(start, rows, stride=block), :] = forces[k, c, x] * scale
 
-    def fill(ref, xs, ys, code_xs, code_ys):
+    def fill(ref, xs, code_xs):
+        size = len(xs) * rows * block
+        ref[:size, :] = own[xs[0] * rows * block : xs[0] * rows * block + size, :]
+        codes = base + code_xs[0] * rows
+        ref[size:, :] = own[codes : codes + len(code_xs) * rows, :]
+
+    fill(up, range(planes - 1, planes), range(planes - 2, planes))
+    for ref in rest:
+        fill(ref, range(2), range(2))
+
+
+def edge_kernel(sizes, own, xm, xp, ym, yp):
+    planes, rows, cases = sizes
+    block = 3 * cases
+    parts = (
+        (xm, rows * block, range(1), range(2)),
+        (own, planes * rows * block, range(planes), range(planes)),
+        (xp, 2 * rows * block, range(2), range(2)),
+    )
+    for ref, low, count, code in ((ym, 0, 2, 2), (yp, rows - 1, 1, 2)):
         line = 0
-        for x in xs:
-            for y in ys:
-                start = (x * rows + y) * block
-                ref[line : line + block, :] = own[start : start + block, :]
-                line += block
-        for x in code_xs:
-            for y in code_ys:
-                start = base + x * rows + y
-                ref[line : line + 1, :] = own[start : start + 1, :]
-                line += 1
+        for source, _, xs, _ in parts:
+            for x in xs:
+                start = (x * rows + low) * block
+                ref[line : line + count * block, :] = source[start : start + count * block, :]
+                line += count * block
+        for source, base, _, xs in parts:
+            for x in xs:
+                start = base + x * rows + (0 if low == 0 else rows - 2)
+                ref[line : line + code, :] = source[start : start + code, :]
+                line += code
         if line < ref.shape[0]:
             ref[line:, :] = jnp.zeros((ref.shape[0] - line, LANES), f32)
 
-    every_x, every_y = range(planes), range(rows)
-    first_x, last_x = range(2), range(planes - 2, planes)
-    first_y, last_y = range(2), range(rows - 2, rows)
-    fill(up, last_x[1:], every_y, last_x, every_y)
-    for ref in down:
-        fill(ref, first_x, every_y, first_x, every_y)
-    fill(ym, every_x, first_y, every_x, first_y)
-    fill(yp, every_x, last_y[1:], every_x, last_y)
-    fill(mm, first_x, first_y, first_x, first_y)
-    fill(mp, first_x, last_y[1:], first_x, last_y)
-    fill(pm, last_x[1:], first_y, last_x, first_y)
-    fill(pp, last_x[1:], last_y[1:], last_x, last_y)
-
 
 def main_kernel(
-    sizes, own, xm, xp, ym, yp, mm, mp, pm, pp, both_out, system_out, stiff_ref, inverse,
+    sizes, own, xm, xp, ym, yp, both_out, system_out, stiff_ref, inverse,
     start, sums, diffs, acc_s, acc_d, w_sums, w_diffs, acc2_s, acc2_d, right, second,
 ):
     planes, rows, cases = sizes
@@ -238,12 +243,8 @@
         (own, every_x, every_y, every_x, every_y),
         (xm, low, every_y, low2, every_y),
         (xp, high_x, every_y, high_x, every_y),
-        (ym, every_x, low, every_x, low2),
-        (yp, every_x, high_y, every_x, high_y),
-        (mm, low, low, low2, low2),
-        (mp, low, high_y, low2, high_y),
-        (pm, high_x, low, high_x, low2),
-        (pp, high_x, high_y, high_x, high_y),
+        (ym, range(-1, planes + 2), low, range(-2, planes + 2), low2),
+        (yp, range(-1, planes + 2), high_y, range(-2, planes + 2), high_y),
     )
     for ref, bx, by, cx, cy in regions:
         base = len(bx) * len(by) * block
@@ -369,11 +370,9 @@
     other = other[:two] + other[two:]
     other = other[:, :cases] + other[:, cases:]
     system_out[...] = jnp.zeros(system_out.shape, f32)
-    system_out[0:cases, 0:cases] = gram[:cases, cases:]
-    system_out[0:cases, cases:two] = other[:cases]
-    system_out[cases:two, 0:cases] = gram[cases:, cases:]
-    system_out[cases:two, cases:two] = other[cases:]
-    system_out[two : two + cases, 0:two] = gram[:cases]
+    system_out[:, 0:two] = gram[:cases]
+    system_out[:, two : two + cases] = other[:cases]
+    system_out[:, two + cases : 2 * two] = other[cases:]
 
 
 def solve_kernel(sizes, system, both, levels, out, mixing, sums, diffs, energy):
@@ -381,7 +380,10 @@
     two = 2 * cases
     nodes_y = rows + 1
     count = planes * rows
-    table = system[...]
+    total = jnp.sum(system[...], axis=0)
+    table = jnp.concatenate(
+        [pltpu.roll(total, LANES - cases, 1), pltpu.roll(total, LANES - two, 1), total], 0
+    )
     lane = lax.broadcasted_iota(jnp.int32, (1, LANES), 1)
     gone = 0
     for pivot in range(two):
@@ -448,14 +450,20 @@
     lax.fori_loop(0, planes, step, 0)
 
 
-def filter_kernel(sizes, totals, start, below, above, own, left, right, levels, out, wide, there):
+def filter_kernel(sizes, counts, start, blocks, levels, out, wide, there):
     planes, rows, _ = sizes
+    totals = (counts[0] * planes, counts[1] * rows)
     weight = [2.5 - math.sqrt(q) for q in range(7)]
-    wide[0:2, 2 : 2 + rows, :] = below[...]
-    wide[2 : 2 + planes, 2 : 2 + rows, :] = own[...]
-    wide[2 + planes :, 2 : 2 + rows, :] = above[...]
-    wide[:, 0:2, :] = left[...]
-    wide[:, 2 + rows : 4 + rows, :] = right[...]
+    sides_x = ((-1, planes - 2, planes, 0), (0, 0, planes, 2), (1, 0, 2, 2 + planes))
+    sides_y = ((-1, rows - 2, rows, 0), (0, 0, rows, 2), (1, 0, 2, 2 + rows))
+    for step_x, x0, x1, to_x in sides_x:
+        for step_y, y0, y1, to_y in sides_y:
+            at_x = start[0] // planes + step_x
+            at_y = start[1] // rows + step_y
+            inside = (at_x >= 0) & (at_x < counts[0]) & (at_y >= 0) & (at_y < counts[1])
+            index = jnp.where(inside, at_x * counts[1] + at_y, 0)
+            value = blocks[index, x0:x1, y0:y1, :]
+            wide[to_x : to_x + x1 - x0, to_y : to_y + y1 - y0, :] = jnp.where(inside, value, 0.0)
     y = lax.broadcasted_iota(jnp.int32, (rows + 4, LANES), 0) + (start[1] - 2)
     in_y = jnp.logical_and(y >= 0, y < totals[1])
     for x in range(planes + 4):
@@ -503,33 +511,33 @@
 
     whole = shape(planes * rows, planes * rows)
     down = [] if planes == 2 else [shape(2 * rows, 2 * rows)]
-    packed = pl.pallas_call(
+    own, up, *down = pl.pallas_call(
         functools.partial(pack_kernel, sizes),
-        out_shape=[
-            whole, shape(rows, 2 * rows), *down, shape(2 * planes, 2 * planes),
-            shape(planes, 2 * planes), shape(4, 4), shape(2, 4), shape(2, 4), shape(1, 4),
-        ],
+        out_shape=[whole, shape(rows, 2 * rows), *down],
         in_specs=[VMEM] * 3,
-        out_specs=[VMEM] * (8 + len(down)),
+        out_specs=[VMEM] * (2 + len(down)),
         compiler_params=PARAMS,
         name="pack",
     )(forces, levels, supports)
-    own, up, *rest = packed
-    down = own if planes == 2 else rest.pop(0)
-    ym, yp, mm, mp, pm, pp = rest
-
-    def moved(value, step_x, step_y):
-        pairs = []
-        for x in range(count_x):
-            for y in range(count_y):
-                if 0 <= x + step_x < count_x and 0 <= y + step_y < count_y:
-                    pairs.append((x * count_y + y, (x + step_x) * count_y + y + step_y))
-        return lax.ppermute(value, ("gx", "gy"), pairs)
-
-    from_xp, from_xm = moved(down, -1, 0), moved(up, 1, 0)
-    from_yp, from_ym = moved(ym, 0, -1), moved(yp, 0, 1)
-    from_pp, from_pm = moved(mm, -1, -1), moved(mp, -1, 1)
-    from_mp, from_mm = moved(pm, 1, -1), moved(pp, 1, 1)
+
+    def moved(value, axis, step):
+        count = lax.axis_size(axis)
+        pairs = [(i, i + step) for i in range(count) if 0 <= i + step < count]
+        return lax.ppermute(value, axis, pairs)
+
+    from_xp = moved(down[0] if down else own, "gx", -1)
+    from_xm = moved(up, "gx", 1)
+    ym, yp = pl.pallas_call(
+        functools.partial(edge_kernel, sizes),
+        out_shape=[
+            shape(2 * (planes + 3), 2 * (planes + 4)), shape(planes + 3, 2 * (planes + 4))
+        ],
+        in_specs=[VMEM] * 3,
+        out_specs=[VMEM] * 2,
+        compiler_params=PARAMS,
+        name="edges",
+    )(own, from_xm, from_xp)
+    from_yp, from_ym = moved(ym, "gy", -1), moved(yp, "gy", 1)
 
     nodes = (planes + 1) * (rows + 1)
     wide = (planes + 3) * (rows + 3)
@@ -539,9 +547,9 @@
         functools.partial(main_kernel, sizes),
         out_shape=[
             jax.ShapeDtypeStruct((4 * cases, nodes * 3 * LANES), bf16),
-            jax.ShapeDtypeStruct((3 * cases, LANES), f32),
+            jax.ShapeDtypeStruct((cases, LANES), f32),
         ],
-        in_specs=[VMEM] * 9,
+        in_specs=[VMEM] * 5,
         out_specs=[VMEM] * 2,
         scratch_shapes=[
             pltpu.VMEM((planes + 4, up8(rows + 4), LANES), f32),
@@ -555,9 +563,9 @@
         ],
         compiler_params=PARAMS,
         name="operator",
-    )(own, from_xm, from_xp, from_ym, from_yp, from_mm, from_mp, from_pm, from_pp)
-
-    system = lax.psum(system, ("gx", "gy"))
+    )(own, from_xm, from_xp, from_ym, from_yp)
+
+    system = lax.all_gather(system, ("gx", "gy"))
 
     weighted = pl.pallas_call(
         functools.partial(solve_kernel, sizes),
@@ -574,22 +582,17 @@
         name="solve",
     )(system, both, levels)
 
-    below = moved(weighted[planes - 2 :], 1, 0)
-    above = moved(weighted[:2], -1, 0)
-    column = jnp.concatenate([below, weighted, above], 0)
-    left = moved(column[:, rows - 2 :], 0, 1)
-    right = moved(column[:, :2], 0, -1)
+    blocks = lax.all_gather(weighted, ("gx", "gy"))
     start = jnp.stack([lax.axis_index("gx") * planes, lax.axis_index("gy") * rows])
-    totals = (count_x * planes, count_y * rows)
     return pl.pallas_call(
-        functools.partial(filter_kernel, sizes, totals),
+        functools.partial(filter_kernel, sizes, (count_x, count_y)),
         out_shape=jax.ShapeDtypeStruct((planes, rows, LANES), f32),
-        in_specs=[pl.BlockSpec(memory_space=pltpu.SMEM)] + [VMEM] * 6,
+        in_specs=[pl.BlockSpec(memory_space=pltpu.SMEM)] + [VMEM] * 2,
         out_specs=VMEM,
         scratch_shapes=[pltpu.VMEM((planes + 4, rows + 4, LANES), f32)] * 2,
         compiler_params=PARAMS,
         name="cone",
-    )(start.astype(jnp.int32), below, above, weighted, left, right, levels)
+    )(start.astype(jnp.int32), blocks, levels)
 
 
 def solution(mesh):

time: 110 us -> 186 us (1.69)
  the two profiles are of different devices: /device:TPU:0 before, /device:TPU:12 now
where the time goes in v1:
time: 186 us
  blocking collectives  136 us (73%)
  Pallas kernels  22.8 us (12%)
  waiting for transfers between devices  14.4 us (8%)
  starting transfers between devices  10.5 us (6%)
  local copies, waits for them, and re-layouts  2.46 us (1%)
    all_gather x1, blocking collectives, local(): blocks = lax.all_gather(weighted, ('gx', 'gy'))  68.4 us
    all_gather x1, blocking collectives, local(): system = lax.all_gather(system, ('gx', 'gy'))  67.2 us
    pallas_call x1, Pallas kernels, local(): pl.pallas_call(functools.partial(main_kernel, sizes), out_shape=[jax.Shap...  15.5 us
    ppermute x4, waiting for transfers between devices, moved(): return lax.ppermute(value, axis, pairs)  14.4 us
    ppermute x4, starting transfers between devices, moved(): return lax.ppermute(value, axis, pairs)  10.5 us
    pallas_call x1, Pallas kernels, local(): pl.pallas_call(functools.partial(solve_kernel, sizes), out_shape=jax.Shap...  5.84 us
  transfers between devices with their start and end apart: 4, of which 3 were waited for; matrix products, arithmetic and copies ran while one was open for 0% of the time, Pallas kernels for 0%

profile of v1, /device:TPU:12, one launch (start us, length us, event | category | flops | bytes accessed | tf_op | source)
XLA Modules:
  0.0 186.0 jit_solution(5727508256870408069)
XLA Ops:
  0.0 0.0 copy-start
  0.0 1.1 copy-done
  1.1 0.0 copy-start.1
  1.1 0.7 copy-done.1
  1.8 0.0 copy-start.3
  1.8 0.7 copy-done.3
  2.5 0.1 pack.1
  2.6 2.8 %collective-permute-start.1 = (f32[1168,128]{1,0:T(8,128)S(1)}, f32[1168,128]{1,0:T(8,128)S(1)}, u32[]{:S(2)}, u32[]{:S(2)}) collective-permute-start(f32[1168,128]{1,0:T(8,128)S(1)} %get-tuple-element.11.own), channel_id=1, source_target_pairs={{4,0},{8,4},{12,8},{16,12},{20,16},{24,20},{28,24},{5,1},{9,5},{13... | collective-permute-start | bytes 1794056 | tf_op jit(solution)/shard_map/ppermute | solution.py:526
  5.4 0.0 copy-start.2
  5.4 1.9 %collective-permute-start = (f32[592,128]{1,0:T(8,128)S(1)}, f32[592,128]{1,0:T(8,128)S(1)}, u32[]{:S(2)}, u32[]{:S(2)}) collective-permute-start(f32[592,128]{1,0:T(8,128)S(1)} %get-tuple-element.12), channel_id=1, source_target_pairs={{0,4},{4,8},{8,12},{12,16},{16,20},{20,24},{24,28},{1,5},{5,9},{9,... | collective-permute-start | bytes 909320 | tf_op jit(solution)/shard_map/ppermute | solution.py:526
  7.3 9.8 %collective-permute-done.xm = f32[592,128]{1,0:T(8,128)S(1)} collective-permute-done((f32[592,128]{1,0:T(8,128)S(1)}, f32[592,128]{1,0:T(8,128)S(1)}, u32[]{:S(2)}, u32[]{:S(2)}) %collective-permute-start) | collective-permute-done | bytes 303136 | tf_op jit(solution)/shard_map/ppermute | solution.py:526
  17.1 0.0 collective-permute-done.1.xp
  17.2 2.4 %collective-permute-start.3 = (f32[736,128]{1,0:T(8,128)S(1)}, f32[736,128]{1,0:T(8,128)S(1)}, u32[]{:S(2)}, u32[]{:S(2)}) collective-permute-start(f32[736,128]{1,0:T(8,128)S(1)} %get-tuple-element.14), channel_id=1, source_target_pairs={{1,0},{2,1},{3,2},{5,4},{6,5},{7,6},{9,8},{10,9},{11,10},{13,12},{... | collective-permute-start | bytes 1130504 | tf_op jit(solution)/shard_map/ppermute | solution.py:526
  19.5 3.5 %collective-permute-start.2 = (f32[376,128]{1,0:T(8,128)S(1)}, f32[376,128]{1,0:T(8,128)S(1)}, u32[]{:S(2)}, u32[]{:S(2)}) collective-permute-start(f32[376,128]{1,0:T(8,128)S(1)} %get-tuple-element.13), channel_id=1, source_target_pairs={{0,1},{1,2},{2,3},{4,5},{5,6},{6,7},{8,9},{9,10},{10,11},{12,13},{... | collective-permute-start | bytes 577544 | tf_op jit(solution)/shard_map/ppermute | solution.py:526
  23.0 0.1 pad_add_fusion.start
  23.1 3.9 %collective-permute-done.2.ym = f32[376,128]{1,0:T(8,128)S(1)} collective-permute-done((f32[376,128]{1,0:T(8,128)S(1)}, f32[376,128]{1,0:T(8,128)S(1)}, u32[]{:S(2)}, u32[]{:S(2)}) %collective-permute-start.2) | collective-permute-done | bytes 192544 | tf_op jit(solution)/shard_map/ppermute | solution.py:526
  27.1 0.7 collective-permute-done.3.yp
  27.7 15.5 %operator.1 = (bf16[96,10368]{1,0:T(8,128)(2,1)S(1)}, f32[24,128]{1,0:T(8,128)S(1)}) custom-call(f32[1168,128]{1,0:T(8,128)S(1)} %get-tuple-element.11.own, f32[592,128]{1,0:T(8,128)S(1)} %collective-permute-done.xm, f32[1168,128]{1,0:T(8,128)S(1)} %collective-permute-done.1.xp, f32[376,128]{1,0:T(8,128)S(1)} %collective-permute-done.2.ym, ...), custom_call_target="tpu_custom_call" | custom-call | tf_op jit(solution)/shard_map/operator/pallas_call | solution.py:546
  43.2 67.2 %all-gather = f32[768,128]{1,0:T(8,128)S(1)} all-gather(f32[24,128]{1,0:T(8,128)S(1)} %get-tuple-element.15), channel_id=2, replica_groups=mesh['gx'=8,'gy'=4] {'gx','gy'}, dimensions={0}, use_global_device_ids=true | all-gather | bytes 405504 | tf_op jit(solution)/shard_map/all_gather | solution.py:568
  110.4 0.0 copy-done.2
  110.4 5.8 %solve.1 = f32[2,8,128]{2,1,0:T(8,128)S(1)} custom-call(f32[32,24,128]{2,1,0:T(8,128)S(1)} %bitcast.4, bf16[96,10368]{1,0:T(8,128)(2,1)S(1)} %get-tuple-element.16.both, s32[2,8,128]{2,1,0:T(8,128)S(1)} %copy-done.2), custom_call_target="tpu_custom_call" | custom-call | tf_op jit(solution)/shard_map/solve/pallas_call | solution.py:570
  116.3 68.4 %all-gather.1 = f32[64,8,128]{2,1,0:T(8,128)S(1)} all-gather(f32[2,8,128]{2,1,0:T(8,128)S(1)} %solve.1), channel_id=3, replica_groups=mesh['gx'=8,'gy'=4] {'gx','gy'}, dimensions={0}, use_global_device_ids=true | all-gather | bytes 270336 | tf_op jit(solution)/shard_map/all_gather | solution.py:585
  184.7 1.3 cone.1
  (1 shorter events, 0.0 us)
Async XLA Ops:
  0.0 1.1 copy-start
  1.1 0.7 copy-start.1
  1.8 0.7 copy-start.3
  2.6 14.5 %collective-permute-start.1 = (f32[1168,128]{1,0:T(8,128)S(1)}, f32[1168,128]{1,0:T(8,128)S(1)}, u32[]{:S(2)}, u32[]{:S(2)}) collective-permute-start(f32[1168,128]{1,0:T(8,128)S(1)} %get-tuple-element.11.own), channel_id=1, source_target_pairs={{4,0},{8,4},{12,8},{16,12},{20,16},{24,20},{28,24},{5,1},{9,5},{13... | collective-permute-start | bytes 1794056 | tf_op jit(solution)/shard_map/ppermute | solution.py:526
  5.4 105.1 %copy-start.2 = (s32[2,8,128]{2,1,0:T(8,128)S(1)}, s32[2,8,128]{2,1,0:T(8,128)}, u32[]{:S(2)}) copy-start(s32[2,8,128]{2,1,0:T(8,128)} %levels.5) | copy-start | bytes 24580
  5.4 11.7 %collective-permute-start = (f32[592,128]{1,0:T(8,128)S(1)}, f32[592,128]{1,0:T(8,128)S(1)}, u32[]{:S(2)}, u32[]{:S(2)}) collective-permute-start(f32[592,128]{1,0:T(8,128)S(1)} %get-tuple-element.12), channel_id=1, source_target_pairs={{0,4},{4,8},{8,12},{12,16},{16,20},{20,24},{24,28},{1,5},{5,9},{9,... | collective-permute-start | bytes 909320 | tf_op jit(solution)/shard_map/ppermute | solution.py:526
  17.2 10.5 %collective-permute-start.3 = (f32[736,128]{1,0:T(8,128)S(1)}, f32[736,128]{1,0:T(8,128)S(1)}, u32[]{:S(2)}, u32[]{:S(2)}) collective-permute-start(f32[736,128]{1,0:T(8,128)S(1)} %get-tuple-element.14), channel_id=1, source_target_pairs={{1,0},{2,1},{3,2},{5,4},{6,5},{7,6},{9,8},{10,9},{11,10},{13,12},{... | collective-permute-start | bytes 1130504 | tf_op jit(solution)/shard_map/ppermute | solution.py:526
  19.5 7.5 %collective-permute-start.2 = (f32[376,128]{1,0:T(8,128)S(1)}, f32[376,128]{1,0:T(8,128)S(1)}, u32[]{:S(2)}, u32[]{:S(2)}) collective-permute-start(f32[376,128]{1,0:T(8,128)S(1)} %get-tuple-element.13), channel_id=1, source_target_pairs={{0,1},{1,2},{2,3},{4,5},{5,6},{6,7},{8,9},{9,10},{10,11},{12,13},{... | collective-permute-start | bytes 577544 | tf_op jit(solution)/shard_map/ppermute | solution.py:526

commit v2 on v1

--- a/solution.py
+++ b/solution.py
@@ -565,7 +565,11 @@
         name="operator",
     )(own, from_xm, from_xp, from_ym, from_yp)
 
-    system = lax.all_gather(system, ("gx", "gy"))
+    def gathered(value):
+        copies = jnp.broadcast_to(value[None], (count_x * count_y, *value.shape))
+        return lax.all_to_all(copies, ("gx", "gy"), 0, 0)
+
+    system = gathered(system)
 
     weighted = pl.pallas_call(
         functools.partial(solve_kernel, sizes),
@@ -582,7 +586,7 @@
         name="solve",
     )(system, both, levels)
 
-    blocks = lax.all_gather(weighted, ("gx", "gy"))
+    blocks = gathered(weighted)
     start = jnp.stack([lax.axis_index("gx") * planes, lax.axis_index("gy") * rows])
     return pl.pallas_call(
         functools.partial(filter_kernel, sizes, (count_x, count_y)),

time: 186 us -> 82.9 us (0.45)
  the two profiles are of different devices: /device:TPU:12 before, /device:TPU:0 now
where the time goes in v2:
time: 82.9 us; the launch traced here: 82.5 us
  blocking collectives  26.4 us (32%)
  Pallas kernels  22.7 us (27%)
  starting transfers between devices  15.1 us (18%)
  waiting for transfers between devices  14.9 us (18%)
  local copies, waits for them, and re-layouts  3.22 us (4%)
    all_to_all x1, blocking collectives, gathered(): return lax.all_to_all(copies, ('gx', 'gy'), 0, 0)  26.4 us
    pallas_call x1, Pallas kernels, local(): pl.pallas_call(functools.partial(main_kernel, sizes), out_shape=[jax.Shap...  15.4 us
    ppermute x4, starting transfers between devices, moved(): return lax.ppermute(value, axis, pairs)  11.2 us
    all_to_all x1, waiting for transfers between devices, gathered(): return lax.all_to_all(copies, ('gx', 'gy'), 0, 0)  10.1 us
    pallas_call x1, Pallas kernels, local(): pl.pallas_call(functools.partial(solve_kernel, sizes), out_shape=jax.Shap...  5.85 us
    ppermute x4, waiting for transfers between devices, moved(): return lax.ppermute(value, axis, pairs)  4.82 us
    all_to_all x1, starting transfers between devices, gathered(): return lax.all_to_all(copies, ('gx', 'gy'), 0, 0)  3.86 us
    unnamed x8, local copies, waits for them, and re-layouts  2.46 us
  transfers between devices with their start and end apart: 5, of which 4 were waited for; matrix products, arithmetic and copies ran while one was open for 0% of the time, Pallas kernels for 0%

profile of v2, /device:TPU:0, one launch (start us, length us, event | category | flops | bytes accessed | tf_op | source)
XLA Modules:
  0.0 82.5 jit_solution(3524619924231657011)
XLA Ops:
  0.0 0.0 copy-start
  0.0 1.1 %copy-done = f32[3,24,2,8,128]{4,3,2,1,0:T(8,128)S(1)} copy-done((f32[3,24,2,8,128]{4,3,2,1,0:T(8,128)S(1)}, f32[3,24,2,8,128]{4,3,2,1,0:T(8,128)}, u32[]{:S(2)}) %copy-start) | copy-done | bytes 589848
  1.1 0.0 copy-start.1
  1.1 0.7 copy-done.1
  1.8 0.0 copy-start.3
  1.8 0.7 copy-done.3
  2.5 0.1 pack.1
  2.6 1.3 %collective-permute-start.1 = (f32[1168,128]{1,0:T(8,128)S(1)}, f32[1168,128]{1,0:T(8,128)S(1)}, u32[]{:S(2)}, u32[]{:S(2)}) collective-permute-start(f32[1168,128]{1,0:T(8,128)S(1)} %get-tuple-element.11.own), channel_id=1, source_target_pairs={{4,0},{8,4},{12,8},{16,12},{20,16},{24,20},{28,24},{5,1},{9,5},{13... | collective-permute-start | bytes 1794056 | tf_op jit(solution)/shard_map/ppermute | solution.py:526
  3.9 3.0 %collective-permute-start = (f32[592,128]{1,0:T(8,128)S(1)}, f32[592,128]{1,0:T(8,128)S(1)}, u32[]{:S(2)}, u32[]{:S(2)}) collective-permute-start(f32[592,128]{1,0:T(8,128)S(1)} %get-tuple-element.12), channel_id=1, source_target_pairs={{0,4},{4,8},{8,12},{12,16},{16,20},{20,24},{24,28},{1,5},{5,9},{9,... | collective-permute-start | bytes 909320 | tf_op jit(solution)/shard_map/ppermute | solution.py:526
  6.9 1.2 %collective-permute-done.xm = f32[592,128]{1,0:T(8,128)S(1)} collective-permute-done((f32[592,128]{1,0:T(8,128)S(1)}, f32[592,128]{1,0:T(8,128)S(1)}, u32[]{:S(2)}, u32[]{:S(2)}) %collective-permute-start) | collective-permute-done | bytes 303136 | tf_op jit(solution)/shard_map/ppermute | solution.py:526
  8.1 0.0 collective-permute-done.1.xp
  8.2 0.0 copy-start.2
  8.2 1.3 %collective-permute-start.3 = (f32[736,128]{1,0:T(8,128)S(1)}, f32[736,128]{1,0:T(8,128)S(1)}, u32[]{:S(2)}, u32[]{:S(2)}) collective-permute-start(f32[736,128]{1,0:T(8,128)S(1)} %get-tuple-element.14), channel_id=1, source_target_pairs={{1,0},{2,1},{3,2},{5,4},{6,5},{7,6},{9,8},{10,9},{11,10},{13,12},{... | collective-permute-start | bytes 1130504 | tf_op jit(solution)/shard_map/ppermute | solution.py:526
  9.5 5.6 %collective-permute-start.2 = (f32[376,128]{1,0:T(8,128)S(1)}, f32[376,128]{1,0:T(8,128)S(1)}, u32[]{:S(2)}, u32[]{:S(2)}) collective-permute-start(f32[376,128]{1,0:T(8,128)S(1)} %get-tuple-element.13), channel_id=1, source_target_pairs={{0,1},{1,2},{2,3},{4,5},{5,6},{6,7},{8,9},{9,10},{10,11},{12,13},{... | collective-permute-start | bytes 577544 | tf_op jit(solution)/shard_map/ppermute | solution.py:526
  15.1 3.1 %collective-permute-done.2.ym = f32[376,128]{1,0:T(8,128)S(1)} collective-permute-done((f32[376,128]{1,0:T(8,128)S(1)}, f32[376,128]{1,0:T(8,128)S(1)}, u32[]{:S(2)}, u32[]{:S(2)}) %collective-permute-start.2) | collective-permute-done | bytes 192544 | tf_op jit(solution)/shard_map/ppermute | solution.py:526
  18.2 0.5 collective-permute-done.3.yp
  18.7 15.4 %operator.1 = (bf16[96,10368]{1,0:T(8,128)(2,1)S(1)}, f32[24,128]{1,0:T(8,128)S(1)}) custom-call(f32[1168,128]{1,0:T(8,128)S(1)} %get-tuple-element.11.own, f32[592,128]{1,0:T(8,128)S(1)} %collective-permute-done.xm, f32[1168,128]{1,0:T(8,128)S(1)} %collective-permute-done.1.xp, f32[376,128]{1,0:T(8,128)S(1)} %collective-permute-done.2.ym, ...), custom_call_target="tpu_custom_call" | custom-call | tf_op jit(solution)/shard_map/operator/pallas_call | solution.py:546
  34.2 26.4 %all_to_all.10.system = f32[32,24,128]{2,1,0:T(8,128)S(1)} all-to-all(f32[32,24,128]{2,1,0:T(8,128)S(1)} %broadcast_in_dim.4), channel_id=1, replica_groups=mesh['gx'=8,'gy'=4] {'gx','gy'}, dimensions={0} | all-to-all | bytes 786432 | tf_op jit(solution)/shard_map/all_to_all | solution.py:570
  60.6 0.0 copy-done.2
  60.6 5.8 %solve.1 = f32[2,8,128]{2,1,0:T(8,128)S(1)} custom-call(f32[32,24,128]{2,1,0:T(8,128)S(1)} %all_to_all.10.system, bf16[96,10368]{1,0:T(8,128)(2,1)S(1)} %get-tuple-element.16.both, s32[2,8,128]{2,1,0:T(8,128)S(1)} %copy-done.2), custom_call_target="tpu_custom_call" | custom-call | tf_op jit(solution)/shard_map/solve/pallas_call | solution.py:574
  66.4 0.7 broadcast_in_dim.5
  67.2 3.9 %all-to-all-start.1 = ((f32[32,2,8,128]{3,2,1,0:T(8,128)}), f32[32,2,8,128]{3,2,1,0:T(8,128)S(1)}, u32[]{:S(2)}, u32[]{:S(2)}) async-start(f32[32,2,8,128]{3,2,1,0:T(8,128)} %broadcast_in_dim.5), calls=%async_computation.1 | async-start | bytes 524288 | tf_op jit(solution)/shard_map/all_to_all | solution.py:570
  71.0 0.1 pad_add_fusion.start
  71.1 10.1 %all-to-all-done.1.blocks = f32[32,2,8,128]{3,2,1,0:T(8,128)S(1)} async-done(((f32[32,2,8,128]{3,2,1,0:T(8,128)}), f32[32,2,8,128]{3,2,1,0:T(8,128)S(1)}, u32[]{:S(2)}, u32[]{:S(2)}) %all-to-all-start.1) | async-done | bytes 262176 | tf_op jit(solution)/shard_map/all_to_all | solution.py:570
  81.2 1.3 %cone.1 = f32[2,8,128]{2,1,0:T(8,128)} custom-call(s32[2]{0:T(128)S(1)} %pad_add_fusion.start, f32[32,2,8,128]{3,2,1,0:T(8,128)S(1)} %all-to-all-done.1.blocks, s32[2,8,128]{2,1,0:T(8,128)S(1)} %copy-done.2), custom_call_target="tpu_custom_call" | custom-call | tf_op jit(solution)/shard_map/cone/pallas_call | solution.py:591
  (2 shorter events, 0.1 us)
Async XLA Ops:
  0.0 1.1 %copy-start = (f32[3,24,2,8,128]{4,3,2,1,0:T(8,128)S(1)}, f32[3,24,2,8,128]{4,3,2,1,0:T(8,128)}, u32[]{:S(2)}) copy-start(f32[3,24,2,8,128]{4,3,2,1,0:T(8,128)} %forces.1) | copy-start | bytes 1769476
  1.1 0.7 copy-start.1
  1.8 0.7 copy-start.3
  2.6 5.5 %collective-permute-start.1 = (f32[1168,128]{1,0:T(8,128)S(1)}, f32[1168,128]{1,0:T(8,128)S(1)}, u32[]{:S(2)}, u32[]{:S(2)}) collective-permute-start(f32[1168,128]{1,0:T(8,128)S(1)} %get-tuple-element.11.own), channel_id=1, source_target_pairs={{4,0},{8,4},{12,8},{16,12},{20,16},{24,20},{28,24},{5,1},{9,5},{13... | collective-permute-start | bytes 1794056 | tf_op jit(solution)/shard_map/ppermute | solution.py:526
  3.9 4.2 %collective-permute-start = (f32[592,128]{1,0:T(8,128)S(1)}, f32[592,128]{1,0:T(8,128)S(1)}, u32[]{:S(2)}, u32[]{:S(2)}) collective-permute-start(f32[592,128]{1,0:T(8,128)S(1)} %get-tuple-element.12), channel_id=1, source_target_pairs={{0,4},{4,8},{8,12},{12,16},{16,20},{20,24},{24,28},{1,5},{5,9},{9,... | collective-permute-start | bytes 909320 | tf_op jit(solution)/shard_map/ppermute | solution.py:526
  8.2 52.4 %copy-start.2 = (s32[2,8,128]{2,1,0:T(8,128)S(1)}, s32[2,8,128]{2,1,0:T(8,128)}, u32[]{:S(2)}) copy-start(s32[2,8,128]{2,1,0:T(8,128)} %levels.5) | copy-start | bytes 24580
  8.2 10.5 %collective-permute-start.3 = (f32[736,128]{1,0:T(8,128)S(1)}, f32[736,128]{1,0:T(8,128)S(1)}, u32[]{:S(2)}, u32[]{:S(2)}) collective-permute-start(f32[736,128]{1,0:T(8,128)S(1)} %get-tuple-element.14), channel_id=1, source_target_pairs={{1,0},{2,1},{3,2},{5,4},{6,5},{7,6},{9,8},{10,9},{11,10},{13,12},{... | collective-permute-start | bytes 1130504 | tf_op jit(solution)/shard_map/ppermute | solution.py:526
  9.5 8.7 %collective-permute-start.2 = (f32[376,128]{1,0:T(8,128)S(1)}, f32[376,128]{1,0:T(8,128)S(1)}, u32[]{:S(2)}, u32[]{:S(2)}) collective-permute-start(f32[376,128]{1,0:T(8,128)S(1)} %get-tuple-element.13), channel_id=1, source_target_pairs={{0,1},{1,2},{2,3},{4,5},{5,6},{6,7},{8,9},{9,10},{10,11},{12,13},{... | collective-permute-start | bytes 577544 | tf_op jit(solution)/shard_map/ppermute | solution.py:526
  67.2 14.1 %all-to-all-start.1 = ((f32[32,2,8,128]{3,2,1,0:T(8,128)}), f32[32,2,8,128]{3,2,1,0:T(8,128)S(1)}, u32[]{:S(2)}, u32[]{:S(2)}) async-start(f32[32,2,8,128]{3,2,1,0:T(8,128)} %broadcast_in_dim.5), calls=%async_computation.1 | async-start | bytes 524288 | tf_op jit(solution)/shard_map/all_to_all | solution.py:570

commit v3 on v1

--- a/solution.py
+++ b/solution.py
@@ -231,7 +231,7 @@
 
 def main_kernel(
     sizes, own, xm, xp, ym, yp, both_out, system_out, stiff_ref, inverse,
-    start, sums, diffs, acc_s, acc_d, w_sums, w_diffs, acc2_s, acc2_d, right, second,
+    start, sums, diffs, acc_s, acc_d, w_sums, w_diffs, acc2_s, acc2_d, right, second, table,
 ):
     planes, rows, cases = sizes
     block = 3 * cases
@@ -369,18 +369,31 @@
     other = lax.dot_general(both_out[...], second[...], contract, preferred_element_type=f32)
     other = other[:two] + other[two:]
     other = other[:, :cases] + other[:, cases:]
-    system_out[...] = jnp.zeros(system_out.shape, f32)
-    system_out[:, 0:two] = gram[:cases]
-    system_out[:, two : two + cases] = other[:cases]
-    system_out[:, two + cases : 2 * two] = other[cases:]
-
-
-def solve_kernel(sizes, system, both, levels, out, mixing, sums, diffs, energy):
+    table[...] = jnp.zeros(table.shape, f32)
+    table[:, 0:two] = gram[:cases]
+    table[:, two : two + cases] = other[:cases]
+    table[:, two + cases : 2 * two] = other[cases:]
+    per = system_out.shape[1]
+    for index in range(system_out.shape[0] * per):
+        line = table[index : index + 1, :] if index < cases else jnp.zeros((1, LANES), f32)
+        system_out[index // per, index % per : index % per + 1, :] = line
+
+
+def sum_kernel(parts, out):
+    total = jnp.sum(parts[...], axis=0)
+    for index in range(out.shape[0]):
+        out[index] = total
+
+
+def solve_kernel(sizes, system, both, levels, out, mixing, sums, diffs, energy, lines):
     planes, rows, cases = sizes
     two = 2 * cases
     nodes_y = rows + 1
     count = planes * rows
-    total = jnp.sum(system[...], axis=0)
+    per = system.shape[1]
+    for index in range(cases):
+        lines[index : index + 1, :] = system[index // per, index % per : index % per + 1, :]
+    total = lines[...]
     table = jnp.concatenate(
         [pltpu.roll(total, LANES - cases, 1), pltpu.roll(total, LANES - two, 1), total], 0
     )
@@ -444,26 +457,36 @@
                 lower = upper
         total = jnp.sum(energy[...], axis=1)
         density = 0.3 + 0.7 * levels[plane].astype(f32) / (LEVELS - 1)
-        out[plane] = (-3.0 / cases) * (density * density * density) * total
+        total = (-3.0 / cases) * (density * density * density) * total
+        for index in range(out.shape[0]):
+            out[index, plane] = total
         return 0
 
     lax.fori_loop(0, planes, step, 0)
 
 
-def filter_kernel(sizes, counts, start, blocks, levels, out, wide, there):
+def border_kernel(sizes, counts, start, blocks, column, edges):
+    planes, rows, _ = sizes
+    for step, low, high, to in ((-1, planes - 2, planes, 0), (0, 0, planes, 2), (1, 0, 2, 2 + planes)):
+        place = start[0] // planes + step
+        inside = (place >= 0) & (place < counts[0])
+        value = blocks[jnp.where(inside, place, 0), low:high]
+        column[to : to + high - low] = jnp.where(inside, value, 0.0)
+    for index in range(counts[1]):
+        first, last = column[:, 0:2, :], column[:, rows - 2 : rows, :]
+        edges[index] = jnp.where(index < start[1] // rows, first, last)
+
+
+def filter_kernel(sizes, counts, start, column, edges, levels, out, wide, there):
     planes, rows, _ = sizes
     totals = (counts[0] * planes, counts[1] * rows)
     weight = [2.5 - math.sqrt(q) for q in range(7)]
-    sides_x = ((-1, planes - 2, planes, 0), (0, 0, planes, 2), (1, 0, 2, 2 + planes))
-    sides_y = ((-1, rows - 2, rows, 0), (0, 0, rows, 2), (1, 0, 2, 2 + rows))
-    for step_x, x0, x1, to_x in sides_x:
-        for step_y, y0, y1, to_y in sides_y:
-            at_x = start[0] // planes + step_x
-            at_y = start[1] // rows + step_y
-            inside = (at_x >= 0) & (at_x < counts[0]) & (at_y >= 0) & (at_y < counts[1])
-            index = jnp.where(inside, at_x * counts[1] + at_y, 0)
-            value = blocks[index, x0:x1, y0:y1, :]
-            wide[to_x : to_x + x1 - x0, to_y : to_y + y1 - y0, :] = jnp.where(inside, value, 0.0)
+    wide[:, 2 : 2 + rows, :] = column[...]
+    for step, to in ((-1, 0), (1, 2 + rows)):
+        place = start[1] // rows + step
+        inside = (place >= 0) & (place < counts[1])
+        value = edges[jnp.where(inside, place, 0)]
+        wide[:, to : to + 2, :] = jnp.where(inside, value, 0.0)
     y = lax.broadcasted_iota(jnp.int32, (rows + 4, LANES), 0) + (start[1] - 2)
     in_y = jnp.logical_and(y >= 0, y < totals[1])
     for x in range(planes + 4):
@@ -539,6 +562,7 @@
     )(own, from_xm, from_xp)
     from_yp, from_ym = moved(ym, "gy", -1), moved(yp, "gy", 1)
 
+    devices = count_x * count_y
     nodes = (planes + 1) * (rows + 1)
     wide = (planes + 3) * (rows + 3)
     acc = pltpu.VMEM(((planes + 3) * (rows + 1), block, LANES), f32)
@@ -547,7 +571,7 @@
         functools.partial(main_kernel, sizes),
         out_shape=[
             jax.ShapeDtypeStruct((4 * cases, nodes * 3 * LANES), bf16),
-            jax.ShapeDtypeStruct((cases, LANES), f32),
+            jax.ShapeDtypeStruct((devices, -(-cases // devices), LANES), f32),
         ],
         in_specs=[VMEM] * 5,
         out_specs=[VMEM] * 2,
@@ -560,16 +584,28 @@
             acc, acc, field, field, field, field,
             pltpu.VMEM((4 * cases, planes * rows * 3 * LANES), bf16),
             pltpu.VMEM((2 * cases, nodes * 3 * LANES), bf16),
+            pltpu.VMEM((cases, LANES), f32),
         ],
         compiler_params=PARAMS,
         name="operator",
     )(own, from_xm, from_xp, from_ym, from_yp)
 
-    system = lax.all_gather(system, ("gx", "gy"))
+    def exchanged(value, axes):
+        return lax.all_to_all(value, axes, 0, 0)
+
+    system = exchanged(system, ("gx", "gy"))
+    system = pl.pallas_call(
+        sum_kernel,
+        out_shape=jax.ShapeDtypeStruct(system.shape, f32),
+        in_specs=[VMEM],
+        out_specs=VMEM,
+        name="sums",
+    )(system)
+    system = exchanged(system, ("gx", "gy"))
 
     weighted = pl.pallas_call(
         functools.partial(solve_kernel, sizes),
-        out_shape=jax.ShapeDtypeStruct((planes, rows, LANES), f32),
+        out_shape=jax.ShapeDtypeStruct((count_x, planes, rows, LANES), f32),
         in_specs=[VMEM] * 3,
         out_specs=VMEM,
         scratch_shapes=[
@@ -577,22 +613,37 @@
             field,
             field,
             pltpu.VMEM((rows, 8, LANES), f32),
+            pltpu.VMEM((cases, LANES), f32),
         ],
         compiler_params=PARAMS,
         name="solve",
     )(system, both, levels)
 
-    blocks = lax.all_gather(weighted, ("gx", "gy"))
+    blocks = exchanged(weighted, "gx")
     start = jnp.stack([lax.axis_index("gx") * planes, lax.axis_index("gy") * rows])
+    start = start.astype(jnp.int32)
+    scalars = pl.BlockSpec(memory_space=pltpu.SMEM)
+    counts = (count_x, count_y)
+    column, edges = pl.pallas_call(
+        functools.partial(border_kernel, sizes, counts),
+        out_shape=[
+            jax.ShapeDtypeStruct((planes + 4, rows, LANES), f32),
+            jax.ShapeDtypeStruct((count_y, planes + 4, 2, LANES), f32),
+        ],
+        in_specs=[scalars, VMEM],
+        out_specs=[VMEM] * 2,
+        name="borders",
+    )(start, blocks)
+    edges = exchanged(edges, "gy")
     return pl.pallas_call(
-        functools.partial(filter_kernel, sizes, (count_x, count_y)),
+        functools.partial(filter_kernel, sizes, counts),
         out_shape=jax.ShapeDtypeStruct((planes, rows, LANES), f32),
-        in_specs=[pl.BlockSpec(memory_space=pltpu.SMEM)] + [VMEM] * 2,
+        in_specs=[scalars] + [VMEM] * 3,
         out_specs=VMEM,
         scratch_shapes=[pltpu.VMEM((planes + 4, rows + 4, LANES), f32)] * 2,
         compiler_params=PARAMS,
         name="cone",
-    )(start.astype(jnp.int32), blocks, levels)
+    )(start, column, edges, levels)
 
 
 def solution(mesh):

time: 186 us -> 96.1 us (0.52)
  the two profiles are of different devices: /device:TPU:12 before, /device:TPU:0 now
where the time goes in v3:
time: 96.1 us; the launch traced here: 95.3 us
  blocking collectives  30.5 us (32%)
  Pallas kernels  26.2 us (27%)
  starting transfers between devices  17.1 us (18%)
  waiting for transfers between devices  16.3 us (17%)
  local copies, waits for them, and re-layouts  4.44 us (5%)
    all_to_all x2, blocking collectives, exchanged(): return lax.all_to_all(value, axes, 0, 0)  30.5 us
    pallas_call x1, Pallas kernels, local(): pl.pallas_call(functools.partial(main_kernel, sizes), out_shape=[jax.Shap...  15.5 us
    all_to_all x2, waiting for transfers between devices, exchanged(): return lax.all_to_all(value, axes, 0, 0)  11.5 us
    ppermute x4, starting transfers between devices, moved(): return lax.ppermute(value, axis, pairs)  11.2 us
    pallas_call x1, Pallas kernels, local(): pl.pallas_call(functools.partial(solve_kernel, sizes), out_shape=jax.Shap...  6.46 us
    all_to_all x2, starting transfers between devices, exchanged(): return lax.all_to_all(value, axes, 0, 0)  5.91 us
    ppermute x4, waiting for transfers between devices, moved(): return lax.ppermute(value, axis, pairs)  4.82 us
    unnamed x14, local copies, waits for them, and re-layouts  4.44 us
  transfers between devices with their start and end apart: 6, of which 5 were waited for; matrix products, arithmetic and copies ran while one was open for 1% of the time, Pallas kernels for 0%

profile of v3, /device:TPU:0, one launch (start us, length us, event | category | flops | bytes accessed | tf_op | source)
XLA Modules:
  0.0 95.3 jit_solution(15014763921295726984)
XLA Ops:
  0.0 0.0 copy-start
  0.0 1.1 %copy-done = f32[3,24,2,8,128]{4,3,2,1,0:T(8,128)S(1)} copy-done((f32[3,24,2,8,128]{4,3,2,1,0:T(8,128)S(1)}, f32[3,24,2,8,128]{4,3,2,1,0:T(8,128)}, u32[]{:S(2)}) %copy-start) | copy-done | bytes 589848
  1.1 0.0 copy-start.1
  1.1 0.7 copy-done.1
  1.8 0.0 copy-start.4
  1.8 0.7 copy-done.4
  2.5 0.1 pack.1
  2.6 0.0 copy-start.2
  2.6 1.3 %collective-permute-start.1 = (f32[1168,128]{1,0:T(8,128)S(1)}, f32[1168,128]{1,0:T(8,128)S(1)}, u32[]{:S(2)}, u32[]{:S(2)}) collective-permute-start(f32[1168,128]{1,0:T(8,128)S(1)} %get-tuple-element.13.own), channel_id=1, source_target_pairs={{4,0},{8,4},{12,8},{16,12},{20,16},{24,20},{28,24},{5,1},{9,5},{13... | collective-permute-start | bytes 1794056 | tf_op jit(solution)/shard_map/ppermute | solution.py:549
  3.9 3.0 %collective-permute-start = (f32[592,128]{1,0:T(8,128)S(1)}, f32[592,128]{1,0:T(8,128)S(1)}, u32[]{:S(2)}, u32[]{:S(2)}) collective-permute-start(f32[592,128]{1,0:T(8,128)S(1)} %get-tuple-element.14), channel_id=1, source_target_pairs={{0,4},{4,8},{8,12},{12,16},{16,20},{20,24},{24,28},{1,5},{5,9},{9,... | collective-permute-start | bytes 909320 | tf_op jit(solution)/shard_map/ppermute | solution.py:549
  7.0 1.2 %collective-permute-done.xm = f32[592,128]{1,0:T(8,128)S(1)} collective-permute-done((f32[592,128]{1,0:T(8,128)S(1)}, f32[592,128]{1,0:T(8,128)S(1)}, u32[]{:S(2)}, u32[]{:S(2)}) %collective-permute-start) | collective-permute-done | bytes 303136 | tf_op jit(solution)/shard_map/ppermute | solution.py:549
  8.1 0.0 collective-permute-done.1.xp
  8.2 1.3 %collective-permute-start.3 = (f32[736,128]{1,0:T(8,128)S(1)}, f32[736,128]{1,0:T(8,128)S(1)}, u32[]{:S(2)}, u32[]{:S(2)}) collective-permute-start(f32[736,128]{1,0:T(8,128)S(1)} %get-tuple-element.16), channel_id=1, source_target_pairs={{1,0},{2,1},{3,2},{5,4},{6,5},{7,6},{9,8},{10,9},{11,10},{13,12},{... | collective-permute-start | bytes 1130504 | tf_op jit(solution)/shard_map/ppermute | solution.py:549
  9.5 5.6 %collective-permute-start.2 = (f32[376,128]{1,0:T(8,128)S(1)}, f32[376,128]{1,0:T(8,128)S(1)}, u32[]{:S(2)}, u32[]{:S(2)}) collective-permute-start(f32[376,128]{1,0:T(8,128)S(1)} %get-tuple-element.15), channel_id=1, source_target_pairs={{0,1},{1,2},{2,3},{4,5},{5,6},{6,7},{8,9},{9,10},{10,11},{12,13},{... | collective-permute-start | bytes 577544 | tf_op jit(solution)/shard_map/ppermute | solution.py:549
  15.1 3.1 %collective-permute-done.2.ym = f32[376,128]{1,0:T(8,128)S(1)} collective-permute-done((f32[376,128]{1,0:T(8,128)S(1)}, f32[376,128]{1,0:T(8,128)S(1)}, u32[]{:S(2)}, u32[]{:S(2)}) %collective-permute-start.2) | collective-permute-done | bytes 192544 | tf_op jit(solution)/shard_map/ppermute | solution.py:549
  18.2 0.5 collective-permute-done.3.yp
  18.7 15.5 %operator.1 = (bf16[96,10368]{1,0:T(8,128)(2,1)S(1)}, f32[32,1,128]{2,1,0:T(1,128)S(1)}) custom-call(f32[1168,128]{1,0:T(8,128)S(1)} %get-tuple-element.13.own, f32[592,128]{1,0:T(8,128)S(1)} %collective-permute-done.xm, f32[1168,128]{1,0:T(8,128)S(1)} %collective-permute-done.1.xp, f32[376,128]{1,0:T(8,128)S(1)} %collective-permute-done.2.ym, ...), custom_call_target="tpu_custom_call" | custom-call | tf_op jit(solution)/shard_map/operator/pallas_call | solution.py:570
  34.2 21.7 %all_to_all.20.parts = f32[32,1,128]{2,1,0:T(1,128)} all-to-all(f32[32,1,128]{2,1,0:T(1,128)S(1)} %get-tuple-element.17), channel_id=1, replica_groups=mesh['gx'=8,'gy'=4] {'gx','gy'}, dimensions={0} | all-to-all | bytes 32768 | tf_op jit(solution)/shard_map/all_to_all | solution.py:594
  55.9 1.4 %sums.1 = f32[32,1,128]{2,1,0:T(1,128)} custom-call(f32[32,1,128]{2,1,0:T(1,128)} %all_to_all.20.parts), custom_call_target="tpu_custom_call" | custom-call | tf_op jit(solution)/shard_map/sums/pallas_call | solution.py:597
  57.2 2.6 %all-to-all-start.1 = ((f32[32,1,128]{2,1,0:T(1,128)}), f32[32,1,128]{2,1,0:T(1,128)S(1)}, u32[]{:S(2)}, u32[]{:S(2)}) async-start(f32[32,1,128]{2,1,0:T(1,128)} %sums.1), calls=%async_computation.1 | async-start | bytes 32768 | tf_op jit(solution)/shard_map/all_to_all | solution.py:594
  59.8 7.2 %all-to-all-done.1.system = f32[32,1,128]{2,1,0:T(1,128)S(1)} async-done(((f32[32,1,128]{2,1,0:T(1,128)}), f32[32,1,128]{2,1,0:T(1,128)S(1)}, u32[]{:S(2)}, u32[]{:S(2)}) %all-to-all-start.1) | async-done | bytes 16416 | tf_op jit(solution)/shard_map/all_to_all | solution.py:594
  67.0 0.0 copy-done.2
  67.0 6.5 %solve.1 = f32[8,2,8,128]{3,2,1,0:T(8,128)} custom-call(f32[32,1,128]{2,1,0:T(1,128)S(1)} %all-to-all-done.1.system, bf16[96,10368]{1,0:T(8,128)(2,1)S(1)} %get-tuple-element.18.both, s32[2,8,128]{2,1,0:T(8,128)S(1)} %copy-done.2), custom_call_target="tpu_custom_call" | custom-call | tf_op jit(solution)/shard_map/solve/pallas_call | solution.py:606
  73.4 3.3 %all-to-all-start.2 = ((f32[8,2,8,128]{3,2,1,0:T(8,128)}), f32[8,2,8,128]{3,2,1,0:T(8,128)S(1)}, u32[]{:S(2)}, u32[]{:S(2)}) async-start(f32[8,2,8,128]{3,2,1,0:T(8,128)} %solve.1), calls=%async_computation.2 | async-start | bytes 131072 | tf_op jit(solution)/shard_map/all_to_all | solution.py:594
  76.8 0.6 pad_add_fusion.start
  77.4 4.4 %all-to-all-done.2.blocks = f32[8,2,8,128]{3,2,1,0:T(8,128)S(1)} async-done(((f32[8,2,8,128]{3,2,1,0:T(8,128)}), f32[8,2,8,128]{3,2,1,0:T(8,128)S(1)}, u32[]{:S(2)}, u32[]{:S(2)}) %all-to-all-start.2) | async-done | bytes 65568 | tf_op jit(solution)/shard_map/all_to_all | solution.py:594
  81.7 0.0 copy-start.6
  81.7 0.6 copy-done.6
  82.4 1.5 %borders.1 = (f32[6,8,128]{2,1,0:T(8,128)}, f32[4,6,2,128]{3,2,1,0:T(2,128)}) custom-call(s32[2]{0:T(128)} %pad_add_fusion.start, f32[8,2,8,128]{3,2,1,0:T(8,128)} %copy-done.6), custom_call_target="tpu_custom_call" | custom-call | tf_op jit(solution)/shard_map/borders/pallas_call | solution.py:627
  83.9 8.9 %all_to_all.21.edges = f32[4,6,2,128]{3,2,1,0:T(2,128)S(1)} all-to-all(f32[4,6,2,128]{3,2,1,0:T(2,128)} %get-tuple-element.20), channel_id=1, replica_groups=mesh['gx'=8,'gy'=4] {'gy'}, dimensions={0} | all-to-all | bytes 49152 | tf_op jit(solution)/shard_map/all_to_all | solution.py:594
  92.7 0.0 copy-start.3
  92.7 0.7 copy-done.3
  93.5 0.0 copy-start.5
  93.5 0.6 copy-done.5
  94.1 1.3 %cone.1 = f32[2,8,128]{2,1,0:T(8,128)} custom-call(s32[2]{0:T(128)S(1)} %copy-done.5, f32[6,8,128]{2,1,0:T(8,128)S(1)} %copy-done.3, f32[4,6,2,128]{3,2,1,0:T(2,128)S(1)} %all_to_all.21.edges, s32[2,8,128]{2,1,0:T(8,128)S(1)} %copy-done.2), custom_call_target="tpu_custom_call" | custom-call | tf_op jit(solution)/shard_map/cone/pallas_call | solution.py:638
  (1 shorter events, 0.0 us)
Async XLA Ops:
  0.0 1.1 %copy-start = (f32[3,24,2,8,128]{4,3,2,1,0:T(8,128)S(1)}, f32[3,24,2,8,128]{4,3,2,1,0:T(8,128)}, u32[]{:S(2)}) copy-start(f32[3,24,2,8,128]{4,3,2,1,0:T(8,128)} %forces.1) | copy-start | bytes 1769476
  1.1 0.7 copy-start.1
  1.8 0.7 copy-start.4
  2.6 64.4 %copy-start.2 = (s32[2,8,128]{2,1,0:T(8,128)S(1)}, s32[2,8,128]{2,1,0:T(8,128)}, u32[]{:S(2)}) copy-start(s32[2,8,128]{2,1,0:T(8,128)} %levels.5) | copy-start | bytes 24580
  2.6 5.5 %collective-permute-start.1 = (f32[1168,128]{1,0:T(8,128)S(1)}, f32[1168,128]{1,0:T(8,128)S(1)}, u32[]{:S(2)}, u32[]{:S(2)}) collective-permute-start(f32[1168,128]{1,0:T(8,128)S(1)} %get-tuple-element.13.own), channel_id=1, source_target_pairs={{4,0},{8,4},{12,8},{16,12},{20,16},{24,20},{28,24},{5,1},{9,5},{13... | collective-permute-start | bytes 1794056 | tf_op jit(solution)/shard_map/ppermute | solution.py:549
  3.9 4.2 %collective-permute-start = (f32[592,128]{1,0:T(8,128)S(1)}, f32[592,128]{1,0:T(8,128)S(1)}, u32[]{:S(2)}, u32[]{:S(2)}) collective-permute-start(f32[592,128]{1,0:T(8,128)S(1)} %get-tuple-element.14), channel_id=1, source_target_pairs={{0,4},{4,8},{8,12},{12,16},{16,20},{20,24},{24,28},{1,5},{5,9},{9,... | collective-permute-start | bytes 909320 | tf_op jit(solution)/shard_map/ppermute | solution.py:549
  8.2 10.5 %collective-permute-start.3 = (f32[736,128]{1,0:T(8,128)S(1)}, f32[736,128]{1,0:T(8,128)S(1)}, u32[]{:S(2)}, u32[]{:S(2)}) collective-permute-start(f32[736,128]{1,0:T(8,128)S(1)} %get-tuple-element.16), channel_id=1, source_target_pairs={{1,0},{2,1},{3,2},{5,4},{6,5},{7,6},{9,8},{10,9},{11,10},{13,12},{... | collective-permute-start | bytes 1130504 | tf_op jit(solution)/shard_map/ppermute | solution.py:549
  9.5 8.7 %collective-permute-start.2 = (f32[376,128]{1,0:T(8,128)S(1)}, f32[376,128]{1,0:T(8,128)S(1)}, u32[]{:S(2)}, u32[]{:S(2)}) collective-permute-start(f32[376,128]{1,0:T(8,128)S(1)} %get-tuple-element.15), channel_id=1, source_target_pairs={{0,1},{1,2},{2,3},{4,5},{5,6},{6,7},{8,9},{9,10},{10,11},{12,13},{... | collective-permute-start | bytes 577544 | tf_op jit(solution)/shard_map/ppermute | solution.py:549
  57.2 9.7 %all-to-all-start.1 = ((f32[32,1,128]{2,1,0:T(1,128)}), f32[32,1,128]{2,1,0:T(1,128)S(1)}, u32[]{:S(2)}, u32[]{:S(2)}) async-start(f32[32,1,128]{2,1,0:T(1,128)} %sums.1), calls=%async_computation.1 | async-start | bytes 32768 | tf_op jit(solution)/shard_map/all_to_all | solution.py:594
  73.4 8.3 %all-to-all-start.2 = ((f32[8,2,8,128]{3,2,1,0:T(8,128)}), f32[8,2,8,128]{3,2,1,0:T(8,128)S(1)}, u32[]{:S(2)}, u32[]{:S(2)}) async-start(f32[8,2,8,128]{3,2,1,0:T(8,128)} %solve.1), calls=%async_computation.2 | async-start | bytes 131072 | tf_op jit(solution)/shard_map/all_to_all | solution.py:594
  81.7 0.6 copy-start.6
  92.7 0.7 copy-start.3
  93.5 0.6 copy-start.5

commit v4 on v2

--- a/solution.py
+++ b/solution.py
@@ -34,6 +34,19 @@
 def shift_up(value):
     lane = lax.broadcasted_iota(jnp.int32, value.shape, value.ndim - 1)
     return jnp.where(lane == 0, 0.0, pltpu.roll(value, 1, value.ndim - 1))
+
+
+def unrolled(count, factor, body):
+    def turn(step, _):
+        for offset in range(factor):
+            body(step * factor + offset)
+        return 0
+
+    turns = count // factor
+    if turns:
+        lax.fori_loop(0, turns, turn, 0)
+    for index in range(turns * factor, count):
+        body(index)
 
 
 def split(value):
@@ -179,20 +192,35 @@
     lax.fori_loop(0, planes * tiles, step, 0)
 
 
-def pack_kernel(sizes, forces, levels, supports, own, up, *rest):
+def pack_kernel(sizes, forces_hbm, levels_hbm, supports_hbm, own, up, *rest):
     planes, rows, cases = sizes
     block = 3 * cases
     base = planes * rows * block
+    *rest, forces, levels, supports, arrived = rest
+    copies = [
+        pltpu.make_async_copy(levels_hbm, levels, arrived.at[3]),
+        pltpu.make_async_copy(supports_hbm, supports, arrived.at[4]),
+    ]
+    copies += [
+        pltpu.make_async_copy(forces_hbm.at[k], forces.at[k], arrived.at[k]) for k in range(3)
+    ]
+    for copy in copies:
+        copy.start()
+    copies[0].wait()
+    copies[1].wait()
+    scales = []
     for x in range(planes):
         density = 0.3 + 0.7 * levels[x].astype(f32) / (LEVELS - 1)
         stiff = density * density * density
         free = supports[x] == 0
         own[base + x * rows : base + (x + 1) * rows, :] = jnp.where(free, stiff, -stiff)
-        scale = jnp.where(free, LOAD, 0.0)
-        for k in range(3):
+        scales.append(jnp.where(free, LOAD, 0.0))
+    for k in range(3):
+        copies[2 + k].wait()
+        for x in range(planes):
             for c in range(cases):
                 start = x * rows * block + k * cases + c
-                own[pl.ds(start, rows, stride=block), :] = forces[k, c, x] * scale
+                own[pl.ds(start, rows, stride=block), :] = forces[k, c, x] * scales[x]
 
     def fill(ref, xs, code_xs):
         size = len(xs) * rows * block
@@ -231,7 +259,7 @@
 
 def main_kernel(
     sizes, own, xm, xp, ym, yp, both_out, system_out, stiff_ref, inverse,
-    start, sums, diffs, acc_s, acc_d, w_sums, w_diffs, acc2_s, acc2_d, right, second,
+    start, sums, diffs, acc_s, acc_d, w_sums, w_diffs, acc2_s, acc2_d, right, table,
 ):
     planes, rows, cases = sizes
     block = 3 * cases
@@ -265,18 +293,16 @@
     for ref, bx, by, _, _ in regions:
         for i, x in enumerate(bx):
 
-            def place(j, _, ref=ref, i=i, x=x, by=by):
+            for j in range(len(by)):
                 y = j + by[0] + 1
-                load = ref[pl.ds(pl.multiple_of((i * len(by) + j) * block, 8), block), :]
-                value = load * inverse[x + 1, pl.ds(y, 1), :]
+                line = (i * len(by) + j) * block
+                load = ref[line : line + block, :]
+                value = load * inverse[x + 1, y : y + 1, :]
                 column = (x + 1) * ys + y
                 start[column] = value
                 moved = shift_down(value)
                 sums[column] = value + moved
                 diffs[column] = moved - value
-                return 0
-
-            lax.fori_loop(0, len(by), place, 0)
 
     nodes_y = rows + 1
     apply_elements(
@@ -301,33 +327,25 @@
             both_out[2 * cases : 4 * cases, lane] = rest
         return force
 
-    def inside(index, _):
-        x, y = index // rows, index % rows
-        force = image(x, y, index)
+    two = 2 * cases
+    count = planes * rows
+
+    def inside(index):
+        force = image(index // rows, index % rows, index)
         load = own[pl.ds(pl.multiple_of(index * block, 8), block), :]
         for k in range(3):
             lines = slice(k * cases, (k + 1) * cases)
             pair = jnp.concatenate([load[lines], force[lines]], 0)
             lane = pl.ds(pl.multiple_of((index * 3 + k) * LANES, LANES), LANES)
             high, rest = split(pair)
-            right[0 : 2 * cases, lane] = high
-            right[2 * cases : 4 * cases, lane] = rest
-        return 0
-
-    count = planes * rows
-    lax.fori_loop(0, count, inside, 0)
-
-    def beyond_y(x, _):
-        image(x, rows, count + x)
-        return 0
-
-    lax.fori_loop(0, planes, beyond_y, 0)
-
-    def beyond_x(y, _):
-        image(planes, y, count + planes + y)
-        return 0
-
-    lax.fori_loop(0, nodes_y, beyond_x, 0)
+            right[0:two, lane] = high
+            right[two : 2 * two, lane] = rest
+
+    unrolled(count, 4, inside)
+    unrolled(planes, 2, lambda x: image(x, rows, count + x))
+    unrolled(nodes_y, 3, lambda y: image(planes, y, count + planes + y))
+    beyond = right.shape[1] - count * 3 * LANES
+    right[0 : 2 * two, count * 3 * LANES :] = jnp.zeros((2 * two, beyond), bf16)
 
     for column in range(nodes_y):
         acc2_s[column] = jnp.zeros((block, LANES), f32)
@@ -342,48 +360,68 @@
             value = force[k * cases : (k + 1) * cases]
             high = value.astype(bf16).astype(f32)
             lane = pl.ds(pl.multiple_of((place * 3 + k) * LANES, LANES), LANES)
-            second[:, lane] = jnp.concatenate([high, value - high], 0).astype(bf16)
-
-    def second_inside(index, _):
-        second_force(index // rows, index % rows, index)
-        return 0
-
-    def second_y(x, _):
-        second_force(x, rows, count + x)
-        return 0
-
-    def second_x(y, _):
-        second_force(planes, y, count + planes + y)
-        return 0
-
-    lax.fori_loop(0, count, second_inside, 0)
-    lax.fori_loop(0, planes, second_y, 0)
-    lax.fori_loop(0, nodes_y, second_x, 0)
+            right[2 * two :, lane] = jnp.concatenate([high, value - high], 0).astype(bf16)
+
+    unrolled(count, 4, lambda index: second_force(index // rows, index % rows, index))
+    unrolled(planes, 2, lambda x: second_force(x, rows, count + x))
+    unrolled(nodes_y, 3, lambda y: second_force(planes, y, count + planes + y))
 
     contract = (((1,), (1,)), ((), ()))
-    width = count * 3 * LANES
-    two = 2 * cases
-    gram = lax.dot_general(both_out[:, :width], right[...], contract, preferred_element_type=f32)
-    gram = gram[:two] + gram[two:]
-    gram = gram[:, :two] + gram[:, two:]
-    other = lax.dot_general(both_out[...], second[...], contract, preferred_element_type=f32)
-    other = other[:two] + other[two:]
-    other = other[:, :cases] + other[:, cases:]
-    system_out[...] = jnp.zeros(system_out.shape, f32)
-    system_out[:, 0:two] = gram[:cases]
-    system_out[:, two : two + cases] = other[:cases]
-    system_out[:, two + cases : 2 * two] = other[cases:]
-
-
-def solve_kernel(sizes, system, both, levels, out, mixing, sums, diffs, energy):
+    product = lax.dot_general(both_out[...], right[...], contract, preferred_element_type=f32)
+    product = product[:two] + product[two:]
+    gram = product[:, :two] + product[:, two : 2 * two]
+    other = product[:, 2 * two : 2 * two + cases] + product[:, 2 * two + cases :]
+    row = lax.broadcasted_iota(jnp.int32, (cases, cases), 0)
+    column = lax.broadcasted_iota(jnp.int32, (cases, cases), 1)
+    load_load, load_image = gram[:cases, :cases], gram[:cases, cases:]
+    mixed, image_image = other[:cases], other[cases:]
+    table[...] = jnp.zeros(table.shape, f32)
+    table[:, 0:cases] = jnp.where(row <= column, load_load, load_image)
+    table[:, cases:two] = jnp.where(row <= column, mixed, image_image)
+    for lane, value in ((two, load_image), (two + 1, image_image)):
+        own_entries = jnp.where(row == column, value, 0.0)
+        table[:, lane : lane + 1] = jnp.sum(own_entries, axis=1, keepdims=True)
+    half = cases // 2
+    folded = table[:half, :] + pltpu.roll(table[half:, :], LANES // 2, 1)
+    depth = system_out.shape[2]
+    for index in range(system_out.shape[0]):
+        for part in range(half // depth):
+            system_out[index, part] = folded[part * depth : (part + 1) * depth]
+
+
+def solve_kernel(
+    sizes, system, both, levels, out, mixing, sums, diffs, energy, square, full
+):
     planes, rows, cases = sizes
     two = 2 * cases
     nodes_y = rows + 1
     count = planes * rows
     total = jnp.sum(system[...], axis=0)
-    table = jnp.concatenate(
-        [pltpu.roll(total, LANES - cases, 1), pltpu.roll(total, LANES - two, 1), total], 0
-    )
+    half, depth = cases // 2, system.shape[2]
+    square[...] = jnp.zeros(square.shape, f32)
+    for part in range(half // depth):
+        value = total[part]
+        square[part * depth : (part + 1) * depth, :] = value
+        lines = slice(half + part * depth, half + (part + 1) * depth)
+        square[lines, :] = pltpu.roll(value, LANES // 2, 1)
+    value, turned = square[0:cases, :], jnp.transpose(square[...])
+    line = lax.broadcasted_iota(jnp.int32, (cases, cases), 0)
+    place = lax.broadcasted_iota(jnp.int32, (cases, cases), 1)
+
+    def mended(start, diagonal=None):
+        kept, other = value[:, start : start + cases], turned[start : start + cases, :cases]
+        if diagonal is None:
+            return jnp.where(line <= place, kept, other)
+        inner = jnp.where(line < place, other, value[:, diagonal : diagonal + 1])
+        return jnp.where(line > place, kept, inner)
+
+    load_image, mixed = mended(0, two), mended(cases)
+    parts = ((load_image, mixed), (mixed, mended(cases, two + 1)), (mended(0), load_image))
+    full[...] = jnp.zeros(full.shape, f32)
+    for index, (left, right) in enumerate(parts):
+        full[index * cases : (index + 1) * cases, 0:cases] = left
+        full[index * cases : (index + 1) * cases, cases:two] = right
+    table = full[...]
     lane = lax.broadcasted_iota(jnp.int32, (1, LANES), 1)
     gone = 0
     for pivot in range(two):
@@ -444,7 +482,9 @@
                 lower = upper
         total = jnp.sum(energy[...], axis=1)
         density = 0.3 + 0.7 * levels[plane].astype(f32) / (LEVELS - 1)
-        out[plane] = (-3.0 / cases) * (density * density * density) * total
+        total = (-3.0 / cases) * (density * density * density) * total
+        for index in range(out.shape[0]):
+            out[index, plane] = total
         return 0
 
     lax.fori_loop(0, planes, step, 0)
@@ -514,8 +554,14 @@
     own, up, *down = pl.pallas_call(
         functools.partial(pack_kernel, sizes),
         out_shape=[whole, shape(rows, 2 * rows), *down],
-        in_specs=[VMEM] * 3,
+        in_specs=[pl.BlockSpec(memory_space=pltpu.HBM)] * 3,
         out_specs=[VMEM] * (2 + len(down)),
+        scratch_shapes=[
+            pltpu.VMEM(forces.shape, f32),
+            pltpu.VMEM(levels.shape, jnp.int32),
+            pltpu.VMEM(levels.shape, jnp.int32),
+            pltpu.SemaphoreType.DMA((5,)),
+        ],
         compiler_params=PARAMS,
         name="pack",
     )(forces, levels, supports)
@@ -539,6 +585,7 @@
     )(own, from_xm, from_xp)
     from_yp, from_ym = moved(ym, "gy", -1), moved(yp, "gy", 1)
 
+    devices = count_x * count_y
     nodes = (planes + 1) * (rows + 1)
     wide = (planes + 3) * (rows + 3)
     acc = pltpu.VMEM(((planes + 3) * (rows + 1), block, LANES), f32)
@@ -547,7 +594,7 @@
         functools.partial(main_kernel, sizes),
         out_shape=[
             jax.ShapeDtypeStruct((4 * cases, nodes * 3 * LANES), bf16),
-            jax.ShapeDtypeStruct((cases, LANES), f32),
+            jax.ShapeDtypeStruct((devices, cases // 8, 4, LANES), f32),
         ],
         in_specs=[VMEM] * 5,
         out_specs=[VMEM] * 2,
@@ -558,22 +605,21 @@
             pltpu.VMEM((wide, block, LANES), f32),
             pltpu.VMEM((wide, block, LANES), f32),
             acc, acc, field, field, field, field,
-            pltpu.VMEM((4 * cases, planes * rows * 3 * LANES), bf16),
-            pltpu.VMEM((2 * cases, nodes * 3 * LANES), bf16),
+            pltpu.VMEM((6 * cases, nodes * 3 * LANES), bf16),
+            pltpu.VMEM((cases, LANES), f32),
         ],
         compiler_params=PARAMS,
         name="operator",
     )(own, from_xm, from_xp, from_ym, from_yp)
 
-    def gathered(value):
-        copies = jnp.broadcast_to(value[None], (count_x * count_y, *value.shape))
+    def gathered(copies):
         return lax.all_to_all(copies, ("gx", "gy"), 0, 0)
 
     system = gathered(system)
 
     weighted = pl.pallas_call(
         functools.partial(solve_kernel, sizes),
-        out_shape=jax.ShapeDtypeStruct((planes, rows, LANES), f32),
+        out_shape=jax.ShapeDtypeStruct((devices, planes, rows, LANES), f32),
         in_specs=[VMEM] * 3,
         out_specs=VMEM,
         scratch_shapes=[
@@ -581,6 +627,8 @@
             field,
             field,
             pltpu.VMEM((rows, 8, LANES), f32),
+            pltpu.VMEM((LANES, LANES), f32),
+            pltpu.VMEM((3 * cases, LANES), f32),
         ],
         compiler_params=PARAMS,
         name="solve",

time: 82.9 us -> 74.5 us (0.90)
  Pallas kernels: 22.7 us -> 17.2 us
  blocking collectives: 26.4 us -> 23.9 us
  starting transfers between devices: 15.1 us -> 13.8 us
    pallas_call x1, Pallas kernels: 15.4 us -> 8.25 us  [local(): pl.pallas_call(functools.partial(main_kernel, sizes), out_shape=[jax.Shap...]
    all_to_all x1, blocking collectives: 26.4 us -> 23.9 us  [gathered(): return lax.all_to_all(copies, ('gx', 'gy'), 0, 0)]
    unnamed x8 -> x10, local copies, waits for them, and re-layouts: 2.46 us -> 4.02 us
    all_to_all x1, starting transfers between devices: 3.86 us -> 2.58 us  [gathered(): return lax.all_to_all(copies, ('gx', 'gy'), 0, 0)]
    pallas_call x1, Pallas kernels: 5.85 us -> 6.72 us  [local(): pl.pallas_call(functools.partial(solve_kernel, sizes), out_shape=jax.Shap...]
where the time goes in v4:
time: 74.5 us; the launch traced here: 74 us
  blocking collectives  23.9 us (32%)
  Pallas kernels  17.2 us (23%)
  waiting for transfers between devices  14.9 us (20%)
  starting transfers between devices  13.8 us (19%)
  local copies, waits for them, and re-layouts  4.02 us (5%)
    all_to_all x1, blocking collectives, gathered(): return lax.all_to_all(copies, ('gx', 'gy'), 0, 0)  23.9 us
    ppermute x4, starting transfers between devices, moved(): return lax.ppermute(value, axis, pairs)  11.2 us
    all_to_all x1, waiting for transfers between devices, gathered(): return lax.all_to_all(copies, ('gx', 'gy'), 0, 0)  10.1 us
    pallas_call x1, Pallas kernels, local(): pl.pallas_call(functools.partial(main_kernel, sizes), out_shape=[jax.Shap...  8.25 us
    pallas_call x1, Pallas kernels, local(): pl.pallas_call(functools.partial(solve_kernel, sizes), out_shape=jax.Shap...  6.72 us
    ppermute x4, waiting for transfers between devices, moved(): return lax.ppermute(value, axis, pairs)  4.82 us
    unnamed x10, local copies, waits for them, and re-layouts  4.02 us
    all_to_all x1, starting transfers between devices, gathered(): return lax.all_to_all(copies, ('gx', 'gy'), 0, 0)  2.58 us
  transfers between devices with their start and end apart: 5, of which 4 were waited for; matrix products, arithmetic and copies ran while one was open for 0% of the time, Pallas kernels for 0%

profile of v4, /device:TPU:0, one launch (start us, length us, event | category | flops | bytes accessed | tf_op | source)
XLA Modules:
  0.0 74.0 jit_solution(16976348254369491630)
XLA Ops:
  0.0 0.0 copy-start.1
  0.0 1.1 %copy-done.1 = f32[3,24,2,8,128]{4,3,2,1,0:T(8,128)S(1)} copy-done((f32[3,24,2,8,128]{4,3,2,1,0:T(8,128)S(1)}, f32[3,24,2,8,128]{4,3,2,1,0:T(8,128)}, u32[]{:S(2)}) %copy-start.1) | copy-done | bytes 589848
  1.1 0.0 copy-start.2
  1.1 0.7 copy-done.2
  1.8 0.0 copy-start.4
  1.8 0.7 copy-done.4
  2.5 0.9 %pack.1 = (f32[1168,128]{1,0:T(8,128)S(1)}, f32[592,128]{1,0:T(8,128)S(1)}) custom-call(f32[3,24,2,8,128]{4,3,2,1,0:T(8,128)S(1)} %copy-done.1, s32[2,8,128]{2,1,0:T(8,128)S(1)} %copy-done.2, s32[2,8,128]{2,1,0:T(8,128)S(1)} %copy-done.4), custom_call_target="tpu_custom_call" | custom-call | tf_op jit(solution)/shard_map/pack/pallas_call | solution.py:554
  3.4 0.0 copy-start.3
  3.4 1.3 %collective-permute-start.1 = (f32[1168,128]{1,0:T(8,128)S(1)}, f32[1168,128]{1,0:T(8,128)S(1)}, u32[]{:S(2)}, u32[]{:S(2)}) collective-permute-start(f32[1168,128]{1,0:T(8,128)S(1)} %get-tuple-element.11.own), channel_id=1, source_target_pairs={{4,0},{8,4},{12,8},{16,12},{20,16},{24,20},{28,24},{5,1},{9,5},{13... | collective-permute-start | bytes 1794056 | tf_op jit(solution)/shard_map/ppermute | solution.py:572
  4.7 3.0 %collective-permute-start = (f32[592,128]{1,0:T(8,128)S(1)}, f32[592,128]{1,0:T(8,128)S(1)}, u32[]{:S(2)}, u32[]{:S(2)}) collective-permute-start(f32[592,128]{1,0:T(8,128)S(1)} %get-tuple-element.12), channel_id=1, source_target_pairs={{0,4},{4,8},{8,12},{12,16},{16,20},{20,24},{24,28},{1,5},{5,9},{9,... | collective-permute-start | bytes 909320 | tf_op jit(solution)/shard_map/ppermute | solution.py:572
  7.8 1.2 %collective-permute-done.xm = f32[592,128]{1,0:T(8,128)S(1)} collective-permute-done((f32[592,128]{1,0:T(8,128)S(1)}, f32[592,128]{1,0:T(8,128)S(1)}, u32[]{:S(2)}, u32[]{:S(2)}) %collective-permute-start) | collective-permute-done | bytes 303136 | tf_op jit(solution)/shard_map/ppermute | solution.py:572
  8.9 0.0 collective-permute-done.1.xp
  9.0 1.3 %collective-permute-start.3 = (f32[736,128]{1,0:T(8,128)S(1)}, f32[736,128]{1,0:T(8,128)S(1)}, u32[]{:S(2)}, u32[]{:S(2)}) collective-permute-start(f32[736,128]{1,0:T(8,128)S(1)} %get-tuple-element.14), channel_id=1, source_target_pairs={{1,0},{2,1},{3,2},{5,4},{6,5},{7,6},{9,8},{10,9},{11,10},{13,12},{... | collective-permute-start | bytes 1130504 | tf_op jit(solution)/shard_map/ppermute | solution.py:572
  10.3 5.6 %collective-permute-start.2 = (f32[376,128]{1,0:T(8,128)S(1)}, f32[376,128]{1,0:T(8,128)S(1)}, u32[]{:S(2)}, u32[]{:S(2)}) collective-permute-start(f32[376,128]{1,0:T(8,128)S(1)} %get-tuple-element.13), channel_id=1, source_target_pairs={{0,1},{1,2},{2,3},{4,5},{5,6},{6,7},{8,9},{9,10},{10,11},{12,13},{... | collective-permute-start | bytes 577544 | tf_op jit(solution)/shard_map/ppermute | solution.py:572
  15.9 3.1 %collective-permute-done.2.ym = f32[376,128]{1,0:T(8,128)S(1)} collective-permute-done((f32[376,128]{1,0:T(8,128)S(1)}, f32[376,128]{1,0:T(8,128)S(1)}, u32[]{:S(2)}, u32[]{:S(2)}) %collective-permute-start.2) | collective-permute-done | bytes 192544 | tf_op jit(solution)/shard_map/ppermute | solution.py:572
  19.0 0.5 collective-permute-done.3.yp
  19.5 8.3 %operator.1 = (bf16[96,10368]{1,0:T(8,128)(2,1)}, f32[32,3,4,128]{3,2,1,0:T(4,128)S(1)}) custom-call(f32[1168,128]{1,0:T(8,128)S(1)} %get-tuple-element.11.own, f32[592,128]{1,0:T(8,128)S(1)} %collective-permute-done.xm, f32[1168,128]{1,0:T(8,128)S(1)} %collective-permute-done.1.xp, f32[376,128]{1,0:T(8,128)S(1)} %collective-permute-done.2.ym, ...), custom_call_target="tpu_custom_call" | custom-call | tf_op jit(solution)/shard_map/operator/pallas_call | solution.py:593
  27.8 23.9 %all_to_all.10.system = f32[32,3,4,128]{3,2,1,0:T(4,128)S(1)} all-to-all(f32[32,3,4,128]{3,2,1,0:T(4,128)S(1)} %get-tuple-element.15), channel_id=1, replica_groups=mesh['gx'=8,'gy'=4] {'gx','gy'}, dimensions={0} | all-to-all | bytes 393216 | tf_op jit(solution)/shard_map/all_to_all | solution.py:616
  51.7 0.0 copy-done.3
  51.7 0.0 copy-start
  51.7 1.6 %copy-done = bf16[96,10368]{1,0:T(8,128)(2,1)S(1)} copy-done((bf16[96,10368]{1,0:T(8,128)(2,1)S(1)}, bf16[96,10368]{1,0:T(8,128)(2,1)}, u32[]{:S(2)}) %copy-start) | copy-done | bytes 1990680
  53.2 6.7 %solve.1 = f32[32,2,8,128]{3,2,1,0:T(8,128)} custom-call(f32[32,3,4,128]{3,2,1,0:T(4,128)S(1)} %all_to_all.10.system, bf16[96,10368]{1,0:T(8,128)(2,1)S(1)} %copy-done, s32[2,8,128]{2,1,0:T(8,128)S(1)} %copy-done.3), custom_call_target="tpu_custom_call" | custom-call | tf_op jit(solution)/shard_map/solve/pallas_call | solution.py:620
  59.9 2.6 %all-to-all-start.1 = ((f32[32,2,8,128]{3,2,1,0:T(8,128)}), f32[32,2,8,128]{3,2,1,0:T(8,128)S(1)}, u32[]{:S(2)}, u32[]{:S(2)}) async-start(f32[32,2,8,128]{3,2,1,0:T(8,128)} %solve.1), calls=%async_computation.1 | async-start | bytes 524288 | tf_op jit(solution)/shard_map/all_to_all | solution.py:616
  62.5 0.1 pad_add_fusion.start
  62.6 10.1 %all-to-all-done.1.blocks = f32[32,2,8,128]{3,2,1,0:T(8,128)S(1)} async-done(((f32[32,2,8,128]{3,2,1,0:T(8,128)}), f32[32,2,8,128]{3,2,1,0:T(8,128)S(1)}, u32[]{:S(2)}, u32[]{:S(2)}) %all-to-all-start.1) | async-done | bytes 262176 | tf_op jit(solution)/shard_map/all_to_all | solution.py:616
  72.7 1.3 %cone.1 = f32[2,8,128]{2,1,0:T(8,128)} custom-call(s32[2]{0:T(128)S(1)} %pad_add_fusion.start, f32[32,2,8,128]{3,2,1,0:T(8,128)S(1)} %all-to-all-done.1.blocks, s32[2,8,128]{2,1,0:T(8,128)S(1)} %copy-done.3), custom_call_target="tpu_custom_call" | custom-call | tf_op jit(solution)/shard_map/cone/pallas_call | solution.py:639
  (1 shorter events, 0.0 us)
Async XLA Ops:
  0.0 1.1 %copy-start.1 = (f32[3,24,2,8,128]{4,3,2,1,0:T(8,128)S(1)}, f32[3,24,2,8,128]{4,3,2,1,0:T(8,128)}, u32[]{:S(2)}) copy-start(f32[3,24,2,8,128]{4,3,2,1,0:T(8,128)} %forces_hbm.1) | copy-start | bytes 1769476
  1.1 0.7 copy-start.2
  1.8 0.7 copy-start.4
  3.4 48.3 %copy-start.3 = (s32[2,8,128]{2,1,0:T(8,128)S(1)}, s32[2,8,128]{2,1,0:T(8,128)}, u32[]{:S(2)}) copy-start(s32[2,8,128]{2,1,0:T(8,128)} %levels.3) | copy-start | bytes 24580
  3.4 5.5 %collective-permute-start.1 = (f32[1168,128]{1,0:T(8,128)S(1)}, f32[1168,128]{1,0:T(8,128)S(1)}, u32[]{:S(2)}, u32[]{:S(2)}) collective-permute-start(f32[1168,128]{1,0:T(8,128)S(1)} %get-tuple-element.11.own), channel_id=1, source_target_pairs={{4,0},{8,4},{12,8},{16,12},{20,16},{24,20},{28,24},{5,1},{9,5},{13... | collective-permute-start | bytes 1794056 | tf_op jit(solution)/shard_map/ppermute | solution.py:572
  4.7 4.2 %collective-permute-start = (f32[592,128]{1,0:T(8,128)S(1)}, f32[592,128]{1,0:T(8,128)S(1)}, u32[]{:S(2)}, u32[]{:S(2)}) collective-permute-start(f32[592,128]{1,0:T(8,128)S(1)} %get-tuple-element.12), channel_id=1, source_target_pairs={{0,4},{4,8},{8,12},{12,16},{16,20},{20,24},{24,28},{1,5},{5,9},{9,... | collective-permute-start | bytes 909320 | tf_op jit(solution)/shard_map/ppermute | solution.py:572
  9.0 10.5 %collective-permute-start.3 = (f32[736,128]{1,0:T(8,128)S(1)}, f32[736,128]{1,0:T(8,128)S(1)}, u32[]{:S(2)}, u32[]{:S(2)}) collective-permute-start(f32[736,128]{1,0:T(8,128)S(1)} %get-tuple-element.14), channel_id=1, source_target_pairs={{1,0},{2,1},{3,2},{5,4},{6,5},{7,6},{9,8},{10,9},{11,10},{13,12},{... | collective-permute-start | bytes 1130504 | tf_op jit(solution)/shard_map/ppermute | solution.py:572
  10.3 8.7 %collective-permute-start.2 = (f32[376,128]{1,0:T(8,128)S(1)}, f32[376,128]{1,0:T(8,128)S(1)}, u32[]{:S(2)}, u32[]{:S(2)}) collective-permute-start(f32[376,128]{1,0:T(8,128)S(1)} %get-tuple-element.13), channel_id=1, source_target_pairs={{0,1},{1,2},{2,3},{4,5},{5,6},{6,7},{8,9},{9,10},{10,11},{12,13},{... | collective-permute-start | bytes 577544 | tf_op jit(solution)/shard_map/ppermute | solution.py:572
  51.7 1.6 %copy-start = (bf16[96,10368]{1,0:T(8,128)(2,1)S(1)}, bf16[96,10368]{1,0:T(8,128)(2,1)}, u32[]{:S(2)}) copy-start(bf16[96,10368]{1,0:T(8,128)(2,1)} %get-tuple-element.16.both) | copy-start | bytes 5971972
  59.9 12.8 %all-to-all-start.1 = ((f32[32,2,8,128]{3,2,1,0:T(8,128)}), f32[32,2,8,128]{3,2,1,0:T(8,128)S(1)}, u32[]{:S(2)}, u32[]{:S(2)}) async-start(f32[32,2,8,128]{3,2,1,0:T(8,128)} %solve.1), calls=%async_computation.1 | async-start | bytes 524288 | tf_op jit(solution)/shard_map/all_to_all | solution.py:616

commit v5 on v4

--- a/solution.py
+++ b/solution.py
@@ -16,7 +16,7 @@
 SHEAR = 1.0 / (2.0 * (1.0 + POISSON))
 DIAGONAL = (LAME + 2.0 * SHEAR) / 9.0 + 2.0 * SHEAR / 9.0
 VMEM = pl.BlockSpec(memory_space=pltpu.VMEM)
-PARAMS = pltpu.CompilerParams(vmem_limit_bytes=50 * 2**20)
+PARAMS = pltpu.CompilerParams(vmem_limit_bytes=30 * 2**20)
 f32 = jnp.float32
 bf16 = jnp.bfloat16
 
@@ -192,35 +192,17 @@
     lax.fori_loop(0, planes * tiles, step, 0)
 
 
-def pack_kernel(sizes, forces_hbm, levels_hbm, supports_hbm, own, up, *rest):
+def pack_kernel(sizes, forces, codes, own, up, *rest):
     planes, rows, cases = sizes
     block = 3 * cases
     base = planes * rows * block
-    *rest, forces, levels, supports, arrived = rest
-    copies = [
-        pltpu.make_async_copy(levels_hbm, levels, arrived.at[3]),
-        pltpu.make_async_copy(supports_hbm, supports, arrived.at[4]),
-    ]
-    copies += [
-        pltpu.make_async_copy(forces_hbm.at[k], forces.at[k], arrived.at[k]) for k in range(3)
-    ]
-    for copy in copies:
-        copy.start()
-    copies[0].wait()
-    copies[1].wait()
-    scales = []
     for x in range(planes):
-        density = 0.3 + 0.7 * levels[x].astype(f32) / (LEVELS - 1)
-        stiff = density * density * density
-        free = supports[x] == 0
-        own[base + x * rows : base + (x + 1) * rows, :] = jnp.where(free, stiff, -stiff)
-        scales.append(jnp.where(free, LOAD, 0.0))
-    for k in range(3):
-        copies[2 + k].wait()
-        for x in range(planes):
+        own[base + x * rows : base + (x + 1) * rows, :] = codes[x]
+        scale = jnp.where(codes[x] > 0.0, LOAD, 0.0)
+        for k in range(3):
             for c in range(cases):
                 start = x * rows * block + k * cases + c
-                own[pl.ds(start, rows, stride=block), :] = forces[k, c, x] * scales[x]
+                own[pl.ds(start, rows, stride=block), :] = forces[k, c, x] * scale
 
     def fill(ref, xs, code_xs):
         size = len(xs) * rows * block
@@ -233,32 +215,60 @@
         fill(ref, range(2), range(2))
 
 
-def edge_kernel(sizes, own, xm, xp, ym, yp):
+def beside(sizes, first, pair, lower, upper):
+    planes, rows, cases = sizes
+    size = rows * 3 * cases
+    even = first // planes % 2 == 0
+
+    def below(line, count):
+        other = pair[pl.ds((planes - 1) * size + line, count), :]
+        return jnp.where(even, lower[pl.ds(line, count), :], other)
+
+    def below_codes(line, count):
+        other = pair[pl.ds(planes * size + (planes - 2) * rows + line, count), :]
+        return jnp.where(even, lower[pl.ds(size + line, count), :], other)
+
+    def above(line, count):
+        return jnp.where(even, pair[pl.ds(line, count), :], upper[pl.ds(line, count), :])
+
+    def above_codes(line, count):
+        other = upper[pl.ds(2 * size + line, count), :]
+        return jnp.where(even, pair[pl.ds(planes * size + line, count), :], other)
+
+    return below, below_codes, above, above_codes
+
+
+def edge_kernel(sizes, start, own, pair, lower, upper, ym, yp):
     planes, rows, cases = sizes
     block = 3 * cases
+    base = planes * rows * block
+    below, below_codes, above, above_codes = beside(sizes, start[0], pair, lower, upper)
     parts = (
-        (xm, rows * block, range(1), range(2)),
-        (own, planes * rows * block, range(planes), range(planes)),
-        (xp, 2 * rows * block, range(2), range(2)),
+        (below, below_codes, 1, 2),
+        (
+            lambda line, count: own[line : line + count, :],
+            lambda line, count: own[base + line : base + line + count, :],
+            planes,
+            planes,
+        ),
+        (above, above_codes, 2, 2),
     )
-    for ref, low, count, code in ((ym, 0, 2, 2), (yp, rows - 1, 1, 2)):
+    for ref, low, count in ((ym, 0, 2), (yp, rows - 1, 1)):
         line = 0
-        for source, _, xs, _ in parts:
-            for x in xs:
-                start = (x * rows + low) * block
-                ref[line : line + count * block, :] = source[start : start + count * block, :]
+        for read, _, xs, _ in parts:
+            for x in range(xs):
+                ref[line : line + count * block, :] = read((x * rows + low) * block, count * block)
                 line += count * block
-        for source, base, _, xs in parts:
-            for x in xs:
-                start = base + x * rows + (0 if low == 0 else rows - 2)
-                ref[line : line + code, :] = source[start : start + code, :]
-                line += code
+        for _, read, _, xs in parts:
+            for x in range(xs):
+                ref[line : line + 2, :] = read(x * rows + (0 if low == 0 else rows - 2), 2)
+                line += 2
         if line < ref.shape[0]:
             ref[line:, :] = jnp.zeros((ref.shape[0] - line, LANES), f32)
 
 
 def main_kernel(
-    sizes, own, xm, xp, ym, yp, both_out, system_out, stiff_ref, inverse,
+    sizes, first, own, pair, lower, upper, ym, yp, both_out, system_out, stiff_ref, inverse,
     start, sums, diffs, acc_s, acc_d, w_sums, w_diffs, acc2_s, acc2_d, right, table,
 ):
     planes, rows, cases = sizes
@@ -267,18 +277,24 @@
     every_x, every_y = range(planes), range(rows)
     low, high_x, high_y = (-1,), (planes, planes + 1), (rows, rows + 1)
     low2 = (-2, -1)
+    below, below_codes, above, above_codes = beside(sizes, first[0], pair, lower, upper)
+
+    def reader(ref, base=0):
+        return lambda line, count: ref[base + line : base + line + count, :]
+
+    def region(ref, bx, by, cx, cy):
+        return (reader(ref), reader(ref, len(bx) * len(by) * block), bx, by, cx, cy)
+
     regions = (
-        (own, every_x, every_y, every_x, every_y),
-        (xm, low, every_y, low2, every_y),
-        (xp, high_x, every_y, high_x, every_y),
-        (ym, range(-1, planes + 2), low, range(-2, planes + 2), low2),
-        (yp, range(-1, planes + 2), high_y, range(-2, planes + 2), high_y),
+        region(own, every_x, every_y, every_x, every_y),
+        (below, below_codes, low, every_y, low2, every_y),
+        (above, above_codes, high_x, every_y, high_x, every_y),
+        region(ym, range(-1, planes + 2), low, range(-2, planes + 2), low2),
+        region(yp, range(-1, planes + 2), high_y, range(-2, planes + 2), high_y),
     )
-    for ref, bx, by, cx, cy in regions:
-        base = len(bx) * len(by) * block
+    for _, read, _, _, cx, cy in regions:
         for i, x in enumerate(cx):
-            line = base + i * len(cy)
-            stiff_ref[x + 2, cy[0] + 2 : cy[0] + 2 + len(cy), :] = ref[line : line + len(cy), :]
+            stiff_ref[x + 2, cy[0] + 2 : cy[0] + 2 + len(cy), :] = read(i * len(cy), len(cy))
     for x in range(-1, planes + 2):
         codes = stiff_ref[x + 2, 0 : ys + 1, :]
         total = jnp.abs(stiff_ref[x + 1, 0 : ys + 1, :]) + jnp.abs(codes)
@@ -290,13 +306,13 @@
     for x in range(planes + 4):
         stiff_ref[x] = jnp.abs(stiff_ref[x])
 
-    for ref, bx, by, _, _ in regions:
+    for read, _, bx, by, _, _ in regions:
         for i, x in enumerate(bx):
 
             for j in range(len(by)):
                 y = j + by[0] + 1
                 line = (i * len(by) + j) * block
-                load = ref[line : line + block, :]
+                load = read(line, block)
                 value = load * inverse[x + 1, y : y + 1, :]
                 column = (x + 1) * ys + y
                 start[column] = value
@@ -390,7 +406,7 @@
 
 
 def solve_kernel(
-    sizes, system, both, levels, out, mixing, sums, diffs, energy, square, full
+    sizes, system, both, codes, out, mixing, sums, diffs, energy, square, full
 ):
     planes, rows, cases = sizes
     two = 2 * cases
@@ -423,17 +439,37 @@
         full[index * cases : (index + 1) * cases, cases:two] = right
     table = full[...]
     lane = lax.broadcasted_iota(jnp.int32, (1, LANES), 1)
-    gone = 0
-    for pivot in range(two):
+    gone, wide = 0, 4
+    for pivot in range(0, two, wide):
         drop = pivot // 8 * 8 - gone
         table = table[drop:]
         gone += drop
         line = pivot - gone
-        row = table[line : line + 1, :]
-        inverse = 1.0 / row[:, pivot : pivot + 1]
-        row = jnp.where(lane == pivot, -inverse, row * inverse)
-        column = table[:, pivot : pivot + 1]
-        table = jnp.where(lane == pivot, 0.0, table) - column * row
+        inner = (lane >= pivot) & (lane < pivot + wide)
+        found = [table[line + p : line + p + 1, :] for p in range(wide)]
+        block = [
+            [jnp.broadcast_to(row[:, pivot + q : pivot + q + 1], row.shape) for q in range(wide)]
+            for row in found
+        ]
+        solved = [
+            jnp.where(lane == pivot + p, -1.0, jnp.where(inner, 0.0, found[p]))
+            for p in range(wide)
+        ]
+        for p in range(wide):
+            inverse = 1.0 / block[p][p]
+            solved[p] = solved[p] * inverse
+            block[p] = [value * inverse for value in block[p]]
+            for q in range(wide):
+                if q != p:
+                    factor = block[q][p]
+                    solved[q] = solved[q] - factor * solved[p]
+                    for r in range(p + 1, wide):
+                        block[q][r] = block[q][r] - factor * block[p][r]
+        update = None
+        for q in range(wide):
+            term = table[:, pivot + q : pivot + q + 1] * solved[q]
+            update = term if update is None else update + term
+        table = jnp.where(inner, 0.0, table) - update
     answer = table[two - gone :, :two]
     high = answer.astype(bf16).astype(f32)
     mixing[...] = jnp.zeros(mixing.shape, f32)
@@ -481,8 +517,7 @@
                     energy[row] += part
                 lower = upper
         total = jnp.sum(energy[...], axis=1)
-        density = 0.3 + 0.7 * levels[plane].astype(f32) / (LEVELS - 1)
-        total = (-3.0 / cases) * (density * density * density) * total
+        total = (-3.0 / cases) * jnp.abs(codes[plane]) * total
         for index in range(out.shape[0]):
             out[index, plane] = total
         return 0
@@ -490,10 +525,47 @@
     lax.fori_loop(0, planes, step, 0)
 
 
-def filter_kernel(sizes, counts, start, blocks, levels, out, wide, there):
+def smooth(ref, x, rows):
+    weight = [2.5 - math.sqrt(q) for q in range(7)]
+    near = {}
+    for dx in range(-2, 3):
+        for dy in range(-2, 3):
+            q = dx * dx + dy * dy
+            if q <= 5:
+                value = ref[x + 2 + dx, 2 + dy : 2 + dy + rows, :]
+                near[q] = value if q not in near else near[q] + value
+    result = None
+    for dz in range(3):
+        part = None
+        for q, value in near.items():
+            if q + dz * dz <= 6:
+                term = weight[q + dz * dz] * value
+                part = term if part is None else part + term
+        if dz == 0:
+            result = part
+        else:
+            place = lax.broadcasted_iota(jnp.int32, part.shape, 1)
+            forward = jnp.where(place >= LANES - dz, 0.0, pltpu.roll(part, LANES - dz, 1))
+            backward = jnp.where(place < dz, 0.0, pltpu.roll(part, dz, 1))
+            result = result + (forward + backward)
+    return result
+
+
+def scale_kernel(sizes, counts, start, levels, out, there):
     planes, rows, _ = sizes
-    totals = (counts[0] * planes, counts[1] * rows)
-    weight = [2.5 - math.sqrt(q) for q in range(7)]
+    y = lax.broadcasted_iota(jnp.int32, (rows + 4, LANES), 0) + (start[1] - 2)
+    in_y = (y >= 0) & (y < counts[1] * rows)
+    for x in range(planes + 4):
+        global_x = start[0] + (x - 2)
+        in_x = (global_x >= 0) & (global_x < counts[0] * planes)
+        there[x] = jnp.where(in_y & in_x, 1.0, 0.0)
+    for x in range(planes):
+        density = 0.3 + 0.7 * levels[x].astype(f32) / (LEVELS - 1)
+        out[x] = 1.0 / (density * smooth(there, x, rows))
+
+
+def filter_kernel(sizes, counts, start, blocks, scale, out, wide):
+    planes, rows, _ = sizes
     sides_x = ((-1, planes - 2, planes, 0), (0, 0, planes, 2), (1, 0, 2, 2 + planes))
     sides_y = ((-1, rows - 2, rows, 0), (0, 0, rows, 2), (1, 0, 2, 2 + rows))
     for step_x, x0, x1, to_x in sides_x:
@@ -504,40 +576,8 @@
             index = jnp.where(inside, at_x * counts[1] + at_y, 0)
             value = blocks[index, x0:x1, y0:y1, :]
             wide[to_x : to_x + x1 - x0, to_y : to_y + y1 - y0, :] = jnp.where(inside, value, 0.0)
-    y = lax.broadcasted_iota(jnp.int32, (rows + 4, LANES), 0) + (start[1] - 2)
-    in_y = jnp.logical_and(y >= 0, y < totals[1])
-    for x in range(planes + 4):
-        global_x = start[0] + (x - 2)
-        in_x = jnp.logical_and(global_x >= 0, global_x < totals[0])
-        there[x] = jnp.where(jnp.logical_and(in_y, in_x), 1.0, 0.0)
-
-    def smooth(ref, x):
-        near = {}
-        for dx in range(-2, 3):
-            for dy in range(-2, 3):
-                q = dx * dx + dy * dy
-                if q <= 5:
-                    value = ref[x + 2 + dx, 2 + dy : 2 + dy + rows, :]
-                    near[q] = value if q not in near else near[q] + value
-        result = 0.0
-        for dz in range(3):
-            part = None
-            for q, value in near.items():
-                if q + dz * dz <= 6:
-                    term = weight[q + dz * dz] * value
-                    part = term if part is None else part + term
-            if dz == 0:
-                result = part
-            else:
-                place = lax.broadcasted_iota(jnp.int32, part.shape, 1)
-                forward = jnp.where(place >= LANES - dz, 0.0, pltpu.roll(part, LANES - dz, 1))
-                backward = jnp.where(place < dz, 0.0, pltpu.roll(part, dz, 1))
-                result = result + (forward + backward)
-        return result
-
     for x in range(planes):
-        density = 0.3 + 0.7 * levels[x].astype(f32) / (LEVELS - 1)
-        out[x] = smooth(wide, x) / (density * smooth(there, x))
+        out[x] = smooth(wide, x, rows) * scale[x]
 
 
 def local(forces, levels, supports):
@@ -549,40 +589,55 @@
     def shape(blocks, codes):
         return jax.ShapeDtypeStruct((blocks * block + up8(codes), LANES), f32)
 
+    density = 0.3 + 0.7 * levels.astype(f32) / (LEVELS - 1)
+    codes = density * density * density
+    codes = jnp.where(supports == 0, codes, -codes)
     whole = shape(planes * rows, planes * rows)
     down = [] if planes == 2 else [shape(2 * rows, 2 * rows)]
     own, up, *down = pl.pallas_call(
         functools.partial(pack_kernel, sizes),
         out_shape=[whole, shape(rows, 2 * rows), *down],
-        in_specs=[pl.BlockSpec(memory_space=pltpu.HBM)] * 3,
+        in_specs=[VMEM] * 2,
         out_specs=[VMEM] * (2 + len(down)),
-        scratch_shapes=[
-            pltpu.VMEM(forces.shape, f32),
-            pltpu.VMEM(levels.shape, jnp.int32),
-            pltpu.VMEM(levels.shape, jnp.int32),
-            pltpu.SemaphoreType.DMA((5,)),
-        ],
         compiler_params=PARAMS,
         name="pack",
-    )(forces, levels, supports)
+    )(forces, codes)
+
+    start = jnp.stack([lax.axis_index("gx") * planes, lax.axis_index("gy") * rows])
+    start = start.astype(jnp.int32)
+    counts = (count_x, count_y)
+    scalars = pl.BlockSpec(memory_space=pltpu.SMEM)
+    scale = pl.pallas_call(
+        functools.partial(scale_kernel, sizes, counts),
+        out_shape=jax.ShapeDtypeStruct((planes, rows, LANES), f32),
+        in_specs=[scalars, VMEM],
+        out_specs=VMEM,
+        scratch_shapes=[pltpu.VMEM((planes + 4, rows + 4, LANES), f32)],
+        compiler_params=PARAMS,
+        name="scale",
+    )(start, levels)
 
     def moved(value, axis, step):
         count = lax.axis_size(axis)
         pairs = [(i, i + step) for i in range(count) if 0 <= i + step < count]
         return lax.ppermute(value, axis, pairs)
 
-    from_xp = moved(down[0] if down else own, "gx", -1)
-    from_xm = moved(up, "gx", 1)
+    def links(first, step):
+        return [(i, i + step) for i in range(first, count_x, 2) if 0 <= i + step < count_x]
+
+    upper = lax.ppermute(down[0] if down else own, "gx", links(2, -1))
+    lower = lax.ppermute(up, "gx", links(1, 1))
+    pair = lax.ppermute(own, "gx", links(0, 1) + links(1, -1))
     ym, yp = pl.pallas_call(
         functools.partial(edge_kernel, sizes),
         out_shape=[
             shape(2 * (planes + 3), 2 * (planes + 4)), shape(planes + 3, 2 * (planes + 4))
         ],
-        in_specs=[VMEM] * 3,
+        in_specs=[scalars] + [VMEM] * 4,
         out_specs=[VMEM] * 2,
         compiler_params=PARAMS,
         name="edges",
-    )(own, from_xm, from_xp)
+    )(start, own, pair, lower, upper)
     from_yp, from_ym = moved(ym, "gy", -1), moved(yp, "gy", 1)
 
     devices = count_x * count_y
@@ -596,7 +651,7 @@
             jax.ShapeDtypeStruct((4 * cases, nodes * 3 * LANES), bf16),
             jax.ShapeDtypeStruct((devices, cases // 8, 4, LANES), f32),
         ],
-        in_specs=[VMEM] * 5,
+        in_specs=[scalars] + [VMEM] * 6,
         out_specs=[VMEM] * 2,
         scratch_shapes=[
             pltpu.VMEM((planes + 4, up8(rows + 4), LANES), f32),
@@ -610,7 +665,7 @@
         ],
         compiler_params=PARAMS,
         name="operator",
-    )(own, from_xm, from_xp, from_ym, from_yp)
+    )(start, own, pair, lower, upper, from_ym, from_yp)
 
     def gathered(copies):
         return lax.all_to_all(copies, ("gx", "gy"), 0, 0)
@@ -632,19 +687,18 @@
         ],
         compiler_params=PARAMS,
         name="solve",
-    )(system, both, levels)
+    )(system, both, codes)
 
     blocks = gathered(weighted)
-    start = jnp.stack([lax.axis_index("gx") * planes, lax.axis_index("gy") * rows])
     return pl.pallas_call(
-        functools.partial(filter_kernel, sizes, (count_x, count_y)),
+        functools.partial(filter_kernel, sizes, counts),
         out_shape=jax.ShapeDtypeStruct((planes, rows, LANES), f32),
-        in_specs=[pl.BlockSpec(memory_space=pltpu.SMEM)] + [VMEM] * 2,
+        in_specs=[scalars] + [VMEM] * 2,
         out_specs=VMEM,
-        scratch_shapes=[pltpu.VMEM((planes + 4, rows + 4, LANES), f32)] * 2,
+        scratch_shapes=[pltpu.VMEM((planes + 4, rows + 4, LANES), f32)],
         compiler_params=PARAMS,
         name="cone",
-    )(start.astype(jnp.int32), blocks, levels)
+    )(start, blocks, scale)
 
 
 def solution(mesh):

time: 74.5 us -> 71.2 us (0.956)
  blocking collectives: 23.9 us -> 28.1 us
  local copies, waits for them, and re-layouts: 4.02 us -> 1.07 us
  starting transfers between devices: 13.8 us -> 11.2 us
  waiting for transfers between devices: 14.9 us -> 13.3 us
  Pallas kernels: 17.2 us -> 16.2 us
    ppermute x4 -> x2, starting transfers between devices: 11.2 us -> 6.78 us  [moved(): return lax.ppermute(value, axis, pairs)]
    all_to_all x1, blocking collectives: 23.9 us -> 28.1 us  [gathered(): return lax.all_to_all(copies, ('gx', 'gy'), 0, 0)]
    unnamed x10 -> x4, local copies, waits for them, and re-layouts: 4.02 us -> 1.07 us
    pallas_call x1, Pallas kernels: 6.72 us -> 4.71 us  [local(): pl.pallas_call(functools.partial(solve_kernel, sizes), out_shape=jax.Shap...]
    ppermute x0 -> x3, starting transfers between devices: none -> 1.88 us  [the longest x1 0.69 us: local(): upper = lax.ppermute(down[0] if down else own, 'gx', links(2, -1))]
    ppermute x4 -> x2, waiting for transfers between devices: 4.82 us -> 3.63 us  [moved(): return lax.ppermute(value, axis, pairs)]
    pallas_call x1, Pallas kernels: 0.93 us -> 0.12 us  [local(): pl.pallas_call(functools.partial(pack_kernel, sizes), out_shape=[whole, s...]
    pallas_call x1 -> x2, Pallas kernels: 1.29 us -> 1.93 us  [the longest x1 1.28 us: local(): pl.pallas_call(functools.partial(filter_kernel, sizes, counts), out_shape...]
  transfers between devices with their start and end apart: 5 -> 6, of which waited for: 4 -> 4; matrix products, arithmetic and copies ran while one was open for 0% -> 0% of each run, Pallas kernels for 0% -> 1%
where the time goes in v5:
time: 71.2 us; the launch traced here: 70.8 us
  blocking collectives  28.1 us (39%)
  Pallas kernels  16.2 us (23%)
  waiting for transfers between devices  13.3 us (19%)
  starting transfers between devices  11.2 us (16%)
  local copies, waits for them, and re-layouts  1.07 us (2%)
  other arithmetic  0.8 us (1%)
    all_to_all x1, blocking collectives, gathered(): return lax.all_to_all(copies, ('gx', 'gy'), 0, 0)  28.1 us
    all_to_all x1, waiting for transfers between devices, gathered(): return lax.all_to_all(copies, ('gx', 'gy'), 0, 0)  9.53 us
    pallas_call x1, Pallas kernels, local(): pl.pallas_call(functools.partial(main_kernel, sizes), out_shape=[jax.Shap...  8.83 us
    ppermute x2, starting transfers between devices, moved(): return lax.ppermute(value, axis, pairs)  6.78 us
    pallas_call x1, Pallas kernels, local(): pl.pallas_call(functools.partial(solve_kernel, sizes), out_shape=jax.Shap...  4.71 us
    ppermute x2, waiting for transfers between devices, moved(): return lax.ppermute(value, axis, pairs)  3.63 us
    all_to_all x1, starting transfers between devices, gathered(): return lax.all_to_all(copies, ('gx', 'gy'), 0, 0)  2.58 us
  transfers between devices with their start and end apart: 6, of which 4 were waited for; matrix products, arithmetic and copies ran while one was open for 0% of the time, Pallas kernels for 1%

profile of v5, /device:TPU:0, one launch (start us, length us, event | category | flops | bytes accessed | tf_op | source)
XLA Modules:
  0.0 70.8 jit_solution(9322774282374072700)
XLA Ops:
  0.0 0.7 %negate_select_fusion.codes = f32[2,8,128]{2,1,0:T(8,128)S(1)} fusion(s32[2,8,128]{2,1,0:T(8,128)} %levels.1, s32[2,8,128]{2,1,0:T(8,128)} %param.5), kind=kLoop, calls=%fused_computation | loop fusion | flops 16384 | bytes 24576 | tf_op jit(solution)/shard_map/jit(_where)/select_n | solution.py:594
  0.7 0.0 copy-start
  0.7 1.1 %copy-done = f32[3,24,2,8,128]{4,3,2,1,0:T(8,128)S(1)} copy-done((f32[3,24,2,8,128]{4,3,2,1,0:T(8,128)S(1)}, f32[3,24,2,8,128]{4,3,2,1,0:T(8,128)}, u32[]{:S(2)}) %copy-start) | copy-done | bytes 589848
  1.8 0.1 pack.1
  1.9 0.5 collective-permute-start
  2.4 0.7 collective-permute-start.2
  3.1 0.7 collective-permute-start.1
  3.8 0.1 pad_add_fusion.start.first
  3.9 0.0 collective-permute-done.1.lower
  3.9 0.2 collective-permute-done.pair
  4.1 0.0 collective-permute-done.2.upper
  4.1 0.6 edges.1
  4.7 1.3 %collective-permute-start.4 = (f32[736,128]{1,0:T(8,128)S(1)}, f32[736,128]{1,0:T(8,128)S(1)}, u32[]{:S(2)}, u32[]{:S(2)}) collective-permute-start(f32[736,128]{1,0:T(8,128)S(1)} %get-tuple-element.14), channel_id=1, source_target_pairs={{1,0},{2,1},{3,2},{5,4},{6,5},{7,6},{9,8},{10,9},{11,10},{13,12},{... | collective-permute-start | bytes 1130504 | tf_op jit(solution)/shard_map/ppermute | solution.py:623
  6.0 5.5 %collective-permute-start.3 = (f32[376,128]{1,0:T(8,128)S(1)}, f32[376,128]{1,0:T(8,128)S(1)}, u32[]{:S(2)}, u32[]{:S(2)}) collective-permute-start(f32[376,128]{1,0:T(8,128)S(1)} %get-tuple-element.13), channel_id=1, source_target_pairs={{0,1},{1,2},{2,3},{4,5},{5,6},{6,7},{8,9},{9,10},{10,11},{12,13},{... | collective-permute-start | bytes 577544 | tf_op jit(solution)/shard_map/ppermute | solution.py:623
  11.5 3.1 %collective-permute-done.3.ym = f32[376,128]{1,0:T(8,128)S(1)} collective-permute-done((f32[376,128]{1,0:T(8,128)S(1)}, f32[376,128]{1,0:T(8,128)S(1)}, u32[]{:S(2)}, u32[]{:S(2)}) %collective-permute-start.3) | collective-permute-done | bytes 192544 | tf_op jit(solution)/shard_map/ppermute | solution.py:623
  14.6 0.5 collective-permute-done.4.yp
  15.1 8.8 %operator.1 = (bf16[96,10368]{1,0:T(8,128)(2,1)S(1)}, f32[32,3,4,128]{3,2,1,0:T(4,128)S(1)}) custom-call(s32[2]{0:T(128)S(1)} %pad_add_fusion.start.first, f32[1168,128]{1,0:T(8,128)S(1)} %get-tuple-element.11.own, f32[1168,128]{1,0:T(8,128)S(1)} %collective-permute-done.pair, f32[592,128]{1,0:T(8,128)S(1)} %collective-permute-done.1.lower, ...), custom_call_target="tpu_custom_call" | custom-call | tf_op jit(solution)/shard_map/operator/pallas_call | solution.py:648
  23.9 0.0 copy-start.1
  23.9 28.1 %all_to_all.10.system = f32[32,3,4,128]{3,2,1,0:T(4,128)S(1)} all-to-all(f32[32,3,4,128]{3,2,1,0:T(4,128)S(1)} %get-tuple-element.15), channel_id=1, replica_groups=mesh['gx'=8,'gy'=4] {'gx','gy'}, dimensions={0} | all-to-all | bytes 393216 | tf_op jit(solution)/shard_map/all_to_all | solution.py:671
  52.0 4.7 %solve.1 = f32[32,2,8,128]{3,2,1,0:T(8,128)} custom-call(f32[32,3,4,128]{3,2,1,0:T(4,128)S(1)} %all_to_all.10.system, bf16[96,10368]{1,0:T(8,128)(2,1)S(1)} %get-tuple-element.16.both, f32[2,8,128]{2,1,0:T(8,128)S(1)} %negate_select_fusion.codes), custom_call_target="tpu_custom_call" | custom-call | tf_op jit(solution)/shard_map/solve/pallas_call | solution.py:675
  56.7 2.6 %all-to-all-start.1 = ((f32[32,2,8,128]{3,2,1,0:T(8,128)}), f32[32,2,8,128]{3,2,1,0:T(8,128)S(1)}, u32[]{:S(2)}, u32[]{:S(2)}) async-start(f32[32,2,8,128]{3,2,1,0:T(8,128)} %solve.1), calls=%async_computation.1 | async-start | bytes 524288 | tf_op jit(solution)/shard_map/all_to_all | solution.py:671
  59.3 0.0 copy-done.1
  59.3 0.7 scale.1
  60.0 9.5 %all-to-all-done.1.blocks = f32[32,2,8,128]{3,2,1,0:T(8,128)S(1)} async-done(((f32[32,2,8,128]{3,2,1,0:T(8,128)}), f32[32,2,8,128]{3,2,1,0:T(8,128)S(1)}, u32[]{:S(2)}, u32[]{:S(2)}) %all-to-all-start.1) | async-done | bytes 262176 | tf_op jit(solution)/shard_map/all_to_all | solution.py:671
  69.5 1.3 %cone.1 = f32[2,8,128]{2,1,0:T(8,128)} custom-call(s32[2]{0:T(128)S(1)} %pad_add_fusion.start.first, f32[32,2,8,128]{3,2,1,0:T(8,128)S(1)} %all-to-all-done.1.blocks, f32[2,8,128]{2,1,0:T(8,128)S(1)} %scale.1), custom_call_target="tpu_custom_call" | custom-call | tf_op jit(solution)/shard_map/cone/pallas_call | solution.py:693
Async XLA Ops:
  0.7 1.1 %copy-start = (f32[3,24,2,8,128]{4,3,2,1,0:T(8,128)S(1)}, f32[3,24,2,8,128]{4,3,2,1,0:T(8,128)}, u32[]{:S(2)}) copy-start(f32[3,24,2,8,128]{4,3,2,1,0:T(8,128)} %forces.1) | copy-start | bytes 1769476
  1.9 2.2 %collective-permute-start = (f32[1168,128]{1,0:T(8,128)S(1)}, f32[1168,128]{1,0:T(8,128)S(1)}, u32[]{:S(2)}, u32[]{:S(2)}) collective-permute-start(f32[1168,128]{1,0:T(8,128)S(1)} %get-tuple-element.11.own), channel_id=1, source_target_pairs={{0,4},{8,12},{16,20},{24,28},{4,0},{12,8},{20,16},{28,24},{1,5},{9... | collective-permute-start | bytes 1794056 | tf_op jit(solution)/shard_map/ppermute | solution.py:630
  2.4 1.6 %collective-permute-start.2 = (f32[1168,128]{1,0:T(8,128)S(1)}, f32[1168,128]{1,0:T(8,128)S(1)}, u32[]{:S(2)}, u32[]{:S(2)}) collective-permute-start(f32[1168,128]{1,0:T(8,128)S(1)} %get-tuple-element.11.own), channel_id=1, source_target_pairs={{8,4},{16,12},{24,20},{9,5},{17,13},{25,21},{10,6},{18,14},{26,22}... | collective-permute-start | bytes 1794056 | tf_op jit(solution)/shard_map/ppermute | solution.py:628
  3.1 0.8 %collective-permute-start.1 = (f32[592,128]{1,0:T(8,128)S(1)}, f32[592,128]{1,0:T(8,128)S(1)}, u32[]{:S(2)}, u32[]{:S(2)}) collective-permute-start(f32[592,128]{1,0:T(8,128)S(1)} %get-tuple-element.12), channel_id=1, source_target_pairs={{4,8},{12,16},{20,24},{5,9},{13,17},{21,25},{6,10},{14,18},{22,26}... | collective-permute-start | bytes 909320 | tf_op jit(solution)/shard_map/ppermute | solution.py:629
  4.7 10.4 %collective-permute-start.4 = (f32[736,128]{1,0:T(8,128)S(1)}, f32[736,128]{1,0:T(8,128)S(1)}, u32[]{:S(2)}, u32[]{:S(2)}) collective-permute-start(f32[736,128]{1,0:T(8,128)S(1)} %get-tuple-element.14), channel_id=1, source_target_pairs={{1,0},{2,1},{3,2},{5,4},{6,5},{7,6},{9,8},{10,9},{11,10},{13,12},{... | collective-permute-start | bytes 1130504 | tf_op jit(solution)/shard_map/ppermute | solution.py:623
  6.0 8.6 %collective-permute-start.3 = (f32[376,128]{1,0:T(8,128)S(1)}, f32[376,128]{1,0:T(8,128)S(1)}, u32[]{:S(2)}, u32[]{:S(2)}) collective-permute-start(f32[376,128]{1,0:T(8,128)S(1)} %get-tuple-element.13), channel_id=1, source_target_pairs={{0,1},{1,2},{2,3},{4,5},{5,6},{6,7},{8,9},{9,10},{10,11},{12,13},{... | collective-permute-start | bytes 577544 | tf_op jit(solution)/shard_map/ppermute | solution.py:623
  23.9 35.4 %copy-start.1 = (s32[2,8,128]{2,1,0:T(8,128)S(1)}, s32[2,8,128]{2,1,0:T(8,128)}, u32[]{:S(2)}) copy-start(s32[2,8,128]{2,1,0:T(8,128)} %levels.1) | copy-start | bytes 24580
  56.7 12.8 %all-to-all-start.1 = ((f32[32,2,8,128]{3,2,1,0:T(8,128)}), f32[32,2,8,128]{3,2,1,0:T(8,128)S(1)}, u32[]{:S(2)}, u32[]{:S(2)}) async-start(f32[32,2,8,128]{3,2,1,0:T(8,128)} %solve.1), calls=%async_computation.1 | async-start | bytes 524288 | tf_op jit(solution)/shard_map/all_to_all | solution.py:671

commit v6 on v5

--- a/solution.py
+++ b/solution.py
@@ -192,7 +192,15 @@
     lax.fori_loop(0, planes * tiles, step, 0)
 
 
-def pack_kernel(sizes, forces, codes, own, up, *rest):
+def edge_rows(rows):
+    return (0, 1, rows - 1)
+
+
+def inner_rows(rows):
+    return tuple(range(2, rows - 1))
+
+
+def pack_kernel(sizes, forces, codes, own, up_e, up_i, down_e, down_i, ym, yp):
     planes, rows, cases = sizes
     block = 3 * cases
     base = planes * rows * block
@@ -204,97 +212,130 @@
                 start = x * rows * block + k * cases + c
                 own[pl.ds(start, rows, stride=block), :] = forces[k, c, x] * scale
 
-    def fill(ref, xs, code_xs):
-        size = len(xs) * rows * block
-        ref[:size, :] = own[xs[0] * rows * block : xs[0] * rows * block + size, :]
-        codes = base + code_xs[0] * rows
-        ref[size:, :] = own[codes : codes + len(code_xs) * rows, :]
-
-    fill(up, range(planes - 1, planes), range(planes - 2, planes))
-    for ref in rest:
-        fill(ref, range(2), range(2))
-
-
-def beside(sizes, first, pair, lower, upper):
-    planes, rows, cases = sizes
-    size = rows * 3 * cases
-    even = first // planes % 2 == 0
-
-    def below(line, count):
-        other = pair[pl.ds((planes - 1) * size + line, count), :]
-        return jnp.where(even, lower[pl.ds(line, count), :], other)
-
-    def below_codes(line, count):
-        other = pair[pl.ds(planes * size + (planes - 2) * rows + line, count), :]
-        return jnp.where(even, lower[pl.ds(size + line, count), :], other)
-
-    def above(line, count):
-        return jnp.where(even, pair[pl.ds(line, count), :], upper[pl.ds(line, count), :])
-
-    def above_codes(line, count):
-        other = upper[pl.ds(2 * size + line, count), :]
-        return jnp.where(even, pair[pl.ds(planes * size + line, count), :], other)
-
-    return below, below_codes, above, above_codes
-
-
-def edge_kernel(sizes, start, own, pair, lower, upper, ym, yp):
+    def fill(ref, xs, ys, code_xs, code_ys):
+        line = 0
+        for x in xs:
+            for y in ys:
+                start = (x * rows + y) * block
+                ref[line : line + block, :] = own[start : start + block, :]
+                line += block
+        for x in code_xs:
+            start = base + x * rows + (code_ys[0] if code_ys else 0)
+            ref[line : line + len(code_ys), :] = own[start : start + len(code_ys), :]
+            line += len(code_ys)
+        if line < ref.shape[0]:
+            ref[line:, :] = jnp.zeros((ref.shape[0] - line, LANES), f32)
+
+    every_x, every_y = range(planes), range(rows)
+    first, last = (0, 1), (planes - 2, planes - 1)
+    fill(up_e, last[1:], edge_rows(rows), last, every_y)
+    fill(up_i, last[1:], inner_rows(rows), (), ())
+    fill(down_e, first, edge_rows(rows), first, every_y)
+    fill(down_i, first, inner_rows(rows), (), ())
+    fill(ym, every_x, (0, 1), every_x, (0, 1))
+    fill(yp, every_x, (rows - 1,), every_x, (rows - 2, rows - 1))
+
+
+def corner_kernel(sizes, start, lower_e, upper_e, ym, yp):
     planes, rows, cases = sizes
     block = 3 * cases
-    base = planes * rows * block
-    below, below_codes, above, above_codes = beside(sizes, start[0], pair, lower, upper)
-    parts = (
-        (below, below_codes, 1, 2),
-        (
-            lambda line, count: own[line : line + count, :],
-            lambda line, count: own[base + line : base + line + count, :],
-            planes,
-            planes,
-        ),
-        (above, above_codes, 2, 2),
-    )
-    for ref, low, count in ((ym, 0, 2), (yp, rows - 1, 1)):
+    even = start[0] // planes % 2 == 0
+    for ref, edges, code in ((ym, (0, 1), 0), (yp, (2,), rows - 2)):
         line = 0
-        for read, _, xs, _ in parts:
-            for x in range(xs):
-                ref[line : line + count * block, :] = read((x * rows + low) * block, count * block)
-                line += count * block
-        for _, read, _, xs in parts:
-            for x in range(xs):
-                ref[line : line + 2, :] = read(x * rows + (0 if low == 0 else rows - 2), 2)
-                line += 2
+        for slot in range(2):
+            for edge in edges:
+                above = upper_e[(slot * 3 + edge) * block : (slot * 3 + edge + 1) * block, :]
+                below = lower_e[edge * block : (edge + 1) * block, :] if slot == 1 else 0.0
+                ref[line : line + block, :] = jnp.where(even, below, above)
+                line += block
+        for slot in range(2):
+            at = slot * rows + code
+            above = upper_e[6 * block + at : 6 * block + at + 2, :]
+            below = lower_e[3 * block + at : 3 * block + at + 2, :]
+            ref[line : line + 2, :] = jnp.where(even, below, above)
+            line += 2
         if line < ref.shape[0]:
             ref[line:, :] = jnp.zeros((ref.shape[0] - line, LANES), f32)
 
 
+def readers(sizes, first, own, pair, lower, upper, y_own, y_pair, y_corner):
+    planes, rows, cases = sizes
+    block = 3 * cases
+    even = first // planes % 2 == 0
+
+    def lines(ref, start, count):
+        return ref[start : start + count, :]
+
+    def inside(ref, x, y):
+        return lines(ref, (x * rows + y) * block, block)
+
+    def split_rows(refs, slot, y):
+        edges, inner = edge_rows(rows), inner_rows(rows)
+        ref, place = (refs[0], edges) if y in edges else (refs[1], inner)
+        return lines(ref, (slot * len(place) + place.index(y)) * block, block)
+
+    def beyond(refs, slot, y):
+        below, above = refs
+        if y < 0:
+            return lines(below, slot * block, block)
+        return lines(above, (slot * 2 + y - rows) * block, block)
+
+    def load(x, y):
+        in_y = 0 <= y < rows
+        if 0 <= x < planes:
+            return inside(own, x, y) if in_y else beyond(y_own, x, y)
+        if x < 0:
+            if in_y:
+                return jnp.where(even, split_rows(lower, 0, y), inside(pair, planes - 1, y))
+            return jnp.where(even, beyond(y_corner, 1, y), beyond(y_pair, planes - 1, y))
+        if in_y:
+            return jnp.where(even, inside(pair, x - planes, y), split_rows(upper, x - planes, y))
+        return jnp.where(even, beyond(y_pair, x - planes, y), beyond(y_corner, x - planes, y))
+
+    def inside_codes(ref, x):
+        return lines(ref, planes * rows * block + x * rows, rows)
+
+    def beyond_codes(refs, slots, slot, y):
+        below, above = refs
+        if y < 0:
+            return lines(below, slots * block + slot * 2, 2)
+        return lines(above, slots * 2 * block + slot * 2, 2)
+
+    def codes(x, y):
+        if 0 <= x < planes:
+            return inside_codes(own, x) if y == 0 else beyond_codes(y_own, planes, x, y)
+        if x < 0:
+            slot = x + 2
+            if y == 0:
+                other = inside_codes(pair, planes + x)
+                return jnp.where(even, lines(lower[0], 3 * block + slot * rows, rows), other)
+            other = beyond_codes(y_pair, planes, planes + x, y)
+            return jnp.where(even, beyond_codes(y_corner, 2, slot, y), other)
+        slot = x - planes
+        if y == 0:
+            other = lines(upper[0], 6 * block + slot * rows, rows)
+            return jnp.where(even, inside_codes(pair, slot), other)
+        other = beyond_codes(y_corner, 2, slot, y)
+        return jnp.where(even, beyond_codes(y_pair, planes, slot, y), other)
+
+    return load, codes
+
+
 def main_kernel(
-    sizes, first, own, pair, lower, upper, ym, yp, both_out, system_out, stiff_ref, inverse,
+    sizes, first, own, pair, lower_e, lower_i, upper_e, upper_i, ym, yp, ym_pair, yp_pair,
+    ym_corner, yp_corner, both_out, system_out, stiff_ref, inverse,
     start, sums, diffs, acc_s, acc_d, w_sums, w_diffs, acc2_s, acc2_d, right, table,
 ):
     planes, rows, cases = sizes
     block = 3 * cases
     xs, ys = planes + 3, rows + 3
-    every_x, every_y = range(planes), range(rows)
-    low, high_x, high_y = (-1,), (planes, planes + 1), (rows, rows + 1)
-    low2 = (-2, -1)
-    below, below_codes, above, above_codes = beside(sizes, first[0], pair, lower, upper)
-
-    def reader(ref, base=0):
-        return lambda line, count: ref[base + line : base + line + count, :]
-
-    def region(ref, bx, by, cx, cy):
-        return (reader(ref), reader(ref, len(bx) * len(by) * block), bx, by, cx, cy)
-
-    regions = (
-        region(own, every_x, every_y, every_x, every_y),
-        (below, below_codes, low, every_y, low2, every_y),
-        (above, above_codes, high_x, every_y, high_x, every_y),
-        region(ym, range(-1, planes + 2), low, range(-2, planes + 2), low2),
-        region(yp, range(-1, planes + 2), high_y, range(-2, planes + 2), high_y),
+    load, signed = readers(
+        sizes, first[0], own, pair, (lower_e, lower_i), (upper_e, upper_i),
+        (ym, yp), (ym_pair, yp_pair), (ym_corner, yp_corner),
     )
-    for _, read, _, _, cx, cy in regions:
-        for i, x in enumerate(cx):
-            stiff_ref[x + 2, cy[0] + 2 : cy[0] + 2 + len(cy), :] = read(i * len(cy), len(cy))
+    for x in range(-2, planes + 2):
+        for y, count in ((-2, 2), (0, rows), (rows, 2)):
+            stiff_ref[x + 2, y + 2 : y + 2 + count, :] = signed(x, y)
     for x in range(-1, planes + 2):
         codes = stiff_ref[x + 2, 0 : ys + 1, :]
         total = jnp.abs(stiff_ref[x + 1, 0 : ys + 1, :]) + jnp.abs(codes)
@@ -306,19 +347,14 @@
     for x in range(planes + 4):
         stiff_ref[x] = jnp.abs(stiff_ref[x])
 
-    for read, _, bx, by, _, _ in regions:
-        for i, x in enumerate(bx):
-
-            for j in range(len(by)):
-                y = j + by[0] + 1
-                line = (i * len(by) + j) * block
-                load = read(line, block)
-                value = load * inverse[x + 1, y : y + 1, :]
-                column = (x + 1) * ys + y
-                start[column] = value
-                moved = shift_down(value)
-                sums[column] = value + moved
-                diffs[column] = moved - value
+    for x in range(-1, planes + 2):
+        for y in range(-1, rows + 2):
+            value = load(x, y) * inverse[x + 1, y + 1 : y + 2, :]
+            column = (x + 1) * ys + y + 1
+            start[column] = value
+            moved = shift_down(value)
+            sums[column] = value + moved
+            diffs[column] = moved - value
 
     nodes_y = rows + 1
     apply_elements(
@@ -348,10 +384,10 @@
 
     def inside(index):
         force = image(index // rows, index % rows, index)
-        load = own[pl.ds(pl.multiple_of(index * block, 8), block), :]
+        given = own[pl.ds(pl.multiple_of(index * block, 8), block), :]
         for k in range(3):
             lines = slice(k * cases, (k + 1) * cases)
-            pair = jnp.concatenate([load[lines], force[lines]], 0)
+            pair = jnp.concatenate([given[lines], force[lines]], 0)
             lane = pl.ds(pl.multiple_of((index * 3 + k) * LANES, LANES), LANES)
             high, rest = split(pair)
             right[0:two, lane] = high
@@ -592,13 +628,20 @@
     density = 0.3 + 0.7 * levels.astype(f32) / (LEVELS - 1)
     codes = density * density * density
     codes = jnp.where(supports == 0, codes, -codes)
-    whole = shape(planes * rows, planes * rows)
-    down = [] if planes == 2 else [shape(2 * rows, 2 * rows)]
-    own, up, *down = pl.pallas_call(
+    edge, inner = len(edge_rows(rows)), len(inner_rows(rows))
+    own, up_e, up_i, down_e, down_i, ym, yp = pl.pallas_call(
         functools.partial(pack_kernel, sizes),
-        out_shape=[whole, shape(rows, 2 * rows), *down],
+        out_shape=[
+            shape(planes * rows, planes * rows),
+            shape(edge, 2 * rows),
+            shape(inner, 0),
+            shape(2 * edge, 2 * rows),
+            shape(2 * inner, 0),
+            shape(2 * planes, 2 * planes),
+            shape(planes, 2 * planes),
+        ],
         in_specs=[VMEM] * 2,
-        out_specs=[VMEM] * (2 + len(down)),
+        out_specs=[VMEM] * 7,
         compiler_params=PARAMS,
         name="pack",
     )(forces, codes)
@@ -625,20 +668,25 @@
     def links(first, step):
         return [(i, i + step) for i in range(first, count_x, 2) if 0 <= i + step < count_x]
 
-    upper = lax.ppermute(down[0] if down else own, "gx", links(2, -1))
-    lower = lax.ppermute(up, "gx", links(1, 1))
-    pair = lax.ppermute(own, "gx", links(0, 1) + links(1, -1))
-    ym, yp = pl.pallas_call(
-        functools.partial(edge_kernel, sizes),
-        out_shape=[
-            shape(2 * (planes + 3), 2 * (planes + 4)), shape(planes + 3, 2 * (planes + 4))
-        ],
-        in_specs=[scalars] + [VMEM] * 4,
+    def swapped(value):
+        return lax.ppermute(value, "gx", links(0, 1) + links(1, -1))
+
+    upper_e = lax.ppermute(down_e, "gx", links(2, -1))
+    lower_e = lax.ppermute(up_e, "gx", links(1, 1))
+    pair = swapped(own)
+    from_yp, from_ym = moved(ym, "gy", -1), moved(yp, "gy", 1)
+    upper_i = lax.ppermute(down_i, "gx", links(2, -1))
+    lower_i = lax.ppermute(up_i, "gx", links(1, 1))
+    corner_m, corner_p = pl.pallas_call(
+        functools.partial(corner_kernel, sizes),
+        out_shape=[shape(4, 4), shape(2, 4)],
+        in_specs=[scalars] + [VMEM] * 2,
         out_specs=[VMEM] * 2,
         compiler_params=PARAMS,
-        name="edges",
-    )(start, own, pair, lower, upper)
-    from_yp, from_ym = moved(ym, "gy", -1), moved(yp, "gy", 1)
+        name="corners",
+    )(start, lower_e, upper_e)
+    corner_yp, corner_ym = moved(corner_m, "gy", -1), moved(corner_p, "gy", 1)
+    pair_yp, pair_ym = swapped(from_yp), swapped(from_ym)
 
     devices = count_x * count_y
     nodes = (planes + 1) * (rows + 1)
@@ -651,7 +699,7 @@
             jax.ShapeDtypeStruct((4 * cases, nodes * 3 * LANES), bf16),
             jax.ShapeDtypeStruct((devices, cases // 8, 4, LANES), f32),
         ],
-        in_specs=[scalars] + [VMEM] * 6,
+        in_specs=[scalars] + [VMEM] * 12,
         out_specs=[VMEM] * 2,
         scratch_shapes=[
             pltpu.VMEM((planes + 4, up8(rows + 4), LANES), f32),
@@ -665,7 +713,10 @@
         ],
         compiler_params=PARAMS,
         name="operator",
-    )(start, own, pair, lower, upper, from_ym, from_yp)
+    )(
+        start, own, pair, lower_e, lower_i, upper_e, upper_i, from_ym, from_yp,
+        pair_ym, pair_yp, corner_ym, corner_yp,
+    )
 
     def gathered(copies):
         return lax.all_to_all(copies, ("gx", "gy"), 0, 0)

time: 71.2 us -> 74.7 us (1.049)
  starting transfers between devices: 11.2 us -> 22.2 us
  blocking collectives: 28.1 us -> 17.9 us
  waiting for transfers between devices: 13.3 us -> 15.9 us
    all_to_all x1, blocking collectives: 28.1 us -> 17.9 us  [gathered(): return lax.all_to_all(copies, ('gx', 'gy'), 0, 0)]
    ppermute x3 -> x7, starting transfers between devices: 1.88 us -> 7.37 us  [the longest x3 4.66 us: swapped(): return lax.ppermute(value, 'gx', links(0, 1) + links(1, -1))]
    ppermute x2 -> x4, starting transfers between devices: 6.78 us -> 12.3 us  [moved(): return lax.ppermute(value, axis, pairs)]
    ppermute x2 -> x4, waiting for transfers between devices: 3.63 us -> 6.36 us  [moved(): return lax.ppermute(value, axis, pairs)]
  transfers between devices with their start and end apart: 6 -> 12, of which waited for: 4 -> 4; matrix products, arithmetic and copies ran while one was open for 0% -> 0% of each run, Pallas kernels for 1% -> 2%
where the time goes in v6:
time: 74.7 us; the launch traced here: 74.3 us
  starting transfers between devices  22.2 us (30%)
  blocking collectives  17.9 us (24%)
  Pallas kernels  16.2 us (22%)
  waiting for transfers between devices  15.9 us (21%)
  local copies, waits for them, and re-layouts  1.07 us (1%)
  other arithmetic  0.8 us (1%)
    all_to_all x1, blocking collectives, gathered(): return lax.all_to_all(copies, ('gx', 'gy'), 0, 0)  17.9 us
    ppermute x4, starting transfers between devices, moved(): return lax.ppermute(value, axis, pairs)  12.3 us
    all_to_all x1, waiting for transfers between devices, gathered(): return lax.all_to_all(copies, ('gx', 'gy'), 0, 0)  9.53 us
    pallas_call x1, Pallas kernels, local(): pl.pallas_call(functools.partial(main_kernel, sizes), out_shape=[jax.Shap...  8.86 us
    ppermute x4, waiting for transfers between devices, moved(): return lax.ppermute(value, axis, pairs)  6.36 us
    pallas_call x1, Pallas kernels, local(): pl.pallas_call(functools.partial(solve_kernel, sizes), out_shape=jax.Shap...  4.69 us
    ppermute x3, starting transfers between devices, swapped(): return lax.ppermute(value, 'gx', links(0, 1) + links(1, -1))  4.66 us
    all_to_all x1, starting transfers between devices, gathered(): return lax.all_to_all(copies, ('gx', 'gy'), 0, 0)  2.58 us
  transfers between devices with their start and end apart: 12, of which 4 were waited for; matrix products, arithmetic and copies ran while one was open for 0% of the time, Pallas kernels for 2%

profile of v6, /device:TPU:0, one launch (start us, length us, event | category | flops | bytes accessed | tf_op | source)
XLA Modules:
  0.0 74.3 jit_solution(10071861915184602201)
XLA Ops:
  0.0 0.7 negate_select_fusion.codes
  0.7 0.0 copy-start
  0.7 1.1 %copy-done = f32[3,24,2,8,128]{4,3,2,1,0:T(8,128)S(1)} copy-done((f32[3,24,2,8,128]{4,3,2,1,0:T(8,128)S(1)}, f32[3,24,2,8,128]{4,3,2,1,0:T(8,128)}, u32[]{:S(2)}) %copy-start) | copy-done | bytes 589848
  1.8 0.2 pack.1
  2.0 0.5 collective-permute-start
  2.5 4.5 %collective-permute-start.5 = (f32[152,128]{1,0:T(8,128)S(1)}, f32[152,128]{1,0:T(8,128)S(1)}, u32[]{:S(2)}, u32[]{:S(2)}) collective-permute-start(f32[152,128]{1,0:T(8,128)S(1)} %get-tuple-element.21), channel_id=1, source_target_pairs={{0,1},{1,2},{2,3},{4,5},{5,6},{6,7},{8,9},{9,10},{10,11},{12,13},{... | collective-permute-start | bytes 233480 | tf_op jit(solution)/shard_map/ppermute | solution.py:666
  7.0 1.3 %collective-permute-start.6 = (f32[296,128]{1,0:T(8,128)S(1)}, f32[296,128]{1,0:T(8,128)S(1)}, u32[]{:S(2)}, u32[]{:S(2)}) collective-permute-start(f32[296,128]{1,0:T(8,128)S(1)} %get-tuple-element.22), channel_id=1, source_target_pairs={{1,0},{2,1},{3,2},{5,4},{6,5},{7,6},{9,8},{10,9},{11,10},{13,12},{... | collective-permute-start | bytes 454664 | tf_op jit(solution)/shard_map/ppermute | solution.py:666
  8.3 0.7 collective-permute-start.1
  9.0 0.7 collective-permute-start.3
  9.6 0.0 collective-permute-done.5.ym
  9.6 0.7 collective-permute-start.4
  10.3 0.0 collective-permute-done.1.lower_e
  10.4 0.7 collective-permute-start.2
  11.0 3.9 %collective-permute-done.6.yp = f32[296,128]{1,0:T(8,128)S(1)} collective-permute-done((f32[296,128]{1,0:T(8,128)S(1)}, f32[296,128]{1,0:T(8,128)S(1)}, u32[]{:S(2)}, u32[]{:S(2)}) %collective-permute-start.6) | collective-permute-done | bytes 151584 | tf_op jit(solution)/shard_map/ppermute | solution.py:666
  14.9 3.9 %collective-permute-start.7 = (f32[152,128]{1,0:T(8,128)S(1)}, f32[152,128]{1,0:T(8,128)S(1)}, u32[]{:S(2)}, u32[]{:S(2)}) collective-permute-start(f32[152,128]{1,0:T(8,128)S(1)} %collective-permute-done.5.ym), channel_id=1, source_target_pairs={{0,4},{8,12},{16,20},{24,28},{4,0},{12,8},{20,16},{28,24},{1,5},{9... | collective-permute-start | bytes 233480 | tf_op jit(solution)/shard_map/ppermute | solution.py:672
  18.8 0.1 pad_add_fusion.start.first
  18.9 0.0 collective-permute-done.3.upper_e
  18.9 0.2 collective-permute-start.8
  19.1 0.6 corners.1
  19.7 0.0 collective-permute-done.7.ym_pair
  19.7 1.3 %collective-permute-start.10 = (f32[296,128]{1,0:T(8,128)S(1)}, f32[296,128]{1,0:T(8,128)S(1)}, u32[]{:S(2)}, u32[]{:S(2)}) collective-permute-start(f32[296,128]{1,0:T(8,128)S(1)} %get-tuple-element.24), channel_id=1, source_target_pairs={{1,0},{2,1},{3,2},{5,4},{6,5},{7,6},{9,8},{10,9},{11,10},{13,12},{... | collective-permute-start | bytes 454664 | tf_op jit(solution)/shard_map/ppermute | solution.py:666
  21.0 0.0 collective-permute-done.2.lower_i
  21.0 5.2 %collective-permute-start.9 = (f32[152,128]{1,0:T(8,128)S(1)}, f32[152,128]{1,0:T(8,128)S(1)}, u32[]{:S(2)}, u32[]{:S(2)}) collective-permute-start(f32[152,128]{1,0:T(8,128)S(1)} %get-tuple-element.23), channel_id=1, source_target_pairs={{0,1},{1,2},{2,3},{4,5},{5,6},{6,7},{8,9},{9,10},{10,11},{12,13},{... | collective-permute-start | bytes 233480 | tf_op jit(solution)/shard_map/ppermute | solution.py:666
  26.2 0.0 collective-permute-done.8.yp_pair
  26.2 2.1 %collective-permute-done.9.ym_corner = f32[152,128]{1,0:T(8,128)S(1)} collective-permute-done((f32[152,128]{1,0:T(8,128)S(1)}, f32[152,128]{1,0:T(8,128)S(1)}, u32[]{:S(2)}, u32[]{:S(2)}) %collective-permute-start.9) | collective-permute-done | bytes 77856 | tf_op jit(solution)/shard_map/ppermute | solution.py:666
  28.3 0.0 collective-permute-done.4.upper_i
  28.3 0.4 collective-permute-done.10.yp_corner
  28.7 0.0 collective-permute-done.pair
  28.7 8.9 %operator.1 = (bf16[96,10368]{1,0:T(8,128)(2,1)S(1)}, f32[32,3,4,128]{3,2,1,0:T(4,128)S(1)}) custom-call(s32[2]{0:T(128)S(1)} %pad_add_fusion.start.first, f32[1168,128]{1,0:T(8,128)S(1)} %get-tuple-element.16.own, f32[1168,128]{1,0:T(8,128)S(1)} %collective-permute-done.pair, f32[232,128]{1,0:T(8,128)S(1)} %collective-permute-done.1.lower_e, ...), custom_call_target="tpu_custom_call" | custom-call | tf_op jit(solution)/shard_map/operator/pallas_call | solution.py:696
  37.6 0.0 copy-start.1
  37.6 17.9 %all_to_all.10.system = f32[32,3,4,128]{3,2,1,0:T(4,128)S(1)} all-to-all(f32[32,3,4,128]{3,2,1,0:T(4,128)S(1)} %get-tuple-element.25), channel_id=1, replica_groups=mesh['gx'=8,'gy'=4] {'gx','gy'}, dimensions={0} | all-to-all | bytes 393216 | tf_op jit(solution)/shard_map/all_to_all | solution.py:722
  55.5 4.7 %solve.1 = f32[32,2,8,128]{3,2,1,0:T(8,128)} custom-call(f32[32,3,4,128]{3,2,1,0:T(4,128)S(1)} %all_to_all.10.system, bf16[96,10368]{1,0:T(8,128)(2,1)S(1)} %get-tuple-element.26.both, f32[2,8,128]{2,1,0:T(8,128)S(1)} %negate_select_fusion.codes), custom_call_target="tpu_custom_call" | custom-call | tf_op jit(solution)/shard_map/solve/pallas_call | solution.py:726
  60.2 2.6 %all-to-all-start.1 = ((f32[32,2,8,128]{3,2,1,0:T(8,128)}), f32[32,2,8,128]{3,2,1,0:T(8,128)S(1)}, u32[]{:S(2)}, u32[]{:S(2)}) async-start(f32[32,2,8,128]{3,2,1,0:T(8,128)} %solve.1), calls=%async_computation.1 | async-start | bytes 524288 | tf_op jit(solution)/shard_map/all_to_all | solution.py:722
  62.8 0.0 copy-done.1
  62.8 0.7 scale.1
  63.4 9.5 %all-to-all-done.1.blocks = f32[32,2,8,128]{3,2,1,0:T(8,128)S(1)} async-done(((f32[32,2,8,128]{3,2,1,0:T(8,128)}), f32[32,2,8,128]{3,2,1,0:T(8,128)S(1)}, u32[]{:S(2)}, u32[]{:S(2)}) %all-to-all-start.1) | async-done | bytes 262176 | tf_op jit(solution)/shard_map/all_to_all | solution.py:722
  73.0 1.3 %cone.1 = f32[2,8,128]{2,1,0:T(8,128)} custom-call(s32[2]{0:T(128)S(1)} %pad_add_fusion.start.first, f32[32,2,8,128]{3,2,1,0:T(8,128)S(1)} %all-to-all-done.1.blocks, f32[2,8,128]{2,1,0:T(8,128)S(1)} %scale.1), custom_call_target="tpu_custom_call" | custom-call | tf_op jit(solution)/shard_map/cone/pallas_call | solution.py:744
Async XLA Ops:
  0.7 1.1 %copy-start = (f32[3,24,2,8,128]{4,3,2,1,0:T(8,128)S(1)}, f32[3,24,2,8,128]{4,3,2,1,0:T(8,128)}, u32[]{:S(2)}) copy-start(f32[3,24,2,8,128]{4,3,2,1,0:T(8,128)} %forces.1) | copy-start | bytes 1769476
  2.0 26.8 %collective-permute-start = (f32[1168,128]{1,0:T(8,128)S(1)}, f32[1168,128]{1,0:T(8,128)S(1)}, u32[]{:S(2)}, u32[]{:S(2)}) collective-permute-start(f32[1168,128]{1,0:T(8,128)S(1)} %get-tuple-element.16.own), channel_id=1, source_target_pairs={{0,4},{8,12},{16,20},{24,28},{4,0},{12,8},{20,16},{28,24},{1,5},{9... | collective-permute-start | bytes 1794056 | tf_op jit(solution)/shard_map/ppermute | solution.py:672
  2.5 7.2 %collective-permute-start.5 = (f32[152,128]{1,0:T(8,128)S(1)}, f32[152,128]{1,0:T(8,128)S(1)}, u32[]{:S(2)}, u32[]{:S(2)}) collective-permute-start(f32[152,128]{1,0:T(8,128)S(1)} %get-tuple-element.21), channel_id=1, source_target_pairs={{0,1},{1,2},{2,3},{4,5},{5,6},{6,7},{8,9},{9,10},{10,11},{12,13},{... | collective-permute-start | bytes 233480 | tf_op jit(solution)/shard_map/ppermute | solution.py:666
  7.0 7.9 %collective-permute-start.6 = (f32[296,128]{1,0:T(8,128)S(1)}, f32[296,128]{1,0:T(8,128)S(1)}, u32[]{:S(2)}, u32[]{:S(2)}) collective-permute-start(f32[296,128]{1,0:T(8,128)S(1)} %get-tuple-element.22), channel_id=1, source_target_pairs={{1,0},{2,1},{3,2},{5,4},{6,5},{7,6},{9,8},{10,9},{11,10},{13,12},{... | collective-permute-start | bytes 454664 | tf_op jit(solution)/shard_map/ppermute | solution.py:666
  8.3 2.1 %collective-permute-start.1 = (f32[232,128]{1,0:T(8,128)S(1)}, f32[232,128]{1,0:T(8,128)S(1)}, u32[]{:S(2)}, u32[]{:S(2)}) collective-permute-start(f32[232,128]{1,0:T(8,128)S(1)} %get-tuple-element.17), channel_id=1, source_target_pairs={{4,8},{12,16},{20,24},{5,9},{13,17},{21,25},{6,10},{14,18},{22,26}... | collective-permute-start | bytes 356360 | tf_op jit(solution)/shard_map/ppermute | solution.py:675
  9.0 9.9 %collective-permute-start.3 = (f32[448,128]{1,0:T(8,128)S(1)}, f32[448,128]{1,0:T(8,128)S(1)}, u32[]{:S(2)}, u32[]{:S(2)}) collective-permute-start(f32[448,128]{1,0:T(8,128)S(1)} %get-tuple-element.19), channel_id=1, source_target_pairs={{8,4},{16,12},{24,20},{9,5},{17,13},{25,21},{10,6},{18,14},{26,22}... | collective-permute-start | bytes 688136 | tf_op jit(solution)/shard_map/ppermute | solution.py:674
  9.6 18.7 %collective-permute-start.4 = (f32[720,128]{1,0:T(8,128)S(1)}, f32[720,128]{1,0:T(8,128)S(1)}, u32[]{:S(2)}, u32[]{:S(2)}) collective-permute-start(f32[720,128]{1,0:T(8,128)S(1)} %get-tuple-element.20), channel_id=1, source_target_pairs={{8,4},{16,12},{24,20},{9,5},{17,13},{25,21},{10,6},{18,14},{26,22}... | collective-permute-start | bytes 1105928 | tf_op jit(solution)/shard_map/ppermute | solution.py:678
  10.4 10.7 %collective-permute-start.2 = (f32[360,128]{1,0:T(8,128)S(1)}, f32[360,128]{1,0:T(8,128)S(1)}, u32[]{:S(2)}, u32[]{:S(2)}) collective-permute-start(f32[360,128]{1,0:T(8,128)S(1)} %get-tuple-element.18), channel_id=1, source_target_pairs={{4,8},{12,16},{20,24},{5,9},{13,17},{21,25},{6,10},{14,18},{22,26}... | collective-permute-start | bytes 552968 | tf_op jit(solution)/shard_map/ppermute | solution.py:679
  14.9 4.8 %collective-permute-start.7 = (f32[152,128]{1,0:T(8,128)S(1)}, f32[152,128]{1,0:T(8,128)S(1)}, u32[]{:S(2)}, u32[]{:S(2)}) collective-permute-start(f32[152,128]{1,0:T(8,128)S(1)} %collective-permute-done.5.ym), channel_id=1, source_target_pairs={{0,4},{8,12},{16,20},{24,28},{4,0},{12,8},{20,16},{28,24},{1,5},{9... | collective-permute-start | bytes 233480 | tf_op jit(solution)/shard_map/ppermute | solution.py:672
  18.9 7.3 %collective-permute-start.8 = (f32[296,128]{1,0:T(8,128)S(1)}, f32[296,128]{1,0:T(8,128)S(1)}, u32[]{:S(2)}, u32[]{:S(2)}) collective-permute-start(f32[296,128]{1,0:T(8,128)S(1)} %collective-permute-done.6.yp), channel_id=1, source_target_pairs={{0,4},{8,12},{16,20},{24,28},{4,0},{12,8},{20,16},{28,24},{1,5},{9... | collective-permute-start | bytes 454664 | tf_op jit(solution)/shard_map/ppermute | solution.py:672
  19.7 9.0 %collective-permute-start.10 = (f32[296,128]{1,0:T(8,128)S(1)}, f32[296,128]{1,0:T(8,128)S(1)}, u32[]{:S(2)}, u32[]{:S(2)}) collective-permute-start(f32[296,128]{1,0:T(8,128)S(1)} %get-tuple-element.24), channel_id=1, source_target_pairs={{1,0},{2,1},{3,2},{5,4},{6,5},{7,6},{9,8},{10,9},{11,10},{13,12},{... | collective-permute-start | bytes 454664 | tf_op jit(solution)/shard_map/ppermute | solution.py:666
  21.0 7.3 %collective-permute-start.9 = (f32[152,128]{1,0:T(8,128)S(1)}, f32[152,128]{1,0:T(8,128)S(1)}, u32[]{:S(2)}, u32[]{:S(2)}) collective-permute-start(f32[152,128]{1,0:T(8,128)S(1)} %get-tuple-element.23), channel_id=1, source_target_pairs={{0,1},{1,2},{2,3},{4,5},{5,6},{6,7},{8,9},{9,10},{10,11},{12,13},{... | collective-permute-start | bytes 233480 | tf_op jit(solution)/shard_map/ppermute | solution.py:666
  37.6 25.2 %copy-start.1 = (s32[2,8,128]{2,1,0:T(8,128)S(1)}, s32[2,8,128]{2,1,0:T(8,128)}, u32[]{:S(2)}) copy-start(s32[2,8,128]{2,1,0:T(8,128)} %levels.1) | copy-start | bytes 24580
  60.2 12.8 %all-to-all-start.1 = ((f32[32,2,8,128]{3,2,1,0:T(8,128)}), f32[32,2,8,128]{3,2,1,0:T(8,128)S(1)}, u32[]{:S(2)}, u32[]{:S(2)}) async-start(f32[32,2,8,128]{3,2,1,0:T(8,128)} %solve.1), calls=%async_computation.1 | async-start | bytes 524288 | tf_op jit(solution)/shard_map/all_to_all | solution.py:722

commit v7 on v6

--- a/solution.py
+++ b/solution.py
@@ -192,15 +192,24 @@
     lax.fori_loop(0, planes * tiles, step, 0)
 
 
-def edge_rows(rows):
-    return (0, 1, rows - 1)
-
-
-def inner_rows(rows):
-    return tuple(range(2, rows - 1))
-
-
-def pack_kernel(sizes, forces, codes, own, up_e, up_i, down_e, down_i, ym, yp):
+def fill(source, base, sizes, ref, xs, ys, code_xs, code_ys):
+    planes, rows, cases = sizes
+    block = 3 * cases
+    line = 0
+    for x in xs:
+        start = (x * rows + ys[0]) * block
+        count = len(ys) * block
+        ref[line : line + count, :] = source[start : start + count, :]
+        line += count
+    for x in code_xs:
+        start = base + x * rows + code_ys[0]
+        ref[line : line + len(code_ys), :] = source[start : start + len(code_ys), :]
+        line += len(code_ys)
+    if line < ref.shape[0]:
+        ref[line:, :] = jnp.zeros((ref.shape[0] - line, LANES), f32)
+
+
+def pack_kernel(sizes, forces, codes, own, up, *down):
     planes, rows, cases = sizes
     block = 3 * cases
     base = planes * rows * block
@@ -212,46 +221,37 @@
                 start = x * rows * block + k * cases + c
                 own[pl.ds(start, rows, stride=block), :] = forces[k, c, x] * scale
 
-    def fill(ref, xs, ys, code_xs, code_ys):
-        line = 0
-        for x in xs:
-            for y in ys:
-                start = (x * rows + y) * block
-                ref[line : line + block, :] = own[start : start + block, :]
-                line += block
-        for x in code_xs:
-            start = base + x * rows + (code_ys[0] if code_ys else 0)
-            ref[line : line + len(code_ys), :] = own[start : start + len(code_ys), :]
-            line += len(code_ys)
-        if line < ref.shape[0]:
-            ref[line:, :] = jnp.zeros((ref.shape[0] - line, LANES), f32)
-
-    every_x, every_y = range(planes), range(rows)
-    first, last = (0, 1), (planes - 2, planes - 1)
-    fill(up_e, last[1:], edge_rows(rows), last, every_y)
-    fill(up_i, last[1:], inner_rows(rows), (), ())
-    fill(down_e, first, edge_rows(rows), first, every_y)
-    fill(down_i, first, inner_rows(rows), (), ())
-    fill(ym, every_x, (0, 1), every_x, (0, 1))
-    fill(yp, every_x, (rows - 1,), every_x, (rows - 2, rows - 1))
-
-
-def corner_kernel(sizes, start, lower_e, upper_e, ym, yp):
+    every_y, last = range(rows), (planes - 2, planes - 1)
+    fill(own, base, sizes, up, last[1:], every_y, last, every_y)
+    for ref in down:
+        fill(own, base, sizes, ref, (0, 1), every_y, (0, 1), every_y)
+
+
+def rows_kernel(sizes, own, ym, yp):
+    planes, rows, cases = sizes
+    base = planes * rows * 3 * cases
+    every_x = range(planes)
+    fill(own, base, sizes, ym, every_x, (0, 1), every_x, (0, 1))
+    fill(own, base, sizes, yp, every_x, (rows - 1,), every_x, (rows - 2, rows - 1))
+
+
+def corner_kernel(sizes, start, lower, upper, ym, yp):
     planes, rows, cases = sizes
     block = 3 * cases
     even = start[0] // planes % 2 == 0
-    for ref, edges, code in ((ym, (0, 1), 0), (yp, (2,), rows - 2)):
+    for ref, edges, code in ((ym, (0, 1), 0), (yp, (rows - 1,), rows - 2)):
         line = 0
         for slot in range(2):
             for edge in edges:
-                above = upper_e[(slot * 3 + edge) * block : (slot * 3 + edge + 1) * block, :]
-                below = lower_e[edge * block : (edge + 1) * block, :] if slot == 1 else 0.0
+                at = slot * rows + edge
+                above = upper[at * block : (at + 1) * block, :]
+                below = lower[edge * block : (edge + 1) * block, :] if slot == 1 else 0.0
                 ref[line : line + block, :] = jnp.where(even, below, above)
                 line += block
         for slot in range(2):
             at = slot * rows + code
-            above = upper_e[6 * block + at : 6 * block + at + 2, :]
-            below = lower_e[3 * block + at : 3 * block + at + 2, :]
+            above = upper[2 * rows * block + at : 2 * rows * block + at + 2, :]
+            below = lower[rows * block + at : rows * block + at + 2, :]
             ref[line : line + 2, :] = jnp.where(even, below, above)
             line += 2
         if line < ref.shape[0]:
@@ -268,11 +268,6 @@
 
     def inside(ref, x, y):
         return lines(ref, (x * rows + y) * block, block)
-
-    def split_rows(refs, slot, y):
-        edges, inner = edge_rows(rows), inner_rows(rows)
-        ref, place = (refs[0], edges) if y in edges else (refs[1], inner)
-        return lines(ref, (slot * len(place) + place.index(y)) * block, block)
 
     def beyond(refs, slot, y):
         below, above = refs
@@ -286,10 +281,10 @@
             return inside(own, x, y) if in_y else beyond(y_own, x, y)
         if x < 0:
             if in_y:
-                return jnp.where(even, split_rows(lower, 0, y), inside(pair, planes - 1, y))
+                return jnp.where(even, inside(lower, 0, y), inside(pair, planes - 1, y))
             return jnp.where(even, beyond(y_corner, 1, y), beyond(y_pair, planes - 1, y))
         if in_y:
-            return jnp.where(even, inside(pair, x - planes, y), split_rows(upper, x - planes, y))
+            return jnp.where(even, inside(pair, x - planes, y), inside(upper, x - planes, y))
         return jnp.where(even, beyond(y_pair, x - planes, y), beyond(y_corner, x - planes, y))
 
     def inside_codes(ref, x):
@@ -308,12 +303,12 @@
             slot = x + 2
             if y == 0:
                 other = inside_codes(pair, planes + x)
-                return jnp.where(even, lines(lower[0], 3 * block + slot * rows, rows), other)
+                return jnp.where(even, lines(lower, (block + slot) * rows, rows), other)
             other = beyond_codes(y_pair, planes, planes + x, y)
             return jnp.where(even, beyond_codes(y_corner, 2, slot, y), other)
         slot = x - planes
         if y == 0:
-            other = lines(upper[0], 6 * block + slot * rows, rows)
+            other = lines(upper, (2 * block + slot) * rows, rows)
             return jnp.where(even, inside_codes(pair, slot), other)
         other = beyond_codes(y_corner, 2, slot, y)
         return jnp.where(even, beyond_codes(y_pair, planes, slot, y), other)
@@ -322,15 +317,15 @@
 
 
 def main_kernel(
-    sizes, first, own, pair, lower_e, lower_i, upper_e, upper_i, ym, yp, ym_pair, yp_pair,
-    ym_corner, yp_corner, both_out, system_out, stiff_ref, inverse,
+    sizes, first, own, pair, lower, upper, ym, yp, ym_pair, yp_pair, ym_corner, yp_corner,
+    both_out, system_out, stiff_ref, inverse,
     start, sums, diffs, acc_s, acc_d, w_sums, w_diffs, acc2_s, acc2_d, right, table,
 ):
     planes, rows, cases = sizes
     block = 3 * cases
     xs, ys = planes + 3, rows + 3
     load, signed = readers(
-        sizes, first[0], own, pair, (lower_e, lower_i), (upper_e, upper_i),
+        sizes, first[0], own, pair, lower, upper,
         (ym, yp), (ym_pair, yp_pair), (ym_corner, yp_corner),
     )
     for x in range(-2, planes + 2):
@@ -628,20 +623,13 @@
     density = 0.3 + 0.7 * levels.astype(f32) / (LEVELS - 1)
     codes = density * density * density
     codes = jnp.where(supports == 0, codes, -codes)
-    edge, inner = len(edge_rows(rows)), len(inner_rows(rows))
-    own, up_e, up_i, down_e, down_i, ym, yp = pl.pallas_call(
+    whole = shape(planes * rows, planes * rows)
+    down = [] if planes == 2 else [shape(2 * rows, 2 * rows)]
+    own, up, *down = pl.pallas_call(
         functools.partial(pack_kernel, sizes),
-        out_shape=[
-            shape(planes * rows, planes * rows),
-            shape(edge, 2 * rows),
-            shape(inner, 0),
-            shape(2 * edge, 2 * rows),
-            shape(2 * inner, 0),
-            shape(2 * planes, 2 * planes),
-            shape(planes, 2 * planes),
-        ],
+        out_shape=[whole, shape(rows, 2 * rows), *down],
         in_specs=[VMEM] * 2,
-        out_specs=[VMEM] * 7,
+        out_specs=[VMEM] * (2 + len(down)),
         compiler_params=PARAMS,
         name="pack",
     )(forces, codes)
@@ -671,12 +659,19 @@
     def swapped(value):
         return lax.ppermute(value, "gx", links(0, 1) + links(1, -1))
 
-    upper_e = lax.ppermute(down_e, "gx", links(2, -1))
-    lower_e = lax.ppermute(up_e, "gx", links(1, 1))
+    upper = lax.ppermute(down[0] if down else own, "gx", links(2, -1))
+    lower = lax.ppermute(up, "gx", links(1, 1))
     pair = swapped(own)
+    own, pair = lax.optimization_barrier((own, pair))
+    ym, yp = pl.pallas_call(
+        functools.partial(rows_kernel, sizes),
+        out_shape=[shape(2 * planes, 2 * planes), shape(planes, 2 * planes)],
+        in_specs=[VMEM],
+        out_specs=[VMEM] * 2,
+        compiler_params=PARAMS,
+        name="rows",
+    )(own)
     from_yp, from_ym = moved(ym, "gy", -1), moved(yp, "gy", 1)
-    upper_i = lax.ppermute(down_i, "gx", links(2, -1))
-    lower_i = lax.ppermute(up_i, "gx", links(1, 1))
     corner_m, corner_p = pl.pallas_call(
         functools.partial(corner_kernel, sizes),
         out_shape=[shape(4, 4), shape(2, 4)],
@@ -684,7 +679,7 @@
         out_specs=[VMEM] * 2,
         compiler_params=PARAMS,
         name="corners",
-    )(start, lower_e, upper_e)
+    )(start, lower, upper)
     corner_yp, corner_ym = moved(corner_m, "gy", -1), moved(corner_p, "gy", 1)
     pair_yp, pair_ym = swapped(from_yp), swapped(from_ym)
 
@@ -699,7 +694,7 @@
             jax.ShapeDtypeStruct((4 * cases, nodes * 3 * LANES), bf16),
             jax.ShapeDtypeStruct((devices, cases // 8, 4, LANES), f32),
         ],
-        in_specs=[scalars] + [VMEM] * 12,
+        in_specs=[scalars] + [VMEM] * 10,
         out_specs=[VMEM] * 2,
         scratch_shapes=[
             pltpu.VMEM((planes + 4, up8(rows + 4), LANES), f32),
@@ -714,7 +709,7 @@
         compiler_params=PARAMS,
         name="operator",
     )(
-        start, own, pair, lower_e, lower_i, upper_e, upper_i, from_ym, from_yp,
+        start, own, pair, lower, upper, from_ym, from_yp,
         pair_ym, pair_yp, corner_ym, corner_yp,
     )
 

time: 74.7 us -> 70.5 us (0.944)
  waiting for transfers between devices: 15.9 us -> 11.7 us
  starting transfers between devices: 22.2 us -> 23.9 us
  blocking collectives: 17.9 us -> 16.3 us
    ppermute x4, waiting for transfers between devices: 6.36 us -> 1.92 us  [moved(): return lax.ppermute(value, axis, pairs)]
    ppermute x4, starting transfers between devices: 12.3 us -> 14.9 us  [moved(): return lax.ppermute(value, axis, pairs)]
    all_to_all x1, blocking collectives: 17.9 us -> 16.3 us  [gathered(): return lax.all_to_all(copies, ('gx', 'gy'), 0, 0)]
    ppermute x4 -> x2, starting transfers between devices: 2.7 us -> 1.37 us  [the longest x1 0.69 us: local(): upper = lax.ppermute(down[0] if down else own, 'gx', links(2, -1))]
  transfers between devices with their start and end apart: 12 -> 10, of which waited for: 4 -> 3; matrix products, arithmetic and copies ran while one was open for 0% -> 0% of each run, Pallas kernels for 2% -> 2%
where the time goes in v7:
time: 70.5 us; the launch traced here: 70.1 us
  starting transfers between devices  23.9 us (34%)
  blocking collectives  16.3 us (23%)
  Pallas kernels  16.2 us (23%)
  waiting for transfers between devices  11.7 us (17%)
  local copies, waits for them, and re-layouts  1.07 us (2%)
  other arithmetic  0.8 us (1%)
    all_to_all x1, blocking collectives, gathered(): return lax.all_to_all(copies, ('gx', 'gy'), 0, 0)  16.3 us
    ppermute x4, starting transfers between devices, moved(): return lax.ppermute(value, axis, pairs)  14.9 us
    all_to_all x1, waiting for transfers between devices, gathered(): return lax.all_to_all(copies, ('gx', 'gy'), 0, 0)  9.53 us
    pallas_call x1, Pallas kernels, local(): pl.pallas_call(functools.partial(main_kernel, sizes), out_shape=[jax.Shap...  8.85 us
    ppermute x3, starting transfers between devices, swapped(): return lax.ppermute(value, 'gx', links(0, 1) + links(1, -1))  4.99 us
    pallas_call x1, Pallas kernels, local(): pl.pallas_call(functools.partial(solve_kernel, sizes), out_shape=jax.Shap...  4.7 us
    all_to_all x1, starting transfers between devices, gathered(): return lax.all_to_all(copies, ('gx', 'gy'), 0, 0)  2.58 us
    ppermute x4, waiting for transfers between devices, moved(): return lax.ppermute(value, axis, pairs)  1.92 us
  transfers between devices with their start and end apart: 10, of which 3 were waited for; matrix products, arithmetic and copies ran while one was open for 0% of the time, Pallas kernels for 2%

profile of v7, /device:TPU:0, one launch (start us, length us, event | category | flops | bytes accessed | tf_op | source)
XLA Modules:
  0.0 70.1 jit_solution(2816150250012095060)
XLA Ops:
  0.0 0.7 %negate_select_fusion.codes = f32[2,8,128]{2,1,0:T(8,128)S(1)} fusion(s32[2,8,128]{2,1,0:T(8,128)} %levels.1, s32[2,8,128]{2,1,0:T(8,128)} %param.5), kind=kLoop, calls=%fused_computation | loop fusion | flops 16384 | bytes 24576 | tf_op jit(solution)/shard_map/jit(_where)/select_n | solution.py:625
  0.7 0.0 copy-start
  0.7 1.1 %copy-done = f32[3,24,2,8,128]{4,3,2,1,0:T(8,128)S(1)} copy-done((f32[3,24,2,8,128]{4,3,2,1,0:T(8,128)S(1)}, f32[3,24,2,8,128]{4,3,2,1,0:T(8,128)}, u32[]{:S(2)}) %copy-start) | copy-done | bytes 589848
  1.8 0.1 pack.1
  1.9 0.5 collective-permute-start
  2.4 0.7 collective-permute-start.2
  3.1 0.7 collective-permute-start.1
  3.8 0.3 collective-permute-done.pair
  4.1 1.3 %collective-permute-start.4 = (f32[296,128]{1,0:T(8,128)S(1)}, f32[296,128]{1,0:T(8,128)S(1)}, u32[]{:S(2)}, u32[]{:S(2)}) collective-permute-start(f32[296,128]{1,0:T(8,128)S(1)} %get-tuple-element.20), channel_id=1, source_target_pairs={{1,0},{2,1},{3,2},{5,4},{6,5},{7,6},{9,8},{10,9},{11,10},{13,12},{... | collective-permute-start | bytes 454664 | tf_op jit(solution)/shard_map/ppermute | solution.py:654
  5.4 5.5 %collective-permute-start.3 = (f32[152,128]{1,0:T(8,128)S(1)}, f32[152,128]{1,0:T(8,128)S(1)}, u32[]{:S(2)}, u32[]{:S(2)}) collective-permute-start(f32[152,128]{1,0:T(8,128)S(1)} %get-tuple-element.19), channel_id=1, source_target_pairs={{0,1},{1,2},{2,3},{4,5},{5,6},{6,7},{8,9},{9,10},{10,11},{12,13},{... | collective-permute-start | bytes 233480 | tf_op jit(solution)/shard_map/ppermute | solution.py:654
  10.9 0.1 pad_add_fusion.start.first
  11.0 0.0 collective-permute-done.1.lower
  11.0 0.0 collective-permute-done.2.upper
  11.0 0.6 corners.1
  11.6 1.3 %collective-permute-start.8 = (f32[296,128]{1,0:T(8,128)S(1)}, f32[296,128]{1,0:T(8,128)S(1)}, u32[]{:S(2)}, u32[]{:S(2)}) collective-permute-start(f32[296,128]{1,0:T(8,128)S(1)} %get-tuple-element.22), channel_id=1, source_target_pairs={{1,0},{2,1},{3,2},{5,4},{6,5},{7,6},{9,8},{10,9},{11,10},{13,12},{... | collective-permute-start | bytes 454664 | tf_op jit(solution)/shard_map/ppermute | solution.py:654
  12.9 0.0 collective-permute-done.4.yp
  12.9 4.4 %collective-permute-start.6 = (f32[296,128]{1,0:T(8,128)S(1)}, f32[296,128]{1,0:T(8,128)S(1)}, u32[]{:S(2)}, u32[]{:S(2)}) collective-permute-start(f32[296,128]{1,0:T(8,128)S(1)} %collective-permute-done.4.yp), channel_id=1, source_target_pairs={{0,4},{8,12},{16,20},{24,28},{4,0},{12,8},{20,16},{28,24},{1,5},{9... | collective-permute-start | bytes 454664 | tf_op jit(solution)/shard_map/ppermute | solution.py:660
  17.3 6.9 %collective-permute-start.7 = (f32[152,128]{1,0:T(8,128)S(1)}, f32[152,128]{1,0:T(8,128)S(1)}, u32[]{:S(2)}, u32[]{:S(2)}) collective-permute-start(f32[152,128]{1,0:T(8,128)S(1)} %get-tuple-element.21), channel_id=1, source_target_pairs={{0,1},{1,2},{2,3},{4,5},{5,6},{6,7},{8,9},{9,10},{10,11},{12,13},{... | collective-permute-start | bytes 233480 | tf_op jit(solution)/shard_map/ppermute | solution.py:654
  24.1 0.0 collective-permute-done.3.ym
  24.2 0.1 collective-permute-start.5
  24.2 1.9 %collective-permute-done.7.ym_corner = f32[152,128]{1,0:T(8,128)S(1)} collective-permute-done((f32[152,128]{1,0:T(8,128)S(1)}, f32[152,128]{1,0:T(8,128)S(1)}, u32[]{:S(2)}, u32[]{:S(2)}) %collective-permute-start.7) | collective-permute-done | bytes 77856 | tf_op jit(solution)/shard_map/ppermute | solution.py:654
  26.1 0.0 collective-permute-done.8.yp_corner
  26.1 0.0 collective-permute-done.5.ym_pair
  26.1 0.0 collective-permute-done.6.yp_pair
  26.2 8.8 %operator.1 = (bf16[96,10368]{1,0:T(8,128)(2,1)S(1)}, f32[32,3,4,128]{3,2,1,0:T(4,128)S(1)}) custom-call(s32[2]{0:T(128)S(1)} %pad_add_fusion.start.first, f32[1168,128]{1,0:T(8,128)S(1)} %get-tuple-element.16.own, f32[1168,128]{1,0:T(8,128)S(1)} %collective-permute-done.pair, f32[592,128]{1,0:T(8,128)S(1)} %collective-permute-done.1.lower, ...), custom_call_target="tpu_custom_call" | custom-call | tf_op jit(solution)/shard_map/operator/pallas_call | solution.py:691
  35.0 0.0 copy-start.1
  35.0 16.3 %all_to_all.10.system = f32[32,3,4,128]{3,2,1,0:T(4,128)S(1)} all-to-all(f32[32,3,4,128]{3,2,1,0:T(4,128)S(1)} %get-tuple-element.23), channel_id=1, replica_groups=mesh['gx'=8,'gy'=4] {'gx','gy'}, dimensions={0} | all-to-all | bytes 393216 | tf_op jit(solution)/shard_map/all_to_all | solution.py:717
  51.3 4.7 %solve.1 = f32[32,2,8,128]{3,2,1,0:T(8,128)} custom-call(f32[32,3,4,128]{3,2,1,0:T(4,128)S(1)} %all_to_all.10.system, bf16[96,10368]{1,0:T(8,128)(2,1)S(1)} %get-tuple-element.24.both, f32[2,8,128]{2,1,0:T(8,128)S(1)} %negate_select_fusion.codes), custom_call_target="tpu_custom_call" | custom-call | tf_op jit(solution)/shard_map/solve/pallas_call | solution.py:721
  56.0 2.6 %all-to-all-start.1 = ((f32[32,2,8,128]{3,2,1,0:T(8,128)}), f32[32,2,8,128]{3,2,1,0:T(8,128)S(1)}, u32[]{:S(2)}, u32[]{:S(2)}) async-start(f32[32,2,8,128]{3,2,1,0:T(8,128)} %solve.1), calls=%async_computation.1 | async-start | bytes 524288 | tf_op jit(solution)/shard_map/all_to_all | solution.py:717
  58.6 0.0 copy-done.1
  58.6 0.7 scale.1
  59.3 9.5 %all-to-all-done.1.blocks = f32[32,2,8,128]{3,2,1,0:T(8,128)S(1)} async-done(((f32[32,2,8,128]{3,2,1,0:T(8,128)}), f32[32,2,8,128]{3,2,1,0:T(8,128)S(1)}, u32[]{:S(2)}, u32[]{:S(2)}) %all-to-all-start.1) | async-done | bytes 262176 | tf_op jit(solution)/shard_map/all_to_all | solution.py:717
  68.8 1.3 %cone.1 = f32[2,8,128]{2,1,0:T(8,128)} custom-call(s32[2]{0:T(128)S(1)} %pad_add_fusion.start.first, f32[32,2,8,128]{3,2,1,0:T(8,128)S(1)} %all-to-all-done.1.blocks, f32[2,8,128]{2,1,0:T(8,128)S(1)} %scale.1), custom_call_target="tpu_custom_call" | custom-call | tf_op jit(solution)/shard_map/cone/pallas_call | solution.py:739
  (1 shorter events, 0.0 us)
Async XLA Ops:
  0.7 1.1 %copy-start = (f32[3,24,2,8,128]{4,3,2,1,0:T(8,128)S(1)}, f32[3,24,2,8,128]{4,3,2,1,0:T(8,128)}, u32[]{:S(2)}) copy-start(f32[3,24,2,8,128]{4,3,2,1,0:T(8,128)} %forces.1) | copy-start | bytes 1769476
  1.9 2.2 %collective-permute-start = (f32[1168,128]{1,0:T(8,128)S(1)}, f32[1168,128]{1,0:T(8,128)S(1)}, u32[]{:S(2)}, u32[]{:S(2)}) collective-permute-start(f32[1168,128]{1,0:T(8,128)S(1)} %get-tuple-element.16.own), channel_id=1, source_target_pairs={{0,4},{8,12},{16,20},{24,28},{4,0},{12,8},{20,16},{28,24},{1,5},{9... | collective-permute-start | bytes 1794056 | tf_op jit(solution)/shard_map/ppermute | solution.py:660
  2.4 8.5 %collective-permute-start.2 = (f32[1168,128]{1,0:T(8,128)S(1)}, f32[1168,128]{1,0:T(8,128)S(1)}, u32[]{:S(2)}, u32[]{:S(2)}) collective-permute-start(f32[1168,128]{1,0:T(8,128)S(1)} %get-tuple-element.16.own), channel_id=1, source_target_pairs={{8,4},{16,12},{24,20},{9,5},{17,13},{25,21},{10,6},{18,14},{26,22}... | collective-permute-start | bytes 1794056 | tf_op jit(solution)/shard_map/ppermute | solution.py:662
  3.1 7.8 %collective-permute-start.1 = (f32[592,128]{1,0:T(8,128)S(1)}, f32[592,128]{1,0:T(8,128)S(1)}, u32[]{:S(2)}, u32[]{:S(2)}) collective-permute-start(f32[592,128]{1,0:T(8,128)S(1)} %get-tuple-element.18), channel_id=1, source_target_pairs={{4,8},{12,16},{20,24},{5,9},{13,17},{21,25},{6,10},{14,18},{22,26}... | collective-permute-start | bytes 909320 | tf_op jit(solution)/shard_map/ppermute | solution.py:663
  4.1 8.8 %collective-permute-start.4 = (f32[296,128]{1,0:T(8,128)S(1)}, f32[296,128]{1,0:T(8,128)S(1)}, u32[]{:S(2)}, u32[]{:S(2)}) collective-permute-start(f32[296,128]{1,0:T(8,128)S(1)} %get-tuple-element.20), channel_id=1, source_target_pairs={{1,0},{2,1},{3,2},{5,4},{6,5},{7,6},{9,8},{10,9},{11,10},{13,12},{... | collective-permute-start | bytes 454664 | tf_op jit(solution)/shard_map/ppermute | solution.py:654
  5.4 18.8 %collective-permute-start.3 = (f32[152,128]{1,0:T(8,128)S(1)}, f32[152,128]{1,0:T(8,128)S(1)}, u32[]{:S(2)}, u32[]{:S(2)}) collective-permute-start(f32[152,128]{1,0:T(8,128)S(1)} %get-tuple-element.19), channel_id=1, source_target_pairs={{0,1},{1,2},{2,3},{4,5},{5,6},{6,7},{8,9},{9,10},{10,11},{12,13},{... | collective-permute-start | bytes 233480 | tf_op jit(solution)/shard_map/ppermute | solution.py:654
  11.6 14.6 %collective-permute-start.8 = (f32[296,128]{1,0:T(8,128)S(1)}, f32[296,128]{1,0:T(8,128)S(1)}, u32[]{:S(2)}, u32[]{:S(2)}) collective-permute-start(f32[296,128]{1,0:T(8,128)S(1)} %get-tuple-element.22), channel_id=1, source_target_pairs={{1,0},{2,1},{3,2},{5,4},{6,5},{7,6},{9,8},{10,9},{11,10},{13,12},{... | collective-permute-start | bytes 454664 | tf_op jit(solution)/shard_map/ppermute | solution.py:654
  12.9 13.3 %collective-permute-start.6 = (f32[296,128]{1,0:T(8,128)S(1)}, f32[296,128]{1,0:T(8,128)S(1)}, u32[]{:S(2)}, u32[]{:S(2)}) collective-permute-start(f32[296,128]{1,0:T(8,128)S(1)} %collective-permute-done.4.yp), channel_id=1, source_target_pairs={{0,4},{8,12},{16,20},{24,28},{4,0},{12,8},{20,16},{28,24},{1,5},{9... | collective-permute-start | bytes 454664 | tf_op jit(solution)/shard_map/ppermute | solution.py:660
  17.3 8.9 %collective-permute-start.7 = (f32[152,128]{1,0:T(8,128)S(1)}, f32[152,128]{1,0:T(8,128)S(1)}, u32[]{:S(2)}, u32[]{:S(2)}) collective-permute-start(f32[152,128]{1,0:T(8,128)S(1)} %get-tuple-element.21), channel_id=1, source_target_pairs={{0,1},{1,2},{2,3},{4,5},{5,6},{6,7},{8,9},{9,10},{10,11},{12,13},{... | collective-permute-start | bytes 233480 | tf_op jit(solution)/shard_map/ppermute | solution.py:654
  24.2 2.0 %collective-permute-start.5 = (f32[152,128]{1,0:T(8,128)S(1)}, f32[152,128]{1,0:T(8,128)S(1)}, u32[]{:S(2)}, u32[]{:S(2)}) collective-permute-start(f32[152,128]{1,0:T(8,128)S(1)} %collective-permute-done.3.ym), channel_id=1, source_target_pairs={{0,4},{8,12},{16,20},{24,28},{4,0},{12,8},{20,16},{28,24},{1,5},{9... | collective-permute-start | bytes 233480 | tf_op jit(solution)/shard_map/ppermute | solution.py:660
  35.0 23.6 %copy-start.1 = (s32[2,8,128]{2,1,0:T(8,128)S(1)}, s32[2,8,128]{2,1,0:T(8,128)}, u32[]{:S(2)}) copy-start(s32[2,8,128]{2,1,0:T(8,128)} %levels.1) | copy-start | bytes 24580
  56.0 12.8 %all-to-all-start.1 = ((f32[32,2,8,128]{3,2,1,0:T(8,128)}), f32[32,2,8,128]{3,2,1,0:T(8,128)S(1)}, u32[]{:S(2)}, u32[]{:S(2)}) async-start(f32[32,2,8,128]{3,2,1,0:T(8,128)} %solve.1), calls=%async_computation.1 | async-start | bytes 524288 | tf_op jit(solution)/shard_map/all_to_all | solution.py:717

commit v8 on v7

--- a/solution.py
+++ b/solution.py
@@ -235,30 +235,22 @@
     fill(own, base, sizes, yp, every_x, (rows - 1,), every_x, (rows - 2, rows - 1))
 
 
-def corner_kernel(sizes, start, lower, upper, ym, yp):
+def corner_kernel(sizes, ym, yp, down, up):
     planes, rows, cases = sizes
     block = 3 * cases
-    even = start[0] // planes % 2 == 0
-    for ref, edges, code in ((ym, (0, 1), 0), (yp, (rows - 1,), rows - 2)):
+    for ref, first, count in ((down, 0, 2), (up, planes - 1, 1)):
         line = 0
-        for slot in range(2):
-            for edge in edges:
-                at = slot * rows + edge
-                above = upper[at * block : (at + 1) * block, :]
-                below = lower[edge * block : (edge + 1) * block, :] if slot == 1 else 0.0
-                ref[line : line + block, :] = jnp.where(even, below, above)
-                line += block
-        for slot in range(2):
-            at = slot * rows + code
-            above = upper[2 * rows * block + at : 2 * rows * block + at + 2, :]
-            below = lower[rows * block + at : rows * block + at + 2, :]
-            ref[line : line + 2, :] = jnp.where(even, below, above)
-            line += 2
-        if line < ref.shape[0]:
-            ref[line:, :] = jnp.zeros((ref.shape[0] - line, LANES), f32)
-
-
-def readers(sizes, first, own, pair, lower, upper, y_own, y_pair, y_corner):
+        for source, width in ((ym, 1), (yp, 2)):
+            size = width * block
+            ref[line : line + count * size, :] = source[first * size : (first + count) * size, :]
+            line += count * size
+            codes = planes * size + (first + count - 2) * 2
+            ref[line : line + 4, :] = source[codes : codes + 4, :]
+            ref[line + 4 : line + 8, :] = jnp.zeros((4, LANES), f32)
+            line += 8
+
+
+def readers(sizes, first, own, pair, lower, upper, y_own, y_pair, corner_low, corner_high):
     planes, rows, cases = sizes
     block = 3 * cases
     even = first // planes % 2 == 0
@@ -274,6 +266,15 @@
         if y < 0:
             return lines(below, slot * block, block)
         return lines(above, (slot * 2 + y - rows) * block, block)
+
+    def corner(ref, count, slot, y):
+        if y < 0:
+            return lines(ref, slot * block, block)
+        return lines(ref, count * block + 8 + (slot * 2 + y - rows) * block, block)
+
+    def corner_codes(ref, count, slot, y):
+        start = count * block if y < 0 else 3 * count * block + 8
+        return lines(ref, start + slot * 2, 2)
 
     def load(x, y):
         in_y = 0 <= y < rows
@@ -282,10 +283,11 @@
         if x < 0:
             if in_y:
                 return jnp.where(even, inside(lower, 0, y), inside(pair, planes - 1, y))
-            return jnp.where(even, beyond(y_corner, 1, y), beyond(y_pair, planes - 1, y))
+            return jnp.where(even, corner(corner_low, 1, 0, y), beyond(y_pair, planes - 1, y))
         if in_y:
             return jnp.where(even, inside(pair, x - planes, y), inside(upper, x - planes, y))
-        return jnp.where(even, beyond(y_pair, x - planes, y), beyond(y_corner, x - planes, y))
+        other = corner(corner_high, 2, x - planes, y)
+        return jnp.where(even, beyond(y_pair, x - planes, y), other)
 
     def inside_codes(ref, x):
         return lines(ref, planes * rows * block + x * rows, rows)
@@ -305,19 +307,19 @@
                 other = inside_codes(pair, planes + x)
                 return jnp.where(even, lines(lower, (block + slot) * rows, rows), other)
             other = beyond_codes(y_pair, planes, planes + x, y)
-            return jnp.where(even, beyond_codes(y_corner, 2, slot, y), other)
+            return jnp.where(even, corner_codes(corner_low, 1, slot, y), other)
         slot = x - planes
         if y == 0:
             other = lines(upper, (2 * block + slot) * rows, rows)
             return jnp.where(even, inside_codes(pair, slot), other)
-        other = beyond_codes(y_corner, 2, slot, y)
+        other = corner_codes(corner_high, 2, slot, y)
         return jnp.where(even, beyond_codes(y_pair, planes, slot, y), other)
 
     return load, codes
 
 
 def main_kernel(
-    sizes, first, own, pair, lower, upper, ym, yp, ym_pair, yp_pair, ym_corner, yp_corner,
+    sizes, first, own, pair, lower, upper, ym, yp, ym_pair, yp_pair, corner_low, corner_high,
     both_out, system_out, stiff_ref, inverse,
     start, sums, diffs, acc_s, acc_d, w_sums, w_diffs, acc2_s, acc2_d, right, table,
 ):
@@ -326,7 +328,7 @@
     xs, ys = planes + 3, rows + 3
     load, signed = readers(
         sizes, first[0], own, pair, lower, upper,
-        (ym, yp), (ym_pair, yp_pair), (ym_corner, yp_corner),
+        (ym, yp), (ym_pair, yp_pair), corner_low, corner_high,
     )
     for x in range(-2, planes + 2):
         for y, count in ((-2, 2), (0, rows), (rows, 2)):
@@ -672,16 +674,20 @@
         name="rows",
     )(own)
     from_yp, from_ym = moved(ym, "gy", -1), moved(yp, "gy", 1)
-    corner_m, corner_p = pl.pallas_call(
+    pair_yp, pair_ym = swapped(from_yp), swapped(from_ym)
+    corner_down, corner_up = pl.pallas_call(
         functools.partial(corner_kernel, sizes),
-        out_shape=[shape(4, 4), shape(2, 4)],
-        in_specs=[scalars] + [VMEM] * 2,
+        out_shape=[
+            jax.ShapeDtypeStruct((6 * block + 16, LANES), f32),
+            jax.ShapeDtypeStruct((3 * block + 16, LANES), f32),
+        ],
+        in_specs=[VMEM] * 2,
         out_specs=[VMEM] * 2,
         compiler_params=PARAMS,
         name="corners",
-    )(start, lower, upper)
-    corner_yp, corner_ym = moved(corner_m, "gy", -1), moved(corner_p, "gy", 1)
-    pair_yp, pair_ym = swapped(from_yp), swapped(from_ym)
+    )(from_ym, from_yp)
+    corner_high = lax.ppermute(corner_down, "gx", links(2, -1))
+    corner_low = lax.ppermute(corner_up, "gx", links(1, 1))
 
     devices = count_x * count_y
     nodes = (planes + 1) * (rows + 1)
@@ -710,7 +716,7 @@
         name="operator",
     )(
         start, own, pair, lower, upper, from_ym, from_yp,
-        pair_ym, pair_yp, corner_ym, corner_yp,
+        pair_ym, pair_yp, corner_low, corner_high,
     )
 
     def gathered(copies):

time: 70.5 us -> 70 us (level)
  starting transfers between devices: 23.9 us -> 20.5 us
  blocking collectives: 16.3 us -> 18.8 us
  waiting for transfers between devices: 11.7 us -> 12.6 us
    ppermute x4 -> x2, starting transfers between devices: 14.9 us -> 6.77 us  [moved(): return lax.ppermute(value, axis, pairs)]
    ppermute x3, starting transfers between devices: 4.99 us -> 8.44 us  [swapped(): return lax.ppermute(value, 'gx', links(0, 1) + links(1, -1))]
    all_to_all x1, blocking collectives: 16.3 us -> 18.8 us  [gathered(): return lax.all_to_all(copies, ('gx', 'gy'), 0, 0)]
    ppermute x0 -> x2, starting transfers between devices: none -> 1.33 us  [the longest x1 0.68 us: local(): corner_high = lax.ppermute(corner_down, 'gx', links(2, -1))]
    ppermute x3, waiting for transfers between devices: 0.27 us -> 1.1 us  [swapped(): return lax.ppermute(value, 'gx', links(0, 1) + links(1, -1))]
    ppermute x4 -> x2, waiting for transfers between devices: 1.92 us -> 2 us  [moved(): return lax.ppermute(value, axis, pairs)]
  transfers between devices with their start and end apart: 10 -> 10, of which waited for: 3 -> 4; matrix products, arithmetic and copies ran while one was open for 0% -> 0% of each run, Pallas kernels for 2% -> 1%
where the time goes in v8:
time: 70 us; the launch traced here: 69.6 us
  starting transfers between devices  20.5 us (29%)
  blocking collectives  18.8 us (27%)
  Pallas kernels  15.7 us (22%)
  waiting for transfers between devices  12.6 us (18%)
  local copies, waits for them, and re-layouts  1.07 us (2%)
  other arithmetic  0.8 us (1%)
    all_to_all x1, blocking collectives, gathered(): return lax.all_to_all(copies, ('gx', 'gy'), 0, 0)  18.8 us
    all_to_all x1, waiting for transfers between devices, gathered(): return lax.all_to_all(copies, ('gx', 'gy'), 0, 0)  9.53 us
    pallas_call x1, Pallas kernels, local(): pl.pallas_call(functools.partial(main_kernel, sizes), out_shape=[jax.Shap...  8.89 us
    ppermute x3, starting transfers between devices, swapped(): return lax.ppermute(value, 'gx', links(0, 1) + links(1, -1))  8.44 us
    ppermute x2, starting transfers between devices, moved(): return lax.ppermute(value, axis, pairs)  6.77 us
    pallas_call x1, Pallas kernels, local(): pl.pallas_call(functools.partial(solve_kernel, sizes), out_shape=jax.Shap...  4.7 us
    all_to_all x1, starting transfers between devices, gathered(): return lax.all_to_all(copies, ('gx', 'gy'), 0, 0)  2.58 us
    ppermute x2, waiting for transfers between devices, moved(): return lax.ppermute(value, axis, pairs)  2 us
  transfers between devices with their start and end apart: 10, of which 4 were waited for; matrix products, arithmetic and copies ran while one was open for 0% of the time, Pallas kernels for 1%

profile of v8, /device:TPU:0, one launch (start us, length us, event | category | flops | bytes accessed | tf_op | source)
XLA Modules:
  0.0 69.6 jit_solution(18357665459892313485)
XLA Ops:
  0.0 0.7 %negate_select_fusion.codes = f32[2,8,128]{2,1,0:T(8,128)S(1)} fusion(s32[2,8,128]{2,1,0:T(8,128)} %levels.1, s32[2,8,128]{2,1,0:T(8,128)} %param.5), kind=kLoop, calls=%fused_computation | loop fusion | flops 16384 | bytes 24576 | tf_op jit(solution)/shard_map/jit(_where)/select_n | solution.py:627
  0.7 0.0 copy-start
  0.7 1.1 %copy-done = f32[3,24,2,8,128]{4,3,2,1,0:T(8,128)S(1)} copy-done((f32[3,24,2,8,128]{4,3,2,1,0:T(8,128)S(1)}, f32[3,24,2,8,128]{4,3,2,1,0:T(8,128)}, u32[]{:S(2)}) %copy-start) | copy-done | bytes 589848
  1.8 0.1 pack.1
  1.9 0.5 collective-permute-start
  2.4 0.7 collective-permute-start.2
  3.1 0.7 collective-permute-start.1
  3.8 0.3 collective-permute-done.pair
  4.1 1.3 %collective-permute-start.4 = (f32[296,128]{1,0:T(8,128)S(1)}, f32[296,128]{1,0:T(8,128)S(1)}, u32[]{:S(2)}, u32[]{:S(2)}) collective-permute-start(f32[296,128]{1,0:T(8,128)S(1)} %get-tuple-element.20), channel_id=1, source_target_pairs={{1,0},{2,1},{3,2},{5,4},{6,5},{7,6},{9,8},{10,9},{11,10},{13,12},{... | collective-permute-start | bytes 454664 | tf_op jit(solution)/shard_map/ppermute | solution.py:656
  5.4 5.5 %collective-permute-start.3 = (f32[152,128]{1,0:T(8,128)S(1)}, f32[152,128]{1,0:T(8,128)S(1)}, u32[]{:S(2)}, u32[]{:S(2)}) collective-permute-start(f32[152,128]{1,0:T(8,128)S(1)} %get-tuple-element.19), channel_id=1, source_target_pairs={{0,1},{1,2},{2,3},{4,5},{5,6},{6,7},{8,9},{9,10},{10,11},{12,13},{... | collective-permute-start | bytes 233480 | tf_op jit(solution)/shard_map/ppermute | solution.py:656
  10.9 2.0 %collective-permute-done.3.ym = f32[152,128]{1,0:T(8,128)S(1)} collective-permute-done((f32[152,128]{1,0:T(8,128)S(1)}, f32[152,128]{1,0:T(8,128)S(1)}, u32[]{:S(2)}, u32[]{:S(2)}) %collective-permute-start.3) | collective-permute-done | bytes 77856 | tf_op jit(solution)/shard_map/ppermute | solution.py:656
  12.9 0.0 collective-permute-done.4.yp
  12.9 0.7 collective-permute-start.8
  13.6 4.0 %collective-permute-start.6 = (f32[296,128]{1,0:T(8,128)S(1)}, f32[296,128]{1,0:T(8,128)S(1)}, u32[]{:S(2)}, u32[]{:S(2)}) collective-permute-start(f32[296,128]{1,0:T(8,128)S(1)} %collective-permute-done.4.yp), channel_id=1, source_target_pairs={{0,4},{8,12},{16,20},{24,28},{4,0},{12,8},{20,16},{28,24},{1,5},{9... | collective-permute-start | bytes 454664 | tf_op jit(solution)/shard_map/ppermute | solution.py:662
  17.5 0.7 collective-permute-start.7
  18.2 0.0 collective-permute-done.1.lower
  18.2 4.0 %collective-permute-start.5 = (f32[152,128]{1,0:T(8,128)S(1)}, f32[152,128]{1,0:T(8,128)S(1)}, u32[]{:S(2)}, u32[]{:S(2)}) collective-permute-start(f32[152,128]{1,0:T(8,128)S(1)} %collective-permute-done.3.ym), channel_id=1, source_target_pairs={{0,4},{8,12},{16,20},{24,28},{4,0},{12,8},{20,16},{28,24},{1,5},{9... | collective-permute-start | bytes 233480 | tf_op jit(solution)/shard_map/ppermute | solution.py:662
  22.2 0.1 pad_add_fusion.first.start
  22.3 0.0 collective-permute-done.2.upper
  22.3 0.8 %collective-permute-done.5.ym_pair = f32[152,128]{1,0:T(8,128)S(1)} collective-permute-done((f32[152,128]{1,0:T(8,128)S(1)}, f32[152,128]{1,0:T(8,128)S(1)}, u32[]{:S(2)}, u32[]{:S(2)}) %collective-permute-start.5) | collective-permute-done | bytes 77856 | tf_op jit(solution)/shard_map/ppermute | solution.py:662
  23.1 0.0 collective-permute-done.7.corner_low
  23.1 0.0 collective-permute-done.6.yp_pair
  23.1 0.0 collective-permute-done.8.corner_high
  23.1 8.9 %operator.1 = (bf16[96,10368]{1,0:T(8,128)(2,1)S(1)}, f32[32,3,4,128]{3,2,1,0:T(4,128)S(1)}) custom-call(s32[2]{0:T(128)S(1)} %pad_add_fusion.first.start, f32[1168,128]{1,0:T(8,128)S(1)} %get-tuple-element.16.own, f32[1168,128]{1,0:T(8,128)S(1)} %collective-permute-done.pair, f32[592,128]{1,0:T(8,128)S(1)} %collective-permute-done.1.lower, ...), custom_call_target="tpu_custom_call" | custom-call | tf_op jit(solution)/shard_map/operator/pallas_call | solution.py:697
  32.0 0.0 copy-start.1
  32.0 18.8 %all_to_all.10.system = f32[32,3,4,128]{3,2,1,0:T(4,128)S(1)} all-to-all(f32[32,3,4,128]{3,2,1,0:T(4,128)S(1)} %get-tuple-element.23), channel_id=1, replica_groups=mesh['gx'=8,'gy'=4] {'gx','gy'}, dimensions={0} | all-to-all | bytes 393216 | tf_op jit(solution)/shard_map/all_to_all | solution.py:723
  50.8 4.7 %solve.1 = f32[32,2,8,128]{3,2,1,0:T(8,128)} custom-call(f32[32,3,4,128]{3,2,1,0:T(4,128)S(1)} %all_to_all.10.system, bf16[96,10368]{1,0:T(8,128)(2,1)S(1)} %get-tuple-element.24.both, f32[2,8,128]{2,1,0:T(8,128)S(1)} %negate_select_fusion.codes), custom_call_target="tpu_custom_call" | custom-call | tf_op jit(solution)/shard_map/solve/pallas_call | solution.py:727
  55.5 2.6 %all-to-all-start.1 = ((f32[32,2,8,128]{3,2,1,0:T(8,128)}), f32[32,2,8,128]{3,2,1,0:T(8,128)S(1)}, u32[]{:S(2)}, u32[]{:S(2)}) async-start(f32[32,2,8,128]{3,2,1,0:T(8,128)} %solve.1), calls=%async_computation.1 | async-start | bytes 524288 | tf_op jit(solution)/shard_map/all_to_all | solution.py:723
  58.1 0.0 copy-done.1
  58.1 0.7 scale.1
  58.8 9.5 %all-to-all-done.1.blocks = f32[32,2,8,128]{3,2,1,0:T(8,128)S(1)} async-done(((f32[32,2,8,128]{3,2,1,0:T(8,128)}), f32[32,2,8,128]{3,2,1,0:T(8,128)S(1)}, u32[]{:S(2)}, u32[]{:S(2)}) %all-to-all-start.1) | async-done | bytes 262176 | tf_op jit(solution)/shard_map/all_to_all | solution.py:723
  68.3 1.3 %cone.1 = f32[2,8,128]{2,1,0:T(8,128)} custom-call(s32[2]{0:T(128)S(1)} %pad_add_fusion.first.start, f32[32,2,8,128]{3,2,1,0:T(8,128)S(1)} %all-to-all-done.1.blocks, f32[2,8,128]{2,1,0:T(8,128)S(1)} %scale.1), custom_call_target="tpu_custom_call" | custom-call | tf_op jit(solution)/shard_map/cone/pallas_call | solution.py:745
  (2 shorter events, 0.0 us)
Async XLA Ops:
  0.7 1.1 %copy-start = (f32[3,24,2,8,128]{4,3,2,1,0:T(8,128)S(1)}, f32[3,24,2,8,128]{4,3,2,1,0:T(8,128)}, u32[]{:S(2)}) copy-start(f32[3,24,2,8,128]{4,3,2,1,0:T(8,128)} %forces.1) | copy-start | bytes 1769476
  1.9 2.2 %collective-permute-start = (f32[1168,128]{1,0:T(8,128)S(1)}, f32[1168,128]{1,0:T(8,128)S(1)}, u32[]{:S(2)}, u32[]{:S(2)}) collective-permute-start(f32[1168,128]{1,0:T(8,128)S(1)} %get-tuple-element.16.own), channel_id=1, source_target_pairs={{0,4},{8,12},{16,20},{24,28},{4,0},{12,8},{20,16},{28,24},{1,5},{9... | collective-permute-start | bytes 1794056 | tf_op jit(solution)/shard_map/ppermute | solution.py:662
  2.4 19.8 %collective-permute-start.2 = (f32[1168,128]{1,0:T(8,128)S(1)}, f32[1168,128]{1,0:T(8,128)S(1)}, u32[]{:S(2)}, u32[]{:S(2)}) collective-permute-start(f32[1168,128]{1,0:T(8,128)S(1)} %get-tuple-element.16.own), channel_id=1, source_target_pairs={{8,4},{16,12},{24,20},{9,5},{17,13},{25,21},{10,6},{18,14},{26,22}... | collective-permute-start | bytes 1794056 | tf_op jit(solution)/shard_map/ppermute | solution.py:664
  3.1 15.1 %collective-permute-start.1 = (f32[592,128]{1,0:T(8,128)S(1)}, f32[592,128]{1,0:T(8,128)S(1)}, u32[]{:S(2)}, u32[]{:S(2)}) collective-permute-start(f32[592,128]{1,0:T(8,128)S(1)} %get-tuple-element.18), channel_id=1, source_target_pairs={{4,8},{12,16},{20,24},{5,9},{13,17},{21,25},{6,10},{14,18},{22,26}... | collective-permute-start | bytes 909320 | tf_op jit(solution)/shard_map/ppermute | solution.py:665
  4.1 8.8 %collective-permute-start.4 = (f32[296,128]{1,0:T(8,128)S(1)}, f32[296,128]{1,0:T(8,128)S(1)}, u32[]{:S(2)}, u32[]{:S(2)}) collective-permute-start(f32[296,128]{1,0:T(8,128)S(1)} %get-tuple-element.20), channel_id=1, source_target_pairs={{1,0},{2,1},{3,2},{5,4},{6,5},{7,6},{9,8},{10,9},{11,10},{13,12},{... | collective-permute-start | bytes 454664 | tf_op jit(solution)/shard_map/ppermute | solution.py:656
  5.4 7.5 %collective-permute-start.3 = (f32[152,128]{1,0:T(8,128)S(1)}, f32[152,128]{1,0:T(8,128)S(1)}, u32[]{:S(2)}, u32[]{:S(2)}) collective-permute-start(f32[152,128]{1,0:T(8,128)S(1)} %get-tuple-element.19), channel_id=1, source_target_pairs={{0,1},{1,2},{2,3},{4,5},{5,6},{6,7},{8,9},{9,10},{10,11},{12,13},{... | collective-permute-start | bytes 233480 | tf_op jit(solution)/shard_map/ppermute | solution.py:656
  12.9 10.2 %collective-permute-start.8 = (f32[448,128]{1,0:T(8,128)S(1)}, f32[448,128]{1,0:T(8,128)S(1)}, u32[]{:S(2)}, u32[]{:S(2)}) collective-permute-start(f32[448,128]{1,0:T(8,128)S(1)} %get-tuple-element.22), channel_id=1, source_target_pairs={{8,4},{16,12},{24,20},{9,5},{17,13},{25,21},{10,6},{18,14},{26,22}... | collective-permute-start | bytes 688136 | tf_op jit(solution)/shard_map/ppermute | solution.py:689
  13.6 9.5 %collective-permute-start.6 = (f32[296,128]{1,0:T(8,128)S(1)}, f32[296,128]{1,0:T(8,128)S(1)}, u32[]{:S(2)}, u32[]{:S(2)}) collective-permute-start(f32[296,128]{1,0:T(8,128)S(1)} %collective-permute-done.4.yp), channel_id=1, source_target_pairs={{0,4},{8,12},{16,20},{24,28},{4,0},{12,8},{20,16},{28,24},{1,5},{9... | collective-permute-start | bytes 454664 | tf_op jit(solution)/shard_map/ppermute | solution.py:662
  17.5 5.6 %collective-permute-start.7 = (f32[232,128]{1,0:T(8,128)S(1)}, f32[232,128]{1,0:T(8,128)S(1)}, u32[]{:S(2)}, u32[]{:S(2)}) collective-permute-start(f32[232,128]{1,0:T(8,128)S(1)} %get-tuple-element.21), channel_id=1, source_target_pairs={{4,8},{12,16},{20,24},{5,9},{13,17},{21,25},{6,10},{14,18},{22,26}... | collective-permute-start | bytes 356360 | tf_op jit(solution)/shard_map/ppermute | solution.py:690
  18.2 4.9 %collective-permute-start.5 = (f32[152,128]{1,0:T(8,128)S(1)}, f32[152,128]{1,0:T(8,128)S(1)}, u32[]{:S(2)}, u32[]{:S(2)}) collective-permute-start(f32[152,128]{1,0:T(8,128)S(1)} %collective-permute-done.3.ym), channel_id=1, source_target_pairs={{0,4},{8,12},{16,20},{24,28},{4,0},{12,8},{20,16},{28,24},{1,5},{9... | collective-permute-start | bytes 233480 | tf_op jit(solution)/shard_map/ppermute | solution.py:662
  32.0 26.1 %copy-start.1 = (s32[2,8,128]{2,1,0:T(8,128)S(1)}, s32[2,8,128]{2,1,0:T(8,128)}, u32[]{:S(2)}) copy-start(s32[2,8,128]{2,1,0:T(8,128)} %levels.1) | copy-start | bytes 24580
  55.5 12.8 %all-to-all-start.1 = ((f32[32,2,8,128]{3,2,1,0:T(8,128)}), f32[32,2,8,128]{3,2,1,0:T(8,128)S(1)}, u32[]{:S(2)}, u32[]{:S(2)}) async-start(f32[32,2,8,128]{3,2,1,0:T(8,128)} %solve.1), calls=%async_computation.1 | async-start | bytes 524288 | tf_op jit(solution)/shard_map/all_to_all | solution.py:723

commit v9 on v8

--- a/solution.py
+++ b/solution.py
@@ -439,13 +439,13 @@
 
 
 def solve_kernel(
-    sizes, system, both, codes, out, mixing, sums, diffs, energy, square, full
+    sizes, system, system_pair, both, codes, out, mixing, sums, diffs, energy, square, full
 ):
     planes, rows, cases = sizes
     two = 2 * cases
     nodes_y = rows + 1
     count = planes * rows
-    total = jnp.sum(system[...], axis=0)
+    total = jnp.sum(system[...], axis=0) + jnp.sum(system_pair[...], axis=0)
     half, depth = cases // 2, system.shape[2]
     square[...] = jnp.zeros(square.shape, f32)
     for part in range(half // depth):
@@ -597,7 +597,7 @@
         out[x] = 1.0 / (density * smooth(there, x, rows))
 
 
-def filter_kernel(sizes, counts, start, blocks, scale, out, wide):
+def filter_kernel(sizes, counts, start, blocks, blocks_pair, scale, out, wide):
     planes, rows, _ = sizes
     sides_x = ((-1, planes - 2, planes, 0), (0, 0, planes, 2), (1, 0, 2, 2 + planes))
     sides_y = ((-1, rows - 2, rows, 0), (0, 0, rows, 2), (1, 0, 2, 2 + rows))
@@ -606,8 +606,8 @@
             at_x = start[0] // planes + step_x
             at_y = start[1] // rows + step_y
             inside = (at_x >= 0) & (at_x < counts[0]) & (at_y >= 0) & (at_y < counts[1])
-            index = jnp.where(inside, at_x * counts[1] + at_y, 0)
-            value = blocks[index, x0:x1, y0:y1, :]
+            index = jnp.where(inside, at_x // 2 * counts[1] + at_y, 0)
+            value = (blocks_pair if step_x else blocks)[index, x0:x1, y0:y1, :]
             wide[to_x : to_x + x1 - x0, to_y : to_y + y1 - y0, :] = jnp.where(inside, value, 0.0)
     for x in range(planes):
         out[x] = smooth(wide, x, rows) * scale[x]
@@ -698,7 +698,7 @@
         functools.partial(main_kernel, sizes),
         out_shape=[
             jax.ShapeDtypeStruct((4 * cases, nodes * 3 * LANES), bf16),
-            jax.ShapeDtypeStruct((devices, cases // 8, 4, LANES), f32),
+            jax.ShapeDtypeStruct((devices // 2, cases // 8, 4, LANES), f32),
         ],
         in_specs=[scalars] + [VMEM] * 10,
         out_specs=[VMEM] * 2,
@@ -719,15 +719,21 @@
         pair_ym, pair_yp, corner_low, corner_high,
     )
 
+    groups = [
+        [x * count_y + y for x in range(side, count_x, 2) for y in range(count_y)]
+        for side in range(2)
+    ]
+
     def gathered(copies):
-        return lax.all_to_all(copies, ("gx", "gy"), 0, 0)
+        mine = lax.all_to_all(copies, ("gx", "gy"), 0, 0, axis_index_groups=groups)
+        return mine, swapped(mine)
 
     system = gathered(system)
 
     weighted = pl.pallas_call(
         functools.partial(solve_kernel, sizes),
-        out_shape=jax.ShapeDtypeStruct((devices, planes, rows, LANES), f32),
-        in_specs=[VMEM] * 3,
+        out_shape=jax.ShapeDtypeStruct((devices // 2, planes, rows, LANES), f32),
+        in_specs=[VMEM] * 4,
         out_specs=VMEM,
         scratch_shapes=[
             pltpu.VMEM((2 * cases, LANES), f32),
@@ -739,18 +745,18 @@
         ],
         compiler_params=PARAMS,
         name="solve",
-    )(system, both, codes)
+    )(*system, both, codes)
 
     blocks = gathered(weighted)
     return pl.pallas_call(
         functools.partial(filter_kernel, sizes, counts),
         out_shape=jax.ShapeDtypeStruct((planes, rows, LANES), f32),
-        in_specs=[scalars] + [VMEM] * 2,
+        in_specs=[scalars] + [VMEM] * 3,
         out_specs=VMEM,
         scratch_shapes=[pltpu.VMEM((planes + 4, rows + 4, LANES), f32)],
         compiler_params=PARAMS,
         name="cone",
-    )(start, blocks, scale)
+    )(start, *blocks, scale)
 
 
 def solution(mesh):

time: 70 us -> 69.2 us (0.989)
  blocking collectives: 18.8 us -> 28.9 us
  waiting for transfers between devices: 12.6 us -> 5.1 us
  starting transfers between devices: 20.5 us -> 17.9 us
    all_to_all x1 -> x2, blocking collectives: 18.8 us -> 28.9 us  [gathered(): mine = lax.all_to_all(copies, ('gx', 'gy'), 0, 0, axis_index_groups=groups)]
    all_to_all x1 -> x0, waiting for transfers between devices: 9.53 us -> none  [gathered(): return lax.all_to_all(copies, ('gx', 'gy'), 0, 0)]
    all_to_all x1 -> x0, starting transfers between devices: 2.58 us -> none  [gathered(): return lax.all_to_all(copies, ('gx', 'gy'), 0, 0)]
    ppermute x3 -> x5, waiting for transfers between devices: 1.1 us -> 3.09 us  [swapped(): return lax.ppermute(value, 'gx', links(0, 1) + links(1, -1))]
    pallas_call x1, Pallas kernels: 4.7 us -> 3.98 us  [local(): pl.pallas_call(functools.partial(solve_kernel, sizes), out_shape=jax.Shap...]
    ppermute x3 -> x5, starting transfers between devices: 8.44 us -> 8.45 us  [swapped(): return lax.ppermute(value, 'gx', links(0, 1) + links(1, -1))]
  transfers between devices with their start and end apart: 10 -> 11, of which waited for: 4 -> 5; matrix products, arithmetic and copies ran while one was open for 0% -> 0% of each run, Pallas kernels for 1% -> 1%
where the time goes in v9:
time: 69.2 us; the launch traced here: 68.8 us
  blocking collectives  28.9 us (42%)
  starting transfers between devices  17.9 us (26%)
  Pallas kernels  15 us (22%)
  waiting for transfers between devices  5.1 us (7%)
  local copies, waits for them, and re-layouts  1.07 us (2%)
  other arithmetic  0.8 us (1%)
    all_to_all x2, blocking collectives, gathered(): mine = lax.all_to_all(copies, ('gx', 'gy'), 0, 0, axis_index_groups=groups)  28.9 us
    pallas_call x1, Pallas kernels, local(): pl.pallas_call(functools.partial(main_kernel, sizes), out_shape=[jax.Shap...  8.88 us
    ppermute x5, starting transfers between devices, swapped(): return lax.ppermute(value, 'gx', links(0, 1) + links(1, -1))  8.45 us
    ppermute x2, starting transfers between devices, moved(): return lax.ppermute(value, axis, pairs)  6.77 us
    pallas_call x1, Pallas kernels, local(): pl.pallas_call(functools.partial(solve_kernel, sizes), out_shape=jax.Shap...  3.98 us
    ppermute x5, waiting for transfers between devices, swapped(): return lax.ppermute(value, 'gx', links(0, 1) + links(1, -1))  3.09 us
    ppermute x2, waiting for transfers between devices, moved(): return lax.ppermute(value, axis, pairs)  2 us
  transfers between devices with their start and end apart: 11, of which 5 were waited for; matrix products, arithmetic and copies ran while one was open for 0% of the time, Pallas kernels for 1%

profile of v9, /device:TPU:0, one launch (start us, length us, event | category | flops | bytes accessed | tf_op | source)
XLA Modules:
  0.0 68.8 jit_solution(11818515770305022284)
XLA Ops:
  0.0 0.7 %negate_select_fusion.codes = f32[2,8,128]{2,1,0:T(8,128)S(1)} fusion(s32[2,8,128]{2,1,0:T(8,128)} %levels.1, s32[2,8,128]{2,1,0:T(8,128)} %param.5), kind=kLoop, calls=%fused_computation | loop fusion | flops 16384 | bytes 24576 | tf_op jit(solution)/shard_map/jit(_where)/select_n | solution.py:627
  0.7 0.0 copy-start
  0.7 1.1 %copy-done = f32[3,24,2,8,128]{4,3,2,1,0:T(8,128)S(1)} copy-done((f32[3,24,2,8,128]{4,3,2,1,0:T(8,128)S(1)}, f32[3,24,2,8,128]{4,3,2,1,0:T(8,128)}, u32[]{:S(2)}) %copy-start) | copy-done | bytes 589848
  1.8 0.1 pack.1
  1.9 0.5 collective-permute-start
  2.4 0.7 collective-permute-start.2
  3.1 0.7 collective-permute-start.1
  3.8 0.3 collective-permute-done.pair
  4.1 1.3 %collective-permute-start.4 = (f32[296,128]{1,0:T(8,128)S(1)}, f32[296,128]{1,0:T(8,128)S(1)}, u32[]{:S(2)}, u32[]{:S(2)}) collective-permute-start(f32[296,128]{1,0:T(8,128)S(1)} %get-tuple-element.20), channel_id=1, source_target_pairs={{1,0},{2,1},{3,2},{5,4},{6,5},{7,6},{9,8},{10,9},{11,10},{13,12},{... | collective-permute-start | bytes 454664 | tf_op jit(solution)/shard_map/ppermute | solution.py:656
  5.4 5.5 %collective-permute-start.3 = (f32[152,128]{1,0:T(8,128)S(1)}, f32[152,128]{1,0:T(8,128)S(1)}, u32[]{:S(2)}, u32[]{:S(2)}) collective-permute-start(f32[152,128]{1,0:T(8,128)S(1)} %get-tuple-element.19), channel_id=1, source_target_pairs={{0,1},{1,2},{2,3},{4,5},{5,6},{6,7},{8,9},{9,10},{10,11},{12,13},{... | collective-permute-start | bytes 233480 | tf_op jit(solution)/shard_map/ppermute | solution.py:656
  10.9 2.0 %collective-permute-done.3.ym = f32[152,128]{1,0:T(8,128)S(1)} collective-permute-done((f32[152,128]{1,0:T(8,128)S(1)}, f32[152,128]{1,0:T(8,128)S(1)}, u32[]{:S(2)}, u32[]{:S(2)}) %collective-permute-start.3) | collective-permute-done | bytes 77856 | tf_op jit(solution)/shard_map/ppermute | solution.py:656
  12.9 0.0 collective-permute-done.4.yp
  12.9 0.7 collective-permute-start.8
  13.6 4.0 %collective-permute-start.6 = (f32[296,128]{1,0:T(8,128)S(1)}, f32[296,128]{1,0:T(8,128)S(1)}, u32[]{:S(2)}, u32[]{:S(2)}) collective-permute-start(f32[296,128]{1,0:T(8,128)S(1)} %collective-permute-done.4.yp), channel_id=1, source_target_pairs={{0,4},{8,12},{16,20},{24,28},{4,0},{12,8},{20,16},{28,24},{1,5},{9... | collective-permute-start | bytes 454664 | tf_op jit(solution)/shard_map/ppermute | solution.py:662
  17.5 0.7 collective-permute-start.7
  18.2 0.0 collective-permute-done.1.lower
  18.2 4.0 %collective-permute-start.5 = (f32[152,128]{1,0:T(8,128)S(1)}, f32[152,128]{1,0:T(8,128)S(1)}, u32[]{:S(2)}, u32[]{:S(2)}) collective-permute-start(f32[152,128]{1,0:T(8,128)S(1)} %collective-permute-done.3.ym), channel_id=1, source_target_pairs={{0,4},{8,12},{16,20},{24,28},{4,0},{12,8},{20,16},{28,24},{1,5},{9... | collective-permute-start | bytes 233480 | tf_op jit(solution)/shard_map/ppermute | solution.py:662
  22.2 0.1 pad_add_fusion.first.start
  22.3 0.0 collective-permute-done.2.upper
  22.3 0.8 %collective-permute-done.5.ym_pair = f32[152,128]{1,0:T(8,128)S(1)} collective-permute-done((f32[152,128]{1,0:T(8,128)S(1)}, f32[152,128]{1,0:T(8,128)S(1)}, u32[]{:S(2)}, u32[]{:S(2)}) %collective-permute-start.5) | collective-permute-done | bytes 77856 | tf_op jit(solution)/shard_map/ppermute | solution.py:662
  23.1 0.0 collective-permute-done.7.corner_low
  23.1 0.0 collective-permute-done.6.yp_pair
  23.1 0.0 collective-permute-done.8.corner_high
  23.1 8.9 %operator.1 = (bf16[96,10368]{1,0:T(8,128)(2,1)S(1)}, f32[16,3,4,128]{3,2,1,0:T(4,128)S(1)}) custom-call(s32[2]{0:T(128)S(1)} %pad_add_fusion.first.start, f32[1168,128]{1,0:T(8,128)S(1)} %get-tuple-element.16.own, f32[1168,128]{1,0:T(8,128)S(1)} %collective-permute-done.pair, f32[592,128]{1,0:T(8,128)S(1)} %collective-permute-done.1.lower, ...), custom_call_target="tpu_custom_call" | custom-call | tf_op jit(solution)/shard_map/operator/pallas_call | solution.py:697
  32.0 0.0 copy-start.1
  32.0 18.0 %all_to_all.10.system = f32[16,3,4,128]{3,2,1,0:T(4,128)S(1)} all-to-all(f32[16,3,4,128]{3,2,1,0:T(4,128)S(1)} %get-tuple-element.23), channel_id=1, replica_groups={{0,1,2,3,8,9,10,11,16,17,18,19,24,25,26,27},{4,5,6,7,12,13,14,15,20,21,..., dimensions={0} | all-to-all | bytes 196608 | tf_op jit(solution)/shard_map/all_to_all | solution.py:728
  50.0 0.0 collective-permute-start.9
  50.0 1.3 %collective-permute-done.9.system_pair = f32[16,3,4,128]{3,2,1,0:T(4,128)S(1)} collective-permute-done((f32[16,3,4,128]{3,2,1,0:T(4,128)S(1)}, f32[16,3,4,128]{3,2,1,0:T(4,128)S(1)}, u32[]{:S(2)}, u32[]{:S(2)}) %collective-permute-start.9) | collective-permute-done | bytes 98336 | tf_op jit(solution)/shard_map/ppermute | solution.py:662
  51.3 4.0 %solve.1 = f32[16,2,8,128]{3,2,1,0:T(8,128)S(1)} custom-call(f32[16,3,4,128]{3,2,1,0:T(4,128)S(1)} %all_to_all.10.system, f32[16,3,4,128]{3,2,1,0:T(4,128)S(1)} %collective-permute-done.9.system_pair, bf16[96,10368]{1,0:T(8,128)(2,1)S(1)} %get-tuple-element.24.both, f32[2,8,128]{2,1,0:T(8,128)S(1)} %negate_select_fusion.codes), custom_call_target="tpu_custom_call" | custom-call | tf_op jit(solution)/shard_map/solve/pallas_call | solution.py:733
  55.3 10.9 %all_to_all.11.blocks = f32[16,2,8,128]{3,2,1,0:T(8,128)S(1)} all-to-all(f32[16,2,8,128]{3,2,1,0:T(8,128)S(1)} %solve.1), channel_id=1, replica_groups={{0,1,2,3,8,9,10,11,16,17,18,19,24,25,26,27},{4,5,6,7,12,13,14,15,20,21,..., dimensions={0} | all-to-all | bytes 262144 | tf_op jit(solution)/shard_map/all_to_all | solution.py:728
  66.2 0.0 collective-permute-start.10
  66.2 0.0 copy-done.1
  66.2 0.7 scale.1
  66.9 0.7 collective-permute-done.10.blocks_pair
  67.5 1.3 %cone.1 = f32[2,8,128]{2,1,0:T(8,128)} custom-call(s32[2]{0:T(128)S(1)} %pad_add_fusion.first.start, f32[16,2,8,128]{3,2,1,0:T(8,128)S(1)} %all_to_all.11.blocks, f32[16,2,8,128]{3,2,1,0:T(8,128)S(1)} %collective-permute-done.10.blocks_pair, f32[2,8,128]{2,1,0:T(8,128)S(1)} %scale.1), custom_call_target="tpu_custom_call" | custom-call | tf_op jit(solution)/shard_map/cone/pallas_call | solution.py:751
  (2 shorter events, 0.0 us)
Async XLA Ops:
  0.7 1.1 %copy-start = (f32[3,24,2,8,128]{4,3,2,1,0:T(8,128)S(1)}, f32[3,24,2,8,128]{4,3,2,1,0:T(8,128)}, u32[]{:S(2)}) copy-start(f32[3,24,2,8,128]{4,3,2,1,0:T(8,128)} %forces.1) | copy-start | bytes 1769476
  1.9 2.2 %collective-permute-start = (f32[1168,128]{1,0:T(8,128)S(1)}, f32[1168,128]{1,0:T(8,128)S(1)}, u32[]{:S(2)}, u32[]{:S(2)}) collective-permute-start(f32[1168,128]{1,0:T(8,128)S(1)} %get-tuple-element.16.own), channel_id=1, source_target_pairs={{0,4},{8,12},{16,20},{24,28},{4,0},{12,8},{20,16},{28,24},{1,5},{9... | collective-permute-start | bytes 1794056 | tf_op jit(solution)/shard_map/ppermute | solution.py:662
  2.4 19.8 %collective-permute-start.2 = (f32[1168,128]{1,0:T(8,128)S(1)}, f32[1168,128]{1,0:T(8,128)S(1)}, u32[]{:S(2)}, u32[]{:S(2)}) collective-permute-start(f32[1168,128]{1,0:T(8,128)S(1)} %get-tuple-element.16.own), channel_id=1, source_target_pairs={{8,4},{16,12},{24,20},{9,5},{17,13},{25,21},{10,6},{18,14},{26,22}... | collective-permute-start | bytes 1794056 | tf_op jit(solution)/shard_map/ppermute | solution.py:664
  3.1 15.1 %collective-permute-start.1 = (f32[592,128]{1,0:T(8,128)S(1)}, f32[592,128]{1,0:T(8,128)S(1)}, u32[]{:S(2)}, u32[]{:S(2)}) collective-permute-start(f32[592,128]{1,0:T(8,128)S(1)} %get-tuple-element.18), channel_id=1, source_target_pairs={{4,8},{12,16},{20,24},{5,9},{13,17},{21,25},{6,10},{14,18},{22,26}... | collective-permute-start | bytes 909320 | tf_op jit(solution)/shard_map/ppermute | solution.py:665
  4.1 8.8 %collective-permute-start.4 = (f32[296,128]{1,0:T(8,128)S(1)}, f32[296,128]{1,0:T(8,128)S(1)}, u32[]{:S(2)}, u32[]{:S(2)}) collective-permute-start(f32[296,128]{1,0:T(8,128)S(1)} %get-tuple-element.20), channel_id=1, source_target_pairs={{1,0},{2,1},{3,2},{5,4},{6,5},{7,6},{9,8},{10,9},{11,10},{13,12},{... | collective-permute-start | bytes 454664 | tf_op jit(solution)/shard_map/ppermute | solution.py:656
  5.4 7.5 %collective-permute-start.3 = (f32[152,128]{1,0:T(8,128)S(1)}, f32[152,128]{1,0:T(8,128)S(1)}, u32[]{:S(2)}, u32[]{:S(2)}) collective-permute-start(f32[152,128]{1,0:T(8,128)S(1)} %get-tuple-element.19), channel_id=1, source_target_pairs={{0,1},{1,2},{2,3},{4,5},{5,6},{6,7},{8,9},{9,10},{10,11},{12,13},{... | collective-permute-start | bytes 233480 | tf_op jit(solution)/shard_map/ppermute | solution.py:656
  12.9 10.2 %collective-permute-start.8 = (f32[448,128]{1,0:T(8,128)S(1)}, f32[448,128]{1,0:T(8,128)S(1)}, u32[]{:S(2)}, u32[]{:S(2)}) collective-permute-start(f32[448,128]{1,0:T(8,128)S(1)} %get-tuple-element.22), channel_id=1, source_target_pairs={{8,4},{16,12},{24,20},{9,5},{17,13},{25,21},{10,6},{18,14},{26,22}... | collective-permute-start | bytes 688136 | tf_op jit(solution)/shard_map/ppermute | solution.py:689
  13.6 9.5 %collective-permute-start.6 = (f32[296,128]{1,0:T(8,128)S(1)}, f32[296,128]{1,0:T(8,128)S(1)}, u32[]{:S(2)}, u32[]{:S(2)}) collective-permute-start(f32[296,128]{1,0:T(8,128)S(1)} %collective-permute-done.4.yp), channel_id=1, source_target_pairs={{0,4},{8,12},{16,20},{24,28},{4,0},{12,8},{20,16},{28,24},{1,5},{9... | collective-permute-start | bytes 454664 | tf_op jit(solution)/shard_map/ppermute | solution.py:662
  17.5 5.6 %collective-permute-start.7 = (f32[232,128]{1,0:T(8,128)S(1)}, f32[232,128]{1,0:T(8,128)S(1)}, u32[]{:S(2)}, u32[]{:S(2)}) collective-permute-start(f32[232,128]{1,0:T(8,128)S(1)} %get-tuple-element.21), channel_id=1, source_target_pairs={{4,8},{12,16},{20,24},{5,9},{13,17},{21,25},{6,10},{14,18},{22,26}... | collective-permute-start | bytes 356360 | tf_op jit(solution)/shard_map/ppermute | solution.py:690
  18.2 4.9 %collective-permute-start.5 = (f32[152,128]{1,0:T(8,128)S(1)}, f32[152,128]{1,0:T(8,128)S(1)}, u32[]{:S(2)}, u32[]{:S(2)}) collective-permute-start(f32[152,128]{1,0:T(8,128)S(1)} %collective-permute-done.3.ym), channel_id=1, source_target_pairs={{0,4},{8,12},{16,20},{24,28},{4,0},{12,8},{20,16},{28,24},{1,5},{9... | collective-permute-start | bytes 233480 | tf_op jit(solution)/shard_map/ppermute | solution.py:662
  32.0 34.2 %copy-start.1 = (s32[2,8,128]{2,1,0:T(8,128)S(1)}, s32[2,8,128]{2,1,0:T(8,128)}, u32[]{:S(2)}) copy-start(s32[2,8,128]{2,1,0:T(8,128)} %levels.1) | copy-start | bytes 24580
  50.0 1.3 %collective-permute-start.9 = (f32[16,3,4,128]{3,2,1,0:T(4,128)S(1)}, f32[16,3,4,128]{3,2,1,0:T(4,128)S(1)}, u32[]{:S(2)}, u32[]{:S(2)}) collective-permute-start(f32[16,3,4,128]{3,2,1,0:T(4,128)S(1)} %all_to_all.10.system), channel_id=1, source_target_pairs={{0,4},{8,12},{16,20},{24,28},{4,0},{12,8},{20,16},{28,24},{1,5},{9... | collective-permute-start | bytes 294920 | tf_op jit(solution)/shard_map/ppermute | solution.py:662
  66.2 1.3 %collective-permute-start.10 = (f32[16,2,8,128]{3,2,1,0:T(8,128)S(1)}, f32[16,2,8,128]{3,2,1,0:T(8,128)S(1)}, u32[]{:S(2)}, u32[]{:S(2)}) collective-permute-start(f32[16,2,8,128]{3,2,1,0:T(8,128)S(1)} %all_to_all.11.blocks), channel_id=1, source_target_pairs={{0,4},{8,12},{16,20},{24,28},{4,0},{12,8},{20,16},{28,24},{1,5},{9... | collective-permute-start | bytes 393224 | tf_op jit(solution)/shard_map/ppermute | solution.py:662

commit v10 on v9

--- a/solution.py
+++ b/solution.py
@@ -250,128 +250,216 @@
             line += 8
 
 
-def readers(sizes, first, own, pair, lower, upper, y_own, y_pair, corner_low, corner_high):
-    planes, rows, cases = sizes
-    block = 3 * cases
-    even = first // planes % 2 == 0
-
-    def lines(ref, start, count):
-        return ref[start : start + count, :]
-
-    def inside(ref, x, y):
-        return lines(ref, (x * rows + y) * block, block)
-
-    def beyond(refs, slot, y):
-        below, above = refs
-        if y < 0:
-            return lines(below, slot * block, block)
-        return lines(above, (slot * 2 + y - rows) * block, block)
-
-    def corner(ref, count, slot, y):
-        if y < 0:
-            return lines(ref, slot * block, block)
-        return lines(ref, count * block + 8 + (slot * 2 + y - rows) * block, block)
-
-    def corner_codes(ref, count, slot, y):
-        start = count * block if y < 0 else 3 * count * block + 8
-        return lines(ref, start + slot * 2, 2)
-
-    def load(x, y):
-        in_y = 0 <= y < rows
-        if 0 <= x < planes:
-            return inside(own, x, y) if in_y else beyond(y_own, x, y)
-        if x < 0:
-            if in_y:
-                return jnp.where(even, inside(lower, 0, y), inside(pair, planes - 1, y))
-            return jnp.where(even, corner(corner_low, 1, 0, y), beyond(y_pair, planes - 1, y))
-        if in_y:
-            return jnp.where(even, inside(pair, x - planes, y), inside(upper, x - planes, y))
-        other = corner(corner_high, 2, x - planes, y)
-        return jnp.where(even, beyond(y_pair, x - planes, y), other)
-
-    def inside_codes(ref, x):
-        return lines(ref, planes * rows * block + x * rows, rows)
-
-    def beyond_codes(refs, slots, slot, y):
-        below, above = refs
-        if y < 0:
-            return lines(below, slots * block + slot * 2, 2)
-        return lines(above, slots * 2 * block + slot * 2, 2)
-
-    def codes(x, y):
-        if 0 <= x < planes:
-            return inside_codes(own, x) if y == 0 else beyond_codes(y_own, planes, x, y)
-        if x < 0:
-            slot = x + 2
-            if y == 0:
-                other = inside_codes(pair, planes + x)
-                return jnp.where(even, lines(lower, (block + slot) * rows, rows), other)
-            other = beyond_codes(y_pair, planes, planes + x, y)
-            return jnp.where(even, corner_codes(corner_low, 1, slot, y), other)
-        slot = x - planes
-        if y == 0:
-            other = lines(upper, (2 * block + slot) * rows, rows)
-            return jnp.where(even, inside_codes(pair, slot), other)
-        other = corner_codes(corner_high, 2, slot, y)
-        return jnp.where(even, beyond_codes(y_pair, planes, slot, y), other)
-
-    return load, codes
-
-
-def main_kernel(
-    sizes, first, own, pair, lower, upper, ym, yp, ym_pair, yp_pair, corner_low, corner_high,
-    both_out, system_out, stiff_ref, inverse,
-    start, sums, diffs, acc_s, acc_d, w_sums, w_diffs, acc2_s, acc2_d, right, table,
-):
-    planes, rows, cases = sizes
-    block = 3 * cases
-    xs, ys = planes + 3, rows + 3
-    load, signed = readers(
-        sizes, first[0], own, pair, lower, upper,
-        (ym, yp), (ym_pair, yp_pair), corner_low, corner_high,
-    )
-    for x in range(-2, planes + 2):
-        for y, count in ((-2, 2), (0, rows), (rows, 2)):
-            stiff_ref[x + 2, y + 2 : y + 2 + count, :] = signed(x, y)
-    for x in range(-1, planes + 2):
-        codes = stiff_ref[x + 2, 0 : ys + 1, :]
-        total = jnp.abs(stiff_ref[x + 1, 0 : ys + 1, :]) + jnp.abs(codes)
+def lines(ref, start, count):
+    return ref[start : start + count, :]
+
+
+def inside(ref, x, y, rows, block):
+    return lines(ref, (x * rows + y) * block, block)
+
+
+def beyond(refs, slot, y, rows, block):
+    below, above = refs
+    if y < 0:
+        return lines(below, slot * block, block)
+    return lines(above, (slot * 2 + y - rows) * block, block)
+
+
+def beyond_codes(refs, slots, slot, y, block):
+    below, above = refs
+    if y < 0:
+        return lines(below, slots * block + slot * 2, 2)
+    return lines(above, slots * 2 * block + slot * 2, 2)
+
+
+def corner(ref, count, slot, y, rows, block):
+    if y < 0:
+        return lines(ref, slot * block, block)
+    return lines(ref, count * block + 8 + (slot * 2 + y - rows) * block, block)
+
+
+def corner_codes(ref, count, slot, y, block):
+    start = count * block if y < 0 else 3 * count * block + 8
+    return lines(ref, start + slot * 2, 2)
+
+
+def node_inverse(signed, count, out):
+    planes = signed.shape[0]
+    for x in range(1, planes):
+        codes = signed[x, 0 : count + 1, :]
+        total = jnp.abs(signed[x - 1, 0 : count + 1, :]) + jnp.abs(codes)
         total = total[:-1] + total[1:]
         total = total + shift_up(total)
         free = codes[1:] > 0.0
         value = 1.0 / (DIAGONAL * jnp.where(free, total, 1.0))
-        inverse[x + 1, 0:ys, :] = jnp.where(free, value, 0.0)
-    for x in range(planes + 4):
-        stiff_ref[x] = jnp.abs(stiff_ref[x])
-
-    for x in range(-1, planes + 2):
+        out[x - 1, 0:count, :] = jnp.where(free, value, 0.0)
+    for x in range(planes):
+        signed[x] = jnp.abs(signed[x])
+
+
+def place_column(sums, diffs, column, value):
+    moved = shift_down(value)
+    sums[column] = value + moved
+    diffs[column] = moved - value
+
+
+def early_kernel(
+    sizes, first, own, pair, ym, yp, ym_pair, yp_pair, start, sums, diffs, acc_s, acc_d,
+    stiff_ref, inverse,
+):
+    planes, rows, cases = sizes
+    block = 3 * cases
+    ys = rows + 3
+    even = first[0] // planes % 2 == 0
+    y_own, y_pair = (ym, yp), (ym_pair, yp_pair)
+
+    def both_ways(w, read):
+        low = read(True, w + 1) if w + 1 < planes else read(False, w + 1 - planes)
+        high = read(False, planes + w - 1) if w < 1 else read(True, w - 1)
+        return jnp.where(even, low, high)
+
+    def codes(w, y):
+        def read(mine, x):
+            if y == 0:
+                return lines(own if mine else pair, (planes * block + x) * rows, rows)
+            return beyond_codes(y_own if mine else y_pair, planes, x, y, block)
+
+        return both_ways(w, read)
+
+    for w in range(-1, planes + 1):
+        for y, count in ((-2, 2), (0, rows), (rows, 2)):
+            stiff_ref[w + 1, y + 2 : y + 2 + count, :] = codes(w, y)
+    node_inverse(stiff_ref, ys, inverse)
+    for w in range(planes + 1):
         for y in range(-1, rows + 2):
-            value = load(x, y) * inverse[x + 1, y + 1 : y + 2, :]
-            column = (x + 1) * ys + y + 1
+
+            def read(mine, x):
+                if 0 <= y < rows:
+                    return inside(own if mine else pair, x, y, rows, block)
+                return beyond(y_own if mine else y_pair, x, y, rows, block)
+
+            value = both_ways(w, read) * inverse[w, y + 1 : y + 2, :]
+            column = w * ys + y + 1
             start[column] = value
-            moved = shift_down(value)
-            sums[column] = value + moved
-            diffs[column] = moved - value
+            place_column(sums, diffs, column, value)
+    for column in range(rows + 1):
+        acc_s[column] = jnp.zeros((block, LANES), f32)
+        acc_d[column] = jnp.zeros((block, LANES), f32)
+    apply_elements(sums, diffs, stiff_ref, acc_s, acc_d, planes, rows + 2, 1, 1, 1, cases)
+
+
+def main_kernel(
+    sizes, first, own, pair, lower, upper, ym, yp, ym_pair, yp_pair, corner_low, corner_high,
+    start, sums_e, diffs_e, acc_se, acc_de,
+    both_out, system_out, stiff_ref, inverse,
+    middle, sums, diffs, acc_s, acc_d, w_sums, w_diffs, acc2_s, acc2_d, right, table,
+):
+    planes, rows, cases = sizes
+    block = 3 * cases
+    ys = rows + 3
+    even = first[0] // planes % 2 == 0
+    y_own, y_pair = (ym, yp), (ym_pair, yp_pair)
+
+    def codes(x, y):
+        def read(mine, plane):
+            if y == 0:
+                return lines(own if mine else pair, (planes * block + plane) * rows, rows)
+            return beyond_codes(y_own if mine else y_pair, planes, plane, y, block)
+
+        if 0 <= x < planes:
+            return read(True, x)
+        ref, count, slot = (lower, 1, x + 2) if x < 0 else (upper, 2, x - planes)
+        if y == 0:
+            outer = lines(ref, (count * block + slot) * rows, rows)
+        else:
+            outer = corner_codes(corner_low if x < 0 else corner_high, count, slot, y, block)
+        inner = read(False, planes + x if x < 0 else x - planes)
+        return jnp.where(even, outer, inner) if x < 0 else jnp.where(even, inner, outer)
+
+    for x in range(-2, planes + 2):
+        for y, count in ((-2, 2), (0, rows), (rows, 2)):
+            stiff_ref[x + 2, y + 2 : y + 2 + count, :] = codes(x, y)
+    node_inverse(stiff_ref, ys, inverse)
+
+    def place(v, x, read):
+        for y in range(-1, rows + 2):
+            value = read(y) * inverse[x + 1, y + 1 : y + 2, :]
+            if v == 1:
+                middle[y + 1] = value
+            place_column(sums, diffs, v * ys + y + 1, value)
+
+    def copy(v, w):
+        for y in range(ys):
+            sums[v * ys + y] = sums_e[w * ys + y]
+            diffs[v * ys + y] = diffs_e[w * ys + y]
+
+    @pl.when(even)
+    def _():
+        def outer(y):
+            if 0 <= y < rows:
+                return inside(lower, 0, y, rows, block)
+            return corner(corner_low, 1, 0, y, rows, block)
+
+        def inner(y):
+            if 0 <= y < rows:
+                return inside(own, 0, y, rows, block)
+            return beyond(y_own, 0, y, rows, block)
+
+        place(0, -1, outer)
+        place(1, 0, inner)
+        copy(2, 0)
+
+    @pl.when(jnp.logical_not(even))
+    def _():
+        def outer(slot):
+            def read(y):
+                if 0 <= y < rows:
+                    return inside(upper, slot, y, rows, block)
+                return corner(corner_high, 2, slot, y, rows, block)
+
+            return read
+
+        copy(0, planes)
+        place(1, planes, outer(0))
+        place(2, planes + 1, outer(1))
 
     nodes_y = rows + 1
-    apply_elements(
-        sums, diffs, stiff_ref, acc_s, acc_d, planes + 2, rows + 2, 1, 1, 1, cases
-    )
+    for column in range(nodes_y):
+        acc_s[column] = jnp.zeros((block, LANES), f32)
+        acc_d[column] = jnp.zeros((block, LANES), f32)
+    layer = jnp.where(even, 1, planes + 1)
+    apply_elements(sums, diffs, stiff_ref, acc_s, acc_d, 2, rows + 2, 1, layer, 1, cases)
+
+    def total(x, y, early, main):
+        low = ([x - 1] if x >= 1 else [], [x + 1] if x <= 1 else [])
+        high = ([x + 1] if x < planes else [], [x - planes + 1] if x >= planes - 1 else [])
+        if low[0] and low[1] and high[0] and high[1]:
+            one = early[jnp.where(even, low[0][0], high[0][0]) * nodes_y + y]
+            return one + main[jnp.where(even, low[1][0], high[1][0]) * nodes_y + y]
+
+        def read(places):
+            found = [early[w * nodes_y + y] for w in places[0]]
+            found += [main[v * nodes_y + y] for v in places[1]]
+            return found[0] if len(found) == 1 else found[0] + found[1]
+
+        return jnp.where(even, read(low), read(high))
 
     def image(x, y, place):
-        column = (x + 1) * nodes_y + y
-        s, d = acc_s[column], acc_d[column]
+        s, d = total(x, y, acc_se, acc_s), total(x, y, acc_de, acc_d)
         force = s - d + shift_up(s + d)
         scaled = force * inverse[x + 1, pl.ds(y + 1, 1), :]
-        moved = shift_down(scaled)
-        w_sums[x * nodes_y + y] = scaled + moved
-        w_diffs[x * nodes_y + y] = moved - scaled
-        value = start[(x + 1) * ys + y + 1]
+        place_column(w_sums, w_diffs, x * nodes_y + y, scaled)
+        if x == 0:
+            value = jnp.where(even, middle[y + 1], start[ys + y + 1])
+        elif x == planes:
+            value = jnp.where(even, start[(planes - 1) * ys + y + 1], middle[y + 1])
+        else:
+            value = start[jnp.where(even, x - 1, x + 1) * ys + y + 1]
         for k in range(3):
             lines = slice(k * cases, (k + 1) * cases)
-            pair = jnp.concatenate([value[lines], scaled[lines]], 0)
+            both = jnp.concatenate([value[lines], scaled[lines]], 0)
             lane = pl.ds(pl.multiple_of((place * 3 + k) * LANES, LANES), LANES)
-            high, rest = split(pair)
+            high, rest = split(both)
             both_out[0 : 2 * cases, lane] = high
             both_out[2 * cases : 4 * cases, lane] = rest
         return force
@@ -379,22 +467,24 @@
     two = 2 * cases
     count = planes * rows
 
-    def inside(index):
-        force = image(index // rows, index % rows, index)
+    def within(x, y):
+        index = x * rows + y
+        force = image(x, y, index)
         given = own[pl.ds(pl.multiple_of(index * block, 8), block), :]
         for k in range(3):
             lines = slice(k * cases, (k + 1) * cases)
-            pair = jnp.concatenate([given[lines], force[lines]], 0)
+            both = jnp.concatenate([given[lines], force[lines]], 0)
             lane = pl.ds(pl.multiple_of((index * 3 + k) * LANES, LANES), LANES)
-            high, rest = split(pair)
+            high, rest = split(both)
             right[0:two, lane] = high
             right[two : 2 * two, lane] = rest
 
-    unrolled(count, 4, inside)
-    unrolled(planes, 2, lambda x: image(x, rows, count + x))
+    for x in range(planes):
+        unrolled(rows, 4, functools.partial(within, x))
+        image(x, rows, count + x)
     unrolled(nodes_y, 3, lambda y: image(planes, y, count + planes + y))
-    beyond = right.shape[1] - count * 3 * LANES
-    right[0 : 2 * two, count * 3 * LANES :] = jnp.zeros((2 * two, beyond), bf16)
+    rest = right.shape[1] - count * 3 * LANES
+    right[0 : 2 * two, count * 3 * LANES :] = jnp.zeros((2 * two, rest), bf16)
 
     for column in range(nodes_y):
         acc2_s[column] = jnp.zeros((block, LANES), f32)
@@ -691,8 +781,26 @@
 
     devices = count_x * count_y
     nodes = (planes + 1) * (rows + 1)
-    wide = (planes + 3) * (rows + 3)
-    acc = pltpu.VMEM(((planes + 3) * (rows + 1), block, LANES), f32)
+    window = jax.ShapeDtypeStruct(((planes + 1) * (rows + 3), block, LANES), f32)
+    partial_forces = jax.ShapeDtypeStruct((nodes, block, LANES), f32)
+    early = pl.pallas_call(
+        functools.partial(early_kernel, sizes),
+        out_shape=[window] * 3 + [partial_forces] * 2,
+        in_specs=[scalars] + [VMEM] * 6,
+        out_specs=[VMEM] * 5,
+        scratch_shapes=[
+            pltpu.VMEM((planes + 2, up8(rows + 4), LANES), f32),
+            pltpu.VMEM((planes + 1, up8(rows + 3), LANES), f32),
+        ],
+        compiler_params=PARAMS,
+        cost_estimate=pl.CostEstimate(
+            flops=200 * planes * rows * block * LANES, bytes_accessed=2**23, transcendentals=0
+        ),
+        name="early",
+    )(start, own, pair, from_ym, from_yp, pair_ym, pair_yp)
+
+    side = pltpu.VMEM((3 * (rows + 3), block, LANES), f32)
+    acc = pltpu.VMEM((3 * (rows + 1), block, LANES), f32)
     field = pltpu.VMEM((nodes, block, LANES), f32)
     both, system = pl.pallas_call(
         functools.partial(main_kernel, sizes),
@@ -700,23 +808,21 @@
             jax.ShapeDtypeStruct((4 * cases, nodes * 3 * LANES), bf16),
             jax.ShapeDtypeStruct((devices // 2, cases // 8, 4, LANES), f32),
         ],
-        in_specs=[scalars] + [VMEM] * 10,
+        in_specs=[scalars] + [VMEM] * 15,
         out_specs=[VMEM] * 2,
         scratch_shapes=[
             pltpu.VMEM((planes + 4, up8(rows + 4), LANES), f32),
             pltpu.VMEM((planes + 3, up8(rows + 3), LANES), f32),
-            pltpu.VMEM((wide, block, LANES), f32),
-            pltpu.VMEM((wide, block, LANES), f32),
-            pltpu.VMEM((wide, block, LANES), f32),
-            acc, acc, field, field, field, field,
+            pltpu.VMEM((rows + 3, block, LANES), f32),
+            side, side, acc, acc, field, field, field, field,
             pltpu.VMEM((6 * cases, nodes * 3 * LANES), bf16),
             pltpu.VMEM((cases, LANES), f32),
         ],
         compiler_params=PARAMS,
         name="operator",
     )(
-        start, own, pair, lower, upper, from_ym, from_yp,
-        pair_ym, pair_yp, corner_low, corner_high,
+        start, own, pair, lower, upper, from_ym, from_yp, pair_ym, pair_yp,
+        corner_low, corner_high, *early,
     )
 
     groups = [

time: 69.2 us -> 67.6 us (0.977)
  starting transfers between devices: 17.9 us -> 12.6 us
  blocking collectives: 28.9 us -> 30.6 us
  Pallas kernels: 15 us -> 16.6 us
    ppermute x5, starting transfers between devices: 8.45 us -> 3.14 us  [swapped(): return lax.ppermute(value, 'gx', links(0, 1) + links(1, -1))]
    pallas_call x0 -> x1, Pallas kernels: none -> 2.38 us  [local(): pl.pallas_call(functools.partial(early_kernel, sizes), out_shape=[window]...]
    all_to_all x2, blocking collectives: 28.9 us -> 30.6 us  [gathered(): mine = lax.all_to_all(copies, ('gx', 'gy'), 0, 0, axis_index_groups=groups)]
    pallas_call x1, Pallas kernels: 8.88 us -> 7.49 us  [local(): pl.pallas_call(functools.partial(main_kernel, sizes), out_shape=[jax.Shap...]
  transfers between devices with their start and end apart: 11 -> 11, of which waited for: 5 -> 6; matrix products, arithmetic and copies ran while one was open for 0% -> 0% of each run, Pallas kernels for 1% -> 6%
where the time goes in v10:
time: 67.6 us; the launch traced here: 67.2 us
  blocking collectives  30.6 us (45%)
  Pallas kernels  16.6 us (25%)
  starting transfers between devices  12.6 us (19%)
  waiting for transfers between devices  5.39 us (8%)
  local copies, waits for them, and re-layouts  1.07 us (2%)
  other arithmetic  0.8 us (1%)
    all_to_all x2, blocking collectives, gathered(): mine = lax.all_to_all(copies, ('gx', 'gy'), 0, 0, axis_index_groups=groups)  30.6 us
    pallas_call x1, Pallas kernels, local(): pl.pallas_call(functools.partial(main_kernel, sizes), out_shape=[jax.Shap...  7.49 us
    ppermute x2, starting transfers between devices, moved(): return lax.ppermute(value, axis, pairs)  6.77 us
    pallas_call x1, Pallas kernels, local(): pl.pallas_call(functools.partial(solve_kernel, sizes), out_shape=jax.Shap...  3.98 us
    ppermute x5, waiting for transfers between devices, swapped(): return lax.ppermute(value, 'gx', links(0, 1) + links(1, -1))  3.77 us
    ppermute x5, starting transfers between devices, swapped(): return lax.ppermute(value, 'gx', links(0, 1) + links(1, -1))  3.14 us
    pallas_call x1, Pallas kernels, local(): pl.pallas_call(functools.partial(early_kernel, sizes), out_shape=[window]...  2.38 us
    ppermute x2, waiting for transfers between devices, moved(): return lax.ppermute(value, axis, pairs)  1.6 us
  transfers between devices with their start and end apart: 11, of which 6 were waited for; matrix products, arithmetic and copies ran while one was open for 0% of the time, Pallas kernels for 6%

profile of v10, /device:TPU:0, one launch (start us, length us, event | category | flops | bytes accessed | tf_op | source)
XLA Modules:
  0.0 67.2 jit_solution(1587293143530218804)
XLA Ops:
  0.0 0.7 %negate_select_fusion.codes = f32[2,8,128]{2,1,0:T(8,128)S(1)} fusion(s32[2,8,128]{2,1,0:T(8,128)} %levels.1, s32[2,8,128]{2,1,0:T(8,128)} %param.5), kind=kLoop, calls=%fused_computation | loop fusion | flops 16384 | bytes 24576 | tf_op jit(solution)/shard_map/jit(_where)/select_n | solution.py:717
  0.7 0.0 copy-start
  0.7 1.1 %copy-done = f32[3,24,2,8,128]{4,3,2,1,0:T(8,128)S(1)} copy-done((f32[3,24,2,8,128]{4,3,2,1,0:T(8,128)S(1)}, f32[3,24,2,8,128]{4,3,2,1,0:T(8,128)}, u32[]{:S(2)}) %copy-start) | copy-done | bytes 589848
  1.8 0.1 pack.1
  1.9 0.5 collective-permute-start
  2.4 0.7 %collective-permute-start.2 = (f32[1168,128]{1,0:T(8,128)S(1)}, f32[1168,128]{1,0:T(8,128)S(1)}, u32[]{:S(2)}, u32[]{:S(2)}) collective-permute-start(f32[1168,128]{1,0:T(8,128)S(1)} %get-tuple-element.21.own), channel_id=1, source_target_pairs={{8,4},{16,12},{24,20},{9,5},{17,13},{25,21},{10,6},{18,14},{26,22}... | collective-permute-start | bytes 1794056 | tf_op jit(solution)/shard_map/ppermute | solution.py:754
  3.1 0.9 %collective-permute-done.pair = f32[1168,128]{1,0:T(8,128)S(1)} collective-permute-done((f32[1168,128]{1,0:T(8,128)S(1)}, f32[1168,128]{1,0:T(8,128)S(1)}, u32[]{:S(2)}, u32[]{:S(2)}) %collective-permute-start) | collective-permute-done | bytes 598048 | tf_op jit(solution)/shard_map/ppermute | solution.py:752
  4.1 1.3 %collective-permute-start.4 = (f32[296,128]{1,0:T(8,128)S(1)}, f32[296,128]{1,0:T(8,128)S(1)}, u32[]{:S(2)}, u32[]{:S(2)}) collective-permute-start(f32[296,128]{1,0:T(8,128)S(1)} %get-tuple-element.25), channel_id=1, source_target_pairs={{1,0},{2,1},{3,2},{5,4},{6,5},{7,6},{9,8},{10,9},{11,10},{13,12},{... | collective-permute-start | bytes 454664 | tf_op jit(solution)/shard_map/ppermute | solution.py:746
  5.4 5.5 %collective-permute-start.3 = (f32[152,128]{1,0:T(8,128)S(1)}, f32[152,128]{1,0:T(8,128)S(1)}, u32[]{:S(2)}, u32[]{:S(2)}) collective-permute-start(f32[152,128]{1,0:T(8,128)S(1)} %get-tuple-element.24), channel_id=1, source_target_pairs={{0,1},{1,2},{2,3},{4,5},{5,6},{6,7},{8,9},{9,10},{10,11},{12,13},{... | collective-permute-start | bytes 233480 | tf_op jit(solution)/shard_map/ppermute | solution.py:746
  10.9 0.7 %collective-permute-start.1 = (f32[592,128]{1,0:T(8,128)S(1)}, f32[592,128]{1,0:T(8,128)S(1)}, u32[]{:S(2)}, u32[]{:S(2)}) collective-permute-start(f32[592,128]{1,0:T(8,128)S(1)} %get-tuple-element.23), channel_id=1, source_target_pairs={{4,8},{12,16},{20,24},{5,9},{13,17},{21,25},{6,10},{14,18},{22,26}... | collective-permute-start | bytes 909320 | tf_op jit(solution)/shard_map/ppermute | solution.py:755
  11.6 1.3 %collective-permute-done.3.ym = f32[152,128]{1,0:T(8,128)S(1)} collective-permute-done((f32[152,128]{1,0:T(8,128)S(1)}, f32[152,128]{1,0:T(8,128)S(1)}, u32[]{:S(2)}, u32[]{:S(2)}) %collective-permute-start.3) | collective-permute-done | bytes 77856 | tf_op jit(solution)/shard_map/ppermute | solution.py:746
  12.9 0.3 collective-permute-done.4.yp
  13.2 0.7 %corners.1 = (f32[448,128]{1,0:T(8,128)S(1)}, f32[232,128]{1,0:T(8,128)}) custom-call(f32[152,128]{1,0:T(8,128)S(1)} %collective-permute-done.3.ym, f32[296,128]{1,0:T(8,128)S(1)} %collective-permute-done.4.yp), custom_call_target="tpu_custom_call" | custom-call | tf_op jit(solution)/shard_map/corners/pallas_call | solution.py:768
  13.8 0.7 collective-permute-start.8
  14.5 2.5 %collective-permute-start.5 = (f32[152,128]{1,0:T(8,128)S(1)}, f32[152,128]{1,0:T(8,128)S(1)}, u32[]{:S(2)}, u32[]{:S(2)}) collective-permute-start(f32[152,128]{1,0:T(8,128)S(1)} %collective-permute-done.3.ym), channel_id=1, source_target_pairs={{0,4},{8,12},{16,20},{24,28},{4,0},{12,8},{20,16},{28,24},{1,5},{9... | collective-permute-start | bytes 233480 | tf_op jit(solution)/shard_map/ppermute | solution.py:752
  17.1 0.1 collective-permute-start.6
  17.1 0.8 %collective-permute-done.5.ym_pair = f32[152,128]{1,0:T(8,128)S(1)} collective-permute-done((f32[152,128]{1,0:T(8,128)S(1)}, f32[152,128]{1,0:T(8,128)S(1)}, u32[]{:S(2)}, u32[]{:S(2)}) %collective-permute-start.5) | collective-permute-done | bytes 77856 | tf_op jit(solution)/shard_map/ppermute | solution.py:752
  18.0 0.7 collective-permute-start.7
  18.6 0.1 pad_add_fusion.first.start
  18.7 0.0 collective-permute-done.6.yp_pair
  18.7 2.4 %early.1 = (f32[33,72,128]{2,1,0:T(8,128)S(1)}, f32[33,72,128]{2,1,0:T(8,128)S(1)}, f32[33,72,128]{2,1,0:T(8,128)S(1)}, f32[27,72,128]{2,1,0:T(8,128)S(1)}, f32[27,72,128]{2,1,0:T(8,128)S(1)}) custom-call(s32[2]{0:T(128)S(1)} %pad_add_fusion.first.start, f32[1168,128]{1,0:T(8,128)S(1)} %get-tuple-element.21.own, f32[1168,128]{1,0:T(8,128)S(1)} %collective-permute-done.pair, ...), custom_call_target="tpu_custom_call" | custom-call | flops 29491200 | bytes 8388608 | tf_op jit(solution)/shard_map/early/pallas_call | solution.py:786
  21.1 0.0 collective-permute-done.1.lower
  21.1 0.0 collective-permute-done.2.upper
  21.1 0.0 collective-permute-done.7.corner_low
  21.1 0.0 collective-permute-done.8.corner_high
  21.1 7.5 %operator.1 = (bf16[96,10368]{1,0:T(8,128)(2,1)S(1)}, f32[16,3,4,128]{3,2,1,0:T(4,128)S(1)}) custom-call(s32[2]{0:T(128)S(1)} %pad_add_fusion.first.start, f32[1168,128]{1,0:T(8,128)S(1)} %get-tuple-element.21.own, f32[1168,128]{1,0:T(8,128)S(1)} %collective-permute-done.pair, f32[592,128]{1,0:T(8,128)S(1)} %collective-permute-done.1.lower, ...), custom_call_target="tpu_custom_call" | custom-call | tf_op jit(solution)/shard_map/operator/pallas_call | solution.py:805
  28.6 19.7 %all_to_all.10.system = f32[16,3,4,128]{3,2,1,0:T(4,128)S(1)} all-to-all(f32[16,3,4,128]{3,2,1,0:T(4,128)S(1)} %get-tuple-element.33), channel_id=1, replica_groups={{0,1,2,3,8,9,10,11,16,17,18,19,24,25,26,27},{4,5,6,7,12,13,14,15,20,21,..., dimensions={0} | all-to-all | bytes 196608 | tf_op jit(solution)/shard_map/all_to_all | solution.py:834
  48.3 0.0 collective-permute-start.9
  48.3 1.3 %collective-permute-done.9.system_pair = f32[16,3,4,128]{3,2,1,0:T(4,128)S(1)} collective-permute-done((f32[16,3,4,128]{3,2,1,0:T(4,128)S(1)}, f32[16,3,4,128]{3,2,1,0:T(4,128)S(1)}, u32[]{:S(2)}, u32[]{:S(2)}) %collective-permute-start.9) | collective-permute-done | bytes 98336 | tf_op jit(solution)/shard_map/ppermute | solution.py:752
  49.6 0.0 copy-start.1
  49.6 4.0 %solve.1 = f32[16,2,8,128]{3,2,1,0:T(8,128)S(1)} custom-call(f32[16,3,4,128]{3,2,1,0:T(4,128)S(1)} %all_to_all.10.system, f32[16,3,4,128]{3,2,1,0:T(4,128)S(1)} %collective-permute-done.9.system_pair, bf16[96,10368]{1,0:T(8,128)(2,1)S(1)} %get-tuple-element.34.both, f32[2,8,128]{2,1,0:T(8,128)S(1)} %negate_select_fusion.codes), custom_call_target="tpu_custom_call" | custom-call | tf_op jit(solution)/shard_map/solve/pallas_call | solution.py:839
  53.6 10.9 %all_to_all.11.blocks = f32[16,2,8,128]{3,2,1,0:T(8,128)S(1)} all-to-all(f32[16,2,8,128]{3,2,1,0:T(8,128)S(1)} %solve.1), channel_id=1, replica_groups={{0,1,2,3,8,9,10,11,16,17,18,19,24,25,26,27},{4,5,6,7,12,13,14,15,20,21,..., dimensions={0} | all-to-all | bytes 262144 | tf_op jit(solution)/shard_map/all_to_all | solution.py:834
  64.5 0.0 collective-permute-start.10
  64.5 0.0 copy-done.1
  64.5 0.7 scale.1
  65.2 0.7 %collective-permute-done.10.blocks_pair = f32[16,2,8,128]{3,2,1,0:T(8,128)S(1)} collective-permute-done((f32[16,2,8,128]{3,2,1,0:T(8,128)S(1)}, f32[16,2,8,128]{3,2,1,0:T(8,128)S(1)}, u32[]{:S(2)}, u32[]{:S(2)}) %collective-permute-start.10) | collective-permute-done | bytes 131104 | tf_op jit(solution)/shard_map/ppermute | solution.py:752
  65.9 1.3 %cone.1 = f32[2,8,128]{2,1,0:T(8,128)} custom-call(s32[2]{0:T(128)S(1)} %pad_add_fusion.first.start, f32[16,2,8,128]{3,2,1,0:T(8,128)S(1)} %all_to_all.11.blocks, f32[16,2,8,128]{3,2,1,0:T(8,128)S(1)} %collective-permute-done.10.blocks_pair, f32[2,8,128]{2,1,0:T(8,128)S(1)} %scale.1), custom_call_target="tpu_custom_call" | custom-call | tf_op jit(solution)/shard_map/cone/pallas_call | solution.py:857
  (1 shorter events, 0.0 us)
Async XLA Ops:
  0.7 1.1 %copy-start = (f32[3,24,2,8,128]{4,3,2,1,0:T(8,128)S(1)}, f32[3,24,2,8,128]{4,3,2,1,0:T(8,128)}, u32[]{:S(2)}) copy-start(f32[3,24,2,8,128]{4,3,2,1,0:T(8,128)} %forces.1) | copy-start | bytes 1769476
  1.9 2.2 %collective-permute-start = (f32[1168,128]{1,0:T(8,128)S(1)}, f32[1168,128]{1,0:T(8,128)S(1)}, u32[]{:S(2)}, u32[]{:S(2)}) collective-permute-start(f32[1168,128]{1,0:T(8,128)S(1)} %get-tuple-element.21.own), channel_id=1, source_target_pairs={{0,4},{8,12},{16,20},{24,28},{4,0},{12,8},{20,16},{28,24},{1,5},{9... | collective-permute-start | bytes 1794056 | tf_op jit(solution)/shard_map/ppermute | solution.py:752
  2.4 18.7 %collective-permute-start.2 = (f32[1168,128]{1,0:T(8,128)S(1)}, f32[1168,128]{1,0:T(8,128)S(1)}, u32[]{:S(2)}, u32[]{:S(2)}) collective-permute-start(f32[1168,128]{1,0:T(8,128)S(1)} %get-tuple-element.21.own), channel_id=1, source_target_pairs={{8,4},{16,12},{24,20},{9,5},{17,13},{25,21},{10,6},{18,14},{26,22}... | collective-permute-start | bytes 1794056 | tf_op jit(solution)/shard_map/ppermute | solution.py:754
  4.1 9.1 %collective-permute-start.4 = (f32[296,128]{1,0:T(8,128)S(1)}, f32[296,128]{1,0:T(8,128)S(1)}, u32[]{:S(2)}, u32[]{:S(2)}) collective-permute-start(f32[296,128]{1,0:T(8,128)S(1)} %get-tuple-element.25), channel_id=1, source_target_pairs={{1,0},{2,1},{3,2},{5,4},{6,5},{7,6},{9,8},{10,9},{11,10},{13,12},{... | collective-permute-start | bytes 454664 | tf_op jit(solution)/shard_map/ppermute | solution.py:746
  5.4 7.5 %collective-permute-start.3 = (f32[152,128]{1,0:T(8,128)S(1)}, f32[152,128]{1,0:T(8,128)S(1)}, u32[]{:S(2)}, u32[]{:S(2)}) collective-permute-start(f32[152,128]{1,0:T(8,128)S(1)} %get-tuple-element.24), channel_id=1, source_target_pairs={{0,1},{1,2},{2,3},{4,5},{5,6},{6,7},{8,9},{9,10},{10,11},{12,13},{... | collective-permute-start | bytes 233480 | tf_op jit(solution)/shard_map/ppermute | solution.py:746
  10.9 10.2 %collective-permute-start.1 = (f32[592,128]{1,0:T(8,128)S(1)}, f32[592,128]{1,0:T(8,128)S(1)}, u32[]{:S(2)}, u32[]{:S(2)}) collective-permute-start(f32[592,128]{1,0:T(8,128)S(1)} %get-tuple-element.23), channel_id=1, source_target_pairs={{4,8},{12,16},{20,24},{5,9},{13,17},{21,25},{6,10},{14,18},{22,26}... | collective-permute-start | bytes 909320 | tf_op jit(solution)/shard_map/ppermute | solution.py:755
  13.8 7.3 %collective-permute-start.8 = (f32[448,128]{1,0:T(8,128)S(1)}, f32[448,128]{1,0:T(8,128)S(1)}, u32[]{:S(2)}, u32[]{:S(2)}) collective-permute-start(f32[448,128]{1,0:T(8,128)S(1)} %get-tuple-element.27), channel_id=1, source_target_pairs={{8,4},{16,12},{24,20},{9,5},{17,13},{25,21},{10,6},{18,14},{26,22}... | collective-permute-start | bytes 688136 | tf_op jit(solution)/shard_map/ppermute | solution.py:779
  14.5 3.5 %collective-permute-start.5 = (f32[152,128]{1,0:T(8,128)S(1)}, f32[152,128]{1,0:T(8,128)S(1)}, u32[]{:S(2)}, u32[]{:S(2)}) collective-permute-start(f32[152,128]{1,0:T(8,128)S(1)} %collective-permute-done.3.ym), channel_id=1, source_target_pairs={{0,4},{8,12},{16,20},{24,28},{4,0},{12,8},{20,16},{28,24},{1,5},{9... | collective-permute-start | bytes 233480 | tf_op jit(solution)/shard_map/ppermute | solution.py:752
  17.1 1.7 %collective-permute-start.6 = (f32[296,128]{1,0:T(8,128)S(1)}, f32[296,128]{1,0:T(8,128)S(1)}, u32[]{:S(2)}, u32[]{:S(2)}) collective-permute-start(f32[296,128]{1,0:T(8,128)S(1)} %collective-permute-done.4.yp), channel_id=1, source_target_pairs={{0,4},{8,12},{16,20},{24,28},{4,0},{12,8},{20,16},{28,24},{1,5},{9... | collective-permute-start | bytes 454664 | tf_op jit(solution)/shard_map/ppermute | solution.py:752
  18.0 3.2 %collective-permute-start.7 = (f32[232,128]{1,0:T(8,128)}, f32[232,128]{1,0:T(8,128)S(1)}, u32[]{:S(2)}, u32[]{:S(2)}) collective-permute-start(f32[232,128]{1,0:T(8,128)} %get-tuple-element.26), channel_id=1, source_target_pairs={{4,8},{12,16},{20,24},{5,9},{13,17},{21,25},{6,10},{14,18},{22,26}... | collective-permute-start | bytes 356360 | tf_op jit(solution)/shard_map/ppermute | solution.py:780
  48.3 1.3 %collective-permute-start.9 = (f32[16,3,4,128]{3,2,1,0:T(4,128)S(1)}, f32[16,3,4,128]{3,2,1,0:T(4,128)S(1)}, u32[]{:S(2)}, u32[]{:S(2)}) collective-permute-start(f32[16,3,4,128]{3,2,1,0:T(4,128)S(1)} %all_to_all.10.system), channel_id=1, source_target_pairs={{0,4},{8,12},{16,20},{24,28},{4,0},{12,8},{20,16},{28,24},{1,5},{9... | collective-permute-start | bytes 294920 | tf_op jit(solution)/shard_map/ppermute | solution.py:752
  49.6 14.9 %copy-start.1 = (s32[2,8,128]{2,1,0:T(8,128)S(1)}, s32[2,8,128]{2,1,0:T(8,128)}, u32[]{:S(2)}) copy-start(s32[2,8,128]{2,1,0:T(8,128)} %levels.1) | copy-start | bytes 24580
  64.5 1.3 %collective-permute-start.10 = (f32[16,2,8,128]{3,2,1,0:T(8,128)S(1)}, f32[16,2,8,128]{3,2,1,0:T(8,128)S(1)}, u32[]{:S(2)}, u32[]{:S(2)}) collective-permute-start(f32[16,2,8,128]{3,2,1,0:T(8,128)S(1)} %all_to_all.11.blocks), channel_id=1, source_target_pairs={{0,4},{8,12},{16,20},{24,28},{4,0},{12,8},{20,16},{28,24},{1,5},{9... | collective-permute-start | bytes 393224 | tf_op jit(solution)/shard_map/ppermute | solution.py:752

commit v11 on v10

--- a/solution.py
+++ b/solution.py
@@ -235,19 +235,27 @@
     fill(own, base, sizes, yp, every_x, (rows - 1,), every_x, (rows - 2, rows - 1))
 
 
-def corner_kernel(sizes, ym, yp, down, up):
+def corner_kernel(sizes, first, ym, yp, edge, second):
     planes, rows, cases = sizes
     block = 3 * cases
-    for ref, first, count in ((down, 0, 2), (up, planes - 1, 1)):
-        line = 0
-        for source, width in ((ym, 1), (yp, 2)):
-            size = width * block
-            ref[line : line + count * size, :] = source[first * size : (first + count) * size, :]
-            line += count * size
-            codes = planes * size + (first + count - 2) * 2
-            ref[line : line + 4, :] = source[codes : codes + 4, :]
-            ref[line + 4 : line + 8, :] = jnp.zeros((4, LANES), f32)
-            line += 8
+    even = first[0] // planes % 2 == 0
+    line = at = 0
+    for source, width in ((ym, 1), (yp, 2)):
+        size = width * block
+        for start in range(0, size, block):
+            last = (planes - 1) * size + start
+            edge[line : line + block, :] = jnp.where(
+                even, source[start : start + block, :], source[last : last + block, :]
+            )
+            line += block
+        low, high = planes * size, planes * size + (planes - 2) * 2
+        edge[line : line + 4, :] = jnp.where(
+            even, source[low : low + 4, :], source[high : high + 4, :]
+        )
+        edge[line + 4 : line + 8, :] = jnp.zeros((4, LANES), f32)
+        line += 8
+        second[at : at + size, :] = source[size : 2 * size, :]
+        at += size
 
 
 def lines(ref, start, count):
@@ -272,15 +280,13 @@
     return lines(above, slots * 2 * block + slot * 2, 2)
 
 
-def corner(ref, count, slot, y, rows, block):
-    if y < 0:
-        return lines(ref, slot * block, block)
-    return lines(ref, count * block + 8 + (slot * 2 + y - rows) * block, block)
-
-
-def corner_codes(ref, count, slot, y, block):
-    start = count * block if y < 0 else 3 * count * block + 8
-    return lines(ref, start + slot * 2, 2)
+def corner(ref, y, rows, block, gap):
+    start = 0 if y < 0 else block + gap + (y - rows) * block
+    return lines(ref, start, block)
+
+
+def corner_codes(ref, slot, y, block):
+    return lines(ref, (block if y < 0 else 3 * block + 8) + slot * 2, 2)
 
 
 def node_inverse(signed, count, out):
@@ -349,7 +355,7 @@
 
 
 def main_kernel(
-    sizes, first, own, pair, lower, upper, ym, yp, ym_pair, yp_pair, corner_low, corner_high,
+    sizes, first, own, pair, lower, upper, ym, yp, ym_pair, yp_pair, corner_edge, corner_second,
     start, sums_e, diffs_e, acc_se, acc_de,
     both_out, system_out, stiff_ref, inverse,
     middle, sums, diffs, acc_s, acc_d, w_sums, w_diffs, acc2_s, acc2_d, right, table,
@@ -372,7 +378,7 @@
         if y == 0:
             outer = lines(ref, (count * block + slot) * rows, rows)
         else:
-            outer = corner_codes(corner_low if x < 0 else corner_high, count, slot, y, block)
+            outer = corner_codes(corner_edge, slot, y, block)
         inner = read(False, planes + x if x < 0 else x - planes)
         return jnp.where(even, outer, inner) if x < 0 else jnp.where(even, inner, outer)
 
@@ -398,7 +404,7 @@
         def outer(y):
             if 0 <= y < rows:
                 return inside(lower, 0, y, rows, block)
-            return corner(corner_low, 1, 0, y, rows, block)
+            return corner(corner_edge, y, rows, block, 8)
 
         def inner(y):
             if 0 <= y < rows:
@@ -411,17 +417,17 @@
 
     @pl.when(jnp.logical_not(even))
     def _():
-        def outer(slot):
+        def outer(slot, corner_ref, gap):
             def read(y):
                 if 0 <= y < rows:
                     return inside(upper, slot, y, rows, block)
-                return corner(corner_high, 2, slot, y, rows, block)
+                return corner(corner_ref, y, rows, block, gap)
 
             return read
 
         copy(0, planes)
-        place(1, planes, outer(0))
-        place(2, planes + 1, outer(1))
+        place(1, planes, outer(0, corner_edge, 8))
+        place(2, planes + 1, outer(1, corner_second, 0))
 
     nodes_y = rows + 1
     for column in range(nodes_y):
@@ -506,14 +512,14 @@
     unrolled(nodes_y, 3, lambda y: second_force(planes, y, count + planes + y))
 
     contract = (((1,), (1,)), ((), ()))
-    product = lax.dot_general(both_out[...], right[...], contract, preferred_element_type=f32)
-    product = product[:two] + product[two:]
-    gram = product[:, :two] + product[:, two : 2 * two]
-    other = product[:, 2 * two : 2 * two + cases] + product[:, 2 * two + cases :]
+    product = lax.dot_general(right[...], both_out[...], contract, preferred_element_type=f32)
+    product = product[:, :two] + product[:, two:]
+    gram = product[:two] + product[two : 2 * two]
+    other = product[2 * two : 2 * two + cases] + product[2 * two + cases :]
     row = lax.broadcasted_iota(jnp.int32, (cases, cases), 0)
     column = lax.broadcasted_iota(jnp.int32, (cases, cases), 1)
-    load_load, load_image = gram[:cases, :cases], gram[:cases, cases:]
-    mixed, image_image = other[:cases], other[cases:]
+    load_load, load_image = gram[:cases, :cases], gram[cases:, :cases]
+    mixed, image_image = other[:, :cases], other[:, cases:]
     table[...] = jnp.zeros(table.shape, f32)
     table[:, 0:cases] = jnp.where(row <= column, load_load, load_image)
     table[:, cases:two] = jnp.where(row <= column, mixed, image_image)
@@ -715,6 +721,10 @@
     density = 0.3 + 0.7 * levels.astype(f32) / (LEVELS - 1)
     codes = density * density * density
     codes = jnp.where(supports == 0, codes, -codes)
+    start = jnp.stack([lax.axis_index("gx") * planes, lax.axis_index("gy") * rows])
+    start = start.astype(jnp.int32)
+    counts = (count_x, count_y)
+    scalars = pl.BlockSpec(memory_space=pltpu.SMEM)
     whole = shape(planes * rows, planes * rows)
     down = [] if planes == 2 else [shape(2 * rows, 2 * rows)]
     own, up, *down = pl.pallas_call(
@@ -725,11 +735,6 @@
         compiler_params=PARAMS,
         name="pack",
     )(forces, codes)
-
-    start = jnp.stack([lax.axis_index("gx") * planes, lax.axis_index("gy") * rows])
-    start = start.astype(jnp.int32)
-    counts = (count_x, count_y)
-    scalars = pl.BlockSpec(memory_space=pltpu.SMEM)
     scale = pl.pallas_call(
         functools.partial(scale_kernel, sizes, counts),
         out_shape=jax.ShapeDtypeStruct((planes, rows, LANES), f32),
@@ -750,6 +755,9 @@
 
     def swapped(value):
         return lax.ppermute(value, "gx", links(0, 1) + links(1, -1))
+
+    def across(value):
+        return lax.ppermute(value, "gx", links(1, 1) + links(2, -1))
 
     upper = lax.ppermute(down[0] if down else own, "gx", links(2, -1))
     lower = lax.ppermute(up, "gx", links(1, 1))
@@ -765,19 +773,19 @@
     )(own)
     from_yp, from_ym = moved(ym, "gy", -1), moved(yp, "gy", 1)
     pair_yp, pair_ym = swapped(from_yp), swapped(from_ym)
-    corner_down, corner_up = pl.pallas_call(
+    corner_edge, corner_second = pl.pallas_call(
         functools.partial(corner_kernel, sizes),
         out_shape=[
-            jax.ShapeDtypeStruct((6 * block + 16, LANES), f32),
             jax.ShapeDtypeStruct((3 * block + 16, LANES), f32),
+            jax.ShapeDtypeStruct((3 * block, LANES), f32),
         ],
-        in_specs=[VMEM] * 2,
+        in_specs=[scalars] + [VMEM] * 2,
         out_specs=[VMEM] * 2,
         compiler_params=PARAMS,
         name="corners",
-    )(from_ym, from_yp)
-    corner_high = lax.ppermute(corner_down, "gx", links(2, -1))
-    corner_low = lax.ppermute(corner_up, "gx", links(1, 1))
+    )(start, from_ym, from_yp)
+    corner_edge = across(corner_edge)
+    corner_second = lax.ppermute(corner_second, "gx", links(2, -1))
 
     devices = count_x * count_y
     nodes = (planes + 1) * (rows + 1)
@@ -822,7 +830,7 @@
         name="operator",
     )(
         start, own, pair, lower, upper, from_ym, from_yp, pair_ym, pair_yp,
-        corner_low, corner_high, *early,
+        corner_edge, corner_second, *early,
     )
 
     groups = [

time: 67.6 us -> 66.4 us (0.982)
  waiting for transfers between devices: 5.39 us -> 3.99 us
    ppermute x5, waiting for transfers between devices: 3.77 us -> 2.67 us  [swapped(): return lax.ppermute(value, 'gx', links(0, 1) + links(1, -1))]
  transfers between devices with their start and end apart: 11 -> 11, of which waited for: 6 -> 4; matrix products, arithmetic and copies ran while one was open for 0% -> 0% of each run, Pallas kernels for 6% -> 6%
where the time goes in v11:
time: 66.4 us; the launch traced here: 65.9 us
  blocking collectives  31.1 us (47%)
  Pallas kernels  16.3 us (25%)
  starting transfers between devices  12.6 us (19%)
  waiting for transfers between devices  3.99 us (6%)
  local copies, waits for them, and re-layouts  1.07 us (2%)
  other arithmetic  0.8 us (1%)
    all_to_all x2, blocking collectives, gathered(): mine = lax.all_to_all(copies, ('gx', 'gy'), 0, 0, axis_index_groups=groups)  31.1 us
    pallas_call x1, Pallas kernels, local(): pl.pallas_call(functools.partial(main_kernel, sizes), out_shape=[jax.Shap...  7.3 us
    ppermute x2, starting transfers between devices, moved(): return lax.ppermute(value, axis, pairs)  6.77 us
    pallas_call x1, Pallas kernels, local(): pl.pallas_call(functools.partial(solve_kernel, sizes), out_shape=jax.Shap...  3.98 us
    ppermute x5, starting transfers between devices, swapped(): return lax.ppermute(value, 'gx', links(0, 1) + links(1, -1))  3.08 us
    ppermute x5, waiting for transfers between devices, swapped(): return lax.ppermute(value, 'gx', links(0, 1) + links(1, -1))  2.67 us
    pallas_call x1, Pallas kernels, local(): pl.pallas_call(functools.partial(early_kernel, sizes), out_shape=[window]...  2.39 us
  transfers between devices with their start and end apart: 11, of which 4 were waited for; matrix products, arithmetic and copies ran while one was open for 0% of the time, Pallas kernels for 6%

profile of v11, /device:TPU:0, one launch (start us, length us, event | category | flops | bytes accessed | tf_op | source)
XLA Modules:
  0.0 65.9 jit_solution(5145703978399998999)
XLA Ops:
  0.0 0.7 %negate_select_fusion.codes = f32[2,8,128]{2,1,0:T(8,128)S(1)} fusion(s32[2,8,128]{2,1,0:T(8,128)} %levels.1, s32[2,8,128]{2,1,0:T(8,128)} %param.5), kind=kLoop, calls=%fused_computation | loop fusion | flops 16384 | bytes 24576 | tf_op jit(solution)/shard_map/jit(_where)/select_n | solution.py:723
  0.7 0.0 copy-start
  0.7 1.1 %copy-done = f32[3,24,2,8,128]{4,3,2,1,0:T(8,128)S(1)} copy-done((f32[3,24,2,8,128]{4,3,2,1,0:T(8,128)S(1)}, f32[3,24,2,8,128]{4,3,2,1,0:T(8,128)}, u32[]{:S(2)}) %copy-start) | copy-done | bytes 589848
  1.8 0.1 pack.1
  1.9 0.5 collective-permute-start
  2.4 0.7 %collective-permute-start.2 = (f32[1168,128]{1,0:T(8,128)S(1)}, f32[1168,128]{1,0:T(8,128)S(1)}, u32[]{:S(2)}, u32[]{:S(2)}) collective-permute-start(f32[1168,128]{1,0:T(8,128)S(1)} %get-tuple-element.21.own), channel_id=1, source_target_pairs={{8,4},{16,12},{24,20},{9,5},{17,13},{25,21},{10,6},{18,14},{26,22}... | collective-permute-start | bytes 1794056 | tf_op jit(solution)/shard_map/ppermute | solution.py:762
  3.1 0.9 %collective-permute-done.pair = f32[1168,128]{1,0:T(8,128)S(1)} collective-permute-done((f32[1168,128]{1,0:T(8,128)S(1)}, f32[1168,128]{1,0:T(8,128)S(1)}, u32[]{:S(2)}, u32[]{:S(2)}) %collective-permute-start) | collective-permute-done | bytes 598048 | tf_op jit(solution)/shard_map/ppermute | solution.py:757
  4.1 1.3 %collective-permute-start.4 = (f32[296,128]{1,0:T(8,128)S(1)}, f32[296,128]{1,0:T(8,128)S(1)}, u32[]{:S(2)}, u32[]{:S(2)}) collective-permute-start(f32[296,128]{1,0:T(8,128)S(1)} %get-tuple-element.25), channel_id=1, source_target_pairs={{1,0},{2,1},{3,2},{5,4},{6,5},{7,6},{9,8},{10,9},{11,10},{13,12},{... | collective-permute-start | bytes 454664 | tf_op jit(solution)/shard_map/ppermute | solution.py:751
  5.4 5.5 %collective-permute-start.3 = (f32[152,128]{1,0:T(8,128)S(1)}, f32[152,128]{1,0:T(8,128)S(1)}, u32[]{:S(2)}, u32[]{:S(2)}) collective-permute-start(f32[152,128]{1,0:T(8,128)S(1)} %get-tuple-element.24), channel_id=1, source_target_pairs={{0,1},{1,2},{2,3},{4,5},{5,6},{6,7},{8,9},{9,10},{10,11},{12,13},{... | collective-permute-start | bytes 233480 | tf_op jit(solution)/shard_map/ppermute | solution.py:751
  10.9 0.7 %collective-permute-start.1 = (f32[592,128]{1,0:T(8,128)S(1)}, f32[592,128]{1,0:T(8,128)S(1)}, u32[]{:S(2)}, u32[]{:S(2)}) collective-permute-start(f32[592,128]{1,0:T(8,128)S(1)} %get-tuple-element.23), channel_id=1, source_target_pairs={{4,8},{12,16},{20,24},{5,9},{13,17},{21,25},{6,10},{14,18},{22,26}... | collective-permute-start | bytes 909320 | tf_op jit(solution)/shard_map/ppermute | solution.py:763
  11.6 1.3 %collective-permute-done.3.ym = f32[152,128]{1,0:T(8,128)S(1)} collective-permute-done((f32[152,128]{1,0:T(8,128)S(1)}, f32[152,128]{1,0:T(8,128)S(1)}, u32[]{:S(2)}, u32[]{:S(2)}) %collective-permute-start.3) | collective-permute-done | bytes 77856 | tf_op jit(solution)/shard_map/ppermute | solution.py:751
  12.9 2.2 %collective-permute-start.5 = (f32[152,128]{1,0:T(8,128)S(1)}, f32[152,128]{1,0:T(8,128)S(1)}, u32[]{:S(2)}, u32[]{:S(2)}) collective-permute-start(f32[152,128]{1,0:T(8,128)S(1)} %collective-permute-done.3.ym), channel_id=1, source_target_pairs={{0,4},{8,12},{16,20},{24,28},{4,0},{12,8},{20,16},{28,24},{1,5},{9... | collective-permute-start | bytes 233480 | tf_op jit(solution)/shard_map/ppermute | solution.py:757
  15.1 0.0 collective-permute-done.4.yp
  15.1 0.1 collective-permute-start.6
  15.2 0.1 pad_add_fusion.first.start
  15.2 0.6 corners.1
  15.8 0.7 %collective-permute-start.7 = (f32[232,128]{1,0:T(8,128)S(1)}, f32[232,128]{1,0:T(8,128)S(1)}, u32[]{:S(2)}, u32[]{:S(2)}) collective-permute-start(f32[232,128]{1,0:T(8,128)S(1)} %get-tuple-element.26), channel_id=1, source_target_pairs={{4,8},{12,16},{20,24},{8,4},{16,12},{24,20},{5,9},{13,17},{21,25},... | collective-permute-start | bytes 356360 | tf_op jit(solution)/shard_map/ppermute | solution.py:760
  16.5 0.0 collective-permute-done.5.ym_pair
  16.5 0.7 %collective-permute-start.8 = (f32[216,128]{1,0:T(8,128)S(1)}, f32[216,128]{1,0:T(8,128)S(1)}, u32[]{:S(2)}, u32[]{:S(2)}) collective-permute-start(f32[216,128]{1,0:T(8,128)S(1)} %get-tuple-element.27), channel_id=1, source_target_pairs={{8,4},{16,12},{24,20},{9,5},{17,13},{25,21},{10,6},{18,14},{26,22}... | collective-permute-start | bytes 331784 | tf_op jit(solution)/shard_map/ppermute | solution.py:788
  17.2 0.0 collective-permute-done.6.yp_pair
  17.2 2.4 %early.1 = (f32[33,72,128]{2,1,0:T(8,128)S(1)}, f32[33,72,128]{2,1,0:T(8,128)S(1)}, f32[33,72,128]{2,1,0:T(8,128)S(1)}, f32[27,72,128]{2,1,0:T(8,128)S(1)}, f32[27,72,128]{2,1,0:T(8,128)S(1)}) custom-call(s32[2]{0:T(128)S(1)} %pad_add_fusion.first.start, f32[1168,128]{1,0:T(8,128)S(1)} %get-tuple-element.21.own, f32[1168,128]{1,0:T(8,128)S(1)} %collective-permute-done.pair, ...), custom_call_target="tpu_custom_call" | custom-call | flops 29491200 | bytes 8388608 | tf_op jit(solution)/shard_map/early/pallas_call | solution.py:794
  19.6 0.0 collective-permute-done.1.lower
  19.6 0.0 collective-permute-done.2.upper
  19.6 0.0 collective-permute-done.8.corner_second
  19.6 0.0 collective-permute-done.7.corner_edge
  19.6 7.3 %operator.1 = (bf16[96,10368]{1,0:T(8,128)(2,1)S(1)}, f32[16,3,4,128]{3,2,1,0:T(4,128)S(1)}) custom-call(s32[2]{0:T(128)S(1)} %pad_add_fusion.first.start, f32[1168,128]{1,0:T(8,128)S(1)} %get-tuple-element.21.own, f32[1168,128]{1,0:T(8,128)S(1)} %collective-permute-done.pair, f32[592,128]{1,0:T(8,128)S(1)} %collective-permute-done.1.lower, ...), custom_call_target="tpu_custom_call" | custom-call | tf_op jit(solution)/shard_map/operator/pallas_call | solution.py:813
  26.9 19.4 %all_to_all.10.system = f32[16,3,4,128]{3,2,1,0:T(4,128)S(1)} all-to-all(f32[16,3,4,128]{3,2,1,0:T(4,128)S(1)} %get-tuple-element.33), channel_id=1, replica_groups={{0,1,2,3,8,9,10,11,16,17,18,19,24,25,26,27},{4,5,6,7,12,13,14,15,20,21,..., dimensions={0} | all-to-all | bytes 196608 | tf_op jit(solution)/shard_map/all_to_all | solution.py:842
  46.4 0.3 collective-permute-start.9
  46.7 1.0 %collective-permute-done.9.system_pair = f32[16,3,4,128]{3,2,1,0:T(4,128)S(1)} collective-permute-done((f32[16,3,4,128]{3,2,1,0:T(4,128)S(1)}, f32[16,3,4,128]{3,2,1,0:T(4,128)S(1)}, u32[]{:S(2)}, u32[]{:S(2)}) %collective-permute-start.9) | collective-permute-done | bytes 98336 | tf_op jit(solution)/shard_map/ppermute | solution.py:757
  47.7 0.0 copy-start.1
  47.7 4.0 %solve.1 = f32[16,2,8,128]{3,2,1,0:T(8,128)S(1)} custom-call(f32[16,3,4,128]{3,2,1,0:T(4,128)S(1)} %all_to_all.10.system, f32[16,3,4,128]{3,2,1,0:T(4,128)S(1)} %collective-permute-done.9.system_pair, bf16[96,10368]{1,0:T(8,128)(2,1)S(1)} %get-tuple-element.34.both, f32[2,8,128]{2,1,0:T(8,128)S(1)} %negate_select_fusion.codes), custom_call_target="tpu_custom_call" | custom-call | tf_op jit(solution)/shard_map/solve/pallas_call | solution.py:847
  51.7 11.6 %all_to_all.11.blocks = f32[16,2,8,128]{3,2,1,0:T(8,128)S(1)} all-to-all(f32[16,2,8,128]{3,2,1,0:T(8,128)S(1)} %solve.1), channel_id=1, replica_groups={{0,1,2,3,8,9,10,11,16,17,18,19,24,25,26,27},{4,5,6,7,12,13,14,15,20,21,..., dimensions={0} | all-to-all | bytes 262144 | tf_op jit(solution)/shard_map/all_to_all | solution.py:842
  63.3 0.0 collective-permute-start.10
  63.3 0.0 copy-done.1
  63.3 0.7 scale.1
  63.9 0.7 %collective-permute-done.10.blocks_pair = f32[16,2,8,128]{3,2,1,0:T(8,128)S(1)} collective-permute-done((f32[16,2,8,128]{3,2,1,0:T(8,128)S(1)}, f32[16,2,8,128]{3,2,1,0:T(8,128)S(1)}, u32[]{:S(2)}, u32[]{:S(2)}) %collective-permute-start.10) | collective-permute-done | bytes 131104 | tf_op jit(solution)/shard_map/ppermute | solution.py:757
  64.6 1.3 %cone.1 = f32[2,8,128]{2,1,0:T(8,128)} custom-call(s32[2]{0:T(128)S(1)} %pad_add_fusion.first.start, f32[16,2,8,128]{3,2,1,0:T(8,128)S(1)} %all_to_all.11.blocks, f32[16,2,8,128]{3,2,1,0:T(8,128)S(1)} %collective-permute-done.10.blocks_pair, f32[2,8,128]{2,1,0:T(8,128)S(1)} %scale.1), custom_call_target="tpu_custom_call" | custom-call | tf_op jit(solution)/shard_map/cone/pallas_call | solution.py:865
  (1 shorter events, 0.0 us)
Async XLA Ops:
  0.7 1.1 %copy-start = (f32[3,24,2,8,128]{4,3,2,1,0:T(8,128)S(1)}, f32[3,24,2,8,128]{4,3,2,1,0:T(8,128)}, u32[]{:S(2)}) copy-start(f32[3,24,2,8,128]{4,3,2,1,0:T(8,128)} %forces.1) | copy-start | bytes 1769476
  1.9 2.2 %collective-permute-start = (f32[1168,128]{1,0:T(8,128)S(1)}, f32[1168,128]{1,0:T(8,128)S(1)}, u32[]{:S(2)}, u32[]{:S(2)}) collective-permute-start(f32[1168,128]{1,0:T(8,128)S(1)} %get-tuple-element.21.own), channel_id=1, source_target_pairs={{0,4},{8,12},{16,20},{24,28},{4,0},{12,8},{20,16},{28,24},{1,5},{9... | collective-permute-start | bytes 1794056 | tf_op jit(solution)/shard_map/ppermute | solution.py:757
  2.4 17.2 %collective-permute-start.2 = (f32[1168,128]{1,0:T(8,128)S(1)}, f32[1168,128]{1,0:T(8,128)S(1)}, u32[]{:S(2)}, u32[]{:S(2)}) collective-permute-start(f32[1168,128]{1,0:T(8,128)S(1)} %get-tuple-element.21.own), channel_id=1, source_target_pairs={{8,4},{16,12},{24,20},{9,5},{17,13},{25,21},{10,6},{18,14},{26,22}... | collective-permute-start | bytes 1794056 | tf_op jit(solution)/shard_map/ppermute | solution.py:762
  4.1 11.0 %collective-permute-start.4 = (f32[296,128]{1,0:T(8,128)S(1)}, f32[296,128]{1,0:T(8,128)S(1)}, u32[]{:S(2)}, u32[]{:S(2)}) collective-permute-start(f32[296,128]{1,0:T(8,128)S(1)} %get-tuple-element.25), channel_id=1, source_target_pairs={{1,0},{2,1},{3,2},{5,4},{6,5},{7,6},{9,8},{10,9},{11,10},{13,12},{... | collective-permute-start | bytes 454664 | tf_op jit(solution)/shard_map/ppermute | solution.py:751
  5.4 7.5 %collective-permute-start.3 = (f32[152,128]{1,0:T(8,128)S(1)}, f32[152,128]{1,0:T(8,128)S(1)}, u32[]{:S(2)}, u32[]{:S(2)}) collective-permute-start(f32[152,128]{1,0:T(8,128)S(1)} %get-tuple-element.24), channel_id=1, source_target_pairs={{0,1},{1,2},{2,3},{4,5},{5,6},{6,7},{8,9},{9,10},{10,11},{12,13},{... | collective-permute-start | bytes 233480 | tf_op jit(solution)/shard_map/ppermute | solution.py:751
  10.9 8.7 %collective-permute-start.1 = (f32[592,128]{1,0:T(8,128)S(1)}, f32[592,128]{1,0:T(8,128)S(1)}, u32[]{:S(2)}, u32[]{:S(2)}) collective-permute-start(f32[592,128]{1,0:T(8,128)S(1)} %get-tuple-element.23), channel_id=1, source_target_pairs={{4,8},{12,16},{20,24},{5,9},{13,17},{21,25},{6,10},{14,18},{22,26}... | collective-permute-start | bytes 909320 | tf_op jit(solution)/shard_map/ppermute | solution.py:763
  12.9 3.6 %collective-permute-start.5 = (f32[152,128]{1,0:T(8,128)S(1)}, f32[152,128]{1,0:T(8,128)S(1)}, u32[]{:S(2)}, u32[]{:S(2)}) collective-permute-start(f32[152,128]{1,0:T(8,128)S(1)} %collective-permute-done.3.ym), channel_id=1, source_target_pairs={{0,4},{8,12},{16,20},{24,28},{4,0},{12,8},{20,16},{28,24},{1,5},{9... | collective-permute-start | bytes 233480 | tf_op jit(solution)/shard_map/ppermute | solution.py:757
  15.1 2.1 %collective-permute-start.6 = (f32[296,128]{1,0:T(8,128)S(1)}, f32[296,128]{1,0:T(8,128)S(1)}, u32[]{:S(2)}, u32[]{:S(2)}) collective-permute-start(f32[296,128]{1,0:T(8,128)S(1)} %collective-permute-done.4.yp), channel_id=1, source_target_pairs={{0,4},{8,12},{16,20},{24,28},{4,0},{12,8},{20,16},{28,24},{1,5},{9... | collective-permute-start | bytes 454664 | tf_op jit(solution)/shard_map/ppermute | solution.py:757
  15.8 3.8 %collective-permute-start.7 = (f32[232,128]{1,0:T(8,128)S(1)}, f32[232,128]{1,0:T(8,128)S(1)}, u32[]{:S(2)}, u32[]{:S(2)}) collective-permute-start(f32[232,128]{1,0:T(8,128)S(1)} %get-tuple-element.26), channel_id=1, source_target_pairs={{4,8},{12,16},{20,24},{8,4},{16,12},{24,20},{5,9},{13,17},{21,25},... | collective-permute-start | bytes 356360 | tf_op jit(solution)/shard_map/ppermute | solution.py:760
  16.5 3.1 %collective-permute-start.8 = (f32[216,128]{1,0:T(8,128)S(1)}, f32[216,128]{1,0:T(8,128)S(1)}, u32[]{:S(2)}, u32[]{:S(2)}) collective-permute-start(f32[216,128]{1,0:T(8,128)S(1)} %get-tuple-element.27), channel_id=1, source_target_pairs={{8,4},{16,12},{24,20},{9,5},{17,13},{25,21},{10,6},{18,14},{26,22}... | collective-permute-start | bytes 331784 | tf_op jit(solution)/shard_map/ppermute | solution.py:788
  46.4 1.3 %collective-permute-start.9 = (f32[16,3,4,128]{3,2,1,0:T(4,128)S(1)}, f32[16,3,4,128]{3,2,1,0:T(4,128)S(1)}, u32[]{:S(2)}, u32[]{:S(2)}) collective-permute-start(f32[16,3,4,128]{3,2,1,0:T(4,128)S(1)} %all_to_all.10.system), channel_id=1, source_target_pairs={{0,4},{8,12},{16,20},{24,28},{4,0},{12,8},{20,16},{28,24},{1,5},{9... | collective-permute-start | bytes 294920 | tf_op jit(solution)/shard_map/ppermute | solution.py:757
  47.7 15.6 %copy-start.1 = (s32[2,8,128]{2,1,0:T(8,128)S(1)}, s32[2,8,128]{2,1,0:T(8,128)}, u32[]{:S(2)}) copy-start(s32[2,8,128]{2,1,0:T(8,128)} %levels.1) | copy-start | bytes 24580
  63.3 1.3 %collective-permute-start.10 = (f32[16,2,8,128]{3,2,1,0:T(8,128)S(1)}, f32[16,2,8,128]{3,2,1,0:T(8,128)S(1)}, u32[]{:S(2)}, u32[]{:S(2)}) collective-permute-start(f32[16,2,8,128]{3,2,1,0:T(8,128)S(1)} %all_to_all.11.blocks), channel_id=1, source_target_pairs={{0,4},{8,12},{16,20},{24,28},{4,0},{12,8},{20,16},{28,24},{1,5},{9... | collective-permute-start | bytes 393224 | tf_op jit(solution)/shard_map/ppermute | solution.py:757

commit v12 on v11

--- a/solution.py
+++ b/solution.py
@@ -134,42 +134,47 @@
     return energy + ((LAME + 4 * SHEAR) / 144) * last
 
 
-def x_modes(sums, diffs, plane, row, tile, cases, columns):
+def x_modes(find, plane, row, tile, cases):
+    sums, diffs, columns, column = find(row)
     out = [[[None] * 3 for _ in range(2)] for _ in range(2)]
     for c, ref in enumerate((sums, diffs)):
         for k in range(3):
             rows = pl.ds(pl.multiple_of(k * cases + tile * 8, 8), 8)
-            one = ref[plane * columns + row, rows, :]
-            two = ref[(plane + 1) * columns + row, rows, :]
+            one = ref[plane * columns + column, rows, :]
+            two = ref[(plane + 1) * columns + column, rows, :]
             out[0][c][k] = one + two
             out[1][c][k] = two - one
     return out
 
 
-def apply_elements(
-    sums, diffs, stiff_ref, acc_s, acc_d, planes, rows, skip, stiff_x, stiff_y, cases
-):
-    columns = rows + 1
-    acc_columns = columns - 2 * skip
+def whole(sums, diffs, columns):
+    return lambda row: (sums, diffs, columns, row)
+
+
+def apply_elements(find, stiff_ref, acc_s, acc_d, planes, rows, kept, stiff_x, stiff_y, cases):
+    columns = len(kept)
     tiles = cases // 8
+    for column in range(columns):
+        acc_s[column] = jnp.zeros(acc_s.shape[1:], f32)
+        acc_d[column] = jnp.zeros(acc_d.shape[1:], f32)
 
     def step(index, _):
         plane, tile = index // tiles, index % tiles
 
         def emit(row, total):
-            if not skip <= row < columns - skip:
+            if row not in kept:
                 return
             for c, acc in enumerate((acc_s, acc_d)):
                 for k in range(3):
                     lines = pl.ds(pl.multiple_of(k * cases + tile * 8, 8), 8)
-                    low = plane * acc_columns + row - skip
+                    low = plane * columns + row - kept[0]
                     acc[low, lines, :] += total[0][c][k] - total[1][c][k]
-                    acc[low + acc_columns, lines, :] = total[0][c][k] + total[1][c][k]
-
-        lower = x_modes(sums, diffs, plane, 0, tile, cases, columns)
+                    acc[low + columns, lines, :] = total[0][c][k] + total[1][c][k]
+
+        lower = x_modes(find, plane, 0, tile, cases)
         carry = None
         for row in range(rows):
-            upper = x_modes(sums, diffs, plane, row + 1, tile, cases, columns)
+            upper = x_modes(find, plane, row + 1, tile, cases)
             stiff = jnp.broadcast_to(
                 stiff_ref[plane + stiff_x, pl.ds(row + stiff_y, 1), :], (8, LANES)
             )
@@ -235,27 +240,23 @@
     fill(own, base, sizes, yp, every_x, (rows - 1,), every_x, (rows - 2, rows - 1))
 
 
-def corner_kernel(sizes, first, ym, yp, edge, second):
+def corner_kernel(sizes, first, ym, yp, out):
     planes, rows, cases = sizes
     block = 3 * cases
     even = first[0] // planes % 2 == 0
-    line = at = 0
+    line = 0
     for source, width in ((ym, 1), (yp, 2)):
         size = width * block
-        for start in range(0, size, block):
-            last = (planes - 1) * size + start
-            edge[line : line + block, :] = jnp.where(
-                even, source[start : start + block, :], source[last : last + block, :]
-            )
-            line += block
-        low, high = planes * size, planes * size + (planes - 2) * 2
-        edge[line : line + 4, :] = jnp.where(
-            even, source[low : low + 4, :], source[high : high + 4, :]
-        )
-        edge[line + 4 : line + 8, :] = jnp.zeros((4, LANES), f32)
-        line += 8
-        second[at : at + size, :] = source[size : 2 * size, :]
-        at += size
+        parts = [(at, (planes - 2) * size + at, block) for at in range(0, 2 * size, block)]
+        parts.append((planes * size, planes * size + (planes - 2) * 2, 4))
+        for low, high, count in parts:
+            value = lines(source, low, count)
+            if low != high:
+                value = jnp.where(even, value, lines(source, high, count))
+            out[line : line + count, :] = value
+            line += count
+        out[line : line + 4, :] = jnp.zeros((4, LANES), f32)
+        line += 4
 
 
 def lines(ref, start, count):
@@ -280,13 +281,13 @@
     return lines(above, slots * 2 * block + slot * 2, 2)
 
 
-def corner(ref, y, rows, block, gap):
-    start = 0 if y < 0 else block + gap + (y - rows) * block
+def corner(ref, slot, y, rows, block):
+    start = slot * block if y < 0 else 2 * block + 8 + (slot * 2 + y - rows) * block
     return lines(ref, start, block)
 
 
 def corner_codes(ref, slot, y, block):
-    return lines(ref, (block if y < 0 else 3 * block + 8) + slot * 2, 2)
+    return lines(ref, (2 * block if y < 0 else 6 * block + 8) + slot * 2, 2)
 
 
 def node_inverse(signed, count, out):
@@ -348,21 +349,158 @@
             column = w * ys + y + 1
             start[column] = value
             place_column(sums, diffs, column, value)
-    for column in range(rows + 1):
-        acc_s[column] = jnp.zeros((block, LANES), f32)
-        acc_d[column] = jnp.zeros((block, LANES), f32)
-    apply_elements(sums, diffs, stiff_ref, acc_s, acc_d, planes, rows + 2, 1, 1, 1, cases)
-
-
-def main_kernel(
-    sizes, first, own, pair, lower, upper, ym, yp, ym_pair, yp_pair, corner_edge, corner_second,
-    start, sums_e, diffs_e, acc_se, acc_de,
-    both_out, system_out, stiff_ref, inverse,
-    middle, sums, diffs, acc_s, acc_d, w_sums, w_diffs, acc2_s, acc2_d, right, table,
+    kept = range(1, rows + 2)
+    find = whole(sums, diffs, ys)
+    apply_elements(find, stiff_ref, acc_s, acc_d, planes, rows + 2, kept, 1, 1, cases)
+
+
+def core_rows(rows):
+    return range(2, rows - 1)
+
+
+def rim_rows(rows):
+    return (0, 1, rows - 1, rows)
+
+
+def rim_columns(planes, rows):
+    own = [(x, y) for x in range(planes) for y in rim_rows(rows) if y < rows]
+    beyond_own = [(x, rows) for x in range(planes)] + [(planes, y) for y in rim_rows(rows)]
+    return own + beyond_own, len(own)
+
+
+def merged(x, planes, even, early, near):
+    low = ([x - 1] if x >= 1 else [], [x + 1] if x <= 1 else [])
+    high = ([x + 1] if x < planes else [], [x - planes + 1] if x >= planes - 1 else [])
+    if low[0] and low[1] and high[0] and high[1]:
+        one = early(jnp.where(even, low[0][0], high[0][0]))
+        return one + near(jnp.where(even, low[1][0], high[1][0]))
+
+    def read(places):
+        found = [early(w) for w in places[0]] + [near(v) for v in places[1]]
+        return found[0] if len(found) == 1 else found[0] + found[1]
+
+    return jnp.where(even, read(low), read(high))
+
+
+def direction_at(x, planes, even, early, middle):
+    if x == 0:
+        return jnp.where(even, middle, early(1))
+    if x == planes:
+        return jnp.where(even, early(planes - 1), middle)
+    return early(jnp.where(even, x - 1, x + 1))
+
+
+def keep_pair(ref, place, one, two, cases):
+    for k in range(3):
+        part = slice(k * cases, (k + 1) * cases)
+        high, rest = split(jnp.concatenate([one[part], two[part]], 0))
+        lane = pl.ds(pl.multiple_of((place * 3 + k) * LANES, LANES), LANES)
+        ref[0 : 2 * cases, lane] = high
+        ref[2 * cases : 4 * cases, lane] = rest
+
+
+def products(first, second):
+    contract = (((1,), (1,)), ((), ()))
+    out = lax.dot_general(first, second, contract, preferred_element_type=f32)
+    left, right = out.shape[0] // 2, out.shape[1] // 2
+    out = out[:, :right] + out[:, right:]
+    return out[:left] + out[left:]
+
+
+def middle_kernel(
+    sizes, first, own, pair, lower, upper, start, sums_e, diffs_e, acc_se, acc_de,
+    sums, diffs, middle, acc_s, acc_d, w_sums, w_diffs, both_out, gram_out,
+    stiff_ref, inverse, right,
 ):
     planes, rows, cases = sizes
     block = 3 * cases
-    ys = rows + 3
+    ys, nodes_y, inner = rows + 3, rows + 1, rows - 1
+    core = core_rows(rows)
+    even = first[0] // planes % 2 == 0
+
+    def codes(x):
+        if 0 <= x < planes:
+            return lines(own, (planes * block + x) * rows, rows)
+        if x < 0:
+            outer = lines(lower, (block + x + 2) * rows, rows)
+            return jnp.where(even, outer, lines(pair, (planes * block + planes + x) * rows, rows))
+        slot = x - planes
+        outer = lines(upper, (2 * block + slot) * rows, rows)
+        return jnp.where(even, lines(pair, (planes * block + slot) * rows, rows), outer)
+
+    for x in range(-2, planes + 2):
+        stiff_ref[x + 2, 0:rows, :] = codes(x)
+    node_inverse(stiff_ref, inner, inverse)
+
+    def place(v, x, ref, slot):
+        for y in range(1, rows):
+            value = inside(ref, slot, y, rows, block) * inverse[x + 1, y - 1 : y, :]
+            if v == 1:
+                middle[y - 1] = value
+            place_column(sums, diffs, v * inner + y - 1, value)
+
+    def copy(v, w):
+        for y in range(1, rows):
+            sums[v * inner + y - 1] = sums_e[w * ys + y + 1]
+            diffs[v * inner + y - 1] = diffs_e[w * ys + y + 1]
+
+    @pl.when(even)
+    def _():
+        place(0, -1, lower, 0)
+        place(1, 0, own, 0)
+        copy(2, 0)
+
+    @pl.when(jnp.logical_not(even))
+    def _():
+        copy(0, planes)
+        place(1, planes, upper, 0)
+        place(2, planes + 1, upper, 1)
+
+    layer = jnp.where(even, 1, planes + 1)
+    find = whole(sums, diffs, inner)
+    apply_elements(find, stiff_ref, acc_s, acc_d, 2, rows - 2, range(inner), layer, 1, cases)
+
+    def image(x, y, place):
+        def total(early, near):
+            return merged(
+                x, planes, even, lambda w: early[w * nodes_y + y],
+                lambda v: near[v * inner + y - 1],
+            )
+
+        s, d = total(acc_se, acc_s), total(acc_de, acc_d)
+        force = s - d + shift_up(s + d)
+        scaled = force * inverse[x + 1, pl.ds(y - 1, 1), :]
+        place_column(w_sums, w_diffs, place, scaled)
+        value = direction_at(x, planes, even, lambda w: start[w * ys + y + 1], middle[y - 1])
+        keep_pair(both_out, place, value, scaled, cases)
+        return force
+
+    def within(x, index):
+        y, place = core[0] + index, x * len(core) + index
+        force = image(x, y, place)
+        given = own[pl.ds(pl.multiple_of((x * rows + y) * block, 8), block), :]
+        keep_pair(right, place, given, force, cases)
+
+    for x in range(planes):
+        unrolled(len(core), len(core), functools.partial(within, x))
+    last = planes * len(core)
+    unrolled(len(core), len(core), lambda index: image(planes, core[0] + index, last + index))
+    gram_out[...] = products(right[...], both_out[:, : last * 3 * LANES])
+
+
+def main_kernel(
+    sizes, first, own, pair, lower, upper, ym, yp, ym_pair, yp_pair, corners,
+    start, sums_e, diffs_e, acc_se, acc_de,
+    sums_m, diffs_m, middle_m, acc_sm, acc_dm, w_sm, w_dm, both_m, gram_m,
+    both_out, system_out, stiff_ref, inverse,
+    middle, sums, diffs, acc_s0, acc_d0, acc_s1, acc_d1, w_sums, w_diffs,
+    acc2_s, acc2_d, right, second_m, second_r, table,
+):
+    planes, rows, cases = sizes
+    block = 3 * cases
+    ys, nodes_y, inner = rows + 3, rows + 1, rows - 1
+    core, rim = core_rows(rows), rim_rows(rows)
+    columns, own_count = rim_columns(planes, rows)
     even = first[0] // planes % 2 == 0
     y_own, y_pair = (ym, yp), (ym_pair, yp_pair)
 
@@ -378,126 +516,83 @@
         if y == 0:
             outer = lines(ref, (count * block + slot) * rows, rows)
         else:
-            outer = corner_codes(corner_edge, slot, y, block)
-        inner = read(False, planes + x if x < 0 else x - planes)
-        return jnp.where(even, outer, inner) if x < 0 else jnp.where(even, inner, outer)
+            outer = corner_codes(corners, slot, y, block)
+        within = read(False, planes + x if x < 0 else x - planes)
+        return jnp.where(even, outer, within) if x < 0 else jnp.where(even, within, outer)
 
     for x in range(-2, planes + 2):
         for y, count in ((-2, 2), (0, rows), (rows, 2)):
             stiff_ref[x + 2, y + 2 : y + 2 + count, :] = codes(x, y)
     node_inverse(stiff_ref, ys, inverse)
 
-    def place(v, x, read):
-        for y in range(-1, rows + 2):
-            value = read(y) * inverse[x + 1, y + 1 : y + 2, :]
-            if v == 1:
-                middle[y + 1] = value
-            place_column(sums, diffs, v * ys + y + 1, value)
+    sides = (-1, 0, rows, rows + 1)
+
+    def place(v, x, ref, slot, beyond_at):
+        for i, y in enumerate(sides):
+            value = inside(ref, slot, y, rows, block) if y == 0 else beyond_at(y)
+            value = value * inverse[x + 1, y + 1 : y + 2, :]
+            if v == 1 and y in (0, rows):
+                middle[y // rows] = value
+            place_column(sums, diffs, v * 4 + i, value)
 
     def copy(v, w):
-        for y in range(ys):
-            sums[v * ys + y] = sums_e[w * ys + y]
-            diffs[v * ys + y] = diffs_e[w * ys + y]
+        for i, y in enumerate(sides):
+            sums[v * 4 + i] = sums_e[w * ys + y + 1]
+            diffs[v * 4 + i] = diffs_e[w * ys + y + 1]
 
     @pl.when(even)
     def _():
-        def outer(y):
-            if 0 <= y < rows:
-                return inside(lower, 0, y, rows, block)
-            return corner(corner_edge, y, rows, block, 8)
-
-        def inner(y):
-            if 0 <= y < rows:
-                return inside(own, 0, y, rows, block)
-            return beyond(y_own, 0, y, rows, block)
-
-        place(0, -1, outer)
-        place(1, 0, inner)
+        place(0, -1, lower, 0, lambda y: corner(corners, 1, y, rows, block))
+        place(1, 0, own, 0, lambda y: beyond(y_own, 0, y, rows, block))
         copy(2, 0)
 
     @pl.when(jnp.logical_not(even))
     def _():
-        def outer(slot, corner_ref, gap):
-            def read(y):
-                if 0 <= y < rows:
-                    return inside(upper, slot, y, rows, block)
-                return corner(corner_ref, y, rows, block, gap)
-
-            return read
-
         copy(0, planes)
-        place(1, planes, outer(0, corner_edge, 8))
-        place(2, planes + 1, outer(1, corner_second, 0))
-
-    nodes_y = rows + 1
-    for column in range(nodes_y):
-        acc_s[column] = jnp.zeros((block, LANES), f32)
-        acc_d[column] = jnp.zeros((block, LANES), f32)
+        place(1, planes, upper, 0, lambda y: corner(corners, 0, y, rows, block))
+        place(2, planes + 1, upper, 1, lambda y: corner(corners, 1, y, rows, block))
+
+    def find_low(row):
+        return (sums, diffs, 4, row) if row < 2 else (sums_m, diffs_m, inner, 0)
+
+    def find_high(row):
+        return (sums, diffs, 4, row + 1) if row else (sums_m, diffs_m, inner, inner - 1)
+
     layer = jnp.where(even, 1, planes + 1)
-    apply_elements(sums, diffs, stiff_ref, acc_s, acc_d, 2, rows + 2, 1, layer, 1, cases)
-
-    def total(x, y, early, main):
-        low = ([x - 1] if x >= 1 else [], [x + 1] if x <= 1 else [])
-        high = ([x + 1] if x < planes else [], [x - planes + 1] if x >= planes - 1 else [])
-        if low[0] and low[1] and high[0] and high[1]:
-            one = early[jnp.where(even, low[0][0], high[0][0]) * nodes_y + y]
-            return one + main[jnp.where(even, low[1][0], high[1][0]) * nodes_y + y]
-
-        def read(places):
-            found = [early[w * nodes_y + y] for w in places[0]]
-            found += [main[v * nodes_y + y] for v in places[1]]
-            return found[0] if len(found) == 1 else found[0] + found[1]
-
-        return jnp.where(even, read(low), read(high))
+    apply_elements(find_low, stiff_ref, acc_s0, acc_d0, 2, 2, range(1, 3), layer, 1, cases)
+    apply_elements(find_high, stiff_ref, acc_s1, acc_d1, 2, 2, range(2), layer, rows + 1, cases)
 
     def image(x, y, place):
-        s, d = total(x, y, acc_se, acc_s), total(x, y, acc_de, acc_d)
+        def total(early, near, low, high):
+            def outer(v):
+                value = low[v * 2 + y] if y < 2 else high[v * 2 + y - inner]
+                return value + near[v * inner + y - 1] if y in (1, inner) else value
+
+            return merged(x, planes, even, lambda w: early[w * nodes_y + y], outer)
+
+        s = total(acc_se, acc_sm, acc_s0, acc_s1)
+        d = total(acc_de, acc_dm, acc_d0, acc_d1)
         force = s - d + shift_up(s + d)
-        scaled = force * inverse[x + 1, pl.ds(y + 1, 1), :]
-        place_column(w_sums, w_diffs, x * nodes_y + y, scaled)
-        if x == 0:
-            value = jnp.where(even, middle[y + 1], start[ys + y + 1])
-        elif x == planes:
-            value = jnp.where(even, start[(planes - 1) * ys + y + 1], middle[y + 1])
-        else:
-            value = start[jnp.where(even, x - 1, x + 1) * ys + y + 1]
-        for k in range(3):
-            lines = slice(k * cases, (k + 1) * cases)
-            both = jnp.concatenate([value[lines], scaled[lines]], 0)
-            lane = pl.ds(pl.multiple_of((place * 3 + k) * LANES, LANES), LANES)
-            high, rest = split(both)
-            both_out[0 : 2 * cases, lane] = high
-            both_out[2 * cases : 4 * cases, lane] = rest
+        scaled = force * inverse[x + 1, y + 1 : y + 2, :]
+        place_column(w_sums, w_diffs, x * len(rim) + rim.index(y), scaled)
+        inner_middle = middle_m[y - 1] if y in (1, inner) else middle[y // rows]
+        value = direction_at(x, planes, even, lambda w: start[w * ys + y + 1], inner_middle)
+        keep_pair(both_out, place, value, scaled, cases)
         return force
 
-    two = 2 * cases
-    count = planes * rows
-
-    def within(x, y):
-        index = x * rows + y
+    for index, (x, y) in enumerate(columns):
         force = image(x, y, index)
-        given = own[pl.ds(pl.multiple_of(index * block, 8), block), :]
-        for k in range(3):
-            lines = slice(k * cases, (k + 1) * cases)
-            both = jnp.concatenate([given[lines], force[lines]], 0)
-            lane = pl.ds(pl.multiple_of((index * 3 + k) * LANES, LANES), LANES)
-            high, rest = split(both)
-            right[0:two, lane] = high
-            right[two : 2 * two, lane] = rest
-
-    for x in range(planes):
-        unrolled(rows, 4, functools.partial(within, x))
-        image(x, rows, count + x)
-    unrolled(nodes_y, 3, lambda y: image(planes, y, count + planes + y))
-    rest = right.shape[1] - count * 3 * LANES
-    right[0 : 2 * two, count * 3 * LANES :] = jnp.zeros((2 * two, rest), bf16)
-
-    for column in range(nodes_y):
-        acc2_s[column] = jnp.zeros((block, LANES), f32)
-        acc2_d[column] = jnp.zeros((block, LANES), f32)
-    apply_elements(w_sums, w_diffs, stiff_ref, acc2_s, acc2_d, planes, rows, 0, 2, 2, cases)
-
-    def second_force(x, y, place):
+        if index < own_count:
+            keep_pair(right, index, inside(own, x, y, rows, block), force, cases)
+
+    def find(row):
+        if row in rim:
+            return w_sums, w_diffs, len(rim), rim.index(row)
+        return w_sm, w_dm, len(core), row - core[0]
+
+    apply_elements(find, stiff_ref, acc2_s, acc2_d, planes, rows, range(nodes_y), 2, 2, cases)
+
+    def second_force(ref, x, y, place):
         column = x * nodes_y + y
         s, d = acc2_s[column], acc2_d[column]
         force = s - d + shift_up(s + d)
@@ -505,17 +600,20 @@
             value = force[k * cases : (k + 1) * cases]
             high = value.astype(bf16).astype(f32)
             lane = pl.ds(pl.multiple_of((place * 3 + k) * LANES, LANES), LANES)
-            right[2 * two :, lane] = jnp.concatenate([high, value - high], 0).astype(bf16)
-
-    unrolled(count, 4, lambda index: second_force(index // rows, index % rows, index))
-    unrolled(planes, 2, lambda x: second_force(x, rows, count + x))
-    unrolled(nodes_y, 3, lambda y: second_force(planes, y, count + planes + y))
-
-    contract = (((1,), (1,)), ((), ()))
-    product = lax.dot_general(right[...], both_out[...], contract, preferred_element_type=f32)
-    product = product[:, :two] + product[:, two:]
-    gram = product[:two] + product[two : 2 * two]
-    other = product[2 * two : 2 * two + cases] + product[2 * two + cases :]
+            ref[:, lane] = jnp.concatenate([high, value - high], 0).astype(bf16)
+
+    unrolled(
+        (planes + 1) * len(core), len(core),
+        lambda index: second_force(
+            second_m, index // len(core), core[0] + index % len(core), index
+        ),
+    )
+    for index, (x, y) in enumerate(columns):
+        second_force(second_r, x, y, index)
+
+    two = 2 * cases
+    gram = products(right[...], both_out[:, : own_count * 3 * LANES]) + gram_m[...]
+    other = products(second_m[...], both_m[...]) + products(second_r[...], both_out[...])
     row = lax.broadcasted_iota(jnp.int32, (cases, cases), 0)
     column = lax.broadcasted_iota(jnp.int32, (cases, cases), 1)
     load_load, load_image = gram[:cases, :cases], gram[cases:, :cases]
@@ -535,7 +633,7 @@
 
 
 def solve_kernel(
-    sizes, system, system_pair, both, codes, out, mixing, sums, diffs, energy, square, full
+    sizes, system, system_pair, both_m, both_r, codes, out, mixing, sums, diffs, energy, square, full
 ):
     planes, rows, cases = sizes
     two = 2 * cases
@@ -607,9 +705,10 @@
     mixing[cases:two, 0:two] = answer - high
     mix = mixing[...][:, : 2 * two].astype(bf16)
 
-    def combined(place, width):
-        lanes = pl.ds(pl.multiple_of(place * 3 * LANES, LANES), width * 3 * LANES)
-        value = jnp.dot(mix, both[:, lanes], preferred_element_type=f32)
+    def combined(ref, place, width):
+        value = jnp.dot(
+            mix, ref[:, place * 3 * LANES : (place + width) * 3 * LANES], preferred_element_type=f32
+        )
         return value[:cases] + value[cases:]
 
     def keep(value, index, column):
@@ -619,26 +718,26 @@
             sums[column, k * cases : (k + 1) * cases, :] = part + moved
             diffs[column, k * cases : (k + 1) * cases, :] = moved - part
 
-    def inside(x, _):
-        value = combined(x * rows, rows)
-        for y in range(rows):
-            keep(value, y, x * nodes_y + y)
-        return 0
-
-    lax.fori_loop(0, planes, inside, 0)
-    value = combined(count, planes + nodes_y)
-    for x in range(planes):
-        keep(value, x, x * nodes_y + rows)
-    for y in range(nodes_y):
-        keep(value, planes + y, planes * nodes_y + y)
-
+    core = core_rows(rows)
+    for x in range(planes + 1):
+        value = combined(both_m, x * len(core), len(core))
+        for index, y in enumerate(core):
+            keep(value, index, x * nodes_y + y)
+    columns, _ = rim_columns(planes, rows)
+    for start in range(0, len(columns), 6):
+        some = columns[start : start + 6]
+        value = combined(both_r, start, len(some))
+        for index, (x, y) in enumerate(some):
+            keep(value, index, x * nodes_y + y)
+
+    find = whole(sums, diffs, nodes_y)
     tiles = cases // 8
 
     def step(plane, _):
         for tile in range(tiles):
-            lower = x_modes(sums, diffs, plane, 0, tile, cases, nodes_y)
+            lower = x_modes(find, plane, 0, tile, cases)
             for row in range(rows):
-                upper = x_modes(sums, diffs, plane, row + 1, tile, cases, nodes_y)
+                upper = x_modes(find, plane, row + 1, tile, cases)
                 part = mode_energy(modes_of(lower, upper))
                 if tile == 0:
                     energy[row] = part
@@ -773,19 +872,16 @@
     )(own)
     from_yp, from_ym = moved(ym, "gy", -1), moved(yp, "gy", 1)
     pair_yp, pair_ym = swapped(from_yp), swapped(from_ym)
-    corner_edge, corner_second = pl.pallas_call(
-        functools.partial(corner_kernel, sizes),
-        out_shape=[
-            jax.ShapeDtypeStruct((3 * block + 16, LANES), f32),
-            jax.ShapeDtypeStruct((3 * block, LANES), f32),
-        ],
-        in_specs=[scalars] + [VMEM] * 2,
-        out_specs=[VMEM] * 2,
-        compiler_params=PARAMS,
-        name="corners",
-    )(start, from_ym, from_yp)
-    corner_edge = across(corner_edge)
-    corner_second = lax.ppermute(corner_second, "gx", links(2, -1))
+    corners = across(
+        pl.pallas_call(
+            functools.partial(corner_kernel, sizes),
+            out_shape=jax.ShapeDtypeStruct((6 * block + 16, LANES), f32),
+            in_specs=[scalars] + [VMEM] * 2,
+            out_specs=VMEM,
+            compiler_params=PARAMS,
+            name="corners",
+        )(start, from_ym, from_yp)
+    )
 
     devices = count_x * count_y
     nodes = (planes + 1) * (rows + 1)
@@ -807,30 +903,62 @@
         name="early",
     )(start, own, pair, from_ym, from_yp, pair_ym, pair_yp)
 
-    side = pltpu.VMEM((3 * (rows + 3), block, LANES), f32)
-    acc = pltpu.VMEM((3 * (rows + 1), block, LANES), f32)
-    field = pltpu.VMEM((nodes, block, LANES), f32)
+    def columns(count):
+        return jax.ShapeDtypeStruct((count, block, LANES), f32)
+
+    def fields(lines, count):
+        return jax.ShapeDtypeStruct((lines * cases, count * 3 * LANES), bf16)
+
+    def scratch(value):
+        return pltpu.VMEM(value.shape, value.dtype)
+
+    core = len(core_rows(rows))
+    middle = pl.pallas_call(
+        functools.partial(middle_kernel, sizes),
+        out_shape=[columns(3 * (rows - 1))] * 2
+        + [columns(rows - 1)]
+        + [columns(3 * (rows - 1))] * 2
+        + [columns((planes + 1) * core)] * 2
+        + [fields(4, (planes + 1) * core), jax.ShapeDtypeStruct((2 * cases, 2 * cases), f32)],
+        in_specs=[scalars] + [VMEM] * 9,
+        out_specs=[VMEM] * 9,
+        scratch_shapes=[
+            pltpu.VMEM((planes + 4, up8(rows), LANES), f32),
+            pltpu.VMEM((planes + 3, up8(rows), LANES), f32),
+            scratch(fields(4, planes * core)),
+        ],
+        compiler_params=PARAMS,
+        name="middle",
+    )(start, own, pair, lower, upper, *early)
+
+    rim, rim_own = rim_columns(planes, rows)
+    field = scratch(columns(nodes))
     both, system = pl.pallas_call(
         functools.partial(main_kernel, sizes),
         out_shape=[
-            jax.ShapeDtypeStruct((4 * cases, nodes * 3 * LANES), bf16),
+            fields(4, len(rim)),
             jax.ShapeDtypeStruct((devices // 2, cases // 8, 4, LANES), f32),
         ],
-        in_specs=[scalars] + [VMEM] * 15,
+        in_specs=[scalars] + [VMEM] * 23,
         out_specs=[VMEM] * 2,
         scratch_shapes=[
             pltpu.VMEM((planes + 4, up8(rows + 4), LANES), f32),
             pltpu.VMEM((planes + 3, up8(rows + 3), LANES), f32),
-            pltpu.VMEM((rows + 3, block, LANES), f32),
-            side, side, acc, acc, field, field, field, field,
-            pltpu.VMEM((6 * cases, nodes * 3 * LANES), bf16),
+            scratch(columns(2)),
+            *[scratch(columns(12))] * 2,
+            *[scratch(columns(6))] * 4,
+            *[scratch(columns((planes + 1) * 4))] * 2,
+            field, field,
+            scratch(fields(4, rim_own)),
+            scratch(fields(2, (planes + 1) * core)),
+            scratch(fields(2, len(rim))),
             pltpu.VMEM((cases, LANES), f32),
         ],
         compiler_params=PARAMS,
         name="operator",
     )(
-        start, own, pair, lower, upper, from_ym, from_yp, pair_ym, pair_yp,
-        corner_edge, corner_second, *early,
+        start, own, pair, lower, upper, from_ym, from_yp, pair_ym, pair_yp, corners,
+        *early, *middle,
     )
 
     groups = [
@@ -847,7 +975,7 @@
     weighted = pl.pallas_call(
         functools.partial(solve_kernel, sizes),
         out_shape=jax.ShapeDtypeStruct((devices // 2, planes, rows, LANES), f32),
-        in_specs=[VMEM] * 4,
+        in_specs=[VMEM] * 5,
         out_specs=VMEM,
         scratch_shapes=[
             pltpu.VMEM((2 * cases, LANES), f32),
@@ -859,7 +987,7 @@
         ],
         compiler_params=PARAMS,
         name="solve",
-    )(*system, both, codes)
+    )(*system, middle[7], both, codes)
 
     blocks = gathered(weighted)
     return pl.pallas_call(

time: 66.4 us -> 65 us (0.979)
  blocking collectives: 31.1 us -> 27.2 us
  waiting for transfers between devices: 3.99 us -> 6.06 us
  starting transfers between devices: 12.6 us -> 13.5 us
    all_to_all x2, blocking collectives: 31.1 us -> 27.2 us  [gathered(): mine = lax.all_to_all(copies, ('gx', 'gy'), 0, 0, axis_index_groups=groups)]
    ppermute x5, starting transfers between devices: 3.08 us -> 4.7 us  [swapped(): return lax.ppermute(value, 'gx', links(0, 1) + links(1, -1))]
    ppermute x5, waiting for transfers between devices: 2.67 us -> 4.13 us  [swapped(): return lax.ppermute(value, 'gx', links(0, 1) + links(1, -1))]
    ppermute x1 -> x0, starting transfers between devices: 0.67 us -> none  [local(): corner_second = lax.ppermute(corner_second, 'gx', links(2, -1))]
    pallas_call x2 -> x3, Pallas kernels: 7.87 us -> 7.92 us  [the longest x1 4.83 us: local(): pl.pallas_call(functools.partial(main_kernel, sizes), out_shape=[fields(4...]
  transfers between devices with their start and end apart: 11 -> 10, of which waited for: 4 -> 5; matrix products, arithmetic and copies ran while one was open for 0% -> 0% of each run, Pallas kernels for 6% -> 10%
where the time goes in v12:
time: 65 us; the launch traced here: 64.6 us
  blocking collectives  27.2 us (42%)
  Pallas kernels  15.8 us (24%)
  starting transfers between devices  13.5 us (21%)
  waiting for transfers between devices  6.06 us (9%)
  local copies, waits for them, and re-layouts  1.07 us (2%)
  other arithmetic  0.8 us (1%)
    all_to_all x2, blocking collectives, gathered(): mine = lax.all_to_all(copies, ('gx', 'gy'), 0, 0, axis_index_groups=groups)  27.2 us
    ppermute x2, starting transfers between devices, moved(): return lax.ppermute(value, axis, pairs)  6.77 us
    pallas_call x1, Pallas kernels, local(): pl.pallas_call(functools.partial(main_kernel, sizes), out_shape=[fields(4...  4.83 us
    ppermute x5, starting transfers between devices, swapped(): return lax.ppermute(value, 'gx', links(0, 1) + links(1, -1))  4.7 us
    ppermute x5, waiting for transfers between devices, swapped(): return lax.ppermute(value, 'gx', links(0, 1) + links(1, -1))  4.13 us
    pallas_call x1, Pallas kernels, local(): pl.pallas_call(functools.partial(solve_kernel, sizes), out_shape=jax.Shap...  3.45 us
    pallas_call x1, Pallas kernels, local(): pl.pallas_call(functools.partial(middle_kernel, sizes), out_shape=[column...  2.53 us
    pallas_call x1, Pallas kernels, local(): pl.pallas_call(functools.partial(early_kernel, sizes), out_shape=[window]...  2.38 us
  transfers between devices with their start and end apart: 10, of which 5 were waited for; matrix products, arithmetic and copies ran while one was open for 0% of the time, Pallas kernels for 10%

profile of v12, /device:TPU:0, one launch (start us, length us, event | category | flops | bytes accessed | tf_op | source)
XLA Modules:
  0.0 64.6 jit_solution(15335499951656360650)
XLA Ops:
  0.0 0.7 %negate_select_fusion.codes = f32[2,8,128]{2,1,0:T(8,128)S(1)} fusion(s32[2,8,128]{2,1,0:T(8,128)} %levels.1, s32[2,8,128]{2,1,0:T(8,128)} %param.5), kind=kLoop, calls=%fused_computation | loop fusion | flops 16384 | bytes 24576 | tf_op jit(solution)/shard_map/jit(_where)/select_n | solution.py:822
  0.7 0.0 copy-start
  0.7 1.1 %copy-done = f32[3,24,2,8,128]{4,3,2,1,0:T(8,128)S(1)} copy-done((f32[3,24,2,8,128]{4,3,2,1,0:T(8,128)S(1)}, f32[3,24,2,8,128]{4,3,2,1,0:T(8,128)}, u32[]{:S(2)}) %copy-start) | copy-done | bytes 589848
  1.8 0.1 pack.1
  1.9 0.5 collective-permute-start
  2.4 0.7 %collective-permute-start.2 = (f32[1168,128]{1,0:T(8,128)S(1)}, f32[1168,128]{1,0:T(8,128)S(1)}, u32[]{:S(2)}, u32[]{:S(2)}) collective-permute-start(f32[1168,128]{1,0:T(8,128)S(1)} %get-tuple-element.28.own), channel_id=1, source_target_pairs={{8,4},{16,12},{24,20},{9,5},{17,13},{25,21},{10,6},{18,14},{26,22}... | collective-permute-start | bytes 1794056 | tf_op jit(solution)/shard_map/ppermute | solution.py:861
  3.1 0.9 %collective-permute-done.pair = f32[1168,128]{1,0:T(8,128)S(1)} collective-permute-done((f32[1168,128]{1,0:T(8,128)S(1)}, f32[1168,128]{1,0:T(8,128)S(1)}, u32[]{:S(2)}, u32[]{:S(2)}) %collective-permute-start) | collective-permute-done | bytes 598048 | tf_op jit(solution)/shard_map/ppermute | solution.py:856
  4.1 1.3 %collective-permute-start.4 = (f32[296,128]{1,0:T(8,128)S(1)}, f32[296,128]{1,0:T(8,128)S(1)}, u32[]{:S(2)}, u32[]{:S(2)}) collective-permute-start(f32[296,128]{1,0:T(8,128)S(1)} %get-tuple-element.32), channel_id=1, source_target_pairs={{1,0},{2,1},{3,2},{5,4},{6,5},{7,6},{9,8},{10,9},{11,10},{13,12},{... | collective-permute-start | bytes 454664 | tf_op jit(solution)/shard_map/ppermute | solution.py:850
  5.4 0.7 %collective-permute-start.1 = (f32[592,128]{1,0:T(8,128)S(1)}, f32[592,128]{1,0:T(8,128)S(1)}, u32[]{:S(2)}, u32[]{:S(2)}) collective-permute-start(f32[592,128]{1,0:T(8,128)S(1)} %get-tuple-element.30), channel_id=1, source_target_pairs={{4,8},{12,16},{20,24},{5,9},{13,17},{21,25},{6,10},{14,18},{22,26}... | collective-permute-start | bytes 909320 | tf_op jit(solution)/shard_map/ppermute | solution.py:862
  6.1 5.5 %collective-permute-start.3 = (f32[152,128]{1,0:T(8,128)S(1)}, f32[152,128]{1,0:T(8,128)S(1)}, u32[]{:S(2)}, u32[]{:S(2)}) collective-permute-start(f32[152,128]{1,0:T(8,128)S(1)} %get-tuple-element.31), channel_id=1, source_target_pairs={{0,1},{1,2},{2,3},{4,5},{5,6},{6,7},{8,9},{9,10},{10,11},{12,13},{... | collective-permute-start | bytes 233480 | tf_op jit(solution)/shard_map/ppermute | solution.py:850
  11.6 0.1 pad_add_fusion.first.start
  11.6 1.9 %collective-permute-done.3.ym = f32[152,128]{1,0:T(8,128)S(1)} collective-permute-done((f32[152,128]{1,0:T(8,128)S(1)}, f32[152,128]{1,0:T(8,128)S(1)}, u32[]{:S(2)}, u32[]{:S(2)}) %collective-permute-start.3) | collective-permute-done | bytes 77856 | tf_op jit(solution)/shard_map/ppermute | solution.py:850
  13.6 0.0 collective-permute-done.4.yp
  13.6 0.6 corners.1
  14.1 0.7 %collective-permute-start.7 = (f32[448,128]{1,0:T(8,128)S(1)}, f32[448,128]{1,0:T(8,128)S(1)}, u32[]{:S(2)}, u32[]{:S(2)}) collective-permute-start(f32[448,128]{1,0:T(8,128)S(1)} %corners.1), channel_id=1, source_target_pairs={{4,8},{12,16},{20,24},{8,4},{16,12},{24,20},{5,9},{13,17},{21,25},... | collective-permute-start | bytes 688136 | tf_op jit(solution)/shard_map/ppermute | solution.py:859
  14.8 4.1 %collective-permute-start.6 = (f32[296,128]{1,0:T(8,128)S(1)}, f32[296,128]{1,0:T(8,128)S(1)}, u32[]{:S(2)}, u32[]{:S(2)}) collective-permute-start(f32[296,128]{1,0:T(8,128)S(1)} %collective-permute-done.4.yp), channel_id=1, source_target_pairs={{0,4},{8,12},{16,20},{24,28},{4,0},{12,8},{20,16},{28,24},{1,5},{9... | collective-permute-start | bytes 454664 | tf_op jit(solution)/shard_map/ppermute | solution.py:856
  18.9 0.1 collective-permute-start.5
  19.0 1.2 %collective-permute-done.5.ym_pair = f32[152,128]{1,0:T(8,128)S(1)} collective-permute-done((f32[152,128]{1,0:T(8,128)S(1)}, f32[152,128]{1,0:T(8,128)S(1)}, u32[]{:S(2)}, u32[]{:S(2)}) %collective-permute-start.5) | collective-permute-done | bytes 77856 | tf_op jit(solution)/shard_map/ppermute | solution.py:856
  20.2 0.0 collective-permute-done.6.yp_pair
  20.2 2.4 %early.1 = (f32[33,72,128]{2,1,0:T(8,128)S(1)}, f32[33,72,128]{2,1,0:T(8,128)S(1)}, f32[33,72,128]{2,1,0:T(8,128)S(1)}, f32[27,72,128]{2,1,0:T(8,128)S(1)}, f32[27,72,128]{2,1,0:T(8,128)S(1)}) custom-call(s32[2]{0:T(128)S(1)} %pad_add_fusion.first.start, f32[1168,128]{1,0:T(8,128)S(1)} %get-tuple-element.28.own, f32[1168,128]{1,0:T(8,128)S(1)} %collective-permute-done.pair, ...), custom_call_target="tpu_custom_call" | custom-call | flops 29491200 | bytes 8388608 | tf_op jit(solution)/shard_map/early/pallas_call | solution.py:890
  22.6 0.0 collective-permute-done.1.lower
  22.6 0.0 collective-permute-done.2.upper
  22.6 2.5 %middle.1 = (f32[21,72,128]{2,1,0:T(8,128)S(1)}, f32[21,72,128]{2,1,0:T(8,128)S(1)}, f32[7,72,128]{2,1,0:T(8,128)S(1)}, f32[21,72,128]{2,1,0:T(8,128)S(1)}, f32[...) custom-call(s32[2]{0:T(128)S(1)} %pad_add_fusion.first.start, ...), custom_call_target="tpu_custom_call" | custom-call | tf_op jit(solution)/shard_map/middle/pallas_call | solution.py:916
  25.1 0.0 collective-permute-done.7.corners
  25.2 4.8 %operator.1 = (bf16[96,4608]{1,0:T(8,128)(2,1)S(1)}, f32[16,3,4,128]{3,2,1,0:T(4,128)S(1)}) custom-call(s32[2]{0:T(128)S(1)} %pad_add_fusion.first.start, f32[1168,128]{1,0:T(8,128)S(1)} %get-tuple-element.28.own, f32[1168,128]{1,0:T(8,128)S(1)} %collective-permute-done.pair, f32[592,128]{1,0:T(8,128)S(1)} %collective-permute-done.1.lower, ...), custom_call_target="tpu_custom_call" | custom-call | tf_op jit(solution)/shard_map/operator/pallas_call | solution.py:936
  30.0 16.3 %all_to_all.10.system = f32[16,3,4,128]{3,2,1,0:T(4,128)S(1)} all-to-all(f32[16,3,4,128]{3,2,1,0:T(4,128)S(1)} %get-tuple-element.47), channel_id=1, replica_groups={{0,1,2,3,8,9,10,11,16,17,18,19,24,25,26,27},{4,5,6,7,12,13,14,15,20,21,..., dimensions={0} | all-to-all | bytes 196608 | tf_op jit(solution)/shard_map/all_to_all | solution.py:970
  46.3 0.0 collective-permute-start.8
  46.3 1.3 %collective-permute-done.8.system_pair = f32[16,3,4,128]{3,2,1,0:T(4,128)S(1)} collective-permute-done((f32[16,3,4,128]{3,2,1,0:T(4,128)S(1)}, f32[16,3,4,128]{3,2,1,0:T(4,128)S(1)}, u32[]{:S(2)}, u32[]{:S(2)}) %collective-permute-start.8) | collective-permute-done | bytes 98336 | tf_op jit(solution)/shard_map/ppermute | solution.py:856
  47.6 0.0 copy-start.1
  47.6 3.4 %solve.1 = f32[16,2,8,128]{3,2,1,0:T(8,128)S(1)} custom-call(f32[16,3,4,128]{3,2,1,0:T(4,128)S(1)} %all_to_all.10.system, f32[16,3,4,128]{3,2,1,0:T(4,128)S(1)} %collective-permute-done.8.system_pair, bf16[96,5760]{1,0:T(8,128)(2,1)S(1)} %get-tuple-element.45.both_m, bf16[96,4608]{1,0:T(8,128)(2,1)S(1)} %get-tuple-element.48.both_r, ...), custom_call_target="tpu_custom_call" | custom-call | tf_op jit(solution)/shard_map/solve/pallas_call | solution.py:975
  51.1 10.9 %all_to_all.11.blocks = f32[16,2,8,128]{3,2,1,0:T(8,128)S(1)} all-to-all(f32[16,2,8,128]{3,2,1,0:T(8,128)S(1)} %solve.1), channel_id=1, replica_groups={{0,1,2,3,8,9,10,11,16,17,18,19,24,25,26,27},{4,5,6,7,12,13,14,15,20,21,..., dimensions={0} | all-to-all | bytes 262144 | tf_op jit(solution)/shard_map/all_to_all | solution.py:970
  62.0 0.0 collective-permute-start.9
  62.0 0.0 copy-done.1
  62.0 0.7 %scale.1 = f32[2,8,128]{2,1,0:T(8,128)S(1)} custom-call(s32[2]{0:T(128)S(1)} %pad_add_fusion.first.start, s32[2,8,128]{2,1,0:T(8,128)S(1)} %copy-done.1), custom_call_target="tpu_custom_call" | custom-call | tf_op jit(solution)/shard_map/scale/pallas_call | solution.py:837
  62.6 0.7 %collective-permute-done.9.blocks_pair = f32[16,2,8,128]{3,2,1,0:T(8,128)S(1)} collective-permute-done((f32[16,2,8,128]{3,2,1,0:T(8,128)S(1)}, f32[16,2,8,128]{3,2,1,0:T(8,128)S(1)}, u32[]{:S(2)}, u32[]{:S(2)}) %collective-permute-start.9) | collective-permute-done | bytes 131104 | tf_op jit(solution)/shard_map/ppermute | solution.py:856
  63.3 1.3 %cone.1 = f32[2,8,128]{2,1,0:T(8,128)} custom-call(s32[2]{0:T(128)S(1)} %pad_add_fusion.first.start, f32[16,2,8,128]{3,2,1,0:T(8,128)S(1)} %all_to_all.11.blocks, f32[16,2,8,128]{3,2,1,0:T(8,128)S(1)} %collective-permute-done.9.blocks_pair, f32[2,8,128]{2,1,0:T(8,128)S(1)} %scale.1), custom_call_target="tpu_custom_call" | custom-call | tf_op jit(solution)/shard_map/cone/pallas_call | solution.py:993
  (1 shorter events, 0.0 us)
Async XLA Ops:
  0.7 1.1 %copy-start = (f32[3,24,2,8,128]{4,3,2,1,0:T(8,128)S(1)}, f32[3,24,2,8,128]{4,3,2,1,0:T(8,128)}, u32[]{:S(2)}) copy-start(f32[3,24,2,8,128]{4,3,2,1,0:T(8,128)} %forces.1) | copy-start | bytes 1769476
  1.9 2.2 %collective-permute-start = (f32[1168,128]{1,0:T(8,128)S(1)}, f32[1168,128]{1,0:T(8,128)S(1)}, u32[]{:S(2)}, u32[]{:S(2)}) collective-permute-start(f32[1168,128]{1,0:T(8,128)S(1)} %get-tuple-element.28.own), channel_id=1, source_target_pairs={{0,4},{8,12},{16,20},{24,28},{4,0},{12,8},{20,16},{28,24},{1,5},{9... | collective-permute-start | bytes 1794056 | tf_op jit(solution)/shard_map/ppermute | solution.py:856
  2.4 20.2 %collective-permute-start.2 = (f32[1168,128]{1,0:T(8,128)S(1)}, f32[1168,128]{1,0:T(8,128)S(1)}, u32[]{:S(2)}, u32[]{:S(2)}) collective-permute-start(f32[1168,128]{1,0:T(8,128)S(1)} %get-tuple-element.28.own), channel_id=1, source_target_pairs={{8,4},{16,12},{24,20},{9,5},{17,13},{25,21},{10,6},{18,14},{26,22}... | collective-permute-start | bytes 1794056 | tf_op jit(solution)/shard_map/ppermute | solution.py:861
  4.1 9.5 %collective-permute-start.4 = (f32[296,128]{1,0:T(8,128)S(1)}, f32[296,128]{1,0:T(8,128)S(1)}, u32[]{:S(2)}, u32[]{:S(2)}) collective-permute-start(f32[296,128]{1,0:T(8,128)S(1)} %get-tuple-element.32), channel_id=1, source_target_pairs={{1,0},{2,1},{3,2},{5,4},{6,5},{7,6},{9,8},{10,9},{11,10},{13,12},{... | collective-permute-start | bytes 454664 | tf_op jit(solution)/shard_map/ppermute | solution.py:850
  5.4 17.2 %collective-permute-start.1 = (f32[592,128]{1,0:T(8,128)S(1)}, f32[592,128]{1,0:T(8,128)S(1)}, u32[]{:S(2)}, u32[]{:S(2)}) collective-permute-start(f32[592,128]{1,0:T(8,128)S(1)} %get-tuple-element.30), channel_id=1, source_target_pairs={{4,8},{12,16},{20,24},{5,9},{13,17},{21,25},{6,10},{14,18},{22,26}... | collective-permute-start | bytes 909320 | tf_op jit(solution)/shard_map/ppermute | solution.py:862
  6.1 7.5 %collective-permute-start.3 = (f32[152,128]{1,0:T(8,128)S(1)}, f32[152,128]{1,0:T(8,128)S(1)}, u32[]{:S(2)}, u32[]{:S(2)}) collective-permute-start(f32[152,128]{1,0:T(8,128)S(1)} %get-tuple-element.31), channel_id=1, source_target_pairs={{0,1},{1,2},{2,3},{4,5},{5,6},{6,7},{8,9},{9,10},{10,11},{12,13},{... | collective-permute-start | bytes 233480 | tf_op jit(solution)/shard_map/ppermute | solution.py:850
  14.1 11.0 %collective-permute-start.7 = (f32[448,128]{1,0:T(8,128)S(1)}, f32[448,128]{1,0:T(8,128)S(1)}, u32[]{:S(2)}, u32[]{:S(2)}) collective-permute-start(f32[448,128]{1,0:T(8,128)S(1)} %corners.1), channel_id=1, source_target_pairs={{4,8},{12,16},{20,24},{8,4},{16,12},{24,20},{5,9},{13,17},{21,25},... | collective-permute-start | bytes 688136 | tf_op jit(solution)/shard_map/ppermute | solution.py:859
  14.8 5.4 %collective-permute-start.6 = (f32[296,128]{1,0:T(8,128)S(1)}, f32[296,128]{1,0:T(8,128)S(1)}, u32[]{:S(2)}, u32[]{:S(2)}) collective-permute-start(f32[296,128]{1,0:T(8,128)S(1)} %collective-permute-done.4.yp), channel_id=1, source_target_pairs={{0,4},{8,12},{16,20},{24,28},{4,0},{12,8},{20,16},{28,24},{1,5},{9... | collective-permute-start | bytes 454664 | tf_op jit(solution)/shard_map/ppermute | solution.py:856
  18.9 1.3 %collective-permute-start.5 = (f32[152,128]{1,0:T(8,128)S(1)}, f32[152,128]{1,0:T(8,128)S(1)}, u32[]{:S(2)}, u32[]{:S(2)}) collective-permute-start(f32[152,128]{1,0:T(8,128)S(1)} %collective-permute-done.3.ym), channel_id=1, source_target_pairs={{0,4},{8,12},{16,20},{24,28},{4,0},{12,8},{20,16},{28,24},{1,5},{9... | collective-permute-start | bytes 233480 | tf_op jit(solution)/shard_map/ppermute | solution.py:856
  46.3 1.3 %collective-permute-start.8 = (f32[16,3,4,128]{3,2,1,0:T(4,128)S(1)}, f32[16,3,4,128]{3,2,1,0:T(4,128)S(1)}, u32[]{:S(2)}, u32[]{:S(2)}) collective-permute-start(f32[16,3,4,128]{3,2,1,0:T(4,128)S(1)} %all_to_all.10.system), channel_id=1, source_target_pairs={{0,4},{8,12},{16,20},{24,28},{4,0},{12,8},{20,16},{28,24},{1,5},{9... | collective-permute-start | bytes 294920 | tf_op jit(solution)/shard_map/ppermute | solution.py:856
  47.6 14.3 %copy-start.1 = (s32[2,8,128]{2,1,0:T(8,128)S(1)}, s32[2,8,128]{2,1,0:T(8,128)}, u32[]{:S(2)}) copy-start(s32[2,8,128]{2,1,0:T(8,128)} %levels.1) | copy-start | bytes 24580
  62.0 1.3 %collective-permute-start.9 = (f32[16,2,8,128]{3,2,1,0:T(8,128)S(1)}, f32[16,2,8,128]{3,2,1,0:T(8,128)S(1)}, u32[]{:S(2)}, u32[]{:S(2)}) collective-permute-start(f32[16,2,8,128]{3,2,1,0:T(8,128)S(1)} %all_to_all.11.blocks), channel_id=1, source_target_pairs={{0,4},{8,12},{16,20},{24,28},{4,0},{12,8},{20,16},{28,24},{1,5},{9... | collective-permute-start | bytes 393224 | tf_op jit(solution)/shard_map/ppermute | solution.py:856

commit v13 on v12

--- a/solution.py
+++ b/solution.py
@@ -214,7 +214,7 @@
         ref[line:, :] = jnp.zeros((ref.shape[0] - line, LANES), f32)
 
 
-def pack_kernel(sizes, forces, codes, own, up, *down):
+def pack_kernel(sizes, forces, codes, own, *down):
     planes, rows, cases = sizes
     block = 3 * cases
     base = planes * rows * block
@@ -226,10 +226,15 @@
                 start = x * rows * block + k * cases + c
                 own[pl.ds(start, rows, stride=block), :] = forces[k, c, x] * scale
 
-    every_y, last = range(rows), (planes - 2, planes - 1)
-    fill(own, base, sizes, up, last[1:], every_y, last, every_y)
+    every_y = range(rows)
     for ref in down:
         fill(own, base, sizes, ref, (0, 1), every_y, (0, 1), every_y)
+
+
+def up_kernel(sizes, begun, own, up):
+    planes, rows, cases = sizes
+    last, every_y = (planes - 2, planes - 1), range(rows)
+    fill(own, planes * rows * 3 * cases, sizes, up, last[1:], every_y, last, every_y)
 
 
 def rows_kernel(sizes, own, ym, yp):
@@ -826,11 +831,11 @@
     scalars = pl.BlockSpec(memory_space=pltpu.SMEM)
     whole = shape(planes * rows, planes * rows)
     down = [] if planes == 2 else [shape(2 * rows, 2 * rows)]
-    own, up, *down = pl.pallas_call(
+    own, *down = pl.pallas_call(
         functools.partial(pack_kernel, sizes),
-        out_shape=[whole, shape(rows, 2 * rows), *down],
+        out_shape=[whole, *down],
         in_specs=[VMEM] * 2,
-        out_specs=[VMEM] * (2 + len(down)),
+        out_specs=[VMEM] * (1 + len(down)),
         compiler_params=PARAMS,
         name="pack",
     )(forces, codes)
@@ -859,7 +864,6 @@
         return lax.ppermute(value, "gx", links(1, 1) + links(2, -1))
 
     upper = lax.ppermute(down[0] if down else own, "gx", links(2, -1))
-    lower = lax.ppermute(up, "gx", links(1, 1))
     pair = swapped(own)
     own, pair = lax.optimization_barrier((own, pair))
     ym, yp = pl.pallas_call(
@@ -871,6 +875,15 @@
         name="rows",
     )(own)
     from_yp, from_ym = moved(ym, "gy", -1), moved(yp, "gy", 1)
+    up = pl.pallas_call(
+        functools.partial(up_kernel, sizes),
+        out_shape=shape(rows, 2 * rows),
+        in_specs=[VMEM] * 2,
+        out_specs=VMEM,
+        compiler_params=PARAMS,
+        name="up",
+    )(swapped(codes), own)
+    lower = lax.ppermute(up, "gx", links(1, 1))
     pair_yp, pair_ym = swapped(from_yp), swapped(from_ym)
     corners = across(
         pl.pallas_call(

time: 65 us -> 63.2 us (0.972)
  blocking collectives: 27.2 us -> 26.4 us
    all_to_all x2, blocking collectives: 27.2 us -> 26.4 us  [gathered(): mine = lax.all_to_all(copies, ('gx', 'gy'), 0, 0, axis_index_groups=groups)]
    ppermute x5 -> x6, starting transfers between devices: 4.7 us -> 4.53 us  [swapped(): return lax.ppermute(value, 'gx', links(0, 1) + links(1, -1))]
    ppermute x5 -> x6, waiting for transfers between devices: 4.13 us -> 4.13 us  [swapped(): return lax.ppermute(value, 'gx', links(0, 1) + links(1, -1))]
  transfers between devices with their start and end apart: 10 -> 11, of which waited for: 5 -> 5; matrix products, arithmetic and copies ran while one was open for 0% -> 0% of each run, Pallas kernels for 10% -> 10%
where the time goes in v13:
time: 63.2 us; the launch traced here: 62.8 us
  blocking collectives  26.4 us (42%)
  Pallas kernels  15.8 us (25%)
  starting transfers between devices  13.1 us (21%)
  waiting for transfers between devices  5.45 us (9%)
  local copies, waits for them, and re-layouts  1.07 us (2%)
  other arithmetic  0.8 us (1%)
    all_to_all x2, blocking collectives, gathered(): mine = lax.all_to_all(copies, ('gx', 'gy'), 0, 0, axis_index_groups=groups)  26.4 us
    ppermute x2, starting transfers between devices, moved(): return lax.ppermute(value, axis, pairs)  6.54 us
    pallas_call x1, Pallas kernels, local(): pl.pallas_call(functools.partial(main_kernel, sizes), out_shape=[fields(4...  4.83 us
    ppermute x6, starting transfers between devices, swapped(): return lax.ppermute(value, 'gx', links(0, 1) + links(1, -1))  4.53 us
    ppermute x6, waiting for transfers between devices, swapped(): return lax.ppermute(value, 'gx', links(0, 1) + links(1, -1))  4.13 us
    pallas_call x1, Pallas kernels, local(): pl.pallas_call(functools.partial(solve_kernel, sizes), out_shape=jax.Shap...  3.45 us
    pallas_call x1, Pallas kernels, local(): pl.pallas_call(functools.partial(middle_kernel, sizes), out_shape=[column...  2.53 us
    pallas_call x1, Pallas kernels, local(): pl.pallas_call(functools.partial(early_kernel, sizes), out_shape=[window]...  2.38 us
  transfers between devices with their start and end apart: 11, of which 5 were waited for; matrix products, arithmetic and copies ran while one was open for 0% of the time, Pallas kernels for 10%

profile of v13, /device:TPU:0, one launch (start us, length us, event | category | flops | bytes accessed | tf_op | source)
XLA Modules:
  0.0 62.8 jit_solution(14858563110594344924)
XLA Ops:
  0.0 0.7 %negate_select_fusion.codes = f32[2,8,128]{2,1,0:T(8,128)S(1)} fusion(s32[2,8,128]{2,1,0:T(8,128)} %levels.1, s32[2,8,128]{2,1,0:T(8,128)} %param.5), kind=kLoop, calls=%fused_computation | loop fusion | flops 16384 | bytes 24576 | tf_op jit(solution)/shard_map/jit(_where)/select_n | solution.py:827
  0.7 0.0 copy-start
  0.7 1.1 %copy-done = f32[3,24,2,8,128]{4,3,2,1,0:T(8,128)S(1)} copy-done((f32[3,24,2,8,128]{4,3,2,1,0:T(8,128)S(1)}, f32[3,24,2,8,128]{4,3,2,1,0:T(8,128)}, u32[]{:S(2)}) %copy-start) | copy-done | bytes 589848
  1.8 0.1 pack.1.own
  1.9 0.5 collective-permute-start
  2.4 0.7 %collective-permute-start.3 = (f32[1168,128]{1,0:T(8,128)S(1)}, f32[1168,128]{1,0:T(8,128)S(1)}, u32[]{:S(2)}, u32[]{:S(2)}) collective-permute-start(f32[1168,128]{1,0:T(8,128)S(1)} %pack.1.own), channel_id=1, source_target_pairs={{8,4},{16,12},{24,20},{9,5},{17,13},{25,21},{10,6},{18,14},{26,22}... | collective-permute-start | bytes 1794056 | tf_op jit(solution)/shard_map/ppermute | solution.py:866
  3.1 0.9 %collective-permute-done.pair = f32[1168,128]{1,0:T(8,128)S(1)} collective-permute-done((f32[1168,128]{1,0:T(8,128)S(1)}, f32[1168,128]{1,0:T(8,128)S(1)}, u32[]{:S(2)}, u32[]{:S(2)}) %collective-permute-start) | collective-permute-done | bytes 598048 | tf_op jit(solution)/shard_map/ppermute | solution.py:861
  4.1 1.3 %collective-permute-start.5 = (f32[296,128]{1,0:T(8,128)S(1)}, f32[296,128]{1,0:T(8,128)S(1)}, u32[]{:S(2)}, u32[]{:S(2)}) collective-permute-start(f32[296,128]{1,0:T(8,128)S(1)} %get-tuple-element.28), channel_id=1, source_target_pairs={{1,0},{2,1},{3,2},{5,4},{6,5},{7,6},{9,8},{10,9},{11,10},{13,12},{... | collective-permute-start | bytes 454664 | tf_op jit(solution)/shard_map/ppermute | solution.py:855
  5.4 0.4 collective-permute-start.1
  5.8 5.2 %collective-permute-start.4 = (f32[152,128]{1,0:T(8,128)S(1)}, f32[152,128]{1,0:T(8,128)S(1)}, u32[]{:S(2)}, u32[]{:S(2)}) collective-permute-start(f32[152,128]{1,0:T(8,128)S(1)} %get-tuple-element.27), channel_id=1, source_target_pairs={{0,1},{1,2},{2,3},{4,5},{5,6},{6,7},{8,9},{9,10},{10,11},{12,13},{... | collective-permute-start | bytes 233480 | tf_op jit(solution)/shard_map/ppermute | solution.py:855
  11.1 0.0 collective-permute-done.1.begun
  11.1 0.7 %collective-permute-start.2 = (f32[592,128]{1,0:T(8,128)S(1)}, f32[592,128]{1,0:T(8,128)S(1)}, u32[]{:S(2)}, u32[]{:S(2)}) collective-permute-start(f32[592,128]{1,0:T(8,128)S(1)} %up.1), channel_id=1, source_target_pairs={{4,8},{12,16},{20,24},{5,9},{13,17},{21,25},{6,10},{14,18},{22,26}... | collective-permute-start | bytes 909320 | tf_op jit(solution)/shard_map/ppermute | solution.py:886
  11.8 0.1 pad_add_fusion.first.start
  11.9 1.3 %collective-permute-done.4.ym = f32[152,128]{1,0:T(8,128)S(1)} collective-permute-done((f32[152,128]{1,0:T(8,128)S(1)}, f32[152,128]{1,0:T(8,128)S(1)}, u32[]{:S(2)}, u32[]{:S(2)}) %collective-permute-start.4) | collective-permute-done | bytes 77856 | tf_op jit(solution)/shard_map/ppermute | solution.py:855
  13.2 0.0 collective-permute-done.5.yp
  13.2 0.6 corners.1
  13.7 0.7 %collective-permute-start.8 = (f32[448,128]{1,0:T(8,128)S(1)}, f32[448,128]{1,0:T(8,128)S(1)}, u32[]{:S(2)}, u32[]{:S(2)}) collective-permute-start(f32[448,128]{1,0:T(8,128)S(1)} %corners.1), channel_id=1, source_target_pairs={{4,8},{12,16},{20,24},{8,4},{16,12},{24,20},{5,9},{13,17},{21,25},... | collective-permute-start | bytes 688136 | tf_op jit(solution)/shard_map/ppermute | solution.py:864
  14.4 3.5 %collective-permute-start.7 = (f32[296,128]{1,0:T(8,128)S(1)}, f32[296,128]{1,0:T(8,128)S(1)}, u32[]{:S(2)}, u32[]{:S(2)}) collective-permute-start(f32[296,128]{1,0:T(8,128)S(1)} %collective-permute-done.5.yp), channel_id=1, source_target_pairs={{0,4},{8,12},{16,20},{24,28},{4,0},{12,8},{20,16},{28,24},{1,5},{9... | collective-permute-start | bytes 454664 | tf_op jit(solution)/shard_map/ppermute | solution.py:861
  17.9 0.1 collective-permute-start.6
  18.0 1.2 %collective-permute-done.6.ym_pair = f32[152,128]{1,0:T(8,128)S(1)} collective-permute-done((f32[152,128]{1,0:T(8,128)S(1)}, f32[152,128]{1,0:T(8,128)S(1)}, u32[]{:S(2)}, u32[]{:S(2)}) %collective-permute-start.6) | collective-permute-done | bytes 77856 | tf_op jit(solution)/shard_map/ppermute | solution.py:861
  19.2 0.0 collective-permute-done.7.yp_pair
  19.2 2.4 %early.1 = (f32[33,72,128]{2,1,0:T(8,128)S(1)}, f32[33,72,128]{2,1,0:T(8,128)S(1)}, f32[33,72,128]{2,1,0:T(8,128)S(1)}, f32[27,72,128]{2,1,0:T(8,128)S(1)}, f32[27,72,128]{2,1,0:T(8,128)S(1)}) custom-call(s32[2]{0:T(128)S(1)} %pad_add_fusion.first.start, f32[1168,128]{1,0:T(8,128)S(1)} %pack.1.own, f32[1168,128]{1,0:T(8,128)S(1)} %collective-permute-done.pair, ...), custom_call_target="tpu_custom_call" | custom-call | flops 29491200 | bytes 8388608 | tf_op jit(solution)/shard_map/early/pallas_call | solution.py:903
  21.6 0.0 collective-permute-done.3.upper
  21.6 0.0 collective-permute-done.2.lower
  21.6 2.5 %middle.1 = (f32[21,72,128]{2,1,0:T(8,128)S(1)}, f32[21,72,128]{2,1,0:T(8,128)S(1)}, f32[7,72,128]{2,1,0:T(8,128)S(1)}, f32[21,72,128]{2,1,0:T(8,128)S(1)}, f32[...) custom-call(s32[2]{0:T(128)S(1)} %pad_add_fusion.first.start, ...), custom_call_target="tpu_custom_call" | custom-call | tf_op jit(solution)/shard_map/middle/pallas_call | solution.py:929
  24.1 0.0 collective-permute-done.8.corners
  24.2 4.8 %operator.1 = (bf16[96,4608]{1,0:T(8,128)(2,1)S(1)}, f32[16,3,4,128]{3,2,1,0:T(4,128)S(1)}) custom-call(s32[2]{0:T(128)S(1)} %pad_add_fusion.first.start, f32[1168,128]{1,0:T(8,128)S(1)} %pack.1.own, f32[1168,128]{1,0:T(8,128)S(1)} %collective-permute-done.pair, f32[592,128]{1,0:T(8,128)S(1)} %collective-permute-done.2.lower, ...), custom_call_target="tpu_custom_call" | custom-call | tf_op jit(solution)/shard_map/operator/pallas_call | solution.py:949
  29.0 15.5 %all_to_all.10.system = f32[16,3,4,128]{3,2,1,0:T(4,128)S(1)} all-to-all(f32[16,3,4,128]{3,2,1,0:T(4,128)S(1)} %get-tuple-element.43), channel_id=1, replica_groups={{0,1,2,3,8,9,10,11,16,17,18,19,24,25,26,27},{4,5,6,7,12,13,14,15,20,21,..., dimensions={0} | all-to-all | bytes 196608 | tf_op jit(solution)/shard_map/all_to_all | solution.py:983
  44.5 0.0 collective-permute-start.9
  44.5 1.3 %collective-permute-done.9.system_pair = f32[16,3,4,128]{3,2,1,0:T(4,128)S(1)} collective-permute-done((f32[16,3,4,128]{3,2,1,0:T(4,128)S(1)}, f32[16,3,4,128]{3,2,1,0:T(4,128)S(1)}, u32[]{:S(2)}, u32[]{:S(2)}) %collective-permute-start.9) | collective-permute-done | bytes 98336 | tf_op jit(solution)/shard_map/ppermute | solution.py:861
  45.8 0.0 copy-start.1
  45.8 3.5 %solve.1 = f32[16,2,8,128]{3,2,1,0:T(8,128)S(1)} custom-call(f32[16,3,4,128]{3,2,1,0:T(4,128)S(1)} %all_to_all.10.system, f32[16,3,4,128]{3,2,1,0:T(4,128)S(1)} %collective-permute-done.9.system_pair, bf16[96,5760]{1,0:T(8,128)(2,1)S(1)} %get-tuple-element.41.both_m, bf16[96,4608]{1,0:T(8,128)(2,1)S(1)} %get-tuple-element.44.both_r, ...), custom_call_target="tpu_custom_call" | custom-call | tf_op jit(solution)/shard_map/solve/pallas_call | solution.py:988
  49.3 10.9 %all_to_all.11.blocks = f32[16,2,8,128]{3,2,1,0:T(8,128)S(1)} all-to-all(f32[16,2,8,128]{3,2,1,0:T(8,128)S(1)} %solve.1), channel_id=1, replica_groups={{0,1,2,3,8,9,10,11,16,17,18,19,24,25,26,27},{4,5,6,7,12,13,14,15,20,21,..., dimensions={0} | all-to-all | bytes 262144 | tf_op jit(solution)/shard_map/all_to_all | solution.py:983
  60.2 0.0 collective-permute-start.10
  60.2 0.0 copy-done.1
  60.2 0.7 %scale.1 = f32[2,8,128]{2,1,0:T(8,128)S(1)} custom-call(s32[2]{0:T(128)S(1)} %pad_add_fusion.first.start, s32[2,8,128]{2,1,0:T(8,128)S(1)} %copy-done.1), custom_call_target="tpu_custom_call" | custom-call | tf_op jit(solution)/shard_map/scale/pallas_call | solution.py:842
  60.8 0.7 %collective-permute-done.10.blocks_pair = f32[16,2,8,128]{3,2,1,0:T(8,128)S(1)} collective-permute-done((f32[16,2,8,128]{3,2,1,0:T(8,128)S(1)}, f32[16,2,8,128]{3,2,1,0:T(8,128)S(1)}, u32[]{:S(2)}, u32[]{:S(2)}) %collective-permute-start.10) | collective-permute-done | bytes 131104 | tf_op jit(solution)/shard_map/ppermute | solution.py:861
  61.5 1.3 %cone.1 = f32[2,8,128]{2,1,0:T(8,128)} custom-call(s32[2]{0:T(128)S(1)} %pad_add_fusion.first.start, f32[16,2,8,128]{3,2,1,0:T(8,128)S(1)} %all_to_all.11.blocks, f32[16,2,8,128]{3,2,1,0:T(8,128)S(1)} %collective-permute-done.10.blocks_pair, f32[2,8,128]{2,1,0:T(8,128)S(1)} %scale.1), custom_call_target="tpu_custom_call" | custom-call | tf_op jit(solution)/shard_map/cone/pallas_call | solution.py:1006
  (2 shorter events, 0.0 us)
Async XLA Ops:
  0.7 1.1 %copy-start = (f32[3,24,2,8,128]{4,3,2,1,0:T(8,128)S(1)}, f32[3,24,2,8,128]{4,3,2,1,0:T(8,128)}, u32[]{:S(2)}) copy-start(f32[3,24,2,8,128]{4,3,2,1,0:T(8,128)} %forces.1) | copy-start | bytes 1769476
  1.9 2.2 %collective-permute-start = (f32[1168,128]{1,0:T(8,128)S(1)}, f32[1168,128]{1,0:T(8,128)S(1)}, u32[]{:S(2)}, u32[]{:S(2)}) collective-permute-start(f32[1168,128]{1,0:T(8,128)S(1)} %pack.1.own), channel_id=1, source_target_pairs={{0,4},{8,12},{16,20},{24,28},{4,0},{12,8},{20,16},{28,24},{1,5},{9... | collective-permute-start | bytes 1794056 | tf_op jit(solution)/shard_map/ppermute | solution.py:861
  2.4 19.2 %collective-permute-start.3 = (f32[1168,128]{1,0:T(8,128)S(1)}, f32[1168,128]{1,0:T(8,128)S(1)}, u32[]{:S(2)}, u32[]{:S(2)}) collective-permute-start(f32[1168,128]{1,0:T(8,128)S(1)} %pack.1.own), channel_id=1, source_target_pairs={{8,4},{16,12},{24,20},{9,5},{17,13},{25,21},{10,6},{18,14},{26,22}... | collective-permute-start | bytes 1794056 | tf_op jit(solution)/shard_map/ppermute | solution.py:866
  4.1 9.1 %collective-permute-start.5 = (f32[296,128]{1,0:T(8,128)S(1)}, f32[296,128]{1,0:T(8,128)S(1)}, u32[]{:S(2)}, u32[]{:S(2)}) collective-permute-start(f32[296,128]{1,0:T(8,128)S(1)} %get-tuple-element.28), channel_id=1, source_target_pairs={{1,0},{2,1},{3,2},{5,4},{6,5},{7,6},{9,8},{10,9},{11,10},{13,12},{... | collective-permute-start | bytes 454664 | tf_op jit(solution)/shard_map/ppermute | solution.py:855
  5.4 5.7 %collective-permute-start.1 = (f32[2,8,128]{2,1,0:T(8,128)S(1)}, f32[2,8,128]{2,1,0:T(8,128)S(1)}, u32[]{:S(2)}, u32[]{:S(2)}) collective-permute-start(f32[2,8,128]{2,1,0:T(8,128)S(1)} %negate_select_fusion.codes), channel_id=1, source_target_pairs={{0,4},{8,12},{16,20},{24,28},{4,0},{12,8},{20,16},{28,24},{1,5},{9... | collective-permute-start | bytes 24584 | tf_op jit(solution)/shard_map/ppermute | solution.py:861
  5.8 7.4 %collective-permute-start.4 = (f32[152,128]{1,0:T(8,128)S(1)}, f32[152,128]{1,0:T(8,128)S(1)}, u32[]{:S(2)}, u32[]{:S(2)}) collective-permute-start(f32[152,128]{1,0:T(8,128)S(1)} %get-tuple-element.27), channel_id=1, source_target_pairs={{0,1},{1,2},{2,3},{4,5},{5,6},{6,7},{8,9},{9,10},{10,11},{12,13},{... | collective-permute-start | bytes 233480 | tf_op jit(solution)/shard_map/ppermute | solution.py:855
  11.1 10.5 %collective-permute-start.2 = (f32[592,128]{1,0:T(8,128)S(1)}, f32[592,128]{1,0:T(8,128)S(1)}, u32[]{:S(2)}, u32[]{:S(2)}) collective-permute-start(f32[592,128]{1,0:T(8,128)S(1)} %up.1), channel_id=1, source_target_pairs={{4,8},{12,16},{20,24},{5,9},{13,17},{21,25},{6,10},{14,18},{22,26}... | collective-permute-start | bytes 909320 | tf_op jit(solution)/shard_map/ppermute | solution.py:886
  13.7 10.4 %collective-permute-start.8 = (f32[448,128]{1,0:T(8,128)S(1)}, f32[448,128]{1,0:T(8,128)S(1)}, u32[]{:S(2)}, u32[]{:S(2)}) collective-permute-start(f32[448,128]{1,0:T(8,128)S(1)} %corners.1), channel_id=1, source_target_pairs={{4,8},{12,16},{20,24},{8,4},{16,12},{24,20},{5,9},{13,17},{21,25},... | collective-permute-start | bytes 688136 | tf_op jit(solution)/shard_map/ppermute | solution.py:864
  14.4 4.8 %collective-permute-start.7 = (f32[296,128]{1,0:T(8,128)S(1)}, f32[296,128]{1,0:T(8,128)S(1)}, u32[]{:S(2)}, u32[]{:S(2)}) collective-permute-start(f32[296,128]{1,0:T(8,128)S(1)} %collective-permute-done.5.yp), channel_id=1, source_target_pairs={{0,4},{8,12},{16,20},{24,28},{4,0},{12,8},{20,16},{28,24},{1,5},{9... | collective-permute-start | bytes 454664 | tf_op jit(solution)/shard_map/ppermute | solution.py:861
  17.9 1.3 %collective-permute-start.6 = (f32[152,128]{1,0:T(8,128)S(1)}, f32[152,128]{1,0:T(8,128)S(1)}, u32[]{:S(2)}, u32[]{:S(2)}) collective-permute-start(f32[152,128]{1,0:T(8,128)S(1)} %collective-permute-done.4.ym), channel_id=1, source_target_pairs={{0,4},{8,12},{16,20},{24,28},{4,0},{12,8},{20,16},{28,24},{1,5},{9... | collective-permute-start | bytes 233480 | tf_op jit(solution)/shard_map/ppermute | solution.py:861
  44.5 1.3 %collective-permute-start.9 = (f32[16,3,4,128]{3,2,1,0:T(4,128)S(1)}, f32[16,3,4,128]{3,2,1,0:T(4,128)S(1)}, u32[]{:S(2)}, u32[]{:S(2)}) collective-permute-start(f32[16,3,4,128]{3,2,1,0:T(4,128)S(1)} %all_to_all.10.system), channel_id=1, source_target_pairs={{0,4},{8,12},{16,20},{24,28},{4,0},{12,8},{20,16},{28,24},{1,5},{9... | collective-permute-start | bytes 294920 | tf_op jit(solution)/shard_map/ppermute | solution.py:861
  45.8 14.4 %copy-start.1 = (s32[2,8,128]{2,1,0:T(8,128)S(1)}, s32[2,8,128]{2,1,0:T(8,128)}, u32[]{:S(2)}) copy-start(s32[2,8,128]{2,1,0:T(8,128)} %levels.1) | copy-start | bytes 24580
  60.2 1.3 %collective-permute-start.10 = (f32[16,2,8,128]{3,2,1,0:T(8,128)S(1)}, f32[16,2,8,128]{3,2,1,0:T(8,128)S(1)}, u32[]{:S(2)}, u32[]{:S(2)}) collective-permute-start(f32[16,2,8,128]{3,2,1,0:T(8,128)S(1)} %all_to_all.11.blocks), channel_id=1, source_target_pairs={{0,4},{8,12},{16,20},{24,28},{4,0},{12,8},{20,16},{28,24},{1,5},{9... | collective-permute-start | bytes 393224 | tf_op jit(solution)/shard_map/ppermute | solution.py:861

commit v14 on v12

--- a/solution.py
+++ b/solution.py
@@ -214,7 +214,7 @@
         ref[line:, :] = jnp.zeros((ref.shape[0] - line, LANES), f32)
 
 
-def pack_kernel(sizes, forces, codes, own, up, *down):
+def pack_kernel(sizes, first, forces, codes, own, edge):
     planes, rows, cases = sizes
     block = 3 * cases
     base = planes * rows * block
@@ -226,10 +226,19 @@
                 start = x * rows * block + k * cases + c
                 own[pl.ds(start, rows, stride=block), :] = forces[k, c, x] * scale
 
-    every_y, last = range(rows), (planes - 2, planes - 1)
-    fill(own, base, sizes, up, last[1:], every_y, last, every_y)
-    for ref in down:
-        fill(own, base, sizes, ref, (0, 1), every_y, (0, 1), every_y)
+    even = first[0] // planes % 2 == 0
+    size = rows * block
+    for line in range(0, size, block):
+        high = lines(own, (planes - 1) * size + line, block)
+        edge[line : line + block, :] = jnp.where(even, lines(own, line, block), high)
+    high = lines(own, base + (planes - 2) * rows, 2 * rows)
+    edge[size:, :] = jnp.where(even, lines(own, base, 2 * rows), high)
+
+
+def second_kernel(sizes, begun, own, second):
+    _, rows, cases = sizes
+    size = rows * 3 * cases
+    second[...] = lines(own, size, size)
 
 
 def rows_kernel(sizes, own, ym, yp):
@@ -408,7 +417,7 @@
 
 
 def middle_kernel(
-    sizes, first, own, pair, lower, upper, start, sums_e, diffs_e, acc_se, acc_de,
+    sizes, first, own, pair, edge, second, start, sums_e, diffs_e, acc_se, acc_de,
     sums, diffs, middle, acc_s, acc_d, w_sums, w_diffs, both_out, gram_out,
     stiff_ref, inverse, right,
 ):
@@ -421,11 +430,10 @@
     def codes(x):
         if 0 <= x < planes:
             return lines(own, (planes * block + x) * rows, rows)
+        slot = x + 2 if x < 0 else x - planes
+        outer = lines(edge, (block + slot) * rows, rows)
         if x < 0:
-            outer = lines(lower, (block + x + 2) * rows, rows)
             return jnp.where(even, outer, lines(pair, (planes * block + planes + x) * rows, rows))
-        slot = x - planes
-        outer = lines(upper, (2 * block + slot) * rows, rows)
         return jnp.where(even, lines(pair, (planes * block + slot) * rows, rows), outer)
 
     for x in range(-2, planes + 2):
@@ -446,15 +454,15 @@
 
     @pl.when(even)
     def _():
-        place(0, -1, lower, 0)
+        place(0, -1, edge, 0)
         place(1, 0, own, 0)
         copy(2, 0)
 
     @pl.when(jnp.logical_not(even))
     def _():
         copy(0, planes)
-        place(1, planes, upper, 0)
-        place(2, planes + 1, upper, 1)
+        place(1, planes, edge, 0)
+        place(2, planes + 1, second, 0)
 
     layer = jnp.where(even, 1, planes + 1)
     find = whole(sums, diffs, inner)
@@ -489,7 +497,7 @@
 
 
 def main_kernel(
-    sizes, first, own, pair, lower, upper, ym, yp, ym_pair, yp_pair, corners,
+    sizes, first, own, pair, edge, second, ym, yp, ym_pair, yp_pair, corners,
     start, sums_e, diffs_e, acc_se, acc_de,
     sums_m, diffs_m, middle_m, acc_sm, acc_dm, w_sm, w_dm, both_m, gram_m,
     both_out, system_out, stiff_ref, inverse,
@@ -512,9 +520,9 @@
 
         if 0 <= x < planes:
             return read(True, x)
-        ref, count, slot = (lower, 1, x + 2) if x < 0 else (upper, 2, x - planes)
+        slot = x + 2 if x < 0 else x - planes
         if y == 0:
-            outer = lines(ref, (count * block + slot) * rows, rows)
+            outer = lines(edge, (block + slot) * rows, rows)
         else:
             outer = corner_codes(corners, slot, y, block)
         within = read(False, planes + x if x < 0 else x - planes)
@@ -542,15 +550,15 @@
 
     @pl.when(even)
     def _():
-        place(0, -1, lower, 0, lambda y: corner(corners, 1, y, rows, block))
+        place(0, -1, edge, 0, lambda y: corner(corners, 1, y, rows, block))
         place(1, 0, own, 0, lambda y: beyond(y_own, 0, y, rows, block))
         copy(2, 0)
 
     @pl.when(jnp.logical_not(even))
     def _():
         copy(0, planes)
-        place(1, planes, upper, 0, lambda y: corner(corners, 0, y, rows, block))
-        place(2, planes + 1, upper, 1, lambda y: corner(corners, 1, y, rows, block))
+        place(1, planes, edge, 0, lambda y: corner(corners, 0, y, rows, block))
+        place(2, planes + 1, second, 0, lambda y: corner(corners, 1, y, rows, block))
 
     def find_low(row):
         return (sums, diffs, 4, row) if row < 2 else (sums_m, diffs_m, inner, 0)
@@ -824,16 +832,14 @@
     start = start.astype(jnp.int32)
     counts = (count_x, count_y)
     scalars = pl.BlockSpec(memory_space=pltpu.SMEM)
-    whole = shape(planes * rows, planes * rows)
-    down = [] if planes == 2 else [shape(2 * rows, 2 * rows)]
-    own, up, *down = pl.pallas_call(
+    own, edge = pl.pallas_call(
         functools.partial(pack_kernel, sizes),
-        out_shape=[whole, shape(rows, 2 * rows), *down],
-        in_specs=[VMEM] * 2,
-        out_specs=[VMEM] * (2 + len(down)),
+        out_shape=[shape(planes * rows, planes * rows), shape(rows, 2 * rows)],
+        in_specs=[scalars] + [VMEM] * 2,
+        out_specs=[VMEM] * 2,
         compiler_params=PARAMS,
         name="pack",
-    )(forces, codes)
+    )(start, forces, codes)
     scale = pl.pallas_call(
         functools.partial(scale_kernel, sizes, counts),
         out_shape=jax.ShapeDtypeStruct((planes, rows, LANES), f32),
@@ -858,8 +864,7 @@
     def across(value):
         return lax.ppermute(value, "gx", links(1, 1) + links(2, -1))
 
-    upper = lax.ppermute(down[0] if down else own, "gx", links(2, -1))
-    lower = lax.ppermute(up, "gx", links(1, 1))
+    edge = across(edge)
     pair = swapped(own)
     own, pair = lax.optimization_barrier((own, pair))
     ym, yp = pl.pallas_call(
@@ -871,7 +876,17 @@
         name="rows",
     )(own)
     from_yp, from_ym = moved(ym, "gy", -1), moved(yp, "gy", 1)
+    second = pl.pallas_call(
+        functools.partial(second_kernel, sizes),
+        out_shape=shape(rows, 0),
+        in_specs=[VMEM] * 2,
+        out_specs=VMEM,
+        compiler_params=PARAMS,
+        name="second",
+    )(swapped(codes), own)
+    second = lax.ppermute(second, "gx", links(2, -1))
     pair_yp, pair_ym = swapped(from_yp), swapped(from_ym)
+    from_ym, from_yp, edge = lax.optimization_barrier((from_ym, from_yp, edge))
     corners = across(
         pl.pallas_call(
             functools.partial(corner_kernel, sizes),
@@ -929,7 +944,7 @@
         ],
         compiler_params=PARAMS,
         name="middle",
-    )(start, own, pair, lower, upper, *early)
+    )(start, own, pair, edge, second, *early)
 
     rim, rim_own = rim_columns(planes, rows)
     field = scratch(columns(nodes))
@@ -957,7 +972,7 @@
         compiler_params=PARAMS,
         name="operator",
     )(
-        start, own, pair, lower, upper, from_ym, from_yp, pair_ym, pair_yp, corners,
+        start, own, pair, edge, second, from_ym, from_yp, pair_ym, pair_yp, corners,
         *early, *middle,
     )
 

time: 65 us -> 64 us (0.985)
  blocking collectives: 27.2 us -> 24.7 us
  starting transfers between devices: 13.5 us -> 15.5 us
  waiting for transfers between devices: 6.06 us -> 4.99 us
    all_to_all x2, blocking collectives: 27.2 us -> 24.7 us  [gathered(): mine = lax.all_to_all(copies, ('gx', 'gy'), 0, 0, axis_index_groups=groups)]
    ppermute x5 -> x6, starting transfers between devices: 4.7 us -> 6.71 us  [swapped(): return lax.ppermute(value, 'gx', links(0, 1) + links(1, -1))]
    ppermute x2, waiting for transfers between devices: 1.93 us -> 0.01 us  [moved(): return lax.ppermute(value, axis, pairs)]
    ppermute x5 -> x6, waiting for transfers between devices: 4.13 us -> 4.98 us  [swapped(): return lax.ppermute(value, 'gx', links(0, 1) + links(1, -1))]
    ppermute x2 -> x1, starting transfers between devices: 1.37 us -> 0.68 us  [local(): second = lax.ppermute(second, 'gx', links(2, -1))]
    ppermute x1 -> x2, starting transfers between devices: 0.68 us -> 1.34 us  [across(): return lax.ppermute(value, 'gx', links(1, 1) + links(2, -1))]
  transfers between devices with their start and end apart: 10 -> 11, of which waited for: 5 -> 5; matrix products, arithmetic and copies ran while one was open for 0% -> 0% of each run, Pallas kernels for 10% -> 10%
where the time goes in v14:
time: 64 us; the launch traced here: 63.6 us
  blocking collectives  24.7 us (39%)
  Pallas kernels  16.4 us (26%)
  starting transfers between devices  15.5 us (24%)
  waiting for transfers between devices  4.99 us (8%)
  local copies, waits for them, and re-layouts  1.07 us (2%)
  other arithmetic  0.8 us (1%)
    all_to_all x2, blocking collectives, gathered(): mine = lax.all_to_all(copies, ('gx', 'gy'), 0, 0, axis_index_groups=groups)  24.7 us
    ppermute x2, starting transfers between devices, moved(): return lax.ppermute(value, axis, pairs)  6.77 us
    ppermute x6, starting transfers between devices, swapped(): return lax.ppermute(value, 'gx', links(0, 1) + links(1, -1))  6.71 us
    ppermute x6, waiting for transfers between devices, swapped(): return lax.ppermute(value, 'gx', links(0, 1) + links(1, -1))  4.98 us
    pallas_call x1, Pallas kernels, local(): pl.pallas_call(functools.partial(main_kernel, sizes), out_shape=[fields(4...  4.85 us
    pallas_call x1, Pallas kernels, local(): pl.pallas_call(functools.partial(solve_kernel, sizes), out_shape=jax.Shap...  3.45 us
    pallas_call x1, Pallas kernels, local(): pl.pallas_call(functools.partial(middle_kernel, sizes), out_shape=[column...  2.56 us
    pallas_call x1, Pallas kernels, local(): pl.pallas_call(functools.partial(early_kernel, sizes), out_shape=[window]...  2.38 us
  transfers between devices with their start and end apart: 11, of which 5 were waited for; matrix products, arithmetic and copies ran while one was open for 0% of the time, Pallas kernels for 10%

profile of v14, /device:TPU:0, one launch (start us, length us, event | category | flops | bytes accessed | tf_op | source)
XLA Modules:
  0.0 63.6 jit_solution(16887923933074270175)
XLA Ops:
  0.0 0.1 pad_add_fusion.first.start
  0.1 0.7 %negate_select_fusion.codes = f32[2,8,128]{2,1,0:T(8,128)S(1)} fusion(s32[2,8,128]{2,1,0:T(8,128)} %levels.1, s32[2,8,128]{2,1,0:T(8,128)} %param.5), kind=kLoop, calls=%fused_computation | loop fusion | flops 16384 | bytes 24576 | tf_op jit(solution)/shard_map/jit(_where)/select_n | solution.py:830
  0.8 0.0 copy-start
  0.8 1.1 %copy-done = f32[3,24,2,8,128]{4,3,2,1,0:T(8,128)S(1)} copy-done((f32[3,24,2,8,128]{4,3,2,1,0:T(8,128)S(1)}, f32[3,24,2,8,128]{4,3,2,1,0:T(8,128)}, u32[]{:S(2)}) %copy-start) | copy-done | bytes 589848
  1.9 0.7 %pack.1 = (f32[1168,128]{1,0:T(8,128)S(1)}, f32[592,128]{1,0:T(8,128)S(1)}) custom-call(s32[2]{0:T(128)S(1)} %pad_add_fusion.first.start, f32[3,24,2,8,128]{4,3,2,1,0:T(8,128)S(1)} %copy-done, f32[2,8,128]{2,1,0:T(8,128)S(1)} %negate_select_fusion.codes), custom_call_target="tpu_custom_call" | custom-call | tf_op jit(solution)/shard_map/pack/pallas_call | solution.py:835
  2.5 0.5 collective-permute-start
  3.1 0.7 %collective-permute-start.3 = (f32[592,128]{1,0:T(8,128)S(1)}, f32[592,128]{1,0:T(8,128)S(1)}, u32[]{:S(2)}, u32[]{:S(2)}) collective-permute-start(f32[592,128]{1,0:T(8,128)S(1)} %get-tuple-element.35), channel_id=1, source_target_pairs={{4,8},{12,16},{20,24},{8,4},{16,12},{24,20},{5,9},{13,17},{21,25},... | collective-permute-start | bytes 909320 | tf_op jit(solution)/shard_map/ppermute | solution.py:865
  3.7 1.0 %collective-permute-done.pair = f32[1168,128]{1,0:T(8,128)S(1)} collective-permute-done((f32[1168,128]{1,0:T(8,128)S(1)}, f32[1168,128]{1,0:T(8,128)S(1)}, u32[]{:S(2)}, u32[]{:S(2)}) %collective-permute-start) | collective-permute-done | bytes 598048 | tf_op jit(solution)/shard_map/ppermute | solution.py:862
  4.7 1.3 %collective-permute-start.2 = (f32[296,128]{1,0:T(8,128)S(1)}, f32[296,128]{1,0:T(8,128)S(1)}, u32[]{:S(2)}, u32[]{:S(2)}) collective-permute-start(f32[296,128]{1,0:T(8,128)S(1)} %get-tuple-element.34), channel_id=1, source_target_pairs={{1,0},{2,1},{3,2},{5,4},{6,5},{7,6},{9,8},{10,9},{11,10},{13,12},{... | collective-permute-start | bytes 454664 | tf_op jit(solution)/shard_map/ppermute | solution.py:856
  6.0 5.5 %collective-permute-start.1 = (f32[152,128]{1,0:T(8,128)S(1)}, f32[152,128]{1,0:T(8,128)S(1)}, u32[]{:S(2)}, u32[]{:S(2)}) collective-permute-start(f32[152,128]{1,0:T(8,128)S(1)} %get-tuple-element.33), channel_id=1, source_target_pairs={{0,1},{1,2},{2,3},{4,5},{5,6},{6,7},{8,9},{9,10},{10,11},{12,13},{... | collective-permute-start | bytes 233480 | tf_op jit(solution)/shard_map/ppermute | solution.py:856
  11.5 1.5 %collective-permute-start.4 = (f32[2,8,128]{2,1,0:T(8,128)S(1)}, f32[2,8,128]{2,1,0:T(8,128)S(1)}, u32[]{:S(2)}, u32[]{:S(2)}) collective-permute-start(f32[2,8,128]{2,1,0:T(8,128)S(1)} %negate_select_fusion.codes), channel_id=1, source_target_pairs={{0,4},{8,12},{16,20},{24,28},{4,0},{12,8},{20,16},{28,24},{1,5},{9... | collective-permute-start | bytes 24584 | tf_op jit(solution)/shard_map/ppermute | solution.py:862
  13.0 0.8 %collective-permute-done.4.begun = f32[2,8,128]{2,1,0:T(8,128)S(1)} collective-permute-done((f32[2,8,128]{2,1,0:T(8,128)S(1)}, f32[2,8,128]{2,1,0:T(8,128)S(1)}, u32[]{:S(2)}, u32[]{:S(2)}) %collective-permute-start.4) | collective-permute-done | bytes 8224 | tf_op jit(solution)/shard_map/ppermute | solution.py:862
  13.8 0.7 %collective-permute-start.5 = (f32[576,128]{1,0:T(8,128)S(1)}, f32[576,128]{1,0:T(8,128)S(1)}, u32[]{:S(2)}, u32[]{:S(2)}) collective-permute-start(f32[576,128]{1,0:T(8,128)S(1)} %second.1), channel_id=1, source_target_pairs={{8,4},{16,12},{24,20},{9,5},{17,13},{25,21},{10,6},{18,14},{26,22}... | collective-permute-start | bytes 884744 | tf_op jit(solution)/shard_map/ppermute | solution.py:887
  14.5 0.0 collective-permute-done.3.edge
  14.5 0.0 collective-permute-done.1.ym
  14.5 0.0 collective-permute-done.2.yp
  14.6 0.6 corners.1
  15.1 0.7 %collective-permute-start.8 = (f32[448,128]{1,0:T(8,128)S(1)}, f32[448,128]{1,0:T(8,128)S(1)}, u32[]{:S(2)}, u32[]{:S(2)}) collective-permute-start(f32[448,128]{1,0:T(8,128)S(1)} %corners.1), channel_id=1, source_target_pairs={{4,8},{12,16},{20,24},{8,4},{16,12},{24,20},{5,9},{13,17},{21,25},... | collective-permute-start | bytes 688136 | tf_op jit(solution)/shard_map/ppermute | solution.py:865
  15.8 4.6 %collective-permute-start.7 = (f32[296,128]{1,0:T(8,128)S(1)}, f32[296,128]{1,0:T(8,128)S(1)}, u32[]{:S(2)}, u32[]{:S(2)}) collective-permute-start(f32[296,128]{1,0:T(8,128)S(1)} %collective-permute-done.2.yp), channel_id=1, source_target_pairs={{0,4},{8,12},{16,20},{24,28},{4,0},{12,8},{20,16},{28,24},{1,5},{9... | collective-permute-start | bytes 454664 | tf_op jit(solution)/shard_map/ppermute | solution.py:862
  20.4 0.1 collective-permute-start.6
  20.5 1.2 %collective-permute-done.6.ym_pair = f32[152,128]{1,0:T(8,128)S(1)} collective-permute-done((f32[152,128]{1,0:T(8,128)S(1)}, f32[152,128]{1,0:T(8,128)S(1)}, u32[]{:S(2)}, u32[]{:S(2)}) %collective-permute-start.6) | collective-permute-done | bytes 77856 | tf_op jit(solution)/shard_map/ppermute | solution.py:862
  21.7 0.0 collective-permute-done.7.yp_pair
  21.7 2.4 %early.1 = (f32[33,72,128]{2,1,0:T(8,128)S(1)}, f32[33,72,128]{2,1,0:T(8,128)S(1)}, f32[33,72,128]{2,1,0:T(8,128)S(1)}, f32[27,72,128]{2,1,0:T(8,128)S(1)}, f32[27,72,128]{2,1,0:T(8,128)S(1)}) custom-call(s32[2]{0:T(128)S(1)} %pad_add_fusion.first.start, f32[1168,128]{1,0:T(8,128)S(1)} %get-tuple-element.31.own, f32[1168,128]{1,0:T(8,128)S(1)} %collective-permute-done.pair, ...), custom_call_target="tpu_custom_call" | custom-call | flops 29491200 | bytes 8388608 | tf_op jit(solution)/shard_map/early/pallas_call | solution.py:905
  24.1 0.0 collective-permute-done.5.second
  24.1 2.6 %middle.1 = (f32[21,72,128]{2,1,0:T(8,128)S(1)}, f32[21,72,128]{2,1,0:T(8,128)S(1)}, f32[7,72,128]{2,1,0:T(8,128)S(1)}, f32[21,72,128]{2,1,0:T(8,128)S(1)}, f32[...) custom-call(s32[2]{0:T(128)S(1)} %pad_add_fusion.first.start, ...), custom_call_target="tpu_custom_call" | custom-call | tf_op jit(solution)/shard_map/middle/pallas_call | solution.py:931
  26.7 0.0 collective-permute-done.8.corners
  26.7 4.8 %operator.1 = (bf16[96,4608]{1,0:T(8,128)(2,1)S(1)}, f32[16,3,4,128]{3,2,1,0:T(4,128)S(1)}) custom-call(s32[2]{0:T(128)S(1)} %pad_add_fusion.first.start, f32[1168,128]{1,0:T(8,128)S(1)} %get-tuple-element.31.own, f32[1168,128]{1,0:T(8,128)S(1)} %collective-permute-done.pair, f32[592,128]{1,0:T(8,128)S(1)} %collective-permute-done.3.edge, ...), custom_call_target="tpu_custom_call" | custom-call | tf_op jit(solution)/shard_map/operator/pallas_call | solution.py:951
  31.5 13.8 %all_to_all.10.system = f32[16,3,4,128]{3,2,1,0:T(4,128)S(1)} all-to-all(f32[16,3,4,128]{3,2,1,0:T(4,128)S(1)} %get-tuple-element.53), channel_id=1, replica_groups={{0,1,2,3,8,9,10,11,16,17,18,19,24,25,26,27},{4,5,6,7,12,13,14,15,20,21,..., dimensions={0} | all-to-all | bytes 196608 | tf_op jit(solution)/shard_map/all_to_all | solution.py:985
  45.3 0.0 collective-permute-start.9
  45.3 1.3 %collective-permute-done.9.system_pair = f32[16,3,4,128]{3,2,1,0:T(4,128)S(1)} collective-permute-done((f32[16,3,4,128]{3,2,1,0:T(4,128)S(1)}, f32[16,3,4,128]{3,2,1,0:T(4,128)S(1)}, u32[]{:S(2)}, u32[]{:S(2)}) %collective-permute-start.9) | collective-permute-done | bytes 98336 | tf_op jit(solution)/shard_map/ppermute | solution.py:862
  46.6 0.0 copy-start.1
  46.6 3.4 %solve.1 = f32[16,2,8,128]{3,2,1,0:T(8,128)S(1)} custom-call(f32[16,3,4,128]{3,2,1,0:T(4,128)S(1)} %all_to_all.10.system, f32[16,3,4,128]{3,2,1,0:T(4,128)S(1)} %collective-permute-done.9.system_pair, bf16[96,5760]{1,0:T(8,128)(2,1)S(1)} %get-tuple-element.51.both_m, bf16[96,4608]{1,0:T(8,128)(2,1)S(1)} %get-tuple-element.54.both_r, ...), custom_call_target="tpu_custom_call" | custom-call | tf_op jit(solution)/shard_map/solve/pallas_call | solution.py:990
  50.0 10.9 %all_to_all.11.blocks = f32[16,2,8,128]{3,2,1,0:T(8,128)S(1)} all-to-all(f32[16,2,8,128]{3,2,1,0:T(8,128)S(1)} %solve.1), channel_id=1, replica_groups={{0,1,2,3,8,9,10,11,16,17,18,19,24,25,26,27},{4,5,6,7,12,13,14,15,20,21,..., dimensions={0} | all-to-all | bytes 262144 | tf_op jit(solution)/shard_map/all_to_all | solution.py:985
  60.9 0.0 collective-permute-start.10
  60.9 0.0 copy-done.1
  60.9 0.7 %scale.1 = f32[2,8,128]{2,1,0:T(8,128)S(1)} custom-call(s32[2]{0:T(128)S(1)} %pad_add_fusion.first.start, s32[2,8,128]{2,1,0:T(8,128)S(1)} %copy-done.1), custom_call_target="tpu_custom_call" | custom-call | tf_op jit(solution)/shard_map/scale/pallas_call | solution.py:843
  61.6 0.7 %collective-permute-done.10.blocks_pair = f32[16,2,8,128]{3,2,1,0:T(8,128)S(1)} collective-permute-done((f32[16,2,8,128]{3,2,1,0:T(8,128)S(1)}, f32[16,2,8,128]{3,2,1,0:T(8,128)S(1)}, u32[]{:S(2)}, u32[]{:S(2)}) %collective-permute-start.10) | collective-permute-done | bytes 131104 | tf_op jit(solution)/shard_map/ppermute | solution.py:862
  62.3 1.3 %cone.1 = f32[2,8,128]{2,1,0:T(8,128)} custom-call(s32[2]{0:T(128)S(1)} %pad_add_fusion.first.start, f32[16,2,8,128]{3,2,1,0:T(8,128)S(1)} %all_to_all.11.blocks, f32[16,2,8,128]{3,2,1,0:T(8,128)S(1)} %collective-permute-done.10.blocks_pair, f32[2,8,128]{2,1,0:T(8,128)S(1)} %scale.1), custom_call_target="tpu_custom_call" | custom-call | tf_op jit(solution)/shard_map/cone/pallas_call | solution.py:1008
  (2 shorter events, 0.0 us)
Async XLA Ops:
  0.8 1.1 %copy-start = (f32[3,24,2,8,128]{4,3,2,1,0:T(8,128)S(1)}, f32[3,24,2,8,128]{4,3,2,1,0:T(8,128)}, u32[]{:S(2)}) copy-start(f32[3,24,2,8,128]{4,3,2,1,0:T(8,128)} %forces.1) | copy-start | bytes 1769476
  2.5 2.2 %collective-permute-start = (f32[1168,128]{1,0:T(8,128)S(1)}, f32[1168,128]{1,0:T(8,128)S(1)}, u32[]{:S(2)}, u32[]{:S(2)}) collective-permute-start(f32[1168,128]{1,0:T(8,128)S(1)} %get-tuple-element.31.own), channel_id=1, source_target_pairs={{0,4},{8,12},{16,20},{24,28},{4,0},{12,8},{20,16},{28,24},{1,5},{9... | collective-permute-start | bytes 1794056 | tf_op jit(solution)/shard_map/ppermute | solution.py:862
  3.1 11.5 %collective-permute-start.3 = (f32[592,128]{1,0:T(8,128)S(1)}, f32[592,128]{1,0:T(8,128)S(1)}, u32[]{:S(2)}, u32[]{:S(2)}) collective-permute-start(f32[592,128]{1,0:T(8,128)S(1)} %get-tuple-element.35), channel_id=1, source_target_pairs={{4,8},{12,16},{20,24},{8,4},{16,12},{24,20},{5,9},{13,17},{21,25},... | collective-permute-start | bytes 909320 | tf_op jit(solution)/shard_map/ppermute | solution.py:865
  4.7 9.8 %collective-permute-start.2 = (f32[296,128]{1,0:T(8,128)S(1)}, f32[296,128]{1,0:T(8,128)S(1)}, u32[]{:S(2)}, u32[]{:S(2)}) collective-permute-start(f32[296,128]{1,0:T(8,128)S(1)} %get-tuple-element.34), channel_id=1, source_target_pairs={{1,0},{2,1},{3,2},{5,4},{6,5},{7,6},{9,8},{10,9},{11,10},{13,12},{... | collective-permute-start | bytes 454664 | tf_op jit(solution)/shard_map/ppermute | solution.py:856
  6.0 8.5 %collective-permute-start.1 = (f32[152,128]{1,0:T(8,128)S(1)}, f32[152,128]{1,0:T(8,128)S(1)}, u32[]{:S(2)}, u32[]{:S(2)}) collective-permute-start(f32[152,128]{1,0:T(8,128)S(1)} %get-tuple-element.33), channel_id=1, source_target_pairs={{0,1},{1,2},{2,3},{4,5},{5,6},{6,7},{8,9},{9,10},{10,11},{12,13},{... | collective-permute-start | bytes 233480 | tf_op jit(solution)/shard_map/ppermute | solution.py:856
  11.5 2.3 %collective-permute-start.4 = (f32[2,8,128]{2,1,0:T(8,128)S(1)}, f32[2,8,128]{2,1,0:T(8,128)S(1)}, u32[]{:S(2)}, u32[]{:S(2)}) collective-permute-start(f32[2,8,128]{2,1,0:T(8,128)S(1)} %negate_select_fusion.codes), channel_id=1, source_target_pairs={{0,4},{8,12},{16,20},{24,28},{4,0},{12,8},{20,16},{28,24},{1,5},{9... | collective-permute-start | bytes 24584 | tf_op jit(solution)/shard_map/ppermute | solution.py:862
  13.8 10.3 %collective-permute-start.5 = (f32[576,128]{1,0:T(8,128)S(1)}, f32[576,128]{1,0:T(8,128)S(1)}, u32[]{:S(2)}, u32[]{:S(2)}) collective-permute-start(f32[576,128]{1,0:T(8,128)S(1)} %second.1), channel_id=1, source_target_pairs={{8,4},{16,12},{24,20},{9,5},{17,13},{25,21},{10,6},{18,14},{26,22}... | collective-permute-start | bytes 884744 | tf_op jit(solution)/shard_map/ppermute | solution.py:887
  15.1 11.5 %collective-permute-start.8 = (f32[448,128]{1,0:T(8,128)S(1)}, f32[448,128]{1,0:T(8,128)S(1)}, u32[]{:S(2)}, u32[]{:S(2)}) collective-permute-start(f32[448,128]{1,0:T(8,128)S(1)} %corners.1), channel_id=1, source_target_pairs={{4,8},{12,16},{20,24},{8,4},{16,12},{24,20},{5,9},{13,17},{21,25},... | collective-permute-start | bytes 688136 | tf_op jit(solution)/shard_map/ppermute | solution.py:865
  15.8 5.9 %collective-permute-start.7 = (f32[296,128]{1,0:T(8,128)S(1)}, f32[296,128]{1,0:T(8,128)S(1)}, u32[]{:S(2)}, u32[]{:S(2)}) collective-permute-start(f32[296,128]{1,0:T(8,128)S(1)} %collective-permute-done.2.yp), channel_id=1, source_target_pairs={{0,4},{8,12},{16,20},{24,28},{4,0},{12,8},{20,16},{28,24},{1,5},{9... | collective-permute-start | bytes 454664 | tf_op jit(solution)/shard_map/ppermute | solution.py:862
  20.4 1.3 %collective-permute-start.6 = (f32[152,128]{1,0:T(8,128)S(1)}, f32[152,128]{1,0:T(8,128)S(1)}, u32[]{:S(2)}, u32[]{:S(2)}) collective-permute-start(f32[152,128]{1,0:T(8,128)S(1)} %collective-permute-done.1.ym), channel_id=1, source_target_pairs={{0,4},{8,12},{16,20},{24,28},{4,0},{12,8},{20,16},{28,24},{1,5},{9... | collective-permute-start | bytes 233480 | tf_op jit(solution)/shard_map/ppermute | solution.py:862
  45.3 1.3 %collective-permute-start.9 = (f32[16,3,4,128]{3,2,1,0:T(4,128)S(1)}, f32[16,3,4,128]{3,2,1,0:T(4,128)S(1)}, u32[]{:S(2)}, u32[]{:S(2)}) collective-permute-start(f32[16,3,4,128]{3,2,1,0:T(4,128)S(1)} %all_to_all.10.system), channel_id=1, source_target_pairs={{0,4},{8,12},{16,20},{24,28},{4,0},{12,8},{20,16},{28,24},{1,5},{9... | collective-permute-start | bytes 294920 | tf_op jit(solution)/shard_map/ppermute | solution.py:862
  46.6 14.3 %copy-start.1 = (s32[2,8,128]{2,1,0:T(8,128)S(1)}, s32[2,8,128]{2,1,0:T(8,128)}, u32[]{:S(2)}) copy-start(s32[2,8,128]{2,1,0:T(8,128)} %levels.1) | copy-start | bytes 24580
  60.9 1.3 %collective-permute-start.10 = (f32[16,2,8,128]{3,2,1,0:T(8,128)S(1)}, f32[16,2,8,128]{3,2,1,0:T(8,128)S(1)}, u32[]{:S(2)}, u32[]{:S(2)}) collective-permute-start(f32[16,2,8,128]{3,2,1,0:T(8,128)S(1)} %all_to_all.11.blocks), channel_id=1, source_target_pairs={{0,4},{8,12},{16,20},{24,28},{4,0},{12,8},{20,16},{28,24},{1,5},{9... | collective-permute-start | bytes 393224 | tf_op jit(solution)/shard_map/ppermute | solution.py:862

commit v15 on v14

--- a/solution.py
+++ b/solution.py
@@ -214,7 +214,7 @@
         ref[line:, :] = jnp.zeros((ref.shape[0] - line, LANES), f32)
 
 
-def pack_kernel(sizes, first, forces, codes, own, edge):
+def pack_kernel(sizes, forces, codes, own, edge):
     planes, rows, cases = sizes
     block = 3 * cases
     base = planes * rows * block
@@ -226,7 +226,7 @@
                 start = x * rows * block + k * cases + c
                 own[pl.ds(start, rows, stride=block), :] = forces[k, c, x] * scale
 
-    even = first[0] // planes % 2 == 0
+    even = lax.axis_index("gx") % 2 == 0
     size = rows * block
     for line in range(0, size, block):
         high = lines(own, (planes - 1) * size + line, block)
@@ -249,10 +249,10 @@
     fill(own, base, sizes, yp, every_x, (rows - 1,), every_x, (rows - 2, rows - 1))
 
 
-def corner_kernel(sizes, first, ym, yp, out):
+def corner_kernel(sizes, ym, yp, out):
     planes, rows, cases = sizes
     block = 3 * cases
-    even = first[0] // planes % 2 == 0
+    even = lax.axis_index("gx") % 2 == 0
     line = 0
     for source, width in ((ym, 1), (yp, 2)):
         size = width * block
@@ -320,13 +320,13 @@
 
 
 def early_kernel(
-    sizes, first, own, pair, ym, yp, ym_pair, yp_pair, start, sums, diffs, acc_s, acc_d,
+    sizes, own, pair, ym, yp, ym_pair, yp_pair, start, sums, diffs, acc_s, acc_d,
     stiff_ref, inverse,
 ):
     planes, rows, cases = sizes
     block = 3 * cases
     ys = rows + 3
-    even = first[0] // planes % 2 == 0
+    even = lax.axis_index("gx") % 2 == 0
     y_own, y_pair = (ym, yp), (ym_pair, yp_pair)
 
     def both_ways(w, read):
@@ -417,7 +417,7 @@
 
 
 def middle_kernel(
-    sizes, first, own, pair, edge, second, start, sums_e, diffs_e, acc_se, acc_de,
+    sizes, own, pair, edge, second, start, sums_e, diffs_e, acc_se, acc_de,
     sums, diffs, middle, acc_s, acc_d, w_sums, w_diffs, both_out, gram_out,
     stiff_ref, inverse, right,
 ):
@@ -425,7 +425,7 @@
     block = 3 * cases
     ys, nodes_y, inner = rows + 3, rows + 1, rows - 1
     core = core_rows(rows)
-    even = first[0] // planes % 2 == 0
+    even = lax.axis_index("gx") % 2 == 0
 
     def codes(x):
         if 0 <= x < planes:
@@ -497,7 +497,7 @@
 
 
 def main_kernel(
-    sizes, first, own, pair, edge, second, ym, yp, ym_pair, yp_pair, corners,
+    sizes, own, pair, edge, second, ym, yp, ym_pair, yp_pair, corners,
     start, sums_e, diffs_e, acc_se, acc_de,
     sums_m, diffs_m, middle_m, acc_sm, acc_dm, w_sm, w_dm, both_m, gram_m,
     both_out, system_out, stiff_ref, inverse,
@@ -509,7 +509,7 @@
     ys, nodes_y, inner = rows + 3, rows + 1, rows - 1
     core, rim = core_rows(rows), rim_rows(rows)
     columns, own_count = rim_columns(planes, rows)
-    even = first[0] // planes % 2 == 0
+    even = lax.axis_index("gx") % 2 == 0
     y_own, y_pair = (ym, yp), (ym_pair, yp_pair)
 
     def codes(x, y):
@@ -787,12 +787,13 @@
     return result
 
 
-def scale_kernel(sizes, counts, start, levels, out, there):
+def scale_kernel(sizes, counts, levels, out, there):
     planes, rows, _ = sizes
-    y = lax.broadcasted_iota(jnp.int32, (rows + 4, LANES), 0) + (start[1] - 2)
+    y = lax.broadcasted_iota(jnp.int32, (rows + 4, LANES), 0)
+    y = y + (lax.axis_index("gy") * rows - 2)
     in_y = (y >= 0) & (y < counts[1] * rows)
     for x in range(planes + 4):
-        global_x = start[0] + (x - 2)
+        global_x = lax.axis_index("gx") * planes + (x - 2)
         in_x = (global_x >= 0) & (global_x < counts[0] * planes)
         there[x] = jnp.where(in_y & in_x, 1.0, 0.0)
     for x in range(planes):
@@ -800,14 +801,14 @@
         out[x] = 1.0 / (density * smooth(there, x, rows))
 
 
-def filter_kernel(sizes, counts, start, blocks, blocks_pair, scale, out, wide):
+def filter_kernel(sizes, counts, blocks, blocks_pair, scale, out, wide):
     planes, rows, _ = sizes
     sides_x = ((-1, planes - 2, planes, 0), (0, 0, planes, 2), (1, 0, 2, 2 + planes))
     sides_y = ((-1, rows - 2, rows, 0), (0, 0, rows, 2), (1, 0, 2, 2 + rows))
     for step_x, x0, x1, to_x in sides_x:
         for step_y, y0, y1, to_y in sides_y:
-            at_x = start[0] // planes + step_x
-            at_y = start[1] // rows + step_y
+            at_x = lax.axis_index("gx") + step_x
+            at_y = lax.axis_index("gy") + step_y
             inside = (at_x >= 0) & (at_x < counts[0]) & (at_y >= 0) & (at_y < counts[1])
             index = jnp.where(inside, at_x // 2 * counts[1] + at_y, 0)
             value = (blocks_pair if step_x else blocks)[index, x0:x1, y0:y1, :]
@@ -828,27 +829,24 @@
     density = 0.3 + 0.7 * levels.astype(f32) / (LEVELS - 1)
     codes = density * density * density
     codes = jnp.where(supports == 0, codes, -codes)
-    start = jnp.stack([lax.axis_index("gx") * planes, lax.axis_index("gy") * rows])
-    start = start.astype(jnp.int32)
     counts = (count_x, count_y)
-    scalars = pl.BlockSpec(memory_space=pltpu.SMEM)
     own, edge = pl.pallas_call(
         functools.partial(pack_kernel, sizes),
         out_shape=[shape(planes * rows, planes * rows), shape(rows, 2 * rows)],
-        in_specs=[scalars] + [VMEM] * 2,
+        in_specs=[VMEM] * 2,
         out_specs=[VMEM] * 2,
         compiler_params=PARAMS,
         name="pack",
-    )(start, forces, codes)
+    )(forces, codes)
     scale = pl.pallas_call(
         functools.partial(scale_kernel, sizes, counts),
         out_shape=jax.ShapeDtypeStruct((planes, rows, LANES), f32),
-        in_specs=[scalars, VMEM],
+        in_specs=[VMEM],
         out_specs=VMEM,
         scratch_shapes=[pltpu.VMEM((planes + 4, rows + 4, LANES), f32)],
         compiler_params=PARAMS,
         name="scale",
-    )(start, levels)
+    )(levels)
 
     def moved(value, axis, step):
         count = lax.axis_size(axis)
@@ -891,11 +889,11 @@
         pl.pallas_call(
             functools.partial(corner_kernel, sizes),
             out_shape=jax.ShapeDtypeStruct((6 * block + 16, LANES), f32),
-            in_specs=[scalars] + [VMEM] * 2,
+            in_specs=[VMEM] * 2,
             out_specs=VMEM,
             compiler_params=PARAMS,
             name="corners",
-        )(start, from_ym, from_yp)
+        )(from_ym, from_yp)
     )
 
     devices = count_x * count_y
@@ -905,7 +903,7 @@
     early = pl.pallas_call(
         functools.partial(early_kernel, sizes),
         out_shape=[window] * 3 + [partial_forces] * 2,
-        in_specs=[scalars] + [VMEM] * 6,
+        in_specs=[VMEM] * 6,
         out_specs=[VMEM] * 5,
         scratch_shapes=[
             pltpu.VMEM((planes + 2, up8(rows + 4), LANES), f32),
@@ -916,7 +914,7 @@
             flops=200 * planes * rows * block * LANES, bytes_accessed=2**23, transcendentals=0
         ),
         name="early",
-    )(start, own, pair, from_ym, from_yp, pair_ym, pair_yp)
+    )(own, pair, from_ym, from_yp, pair_ym, pair_yp)
 
     def columns(count):
         return jax.ShapeDtypeStruct((count, block, LANES), f32)
@@ -935,7 +933,7 @@
         + [columns(3 * (rows - 1))] * 2
         + [columns((planes + 1) * core)] * 2
         + [fields(4, (planes + 1) * core), jax.ShapeDtypeStruct((2 * cases, 2 * cases), f32)],
-        in_specs=[scalars] + [VMEM] * 9,
+        in_specs=[VMEM] * 9,
         out_specs=[VMEM] * 9,
         scratch_shapes=[
             pltpu.VMEM((planes + 4, up8(rows), LANES), f32),
@@ -944,7 +942,7 @@
         ],
         compiler_params=PARAMS,
         name="middle",
-    )(start, own, pair, edge, second, *early)
+    )(own, pair, edge, second, *early)
 
     rim, rim_own = rim_columns(planes, rows)
     field = scratch(columns(nodes))
@@ -954,7 +952,7 @@
             fields(4, len(rim)),
             jax.ShapeDtypeStruct((devices // 2, cases // 8, 4, LANES), f32),
         ],
-        in_specs=[scalars] + [VMEM] * 23,
+        in_specs=[VMEM] * 23,
         out_specs=[VMEM] * 2,
         scratch_shapes=[
             pltpu.VMEM((planes + 4, up8(rows + 4), LANES), f32),
@@ -972,7 +970,7 @@
         compiler_params=PARAMS,
         name="operator",
     )(
-        start, own, pair, edge, second, from_ym, from_yp, pair_ym, pair_yp, corners,
+        own, pair, edge, second, from_ym, from_yp, pair_ym, pair_yp, corners,
         *early, *middle,
     )
 
@@ -1008,12 +1006,12 @@
     return pl.pallas_call(
         functools.partial(filter_kernel, sizes, counts),
         out_shape=jax.ShapeDtypeStruct((planes, rows, LANES), f32),
-        in_specs=[scalars] + [VMEM] * 3,
+        in_specs=[VMEM] * 3,
         out_specs=VMEM,
         scratch_shapes=[pltpu.VMEM((planes + 4, rows + 4, LANES), f32)],
         compiler_params=PARAMS,
         name="cone",
-    )(start, *blocks, scale)
+    )(*blocks, scale)
 
 
 def solution(mesh):

time: 64 us -> 61.9 us (0.967)
  Pallas kernels: 16.4 us -> 12.6 us
  blocking collectives: 24.7 us -> 26 us
    all_to_all x2, blocking collectives: 24.7 us -> 26 us  [gathered(): mine = lax.all_to_all(copies, ('gx', 'gy'), 0, 0, axis_index_groups=groups)]
  transfers between devices with their start and end apart: 11 -> 11, of which waited for: 5 -> 5; matrix products, arithmetic and copies ran while one was open for 0% -> 0% of each run, Pallas kernels for 10% -> 6%
where the time goes in v15:
time: 61.9 us; the launch traced here: 61.5 us
  blocking collectives  26 us (42%)
  starting transfers between devices  15.5 us (25%)
  Pallas kernels  12.6 us (20%)
  waiting for transfers between devices  5.53 us (9%)
  local copies, waits for them, and re-layouts  1.07 us (2%)
  other arithmetic  0.72 us (1%)
    all_to_all x2, blocking collectives, gathered(): mine = lax.all_to_all(copies, ('gx', 'gy'), 0, 0, axis_index_groups=groups)  26 us
    ppermute x2, starting transfers between devices, moved(): return lax.ppermute(value, axis, pairs)  6.77 us
    ppermute x6, starting transfers between devices, swapped(): return lax.ppermute(value, 'gx', links(0, 1) + links(1, -1))  6.71 us
    ppermute x6, waiting for transfers between devices, swapped(): return lax.ppermute(value, 'gx', links(0, 1) + links(1, -1))  5.52 us
    pallas_call x1, Pallas kernels, local(): pl.pallas_call(functools.partial(main_kernel, sizes), out_shape=[fields(4...  4.27 us
    pallas_call x1, Pallas kernels, local(): pl.pallas_call(functools.partial(solve_kernel, sizes), out_shape=jax.Shap...  3.44 us
    pallas_call x1, Pallas kernels, local(): pl.pallas_call(functools.partial(middle_kernel, sizes), out_shape=[column...  2.01 us
    pallas_call x1, Pallas kernels, local(): pl.pallas_call(functools.partial(early_kernel, sizes), out_shape=[window]...  1.82 us
  transfers between devices with their start and end apart: 11, of which 5 were waited for; matrix products, arithmetic and copies ran while one was open for 0% of the time, Pallas kernels for 6%

profile of v15, /device:TPU:0, one launch (start us, length us, event | category | flops | bytes accessed | tf_op | source)
XLA Modules:
  0.0 61.5 jit_solution(4608924169666759041)
XLA Ops:
  0.0 0.7 %negate_select_fusion.codes = f32[2,8,128]{2,1,0:T(8,128)S(1)} fusion(s32[2,8,128]{2,1,0:T(8,128)} %levels.1, s32[2,8,128]{2,1,0:T(8,128)} %param.5), kind=kLoop, calls=%fused_computation | loop fusion | flops 16384 | bytes 24576 | tf_op jit(solution)/shard_map/jit(_where)/select_n | solution.py:831
  0.7 0.0 copy-start
  0.7 1.1 %copy-done = f32[3,24,2,8,128]{4,3,2,1,0:T(8,128)S(1)} copy-done((f32[3,24,2,8,128]{4,3,2,1,0:T(8,128)S(1)}, f32[3,24,2,8,128]{4,3,2,1,0:T(8,128)}, u32[]{:S(2)}) %copy-start) | copy-done | bytes 589848
  1.8 0.1 pack.1
  1.9 0.5 collective-permute-start
  2.4 0.7 %collective-permute-start.3 = (f32[592,128]{1,0:T(8,128)S(1)}, f32[592,128]{1,0:T(8,128)S(1)}, u32[]{:S(2)}, u32[]{:S(2)}) collective-permute-start(f32[592,128]{1,0:T(8,128)S(1)} %get-tuple-element.35), channel_id=1, source_target_pairs={{4,8},{12,16},{20,24},{8,4},{16,12},{24,20},{5,9},{13,17},{21,25},... | collective-permute-start | bytes 909320 | tf_op jit(solution)/shard_map/ppermute | solution.py:863
  3.1 1.0 %collective-permute-done.pair = f32[1168,128]{1,0:T(8,128)S(1)} collective-permute-done((f32[1168,128]{1,0:T(8,128)S(1)}, f32[1168,128]{1,0:T(8,128)S(1)}, u32[]{:S(2)}, u32[]{:S(2)}) %collective-permute-start) | collective-permute-done | bytes 598048 | tf_op jit(solution)/shard_map/ppermute | solution.py:860
  4.1 1.3 %collective-permute-start.2 = (f32[296,128]{1,0:T(8,128)S(1)}, f32[296,128]{1,0:T(8,128)S(1)}, u32[]{:S(2)}, u32[]{:S(2)}) collective-permute-start(f32[296,128]{1,0:T(8,128)S(1)} %get-tuple-element.34), channel_id=1, source_target_pairs={{1,0},{2,1},{3,2},{5,4},{6,5},{7,6},{9,8},{10,9},{11,10},{13,12},{... | collective-permute-start | bytes 454664 | tf_op jit(solution)/shard_map/ppermute | solution.py:854
  5.4 5.5 %collective-permute-start.1 = (f32[152,128]{1,0:T(8,128)S(1)}, f32[152,128]{1,0:T(8,128)S(1)}, u32[]{:S(2)}, u32[]{:S(2)}) collective-permute-start(f32[152,128]{1,0:T(8,128)S(1)} %get-tuple-element.33), channel_id=1, source_target_pairs={{0,1},{1,2},{2,3},{4,5},{5,6},{6,7},{8,9},{9,10},{10,11},{12,13},{... | collective-permute-start | bytes 233480 | tf_op jit(solution)/shard_map/ppermute | solution.py:854
  10.9 1.5 %collective-permute-start.4 = (f32[2,8,128]{2,1,0:T(8,128)S(1)}, f32[2,8,128]{2,1,0:T(8,128)S(1)}, u32[]{:S(2)}, u32[]{:S(2)}) collective-permute-start(f32[2,8,128]{2,1,0:T(8,128)S(1)} %negate_select_fusion.codes), channel_id=1, source_target_pairs={{0,4},{8,12},{16,20},{24,28},{4,0},{12,8},{20,16},{28,24},{1,5},{9... | collective-permute-start | bytes 24584 | tf_op jit(solution)/shard_map/ppermute | solution.py:860
  12.4 0.8 %collective-permute-done.4.begun = f32[2,8,128]{2,1,0:T(8,128)S(1)} collective-permute-done((f32[2,8,128]{2,1,0:T(8,128)S(1)}, f32[2,8,128]{2,1,0:T(8,128)S(1)}, u32[]{:S(2)}, u32[]{:S(2)}) %collective-permute-start.4) | collective-permute-done | bytes 8224 | tf_op jit(solution)/shard_map/ppermute | solution.py:860
  13.2 0.7 %collective-permute-start.5 = (f32[576,128]{1,0:T(8,128)S(1)}, f32[576,128]{1,0:T(8,128)S(1)}, u32[]{:S(2)}, u32[]{:S(2)}) collective-permute-start(f32[576,128]{1,0:T(8,128)S(1)} %second.1), channel_id=1, source_target_pairs={{8,4},{16,12},{24,20},{9,5},{17,13},{25,21},{10,6},{18,14},{26,22}... | collective-permute-start | bytes 884744 | tf_op jit(solution)/shard_map/ppermute | solution.py:885
  13.9 0.0 collective-permute-done.3.edge
  13.9 0.0 collective-permute-done.1.ym
  13.9 0.0 collective-permute-done.2.yp
  14.0 0.7 %collective-permute-start.8 = (f32[448,128]{1,0:T(8,128)S(1)}, f32[448,128]{1,0:T(8,128)S(1)}, u32[]{:S(2)}, u32[]{:S(2)}) collective-permute-start(f32[448,128]{1,0:T(8,128)S(1)} %corners.1), channel_id=1, source_target_pairs={{4,8},{12,16},{20,24},{8,4},{16,12},{24,20},{5,9},{13,17},{21,25},... | collective-permute-start | bytes 688136 | tf_op jit(solution)/shard_map/ppermute | solution.py:863
  14.6 4.6 %collective-permute-start.7 = (f32[296,128]{1,0:T(8,128)S(1)}, f32[296,128]{1,0:T(8,128)S(1)}, u32[]{:S(2)}, u32[]{:S(2)}) collective-permute-start(f32[296,128]{1,0:T(8,128)S(1)} %collective-permute-done.2.yp), channel_id=1, source_target_pairs={{0,4},{8,12},{16,20},{24,28},{4,0},{12,8},{20,16},{28,24},{1,5},{9... | collective-permute-start | bytes 454664 | tf_op jit(solution)/shard_map/ppermute | solution.py:860
  19.3 0.1 collective-permute-start.6
  19.4 1.2 %collective-permute-done.6.ym_pair = f32[152,128]{1,0:T(8,128)S(1)} collective-permute-done((f32[152,128]{1,0:T(8,128)S(1)}, f32[152,128]{1,0:T(8,128)S(1)}, u32[]{:S(2)}, u32[]{:S(2)}) %collective-permute-start.6) | collective-permute-done | bytes 77856 | tf_op jit(solution)/shard_map/ppermute | solution.py:860
  20.6 0.0 collective-permute-done.7.yp_pair
  20.6 1.8 %early.1 = (f32[33,72,128]{2,1,0:T(8,128)S(1)}, f32[33,72,128]{2,1,0:T(8,128)S(1)}, f32[33,72,128]{2,1,0:T(8,128)S(1)}, f32[27,72,128]{2,1,0:T(8,128)S(1)}, f32[27,72,128]{2,1,0:T(8,128)S(1)}) custom-call(f32[1168,128]{1,0:T(8,128)S(1)} %get-tuple-element.31.own, f32[1168,128]{1,0:T(8,128)S(1)} %collective-permute-done.pair, ...), custom_call_target="tpu_custom_call" | custom-call | flops 29491200 | bytes 8388608 | tf_op jit(solution)/shard_map/early/pallas_call | solution.py:903
  22.4 0.0 collective-permute-done.5.second
  22.4 2.0 %middle.1 = (f32[21,72,128]{2,1,0:T(8,128)S(1)}, f32[21,72,128]{2,1,0:T(8,128)S(1)}, f32[7,72,128]{2,1,0:T(8,128)S(1)}, f32[21,72,128]{2,1,0:T(8,128)S(1)}, f32[...) custom-call(f32[1168,128]{1,0:T(8,128)S(1)} %get-tuple-element.31.ow, ...), custom_call_target="tpu_custom_call" | custom-call | tf_op jit(solution)/shard_map/middle/pallas_call | solution.py:929
  24.4 0.0 collective-permute-done.8.corners
  24.4 4.3 %operator.1 = (bf16[96,4608]{1,0:T(8,128)(2,1)S(1)}, f32[16,3,4,128]{3,2,1,0:T(4,128)S(1)}) custom-call(f32[1168,128]{1,0:T(8,128)S(1)} %get-tuple-element.31.own, f32[1168,128]{1,0:T(8,128)S(1)} %collective-permute-done.pair, f32[592,128]{1,0:T(8,128)S(1)} %collective-permute-done.3.edge, f32[576,128]{1,0:T(8,128)S(1)} %collective-permute-done.5.second, ...), custom_call_target="tpu_custom_call" | custom-call | tf_op jit(solution)/shard_map/operator/pallas_call | solution.py:949
  28.7 15.1 %all_to_all.10.system = f32[16,3,4,128]{3,2,1,0:T(4,128)S(1)} all-to-all(f32[16,3,4,128]{3,2,1,0:T(4,128)S(1)} %get-tuple-element.53), channel_id=1, replica_groups={{0,1,2,3,8,9,10,11,16,17,18,19,24,25,26,27},{4,5,6,7,12,13,14,15,20,21,..., dimensions={0} | all-to-all | bytes 196608 | tf_op jit(solution)/shard_map/all_to_all | solution.py:983
  43.8 0.0 collective-permute-start.9
  43.8 1.3 %collective-permute-done.9.system_pair = f32[16,3,4,128]{3,2,1,0:T(4,128)S(1)} collective-permute-done((f32[16,3,4,128]{3,2,1,0:T(4,128)S(1)}, f32[16,3,4,128]{3,2,1,0:T(4,128)S(1)}, u32[]{:S(2)}, u32[]{:S(2)}) %collective-permute-start.9) | collective-permute-done | bytes 98336 | tf_op jit(solution)/shard_map/ppermute | solution.py:860
  45.1 0.0 copy-start.1
  45.1 3.4 %solve.1 = f32[16,2,8,128]{3,2,1,0:T(8,128)S(1)} custom-call(f32[16,3,4,128]{3,2,1,0:T(4,128)S(1)} %all_to_all.10.system, f32[16,3,4,128]{3,2,1,0:T(4,128)S(1)} %collective-permute-done.9.system_pair, bf16[96,5760]{1,0:T(8,128)(2,1)S(1)} %get-tuple-element.51.both_m, bf16[96,4608]{1,0:T(8,128)(2,1)S(1)} %get-tuple-element.54.both_r, ...), custom_call_target="tpu_custom_call" | custom-call | tf_op jit(solution)/shard_map/solve/pallas_call | solution.py:988
  48.6 10.9 %all_to_all.11.blocks = f32[16,2,8,128]{3,2,1,0:T(8,128)S(1)} all-to-all(f32[16,2,8,128]{3,2,1,0:T(8,128)S(1)} %solve.1), channel_id=1, replica_groups={{0,1,2,3,8,9,10,11,16,17,18,19,24,25,26,27},{4,5,6,7,12,13,14,15,20,21,..., dimensions={0} | all-to-all | bytes 262144 | tf_op jit(solution)/shard_map/all_to_all | solution.py:983
  59.5 0.0 collective-permute-start.10
  59.5 0.0 copy-done.1
  59.5 0.1 scale.1
  59.6 1.2 %collective-permute-done.10.blocks_pair = f32[16,2,8,128]{3,2,1,0:T(8,128)S(1)} collective-permute-done((f32[16,2,8,128]{3,2,1,0:T(8,128)S(1)}, f32[16,2,8,128]{3,2,1,0:T(8,128)S(1)}, u32[]{:S(2)}, u32[]{:S(2)}) %collective-permute-start.10) | collective-permute-done | bytes 131104 | tf_op jit(solution)/shard_map/ppermute | solution.py:860
  60.8 0.7 %cone.1 = f32[2,8,128]{2,1,0:T(8,128)} custom-call(f32[16,2,8,128]{3,2,1,0:T(8,128)S(1)} %all_to_all.11.blocks, f32[16,2,8,128]{3,2,1,0:T(8,128)S(1)} %collective-permute-done.10.blocks_pair, f32[2,8,128]{2,1,0:T(8,128)S(1)} %scale.1), custom_call_target="tpu_custom_call" | custom-call | tf_op jit(solution)/shard_map/cone/pallas_call | solution.py:1006
  (3 shorter events, 0.1 us)
Async XLA Ops:
  0.7 1.1 %copy-start = (f32[3,24,2,8,128]{4,3,2,1,0:T(8,128)S(1)}, f32[3,24,2,8,128]{4,3,2,1,0:T(8,128)}, u32[]{:S(2)}) copy-start(f32[3,24,2,8,128]{4,3,2,1,0:T(8,128)} %forces.1) | copy-start | bytes 1769476
  1.9 2.2 %collective-permute-start = (f32[1168,128]{1,0:T(8,128)S(1)}, f32[1168,128]{1,0:T(8,128)S(1)}, u32[]{:S(2)}, u32[]{:S(2)}) collective-permute-start(f32[1168,128]{1,0:T(8,128)S(1)} %get-tuple-element.31.own), channel_id=1, source_target_pairs={{0,4},{8,12},{16,20},{24,28},{4,0},{12,8},{20,16},{28,24},{1,5},{9... | collective-permute-start | bytes 1794056 | tf_op jit(solution)/shard_map/ppermute | solution.py:860
  2.4 11.5 %collective-permute-start.3 = (f32[592,128]{1,0:T(8,128)S(1)}, f32[592,128]{1,0:T(8,128)S(1)}, u32[]{:S(2)}, u32[]{:S(2)}) collective-permute-start(f32[592,128]{1,0:T(8,128)S(1)} %get-tuple-element.35), channel_id=1, source_target_pairs={{4,8},{12,16},{20,24},{8,4},{16,12},{24,20},{5,9},{13,17},{21,25},... | collective-permute-start | bytes 909320 | tf_op jit(solution)/shard_map/ppermute | solution.py:863
  4.1 9.8 %collective-permute-start.2 = (f32[296,128]{1,0:T(8,128)S(1)}, f32[296,128]{1,0:T(8,128)S(1)}, u32[]{:S(2)}, u32[]{:S(2)}) collective-permute-start(f32[296,128]{1,0:T(8,128)S(1)} %get-tuple-element.34), channel_id=1, source_target_pairs={{1,0},{2,1},{3,2},{5,4},{6,5},{7,6},{9,8},{10,9},{11,10},{13,12},{... | collective-permute-start | bytes 454664 | tf_op jit(solution)/shard_map/ppermute | solution.py:854
  5.4 8.5 %collective-permute-start.1 = (f32[152,128]{1,0:T(8,128)S(1)}, f32[152,128]{1,0:T(8,128)S(1)}, u32[]{:S(2)}, u32[]{:S(2)}) collective-permute-start(f32[152,128]{1,0:T(8,128)S(1)} %get-tuple-element.33), channel_id=1, source_target_pairs={{0,1},{1,2},{2,3},{4,5},{5,6},{6,7},{8,9},{9,10},{10,11},{12,13},{... | collective-permute-start | bytes 233480 | tf_op jit(solution)/shard_map/ppermute | solution.py:854
  10.9 2.3 %collective-permute-start.4 = (f32[2,8,128]{2,1,0:T(8,128)S(1)}, f32[2,8,128]{2,1,0:T(8,128)S(1)}, u32[]{:S(2)}, u32[]{:S(2)}) collective-permute-start(f32[2,8,128]{2,1,0:T(8,128)S(1)} %negate_select_fusion.codes), channel_id=1, source_target_pairs={{0,4},{8,12},{16,20},{24,28},{4,0},{12,8},{20,16},{28,24},{1,5},{9... | collective-permute-start | bytes 24584 | tf_op jit(solution)/shard_map/ppermute | solution.py:860
  13.2 9.2 %collective-permute-start.5 = (f32[576,128]{1,0:T(8,128)S(1)}, f32[576,128]{1,0:T(8,128)S(1)}, u32[]{:S(2)}, u32[]{:S(2)}) collective-permute-start(f32[576,128]{1,0:T(8,128)S(1)} %second.1), channel_id=1, source_target_pairs={{8,4},{16,12},{24,20},{9,5},{17,13},{25,21},{10,6},{18,14},{26,22}... | collective-permute-start | bytes 884744 | tf_op jit(solution)/shard_map/ppermute | solution.py:885
  14.0 10.4 %collective-permute-start.8 = (f32[448,128]{1,0:T(8,128)S(1)}, f32[448,128]{1,0:T(8,128)S(1)}, u32[]{:S(2)}, u32[]{:S(2)}) collective-permute-start(f32[448,128]{1,0:T(8,128)S(1)} %corners.1), channel_id=1, source_target_pairs={{4,8},{12,16},{20,24},{8,4},{16,12},{24,20},{5,9},{13,17},{21,25},... | collective-permute-start | bytes 688136 | tf_op jit(solution)/shard_map/ppermute | solution.py:863
  14.6 5.9 %collective-permute-start.7 = (f32[296,128]{1,0:T(8,128)S(1)}, f32[296,128]{1,0:T(8,128)S(1)}, u32[]{:S(2)}, u32[]{:S(2)}) collective-permute-start(f32[296,128]{1,0:T(8,128)S(1)} %collective-permute-done.2.yp), channel_id=1, source_target_pairs={{0,4},{8,12},{16,20},{24,28},{4,0},{12,8},{20,16},{28,24},{1,5},{9... | collective-permute-start | bytes 454664 | tf_op jit(solution)/shard_map/ppermute | solution.py:860
  19.3 1.3 %collective-permute-start.6 = (f32[152,128]{1,0:T(8,128)S(1)}, f32[152,128]{1,0:T(8,128)S(1)}, u32[]{:S(2)}, u32[]{:S(2)}) collective-permute-start(f32[152,128]{1,0:T(8,128)S(1)} %collective-permute-done.1.ym), channel_id=1, source_target_pairs={{0,4},{8,12},{16,20},{24,28},{4,0},{12,8},{20,16},{28,24},{1,5},{9... | collective-permute-start | bytes 233480 | tf_op jit(solution)/shard_map/ppermute | solution.py:860
  43.8 1.3 %collective-permute-start.9 = (f32[16,3,4,128]{3,2,1,0:T(4,128)S(1)}, f32[16,3,4,128]{3,2,1,0:T(4,128)S(1)}, u32[]{:S(2)}, u32[]{:S(2)}) collective-permute-start(f32[16,3,4,128]{3,2,1,0:T(4,128)S(1)} %all_to_all.10.system), channel_id=1, source_target_pairs={{0,4},{8,12},{16,20},{24,28},{4,0},{12,8},{20,16},{28,24},{1,5},{9... | collective-permute-start | bytes 294920 | tf_op jit(solution)/shard_map/ppermute | solution.py:860
  45.1 14.3 %copy-start.1 = (s32[2,8,128]{2,1,0:T(8,128)S(1)}, s32[2,8,128]{2,1,0:T(8,128)}, u32[]{:S(2)}) copy-start(s32[2,8,128]{2,1,0:T(8,128)} %levels.1) | copy-start | bytes 24580
  59.5 1.3 %collective-permute-start.10 = (f32[16,2,8,128]{3,2,1,0:T(8,128)S(1)}, f32[16,2,8,128]{3,2,1,0:T(8,128)S(1)}, u32[]{:S(2)}, u32[]{:S(2)}) collective-permute-start(f32[16,2,8,128]{3,2,1,0:T(8,128)S(1)} %all_to_all.11.blocks), channel_id=1, source_target_pairs={{0,4},{8,12},{16,20},{24,28},{4,0},{12,8},{20,16},{28,24},{1,5},{9... | collective-permute-start | bytes 393224 | tf_op jit(solution)/shard_map/ppermute | solution.py:860

commit v16 on v15

--- a/solution.py
+++ b/solution.py
@@ -418,7 +418,7 @@
 
 def middle_kernel(
     sizes, own, pair, edge, second, start, sums_e, diffs_e, acc_se, acc_de,
-    sums, diffs, middle, acc_s, acc_d, w_sums, w_diffs, both_out, gram_out,
+    sums, diffs, middle, acc_s, acc_d, w_sums, w_diffs, both_out, gram_out, acc2_s, acc2_d,
     stiff_ref, inverse, right,
 ):
     planes, rows, cases = sizes
@@ -495,14 +495,20 @@
     unrolled(len(core), len(core), lambda index: image(planes, core[0] + index, last + index))
     gram_out[...] = products(right[...], both_out[:, : last * 3 * LANES])
 
+    find = whole(w_sums, w_diffs, len(core))
+    kept = range(len(core))
+    apply_elements(
+        find, stiff_ref, acc2_s, acc2_d, planes, len(core) - 1, kept, 2, core[0], cases
+    )
+
 
 def main_kernel(
     sizes, own, pair, edge, second, ym, yp, ym_pair, yp_pair, corners,
     start, sums_e, diffs_e, acc_se, acc_de,
     sums_m, diffs_m, middle_m, acc_sm, acc_dm, w_sm, w_dm, both_m, gram_m,
-    both_out, system_out, stiff_ref, inverse,
+    acc2_sm, acc2_dm, both_out, system_out, stiff_ref, inverse,
     middle, sums, diffs, acc_s0, acc_d0, acc_s1, acc_d1, w_sums, w_diffs,
-    acc2_s, acc2_d, right, second_m, second_r, table,
+    acc2_s0, acc2_d0, acc2_s1, acc2_d1, right, second_m, second_r, table,
 ):
     planes, rows, cases = sizes
     block = 3 * cases
@@ -598,24 +604,32 @@
             return w_sums, w_diffs, len(rim), rim.index(row)
         return w_sm, w_dm, len(core), row - core[0]
 
-    apply_elements(find, stiff_ref, acc2_s, acc2_d, planes, rows, range(nodes_y), 2, 2, cases)
+    def find_last(row):
+        return find(row + rows - 2)
+
+    low, high = (acc2_s0, acc2_d0), (acc2_s1, acc2_d1)
+    apply_elements(find, stiff_ref, *low, planes, 2, range(3), 2, 2, cases)
+    apply_elements(find_last, stiff_ref, *high, planes, 2, range(3), 2, rows, cases)
 
     def second_force(ref, x, y, place):
-        column = x * nodes_y + y
-        s, d = acc2_s[column], acc2_d[column]
+        s, d = None, None
+        for parts, width, first in (
+            (low, 3, 0), ((acc2_sm, acc2_dm), len(core), core[0]), (high, 3, rows - 2)
+        ):
+            if first <= y < first + width:
+                column = x * width + y - first
+                more = parts[0][column], parts[1][column]
+                s, d = more if s is None else (s + more[0], d + more[1])
         force = s - d + shift_up(s + d)
         for k in range(3):
             value = force[k * cases : (k + 1) * cases]
-            high = value.astype(bf16).astype(f32)
+            top = value.astype(bf16).astype(f32)
             lane = pl.ds(pl.multiple_of((place * 3 + k) * LANES, LANES), LANES)
-            ref[:, lane] = jnp.concatenate([high, value - high], 0).astype(bf16)
-
-    unrolled(
-        (planes + 1) * len(core), len(core),
-        lambda index: second_force(
-            second_m, index // len(core), core[0] + index % len(core), index
-        ),
-    )
+            ref[:, lane] = jnp.concatenate([top, value - top], 0).astype(bf16)
+
+    for x in range(planes + 1):
+        for index, y in enumerate(core):
+            second_force(second_m, x, y, x * len(core) + index)
     for index, (x, y) in enumerate(columns):
         second_force(second_r, x, y, index)
 
@@ -641,13 +655,13 @@
 
 
 def solve_kernel(
-    sizes, system, system_pair, both_m, both_r, codes, out, mixing, sums, diffs, energy, square, full
+    sizes, system, both_m, both_r, codes, out, mixing, sums, diffs, energy, square, full
 ):
     planes, rows, cases = sizes
     two = 2 * cases
     nodes_y = rows + 1
     count = planes * rows
-    total = jnp.sum(system[...], axis=0) + jnp.sum(system_pair[...], axis=0)
+    total = jnp.sum(system[...], axis=0)
     half, depth = cases // 2, system.shape[2]
     square[...] = jnp.zeros(square.shape, f32)
     for part in range(half // depth):
@@ -674,7 +688,7 @@
         full[index * cases : (index + 1) * cases, cases:two] = right
     table = full[...]
     lane = lax.broadcasted_iota(jnp.int32, (1, LANES), 1)
-    gone, wide = 0, 4
+    gone, wide = 0, 8
     for pivot in range(0, two, wide):
         drop = pivot // 8 * 8 - gone
         table = table[drop:]
@@ -932,9 +946,10 @@
         + [columns(rows - 1)]
         + [columns(3 * (rows - 1))] * 2
         + [columns((planes + 1) * core)] * 2
-        + [fields(4, (planes + 1) * core), jax.ShapeDtypeStruct((2 * cases, 2 * cases), f32)],
+        + [fields(4, (planes + 1) * core), jax.ShapeDtypeStruct((2 * cases, 2 * cases), f32)]
+        + [columns((planes + 1) * core)] * 2,
         in_specs=[VMEM] * 9,
-        out_specs=[VMEM] * 9,
+        out_specs=[VMEM] * 11,
         scratch_shapes=[
             pltpu.VMEM((planes + 4, up8(rows), LANES), f32),
             pltpu.VMEM((planes + 3, up8(rows), LANES), f32),
@@ -945,14 +960,13 @@
     )(own, pair, edge, second, *early)
 
     rim, rim_own = rim_columns(planes, rows)
-    field = scratch(columns(nodes))
     both, system = pl.pallas_call(
         functools.partial(main_kernel, sizes),
         out_shape=[
             fields(4, len(rim)),
-            jax.ShapeDtypeStruct((devices // 2, cases // 8, 4, LANES), f32),
+            jax.ShapeDtypeStruct((devices, cases // 8, 4, LANES), f32),
         ],
-        in_specs=[VMEM] * 23,
+        in_specs=[VMEM] * 25,
         out_specs=[VMEM] * 2,
         scratch_shapes=[
             pltpu.VMEM((planes + 4, up8(rows + 4), LANES), f32),
@@ -961,7 +975,7 @@
             *[scratch(columns(12))] * 2,
             *[scratch(columns(6))] * 4,
             *[scratch(columns((planes + 1) * 4))] * 2,
-            field, field,
+            *[scratch(columns((planes + 1) * 3))] * 4,
             scratch(fields(4, rim_own)),
             scratch(fields(2, (planes + 1) * core)),
             scratch(fields(2, len(rim))),
@@ -983,24 +997,24 @@
         mine = lax.all_to_all(copies, ("gx", "gy"), 0, 0, axis_index_groups=groups)
         return mine, swapped(mine)
 
-    system = gathered(system)
+    system = lax.all_to_all(system, ("gx", "gy"), 0, 0)
 
     weighted = pl.pallas_call(
         functools.partial(solve_kernel, sizes),
         out_shape=jax.ShapeDtypeStruct((devices // 2, planes, rows, LANES), f32),
-        in_specs=[VMEM] * 5,
+        in_specs=[VMEM] * 4,
         out_specs=VMEM,
         scratch_shapes=[
             pltpu.VMEM((2 * cases, LANES), f32),
-            field,
-            field,
+            scratch(columns(nodes)),
+            scratch(columns(nodes)),
             pltpu.VMEM((rows, 8, LANES), f32),
             pltpu.VMEM((LANES, LANES), f32),
             pltpu.VMEM((3 * cases, LANES), f32),
         ],
         compiler_params=PARAMS,
         name="solve",
-    )(*system, middle[7], both, codes)
+    )(system, middle[7], both, codes)
 
     blocks = gathered(weighted)
     return pl.pallas_call(

time: 61.9 us -> 60 us (0.969)
  waiting for transfers between devices: 5.53 us -> 4.23 us
    all_to_all x2 -> x1, blocking collectives: 26 us -> 10.7 us  [gathered(): mine = lax.all_to_all(copies, ('gx', 'gy'), 0, 0, axis_index_groups=groups)]
    all_to_all x0 -> x1, blocking collectives: none -> 15.2 us  [local(): system = lax.all_to_all(system, ('gx', 'gy'), 0, 0)]
    ppermute x6 -> x5, waiting for transfers between devices: 5.52 us -> 4.22 us  [swapped(): return lax.ppermute(value, 'gx', links(0, 1) + links(1, -1))]
    pallas_call x1, Pallas kernels: 4.27 us -> 3.56 us  [local(): pl.pallas_call(functools.partial(main_kernel, sizes), out_shape=[fields(4...]
    ppermute x6 -> x5, starting transfers between devices: 6.71 us -> 6.71 us  [swapped(): return lax.ppermute(value, 'gx', links(0, 1) + links(1, -1))]
  transfers between devices with their start and end apart: 11 -> 10, of which waited for: 5 -> 4; matrix products, arithmetic and copies ran while one was open for 0% -> 0% of each run, Pallas kernels for 6% -> 8%
where the time goes in v16:
time: 60 us; the launch traced here: 59.6 us
  blocking collectives  25.9 us (43%)
  starting transfers between devices  15.5 us (26%)
  Pallas kernels  12.1 us (20%)
  waiting for transfers between devices  4.23 us (7%)
  local copies, waits for them, and re-layouts  1.07 us (2%)
  other arithmetic  0.72 us (1%)
    all_to_all x1, blocking collectives, local(): system = lax.all_to_all(system, ('gx', 'gy'), 0, 0)  15.2 us
    all_to_all x1, blocking collectives, gathered(): mine = lax.all_to_all(copies, ('gx', 'gy'), 0, 0, axis_index_groups=groups)  10.7 us
    ppermute x2, starting transfers between devices, moved(): return lax.ppermute(value, axis, pairs)  6.77 us
    ppermute x5, starting transfers between devices, swapped(): return lax.ppermute(value, 'gx', links(0, 1) + links(1, -1))  6.71 us
    ppermute x5, waiting for transfers between devices, swapped(): return lax.ppermute(value, 'gx', links(0, 1) + links(1, -1))  4.22 us
    pallas_call x1, Pallas kernels, local(): pl.pallas_call(functools.partial(main_kernel, sizes), out_shape=[fields(4...  3.56 us
    pallas_call x1, Pallas kernels, local(): pl.pallas_call(functools.partial(solve_kernel, sizes), out_shape=jax.Shap...  3.09 us
    pallas_call x1, Pallas kernels, local(): pl.pallas_call(functools.partial(middle_kernel, sizes), out_shape=[column...  2.57 us
  transfers between devices with their start and end apart: 10, of which 4 were waited for; matrix products, arithmetic and copies ran while one was open for 0% of the time, Pallas kernels for 8%

profile of v16, /device:TPU:0, one launch (start us, length us, event | category | flops | bytes accessed | tf_op | source)
XLA Modules:
  0.0 59.6 jit_solution(8854102147503979784)
XLA Ops:
  0.0 0.7 %negate_select_fusion.codes = f32[2,8,128]{2,1,0:T(8,128)S(1)} fusion(s32[2,8,128]{2,1,0:T(8,128)} %levels.1, s32[2,8,128]{2,1,0:T(8,128)} %param.5), kind=kLoop, calls=%fused_computation | loop fusion | flops 16384 | bytes 24576 | tf_op jit(solution)/shard_map/jit(_where)/select_n | solution.py:845
  0.7 0.0 copy-start
  0.7 1.1 %copy-done = f32[3,24,2,8,128]{4,3,2,1,0:T(8,128)S(1)} copy-done((f32[3,24,2,8,128]{4,3,2,1,0:T(8,128)S(1)}, f32[3,24,2,8,128]{4,3,2,1,0:T(8,128)}, u32[]{:S(2)}) %copy-start) | copy-done | bytes 589848
  1.8 0.1 pack.1
  1.9 0.5 collective-permute-start
  2.4 0.7 %collective-permute-start.3 = (f32[592,128]{1,0:T(8,128)S(1)}, f32[592,128]{1,0:T(8,128)S(1)}, u32[]{:S(2)}, u32[]{:S(2)}) collective-permute-start(f32[592,128]{1,0:T(8,128)S(1)} %get-tuple-element.37), channel_id=1, source_target_pairs={{4,8},{12,16},{20,24},{8,4},{16,12},{24,20},{5,9},{13,17},{21,25},... | collective-permute-start | bytes 909320 | tf_op jit(solution)/shard_map/ppermute | solution.py:877
  3.1 1.0 %collective-permute-done.pair = f32[1168,128]{1,0:T(8,128)S(1)} collective-permute-done((f32[1168,128]{1,0:T(8,128)S(1)}, f32[1168,128]{1,0:T(8,128)S(1)}, u32[]{:S(2)}, u32[]{:S(2)}) %collective-permute-start) | collective-permute-done | bytes 598048 | tf_op jit(solution)/shard_map/ppermute | solution.py:874
  4.1 1.3 %collective-permute-start.2 = (f32[296,128]{1,0:T(8,128)S(1)}, f32[296,128]{1,0:T(8,128)S(1)}, u32[]{:S(2)}, u32[]{:S(2)}) collective-permute-start(f32[296,128]{1,0:T(8,128)S(1)} %get-tuple-element.36), channel_id=1, source_target_pairs={{1,0},{2,1},{3,2},{5,4},{6,5},{7,6},{9,8},{10,9},{11,10},{13,12},{... | collective-permute-start | bytes 454664 | tf_op jit(solution)/shard_map/ppermute | solution.py:868
  5.4 5.5 %collective-permute-start.1 = (f32[152,128]{1,0:T(8,128)S(1)}, f32[152,128]{1,0:T(8,128)S(1)}, u32[]{:S(2)}, u32[]{:S(2)}) collective-permute-start(f32[152,128]{1,0:T(8,128)S(1)} %get-tuple-element.35), channel_id=1, source_target_pairs={{0,1},{1,2},{2,3},{4,5},{5,6},{6,7},{8,9},{9,10},{10,11},{12,13},{... | collective-permute-start | bytes 233480 | tf_op jit(solution)/shard_map/ppermute | solution.py:868
  10.9 1.5 %collective-permute-start.4 = (f32[2,8,128]{2,1,0:T(8,128)S(1)}, f32[2,8,128]{2,1,0:T(8,128)S(1)}, u32[]{:S(2)}, u32[]{:S(2)}) collective-permute-start(f32[2,8,128]{2,1,0:T(8,128)S(1)} %negate_select_fusion.codes), channel_id=1, source_target_pairs={{0,4},{8,12},{16,20},{24,28},{4,0},{12,8},{20,16},{28,24},{1,5},{9... | collective-permute-start | bytes 24584 | tf_op jit(solution)/shard_map/ppermute | solution.py:874
  12.4 0.8 %collective-permute-done.4.begun = f32[2,8,128]{2,1,0:T(8,128)S(1)} collective-permute-done((f32[2,8,128]{2,1,0:T(8,128)S(1)}, f32[2,8,128]{2,1,0:T(8,128)S(1)}, u32[]{:S(2)}, u32[]{:S(2)}) %collective-permute-start.4) | collective-permute-done | bytes 8224 | tf_op jit(solution)/shard_map/ppermute | solution.py:874
  13.2 0.7 %collective-permute-start.5 = (f32[576,128]{1,0:T(8,128)S(1)}, f32[576,128]{1,0:T(8,128)S(1)}, u32[]{:S(2)}, u32[]{:S(2)}) collective-permute-start(f32[576,128]{1,0:T(8,128)S(1)} %second.1), channel_id=1, source_target_pairs={{8,4},{16,12},{24,20},{9,5},{17,13},{25,21},{10,6},{18,14},{26,22}... | collective-permute-start | bytes 884744 | tf_op jit(solution)/shard_map/ppermute | solution.py:899
  13.9 0.0 collective-permute-done.3.edge
  13.9 0.0 collective-permute-done.1.ym
  13.9 0.0 collective-permute-done.2.yp
  14.0 0.7 %collective-permute-start.8 = (f32[448,128]{1,0:T(8,128)S(1)}, f32[448,128]{1,0:T(8,128)S(1)}, u32[]{:S(2)}, u32[]{:S(2)}) collective-permute-start(f32[448,128]{1,0:T(8,128)S(1)} %corners.1), channel_id=1, source_target_pairs={{4,8},{12,16},{20,24},{8,4},{16,12},{24,20},{5,9},{13,17},{21,25},... | collective-permute-start | bytes 688136 | tf_op jit(solution)/shard_map/ppermute | solution.py:877
  14.6 4.6 %collective-permute-start.7 = (f32[296,128]{1,0:T(8,128)S(1)}, f32[296,128]{1,0:T(8,128)S(1)}, u32[]{:S(2)}, u32[]{:S(2)}) collective-permute-start(f32[296,128]{1,0:T(8,128)S(1)} %collective-permute-done.2.yp), channel_id=1, source_target_pairs={{0,4},{8,12},{16,20},{24,28},{4,0},{12,8},{20,16},{28,24},{1,5},{9... | collective-permute-start | bytes 454664 | tf_op jit(solution)/shard_map/ppermute | solution.py:874
  19.3 0.1 collective-permute-start.6
  19.4 1.2 %collective-permute-done.6.ym_pair = f32[152,128]{1,0:T(8,128)S(1)} collective-permute-done((f32[152,128]{1,0:T(8,128)S(1)}, f32[152,128]{1,0:T(8,128)S(1)}, u32[]{:S(2)}, u32[]{:S(2)}) %collective-permute-start.6) | collective-permute-done | bytes 77856 | tf_op jit(solution)/shard_map/ppermute | solution.py:874
  20.6 0.0 collective-permute-done.7.yp_pair
  20.6 1.8 %early.1 = (f32[33,72,128]{2,1,0:T(8,128)S(1)}, f32[33,72,128]{2,1,0:T(8,128)S(1)}, f32[33,72,128]{2,1,0:T(8,128)S(1)}, f32[27,72,128]{2,1,0:T(8,128)S(1)}, f32[27,72,128]{2,1,0:T(8,128)S(1)}) custom-call(f32[1168,128]{1,0:T(8,128)S(1)} %get-tuple-element.33.own, f32[1168,128]{1,0:T(8,128)S(1)} %collective-permute-done.pair, ...), custom_call_target="tpu_custom_call" | custom-call | flops 29491200 | bytes 8388608 | tf_op jit(solution)/shard_map/early/pallas_call | solution.py:917
  22.4 0.0 collective-permute-done.5.second
  22.4 2.6 %middle.1 = (f32[21,72,128]{2,1,0:T(8,128)S(1)}, f32[21,72,128]{2,1,0:T(8,128)S(1)}, f32[7,72,128]{2,1,0:T(8,128)S(1)}, f32[21,72,128]{2,1,0:T(8,128)S(1)}, f32[...) custom-call(f32[1168,128]{1,0:T(8,128)S(1)} %get-tuple-element.33.ow, ...), custom_call_target="tpu_custom_call" | custom-call | tf_op jit(solution)/shard_map/middle/pallas_call | solution.py:943
  25.0 0.0 collective-permute-done.8.corners
  25.0 3.6 %operator.1 = (bf16[96,4608]{1,0:T(8,128)(2,1)S(1)}, f32[32,3,4,128]{3,2,1,0:T(4,128)S(1)}) custom-call(f32[1168,128]{1,0:T(8,128)S(1)} %get-tuple-element.33.own, f32[1168,128]{1,0:T(8,128)S(1)} %collective-permute-done.pair, f32[592,128]{1,0:T(8,128)S(1)} %collective-permute-done.3.edge, f32[576,128]{1,0:T(8,128)S(1)} %collective-permute-done.5.second, ...), custom_call_target="tpu_custom_call" | custom-call | tf_op jit(solution)/shard_map/operator/pallas_call | solution.py:963
  28.5 15.2 %all_to_all.10.system = f32[32,3,4,128]{3,2,1,0:T(4,128)S(1)} all-to-all(f32[32,3,4,128]{3,2,1,0:T(4,128)S(1)} %get-tuple-element.57), channel_id=1, replica_groups=mesh['gx'=8,'gy'=4] {'gx','gy'}, dimensions={0} | all-to-all | bytes 393216 | tf_op jit(solution)/shard_map/all_to_all | solution.py:1000
  43.7 0.0 copy-start.1
  43.7 3.1 %solve.1 = f32[16,2,8,128]{3,2,1,0:T(8,128)S(1)} custom-call(f32[32,3,4,128]{3,2,1,0:T(4,128)S(1)} %all_to_all.10.system, bf16[96,5760]{1,0:T(8,128)(2,1)S(1)} %get-tuple-element.53.both_m, bf16[96,4608]{1,0:T(8,128)(2,1)S(1)} %get-tuple-element.58.both_r, f32[2,8,128]{2,1,0:T(8,128)S(1)} %negate_select_fusion.codes), custom_call_target="tpu_custom_call" | custom-call | tf_op jit(solution)/shard_map/solve/pallas_call | solution.py:1002
  46.8 10.7 %all_to_all.11.blocks = f32[16,2,8,128]{3,2,1,0:T(8,128)S(1)} all-to-all(f32[16,2,8,128]{3,2,1,0:T(8,128)S(1)} %solve.1), channel_id=1, replica_groups={{0,1,2,3,8,9,10,11,16,17,18,19,24,25,26,27},{4,5,6,7,12,13,14,15,20,21,..., dimensions={0} | all-to-all | bytes 262144 | tf_op jit(solution)/shard_map/all_to_all | solution.py:997
  57.5 0.0 collective-permute-start.9
  57.5 0.0 copy-done.1
  57.5 0.1 scale.1
  57.7 1.2 %collective-permute-done.9.blocks_pair = f32[16,2,8,128]{3,2,1,0:T(8,128)S(1)} collective-permute-done((f32[16,2,8,128]{3,2,1,0:T(8,128)S(1)}, f32[16,2,8,128]{3,2,1,0:T(8,128)S(1)}, u32[]{:S(2)}, u32[]{:S(2)}) %collective-permute-start.9) | collective-permute-done | bytes 131104 | tf_op jit(solution)/shard_map/ppermute | solution.py:874
  58.9 0.7 %cone.1 = f32[2,8,128]{2,1,0:T(8,128)} custom-call(f32[16,2,8,128]{3,2,1,0:T(8,128)S(1)} %all_to_all.11.blocks, f32[16,2,8,128]{3,2,1,0:T(8,128)S(1)} %collective-permute-done.9.blocks_pair, f32[2,8,128]{2,1,0:T(8,128)S(1)} %scale.1), custom_call_target="tpu_custom_call" | custom-call | tf_op jit(solution)/shard_map/cone/pallas_call | solution.py:1020
  (3 shorter events, 0.1 us)
Async XLA Ops:
  0.7 1.1 %copy-start = (f32[3,24,2,8,128]{4,3,2,1,0:T(8,128)S(1)}, f32[3,24,2,8,128]{4,3,2,1,0:T(8,128)}, u32[]{:S(2)}) copy-start(f32[3,24,2,8,128]{4,3,2,1,0:T(8,128)} %forces.1) | copy-start | bytes 1769476
  1.9 2.2 %collective-permute-start = (f32[1168,128]{1,0:T(8,128)S(1)}, f32[1168,128]{1,0:T(8,128)S(1)}, u32[]{:S(2)}, u32[]{:S(2)}) collective-permute-start(f32[1168,128]{1,0:T(8,128)S(1)} %get-tuple-element.33.own), channel_id=1, source_target_pairs={{0,4},{8,12},{16,20},{24,28},{4,0},{12,8},{20,16},{28,24},{1,5},{9... | collective-permute-start | bytes 1794056 | tf_op jit(solution)/shard_map/ppermute | solution.py:874
  2.4 11.5 %collective-permute-start.3 = (f32[592,128]{1,0:T(8,128)S(1)}, f32[592,128]{1,0:T(8,128)S(1)}, u32[]{:S(2)}, u32[]{:S(2)}) collective-permute-start(f32[592,128]{1,0:T(8,128)S(1)} %get-tuple-element.37), channel_id=1, source_target_pairs={{4,8},{12,16},{20,24},{8,4},{16,12},{24,20},{5,9},{13,17},{21,25},... | collective-permute-start | bytes 909320 | tf_op jit(solution)/shard_map/ppermute | solution.py:877
  4.1 9.8 %collective-permute-start.2 = (f32[296,128]{1,0:T(8,128)S(1)}, f32[296,128]{1,0:T(8,128)S(1)}, u32[]{:S(2)}, u32[]{:S(2)}) collective-permute-start(f32[296,128]{1,0:T(8,128)S(1)} %get-tuple-element.36), channel_id=1, source_target_pairs={{1,0},{2,1},{3,2},{5,4},{6,5},{7,6},{9,8},{10,9},{11,10},{13,12},{... | collective-permute-start | bytes 454664 | tf_op jit(solution)/shard_map/ppermute | solution.py:868
  5.4 8.5 %collective-permute-start.1 = (f32[152,128]{1,0:T(8,128)S(1)}, f32[152,128]{1,0:T(8,128)S(1)}, u32[]{:S(2)}, u32[]{:S(2)}) collective-permute-start(f32[152,128]{1,0:T(8,128)S(1)} %get-tuple-element.35), channel_id=1, source_target_pairs={{0,1},{1,2},{2,3},{4,5},{5,6},{6,7},{8,9},{9,10},{10,11},{12,13},{... | collective-permute-start | bytes 233480 | tf_op jit(solution)/shard_map/ppermute | solution.py:868
  10.9 2.3 %collective-permute-start.4 = (f32[2,8,128]{2,1,0:T(8,128)S(1)}, f32[2,8,128]{2,1,0:T(8,128)S(1)}, u32[]{:S(2)}, u32[]{:S(2)}) collective-permute-start(f32[2,8,128]{2,1,0:T(8,128)S(1)} %negate_select_fusion.codes), channel_id=1, source_target_pairs={{0,4},{8,12},{16,20},{24,28},{4,0},{12,8},{20,16},{28,24},{1,5},{9... | collective-permute-start | bytes 24584 | tf_op jit(solution)/shard_map/ppermute | solution.py:874
  13.2 9.2 %collective-permute-start.5 = (f32[576,128]{1,0:T(8,128)S(1)}, f32[576,128]{1,0:T(8,128)S(1)}, u32[]{:S(2)}, u32[]{:S(2)}) collective-permute-start(f32[576,128]{1,0:T(8,128)S(1)} %second.1), channel_id=1, source_target_pairs={{8,4},{16,12},{24,20},{9,5},{17,13},{25,21},{10,6},{18,14},{26,22}... | collective-permute-start | bytes 884744 | tf_op jit(solution)/shard_map/ppermute | solution.py:899
  14.0 11.0 %collective-permute-start.8 = (f32[448,128]{1,0:T(8,128)S(1)}, f32[448,128]{1,0:T(8,128)S(1)}, u32[]{:S(2)}, u32[]{:S(2)}) collective-permute-start(f32[448,128]{1,0:T(8,128)S(1)} %corners.1), channel_id=1, source_target_pairs={{4,8},{12,16},{20,24},{8,4},{16,12},{24,20},{5,9},{13,17},{21,25},... | collective-permute-start | bytes 688136 | tf_op jit(solution)/shard_map/ppermute | solution.py:877
  14.6 5.9 %collective-permute-start.7 = (f32[296,128]{1,0:T(8,128)S(1)}, f32[296,128]{1,0:T(8,128)S(1)}, u32[]{:S(2)}, u32[]{:S(2)}) collective-permute-start(f32[296,128]{1,0:T(8,128)S(1)} %collective-permute-done.2.yp), channel_id=1, source_target_pairs={{0,4},{8,12},{16,20},{24,28},{4,0},{12,8},{20,16},{28,24},{1,5},{9... | collective-permute-start | bytes 454664 | tf_op jit(solution)/shard_map/ppermute | solution.py:874
  19.3 1.3 %collective-permute-start.6 = (f32[152,128]{1,0:T(8,128)S(1)}, f32[152,128]{1,0:T(8,128)S(1)}, u32[]{:S(2)}, u32[]{:S(2)}) collective-permute-start(f32[152,128]{1,0:T(8,128)S(1)} %collective-permute-done.1.ym), channel_id=1, source_target_pairs={{0,4},{8,12},{16,20},{24,28},{4,0},{12,8},{20,16},{28,24},{1,5},{9... | collective-permute-start | bytes 233480 | tf_op jit(solution)/shard_map/ppermute | solution.py:874
  43.7 13.8 %copy-start.1 = (s32[2,8,128]{2,1,0:T(8,128)S(1)}, s32[2,8,128]{2,1,0:T(8,128)}, u32[]{:S(2)}) copy-start(s32[2,8,128]{2,1,0:T(8,128)} %levels.1) | copy-start | bytes 24580
  57.5 1.3 %collective-permute-start.9 = (f32[16,2,8,128]{3,2,1,0:T(8,128)S(1)}, f32[16,2,8,128]{3,2,1,0:T(8,128)S(1)}, u32[]{:S(2)}, u32[]{:S(2)}) collective-permute-start(f32[16,2,8,128]{3,2,1,0:T(8,128)S(1)} %all_to_all.11.blocks), channel_id=1, source_target_pairs={{0,4},{8,12},{16,20},{24,28},{4,0},{12,8},{20,16},{28,24},{1,5},{9... | collective-permute-start | bytes 393224 | tf_op jit(solution)/shard_map/ppermute | solution.py:874

commit v17 on v16

--- a/solution.py
+++ b/solution.py
@@ -185,10 +185,13 @@
                 for c in range(2):
                     for k in range(3):
                         one, two = forces[a][0][c][k], forces[a][1][c][k]
-                        low = -two if one is None else one - two
-                        high = two if one is None else one + two
-                        here[a][c][k] = low if carry is None else carry[a][c][k] + low
-                        following[a][c][k] = high
+                        if one is None:
+                            here[a][c][k] = -two if carry is None else carry[a][c][k] - two
+                            following[a][c][k] = two
+                        else:
+                            low = one - two
+                            here[a][c][k] = low if carry is None else carry[a][c][k] + low
+                            following[a][c][k] = one + two
             emit(row, here)
             carry, lower = following, upper
         emit(rows, carry)
@@ -416,6 +419,25 @@
     return out[:left] + out[left:]
 
 
+def folds(cases):
+    two, count, rest = 2 * cases, 5 * cases // 12, cases // 6
+    first, part = 2 * two, LANES - 2 * two
+    return (
+        ((slice(0, count), slice(0, two)), (slice(0, count), slice(0, two))),
+        ((slice(0, count), slice(two, first)), (slice(count, 2 * count), slice(0, two))),
+        ((slice(0, rest), slice(first, LANES)), (slice(2 * count, cases), slice(0, part))),
+        (
+            (slice(rest, 2 * rest), slice(first, first + two - part)),
+            (slice(2 * count, cases), slice(part, two)),
+        ),
+    )
+
+
+def diagonal_place(cases, index):
+    line = cases // 3 + index
+    return slice(line, line + 1), slice(4 * cases, 5 * cases)
+
+
 def middle_kernel(
     sizes, own, pair, edge, second, start, sums_e, diffs_e, acc_se, acc_de,
     sums, diffs, middle, acc_s, acc_d, w_sums, w_diffs, both_out, gram_out, acc2_s, acc2_d,
@@ -508,7 +530,7 @@
     sums_m, diffs_m, middle_m, acc_sm, acc_dm, w_sm, w_dm, both_m, gram_m,
     acc2_sm, acc2_dm, both_out, system_out, stiff_ref, inverse,
     middle, sums, diffs, acc_s0, acc_d0, acc_s1, acc_d1, w_sums, w_diffs,
-    acc2_s0, acc2_d0, acc2_s1, acc2_d1, right, second_m, second_r, table,
+    acc2_s0, acc2_d0, acc2_s1, acc2_d1, right, second_m, second_r, table, dense,
 ):
     planes, rows, cases = sizes
     block = 3 * cases
@@ -640,35 +662,34 @@
     column = lax.broadcasted_iota(jnp.int32, (cases, cases), 1)
     load_load, load_image = gram[:cases, :cases], gram[cases:, :cases]
     mixed, image_image = other[:, :cases], other[:, cases:]
-    table[...] = jnp.zeros(table.shape, f32)
     table[:, 0:cases] = jnp.where(row <= column, load_load, load_image)
     table[:, cases:two] = jnp.where(row <= column, mixed, image_image)
-    for lane, value in ((two, load_image), (two + 1, image_image)):
-        own_entries = jnp.where(row == column, value, 0.0)
-        table[:, lane : lane + 1] = jnp.sum(own_entries, axis=1, keepdims=True)
-    half = cases // 2
-    folded = table[:half, :] + pltpu.roll(table[half:, :], LANES // 2, 1)
+    dense[...] = jnp.zeros(dense.shape, f32)
+    for target, source in folds(cases):
+        dense[target] = table[source]
+    for index, value in enumerate((load_image, image_image)):
+        diagonal = jnp.sum(jnp.where(row == column, value, 0.0), axis=0, keepdims=True)
+        dense[diagonal_place(cases, index)] = diagonal
     depth = system_out.shape[2]
     for index in range(system_out.shape[0]):
-        for part in range(half // depth):
-            system_out[index, part] = folded[part * depth : (part + 1) * depth]
+        for part in range(system_out.shape[1]):
+            system_out[index, part] = dense[part * depth : (part + 1) * depth, :]
 
 
 def solve_kernel(
-    sizes, system, both_m, both_r, codes, out, mixing, sums, diffs, energy, square, full
+    sizes, system, both_m, both_r, codes, out, mixing, sums, diffs, energy, square, full, dense
 ):
     planes, rows, cases = sizes
     two = 2 * cases
     nodes_y = rows + 1
     count = planes * rows
     total = jnp.sum(system[...], axis=0)
-    half, depth = cases // 2, system.shape[2]
+    depth = system.shape[2]
+    for part in range(system.shape[1]):
+        dense[part * depth : (part + 1) * depth, :] = total[part]
     square[...] = jnp.zeros(square.shape, f32)
-    for part in range(half // depth):
-        value = total[part]
-        square[part * depth : (part + 1) * depth, :] = value
-        lines = slice(half + part * depth, half + (part + 1) * depth)
-        square[lines, :] = pltpu.roll(value, LANES // 2, 1)
+    for source, target in folds(cases):
+        square[target] = dense[source]
     value, turned = square[0:cases, :], jnp.transpose(square[...])
     line = lax.broadcasted_iota(jnp.int32, (cases, cases), 0)
     place = lax.broadcasted_iota(jnp.int32, (cases, cases), 1)
@@ -677,11 +698,11 @@
         kept, other = value[:, start : start + cases], turned[start : start + cases, :cases]
         if diagonal is None:
             return jnp.where(line <= place, kept, other)
-        inner = jnp.where(line < place, other, value[:, diagonal : diagonal + 1])
+        inner = jnp.where(line < place, other, dense[diagonal_place(cases, diagonal)])
         return jnp.where(line > place, kept, inner)
 
-    load_image, mixed = mended(0, two), mended(cases)
-    parts = ((load_image, mixed), (mixed, mended(cases, two + 1)), (mended(0), load_image))
+    load_image, mixed = mended(0, 0), mended(cases)
+    parts = ((load_image, mixed), (mixed, mended(cases, 1)), (mended(0), load_image))
     full[...] = jnp.zeros(full.shape, f32)
     for index, (left, right) in enumerate(parts):
         full[index * cases : (index + 1) * cases, 0:cases] = left
@@ -964,7 +985,7 @@
         functools.partial(main_kernel, sizes),
         out_shape=[
             fields(4, len(rim)),
-            jax.ShapeDtypeStruct((devices, cases // 8, 4, LANES), f32),
+            jax.ShapeDtypeStruct((devices, 5 * cases // 24, 2, LANES), f32),
         ],
         in_specs=[VMEM] * 25,
         out_specs=[VMEM] * 2,
@@ -980,6 +1001,7 @@
             scratch(fields(2, (planes + 1) * core)),
             scratch(fields(2, len(rim))),
             pltpu.VMEM((cases, LANES), f32),
+            pltpu.VMEM((5 * cases // 12, LANES), f32),
         ],
         compiler_params=PARAMS,
         name="operator",
@@ -1011,6 +1033,7 @@
             pltpu.VMEM((rows, 8, LANES), f32),
             pltpu.VMEM((LANES, LANES), f32),
             pltpu.VMEM((3 * cases, LANES), f32),
+            pltpu.VMEM((5 * cases // 12, LANES), f32),
         ],
         compiler_params=PARAMS,
         name="solve",

time: 60 us -> 59.4 us (0.990)
  blocking collectives: 25.9 us -> 25.2 us
where the time goes in v17:
time: 59.4 us; the launch traced here: 59 us
  blocking collectives  25.2 us (42%)
  starting transfers between devices  15.5 us (26%)
  Pallas kernels  12.1 us (20%)
  waiting for transfers between devices  4.23 us (7%)
  local copies, waits for them, and re-layouts  1.07 us (2%)
  other arithmetic  0.72 us (1%)
    all_to_all x1, blocking collectives, local(): system = lax.all_to_all(system, ('gx', 'gy'), 0, 0)  14.7 us
    all_to_all x1, blocking collectives, gathered(): mine = lax.all_to_all(copies, ('gx', 'gy'), 0, 0, axis_index_groups=groups)  10.5 us
    ppermute x2, starting transfers between devices, moved(): return lax.ppermute(value, axis, pairs)  6.77 us
    ppermute x5, starting transfers between devices, swapped(): return lax.ppermute(value, 'gx', links(0, 1) + links(1, -1))  6.71 us
    ppermute x5, waiting for transfers between devices, swapped(): return lax.ppermute(value, 'gx', links(0, 1) + links(1, -1))  4.22 us
    pallas_call x1, Pallas kernels, local(): pl.pallas_call(functools.partial(main_kernel, sizes), out_shape=[fields(4...  3.59 us
    pallas_call x1, Pallas kernels, local(): pl.pallas_call(functools.partial(solve_kernel, sizes), out_shape=jax.Shap...  3.11 us
    pallas_call x1, Pallas kernels, local(): pl.pallas_call(functools.partial(middle_kernel, sizes), out_shape=[column...  2.56 us
  transfers between devices with their start and end apart: 10, of which 4 were waited for; matrix products, arithmetic and copies ran while one was open for 0% of the time, Pallas kernels for 8%

profile of v17, /device:TPU:0, one launch (start us, length us, event | category | flops | bytes accessed | tf_op | source)
XLA Modules:
  0.0 59.0 jit_solution(4324277836175019181)
XLA Ops:
  0.0 0.7 %negate_select_fusion.codes = f32[2,8,128]{2,1,0:T(8,128)S(1)} fusion(s32[2,8,128]{2,1,0:T(8,128)} %levels.1, s32[2,8,128]{2,1,0:T(8,128)} %param.5), kind=kLoop, calls=%fused_computation | loop fusion | flops 16384 | bytes 24576 | tf_op jit(solution)/shard_map/jit(_where)/select_n | solution.py:866
  0.7 0.0 copy-start
  0.7 1.1 %copy-done = f32[3,24,2,8,128]{4,3,2,1,0:T(8,128)S(1)} copy-done((f32[3,24,2,8,128]{4,3,2,1,0:T(8,128)S(1)}, f32[3,24,2,8,128]{4,3,2,1,0:T(8,128)}, u32[]{:S(2)}) %copy-start) | copy-done | bytes 589848
  1.8 0.1 pack.1
  1.9 0.5 collective-permute-start
  2.4 0.7 %collective-permute-start.3 = (f32[592,128]{1,0:T(8,128)S(1)}, f32[592,128]{1,0:T(8,128)S(1)}, u32[]{:S(2)}, u32[]{:S(2)}) collective-permute-start(f32[592,128]{1,0:T(8,128)S(1)} %get-tuple-element.37), channel_id=1, source_target_pairs={{4,8},{12,16},{20,24},{8,4},{16,12},{24,20},{5,9},{13,17},{21,25},... | collective-permute-start | bytes 909320 | tf_op jit(solution)/shard_map/ppermute | solution.py:898
  3.1 1.0 %collective-permute-done.pair = f32[1168,128]{1,0:T(8,128)S(1)} collective-permute-done((f32[1168,128]{1,0:T(8,128)S(1)}, f32[1168,128]{1,0:T(8,128)S(1)}, u32[]{:S(2)}, u32[]{:S(2)}) %collective-permute-start) | collective-permute-done | bytes 598048 | tf_op jit(solution)/shard_map/ppermute | solution.py:895
  4.1 1.3 %collective-permute-start.2 = (f32[296,128]{1,0:T(8,128)S(1)}, f32[296,128]{1,0:T(8,128)S(1)}, u32[]{:S(2)}, u32[]{:S(2)}) collective-permute-start(f32[296,128]{1,0:T(8,128)S(1)} %get-tuple-element.36), channel_id=1, source_target_pairs={{1,0},{2,1},{3,2},{5,4},{6,5},{7,6},{9,8},{10,9},{11,10},{13,12},{... | collective-permute-start | bytes 454664 | tf_op jit(solution)/shard_map/ppermute | solution.py:889
  5.4 5.5 %collective-permute-start.1 = (f32[152,128]{1,0:T(8,128)S(1)}, f32[152,128]{1,0:T(8,128)S(1)}, u32[]{:S(2)}, u32[]{:S(2)}) collective-permute-start(f32[152,128]{1,0:T(8,128)S(1)} %get-tuple-element.35), channel_id=1, source_target_pairs={{0,1},{1,2},{2,3},{4,5},{5,6},{6,7},{8,9},{9,10},{10,11},{12,13},{... | collective-permute-start | bytes 233480 | tf_op jit(solution)/shard_map/ppermute | solution.py:889
  10.9 1.5 %collective-permute-start.4 = (f32[2,8,128]{2,1,0:T(8,128)S(1)}, f32[2,8,128]{2,1,0:T(8,128)S(1)}, u32[]{:S(2)}, u32[]{:S(2)}) collective-permute-start(f32[2,8,128]{2,1,0:T(8,128)S(1)} %negate_select_fusion.codes), channel_id=1, source_target_pairs={{0,4},{8,12},{16,20},{24,28},{4,0},{12,8},{20,16},{28,24},{1,5},{9... | collective-permute-start | bytes 24584 | tf_op jit(solution)/shard_map/ppermute | solution.py:895
  12.4 0.8 %collective-permute-done.4.begun = f32[2,8,128]{2,1,0:T(8,128)S(1)} collective-permute-done((f32[2,8,128]{2,1,0:T(8,128)S(1)}, f32[2,8,128]{2,1,0:T(8,128)S(1)}, u32[]{:S(2)}, u32[]{:S(2)}) %collective-permute-start.4) | collective-permute-done | bytes 8224 | tf_op jit(solution)/shard_map/ppermute | solution.py:895
  13.2 0.7 %collective-permute-start.5 = (f32[576,128]{1,0:T(8,128)S(1)}, f32[576,128]{1,0:T(8,128)S(1)}, u32[]{:S(2)}, u32[]{:S(2)}) collective-permute-start(f32[576,128]{1,0:T(8,128)S(1)} %second.1), channel_id=1, source_target_pairs={{8,4},{16,12},{24,20},{9,5},{17,13},{25,21},{10,6},{18,14},{26,22}... | collective-permute-start | bytes 884744 | tf_op jit(solution)/shard_map/ppermute | solution.py:920
  13.9 0.0 collective-permute-done.3.edge
  13.9 0.0 collective-permute-done.1.ym
  13.9 0.0 collective-permute-done.2.yp
  14.0 0.7 %collective-permute-start.8 = (f32[448,128]{1,0:T(8,128)S(1)}, f32[448,128]{1,0:T(8,128)S(1)}, u32[]{:S(2)}, u32[]{:S(2)}) collective-permute-start(f32[448,128]{1,0:T(8,128)S(1)} %corners.1), channel_id=1, source_target_pairs={{4,8},{12,16},{20,24},{8,4},{16,12},{24,20},{5,9},{13,17},{21,25},... | collective-permute-start | bytes 688136 | tf_op jit(solution)/shard_map/ppermute | solution.py:898
  14.6 4.6 %collective-permute-start.7 = (f32[296,128]{1,0:T(8,128)S(1)}, f32[296,128]{1,0:T(8,128)S(1)}, u32[]{:S(2)}, u32[]{:S(2)}) collective-permute-start(f32[296,128]{1,0:T(8,128)S(1)} %collective-permute-done.2.yp), channel_id=1, source_target_pairs={{0,4},{8,12},{16,20},{24,28},{4,0},{12,8},{20,16},{28,24},{1,5},{9... | collective-permute-start | bytes 454664 | tf_op jit(solution)/shard_map/ppermute | solution.py:895
  19.3 0.1 collective-permute-start.6
  19.4 1.2 %collective-permute-done.6.ym_pair = f32[152,128]{1,0:T(8,128)S(1)} collective-permute-done((f32[152,128]{1,0:T(8,128)S(1)}, f32[152,128]{1,0:T(8,128)S(1)}, u32[]{:S(2)}, u32[]{:S(2)}) %collective-permute-start.6) | collective-permute-done | bytes 77856 | tf_op jit(solution)/shard_map/ppermute | solution.py:895
  20.6 0.0 collective-permute-done.7.yp_pair
  20.6 1.8 %early.1 = (f32[33,72,128]{2,1,0:T(8,128)S(1)}, f32[33,72,128]{2,1,0:T(8,128)S(1)}, f32[33,72,128]{2,1,0:T(8,128)S(1)}, f32[27,72,128]{2,1,0:T(8,128)S(1)}, f32[27,72,128]{2,1,0:T(8,128)S(1)}) custom-call(f32[1168,128]{1,0:T(8,128)S(1)} %get-tuple-element.33.own, f32[1168,128]{1,0:T(8,128)S(1)} %collective-permute-done.pair, ...), custom_call_target="tpu_custom_call" | custom-call | flops 29491200 | bytes 8388608 | tf_op jit(solution)/shard_map/early/pallas_call | solution.py:938
  22.4 0.0 collective-permute-done.5.second
  22.4 2.6 %middle.1 = (f32[21,72,128]{2,1,0:T(8,128)S(1)}, f32[21,72,128]{2,1,0:T(8,128)S(1)}, f32[7,72,128]{2,1,0:T(8,128)S(1)}, f32[21,72,128]{2,1,0:T(8,128)S(1)}, f32[...) custom-call(f32[1168,128]{1,0:T(8,128)S(1)} %get-tuple-element.33.ow, ...), custom_call_target="tpu_custom_call" | custom-call | tf_op jit(solution)/shard_map/middle/pallas_call | solution.py:964
  24.9 0.0 collective-permute-done.8.corners
  25.0 3.6 %operator.1 = (bf16[96,4608]{1,0:T(8,128)(2,1)S(1)}, f32[32,5,2,128]{3,2,1,0:T(2,128)S(1)}) custom-call(f32[1168,128]{1,0:T(8,128)S(1)} %get-tuple-element.33.own, f32[1168,128]{1,0:T(8,128)S(1)} %collective-permute-done.pair, f32[592,128]{1,0:T(8,128)S(1)} %collective-permute-done.3.edge, f32[576,128]{1,0:T(8,128)S(1)} %collective-permute-done.5.second, ...), custom_call_target="tpu_custom_call" | custom-call | tf_op jit(solution)/shard_map/operator/pallas_call | solution.py:984
  28.6 14.7 %all_to_all.10.system = f32[32,5,2,128]{3,2,1,0:T(2,128)S(1)} all-to-all(f32[32,5,2,128]{3,2,1,0:T(2,128)S(1)} %get-tuple-element.57), channel_id=1, replica_groups=mesh['gx'=8,'gy'=4] {'gx','gy'}, dimensions={0} | all-to-all | bytes 327680 | tf_op jit(solution)/shard_map/all_to_all | solution.py:1022
  43.3 0.0 copy-start.1
  43.3 3.1 %solve.1 = f32[16,2,8,128]{3,2,1,0:T(8,128)S(1)} custom-call(f32[32,5,2,128]{3,2,1,0:T(2,128)S(1)} %all_to_all.10.system, bf16[96,5760]{1,0:T(8,128)(2,1)S(1)} %get-tuple-element.53.both_m, bf16[96,4608]{1,0:T(8,128)(2,1)S(1)} %get-tuple-element.58.both_r, f32[2,8,128]{2,1,0:T(8,128)S(1)} %negate_select_fusion.codes), custom_call_target="tpu_custom_call" | custom-call | tf_op jit(solution)/shard_map/solve/pallas_call | solution.py:1024
  46.4 10.5 %all_to_all.11.blocks = f32[16,2,8,128]{3,2,1,0:T(8,128)S(1)} all-to-all(f32[16,2,8,128]{3,2,1,0:T(8,128)S(1)} %solve.1), channel_id=1, replica_groups={{0,1,2,3,8,9,10,11,16,17,18,19,24,25,26,27},{4,5,6,7,12,13,14,15,20,21,..., dimensions={0} | all-to-all | bytes 262144 | tf_op jit(solution)/shard_map/all_to_all | solution.py:1019
  56.9 0.0 collective-permute-start.9
  56.9 0.0 copy-done.1
  56.9 0.1 scale.1
  57.0 1.2 %collective-permute-done.9.blocks_pair = f32[16,2,8,128]{3,2,1,0:T(8,128)S(1)} collective-permute-done((f32[16,2,8,128]{3,2,1,0:T(8,128)S(1)}, f32[16,2,8,128]{3,2,1,0:T(8,128)S(1)}, u32[]{:S(2)}, u32[]{:S(2)}) %collective-permute-start.9) | collective-permute-done | bytes 131104 | tf_op jit(solution)/shard_map/ppermute | solution.py:895
  58.3 0.7 %cone.1 = f32[2,8,128]{2,1,0:T(8,128)} custom-call(f32[16,2,8,128]{3,2,1,0:T(8,128)S(1)} %all_to_all.11.blocks, f32[16,2,8,128]{3,2,1,0:T(8,128)S(1)} %collective-permute-done.9.blocks_pair, f32[2,8,128]{2,1,0:T(8,128)S(1)} %scale.1), custom_call_target="tpu_custom_call" | custom-call | tf_op jit(solution)/shard_map/cone/pallas_call | solution.py:1043
  (3 shorter events, 0.1 us)
Async XLA Ops:
  0.7 1.1 %copy-start = (f32[3,24,2,8,128]{4,3,2,1,0:T(8,128)S(1)}, f32[3,24,2,8,128]{4,3,2,1,0:T(8,128)}, u32[]{:S(2)}) copy-start(f32[3,24,2,8,128]{4,3,2,1,0:T(8,128)} %forces.1) | copy-start | bytes 1769476
  1.9 2.2 %collective-permute-start = (f32[1168,128]{1,0:T(8,128)S(1)}, f32[1168,128]{1,0:T(8,128)S(1)}, u32[]{:S(2)}, u32[]{:S(2)}) collective-permute-start(f32[1168,128]{1,0:T(8,128)S(1)} %get-tuple-element.33.own), channel_id=1, source_target_pairs={{0,4},{8,12},{16,20},{24,28},{4,0},{12,8},{20,16},{28,24},{1,5},{9... | collective-permute-start | bytes 1794056 | tf_op jit(solution)/shard_map/ppermute | solution.py:895
  2.4 11.5 %collective-permute-start.3 = (f32[592,128]{1,0:T(8,128)S(1)}, f32[592,128]{1,0:T(8,128)S(1)}, u32[]{:S(2)}, u32[]{:S(2)}) collective-permute-start(f32[592,128]{1,0:T(8,128)S(1)} %get-tuple-element.37), channel_id=1, source_target_pairs={{4,8},{12,16},{20,24},{8,4},{16,12},{24,20},{5,9},{13,17},{21,25},... | collective-permute-start | bytes 909320 | tf_op jit(solution)/shard_map/ppermute | solution.py:898
  4.1 9.8 %collective-permute-start.2 = (f32[296,128]{1,0:T(8,128)S(1)}, f32[296,128]{1,0:T(8,128)S(1)}, u32[]{:S(2)}, u32[]{:S(2)}) collective-permute-start(f32[296,128]{1,0:T(8,128)S(1)} %get-tuple-element.36), channel_id=1, source_target_pairs={{1,0},{2,1},{3,2},{5,4},{6,5},{7,6},{9,8},{10,9},{11,10},{13,12},{... | collective-permute-start | bytes 454664 | tf_op jit(solution)/shard_map/ppermute | solution.py:889
  5.4 8.5 %collective-permute-start.1 = (f32[152,128]{1,0:T(8,128)S(1)}, f32[152,128]{1,0:T(8,128)S(1)}, u32[]{:S(2)}, u32[]{:S(2)}) collective-permute-start(f32[152,128]{1,0:T(8,128)S(1)} %get-tuple-element.35), channel_id=1, source_target_pairs={{0,1},{1,2},{2,3},{4,5},{5,6},{6,7},{8,9},{9,10},{10,11},{12,13},{... | collective-permute-start | bytes 233480 | tf_op jit(solution)/shard_map/ppermute | solution.py:889
  10.9 2.3 %collective-permute-start.4 = (f32[2,8,128]{2,1,0:T(8,128)S(1)}, f32[2,8,128]{2,1,0:T(8,128)S(1)}, u32[]{:S(2)}, u32[]{:S(2)}) collective-permute-start(f32[2,8,128]{2,1,0:T(8,128)S(1)} %negate_select_fusion.codes), channel_id=1, source_target_pairs={{0,4},{8,12},{16,20},{24,28},{4,0},{12,8},{20,16},{28,24},{1,5},{9... | collective-permute-start | bytes 24584 | tf_op jit(solution)/shard_map/ppermute | solution.py:895
  13.2 9.2 %collective-permute-start.5 = (f32[576,128]{1,0:T(8,128)S(1)}, f32[576,128]{1,0:T(8,128)S(1)}, u32[]{:S(2)}, u32[]{:S(2)}) collective-permute-start(f32[576,128]{1,0:T(8,128)S(1)} %second.1), channel_id=1, source_target_pairs={{8,4},{16,12},{24,20},{9,5},{17,13},{25,21},{10,6},{18,14},{26,22}... | collective-permute-start | bytes 884744 | tf_op jit(solution)/shard_map/ppermute | solution.py:920
  14.0 11.0 %collective-permute-start.8 = (f32[448,128]{1,0:T(8,128)S(1)}, f32[448,128]{1,0:T(8,128)S(1)}, u32[]{:S(2)}, u32[]{:S(2)}) collective-permute-start(f32[448,128]{1,0:T(8,128)S(1)} %corners.1), channel_id=1, source_target_pairs={{4,8},{12,16},{20,24},{8,4},{16,12},{24,20},{5,9},{13,17},{21,25},... | collective-permute-start | bytes 688136 | tf_op jit(solution)/shard_map/ppermute | solution.py:898
  14.6 5.9 %collective-permute-start.7 = (f32[296,128]{1,0:T(8,128)S(1)}, f32[296,128]{1,0:T(8,128)S(1)}, u32[]{:S(2)}, u32[]{:S(2)}) collective-permute-start(f32[296,128]{1,0:T(8,128)S(1)} %collective-permute-done.2.yp), channel_id=1, source_target_pairs={{0,4},{8,12},{16,20},{24,28},{4,0},{12,8},{20,16},{28,24},{1,5},{9... | collective-permute-start | bytes 454664 | tf_op jit(solution)/shard_map/ppermute | solution.py:895
  19.3 1.3 %collective-permute-start.6 = (f32[152,128]{1,0:T(8,128)S(1)}, f32[152,128]{1,0:T(8,128)S(1)}, u32[]{:S(2)}, u32[]{:S(2)}) collective-permute-start(f32[152,128]{1,0:T(8,128)S(1)} %collective-permute-done.1.ym), channel_id=1, source_target_pairs={{0,4},{8,12},{16,20},{24,28},{4,0},{12,8},{20,16},{28,24},{1,5},{9... | collective-permute-start | bytes 233480 | tf_op jit(solution)/shard_map/ppermute | solution.py:895
  43.3 13.6 %copy-start.1 = (s32[2,8,128]{2,1,0:T(8,128)S(1)}, s32[2,8,128]{2,1,0:T(8,128)}, u32[]{:S(2)}) copy-start(s32[2,8,128]{2,1,0:T(8,128)} %levels.1) | copy-start | bytes 24580
  56.9 1.3 %collective-permute-start.9 = (f32[16,2,8,128]{3,2,1,0:T(8,128)S(1)}, f32[16,2,8,128]{3,2,1,0:T(8,128)S(1)}, u32[]{:S(2)}, u32[]{:S(2)}) collective-permute-start(f32[16,2,8,128]{3,2,1,0:T(8,128)S(1)} %all_to_all.11.blocks), channel_id=1, source_target_pairs={{0,4},{8,12},{16,20},{24,28},{4,0},{12,8},{20,16},{28,24},{1,5},{9... | collective-permute-start | bytes 393224 | tf_op jit(solution)/shard_map/ppermute | solution.py:895

commit v18 on v17

--- a/solution.py
+++ b/solution.py
@@ -374,6 +374,14 @@
     return (0, 1, rows - 1, rows)
 
 
+def core_columns(planes, rows):
+    core = core_rows(rows)
+    inner, outer = core[1:-1], (core[0], core[-1])
+    first = [(x, y) for x in range(planes + 1) for y in inner]
+    last = [(x, y) for x in range(planes + 1) for y in outer]
+    return first, last, planes * len(inner), planes * len(outer)
+
+
 def rim_columns(planes, rows):
     own = [(x, y) for x in range(planes) for y in rim_rows(rows) if y < rows]
     beyond_own = [(x, rows) for x in range(planes)] + [(planes, y) for y in rim_rows(rows)]
@@ -409,6 +417,15 @@
         lane = pl.ds(pl.multiple_of((place * 3 + k) * LANES, LANES), LANES)
         ref[0 : 2 * cases, lane] = high
         ref[2 * cases : 4 * cases, lane] = rest
+
+
+def keep_split(ref, place, value, cases):
+    for k in range(3):
+        part = value[k * cases : (k + 1) * cases]
+        high = part.astype(bf16).astype(f32)
+        ref[:, (place * 3 + k) * LANES : (place * 3 + k + 1) * LANES] = jnp.concatenate(
+            [high, part - high], 0
+        ).astype(bf16)
 
 
 def products(first, second):
@@ -440,8 +457,8 @@
 
 def middle_kernel(
     sizes, own, pair, edge, second, start, sums_e, diffs_e, acc_se, acc_de,
-    sums, diffs, middle, acc_s, acc_d, w_sums, w_diffs, both_out, gram_out, acc2_s, acc2_d,
-    stiff_ref, inverse, right,
+    sums, diffs, middle, acc_s, acc_d, w_sums, w_diffs, both_out, gram_out, other_out,
+    acc2_s, acc2_d, stiff_ref, inverse, right, again,
 ):
     planes, rows, cases = sizes
     block = 3 * cases
@@ -500,35 +517,40 @@
         s, d = total(acc_se, acc_s), total(acc_de, acc_d)
         force = s - d + shift_up(s + d)
         scaled = force * inverse[x + 1, pl.ds(y - 1, 1), :]
-        place_column(w_sums, w_diffs, place, scaled)
+        place_column(w_sums, w_diffs, x * len(core) + y - core[0], scaled)
         value = direction_at(x, planes, even, lambda w: start[w * ys + y + 1], middle[y - 1])
         keep_pair(both_out, place, value, scaled, cases)
         return force
 
-    def within(x, index):
-        y, place = core[0] + index, x * len(core) + index
-        force = image(x, y, place)
-        given = own[pl.ds(pl.multiple_of((x * rows + y) * block, 8), block), :]
-        keep_pair(right, place, given, force, cases)
-
-    for x in range(planes):
-        unrolled(len(core), len(core), functools.partial(within, x))
-    last = planes * len(core)
-    unrolled(len(core), len(core), lambda index: image(planes, core[0] + index, last + index))
-    gram_out[...] = products(right[...], both_out[:, : last * 3 * LANES])
+    inner_columns, outer_columns, inner_own, outer_own = core_columns(planes, rows)
+    count = len(inner_columns)
+    for index, (x, y) in enumerate(inner_columns + outer_columns):
+        force = image(x, y, index)
+        if x < planes:
+            place = index if index < count else inner_own + index - count
+            keep_pair(right, place, inside(own, x, y, rows, block), force, cases)
+    width = 3 * LANES
+    gram = products(right[:, : inner_own * width], both_out[:, : inner_own * width])
+    outer_part = both_out[:, count * width : (count + outer_own) * width]
+    gram_out[...] = gram + products(right[:, inner_own * width :], outer_part)
 
     find = whole(w_sums, w_diffs, len(core))
     kept = range(len(core))
     apply_elements(
         find, stiff_ref, acc2_s, acc2_d, planes, len(core) - 1, kept, 2, core[0], cases
     )
+    for index, (x, y) in enumerate(inner_columns):
+        column = x * len(core) + y - core[0]
+        s, d = acc2_s[column], acc2_d[column]
+        keep_split(again, index, s - d + shift_up(s + d), cases)
+    other_out[...] = products(again[...], both_out[:, : count * width])
 
 
 def main_kernel(
     sizes, own, pair, edge, second, ym, yp, ym_pair, yp_pair, corners,
     start, sums_e, diffs_e, acc_se, acc_de,
     sums_m, diffs_m, middle_m, acc_sm, acc_dm, w_sm, w_dm, both_m, gram_m,
-    acc2_sm, acc2_dm, both_out, system_out, stiff_ref, inverse,
+    other_m, acc2_sm, acc2_dm, both_out, system_out, stiff_ref, inverse,
     middle, sums, diffs, acc_s0, acc_d0, acc_s1, acc_d1, w_sums, w_diffs,
     acc2_s0, acc2_d0, acc2_s1, acc2_d1, right, second_m, second_r, table, dense,
 ):
@@ -633,7 +655,7 @@
     apply_elements(find, stiff_ref, *low, planes, 2, range(3), 2, 2, cases)
     apply_elements(find_last, stiff_ref, *high, planes, 2, range(3), 2, rows, cases)
 
-    def second_force(ref, x, y, place):
+    def second_force(x, y):
         s, d = None, None
         for parts, width, first in (
             (low, 3, 0), ((acc2_sm, acc2_dm), len(core), core[0]), (high, 3, rows - 2)
@@ -642,22 +664,18 @@
                 column = x * width + y - first
                 more = parts[0][column], parts[1][column]
                 s, d = more if s is None else (s + more[0], d + more[1])
-        force = s - d + shift_up(s + d)
-        for k in range(3):
-            value = force[k * cases : (k + 1) * cases]
-            top = value.astype(bf16).astype(f32)
-            lane = pl.ds(pl.multiple_of((place * 3 + k) * LANES, LANES), LANES)
-            ref[:, lane] = jnp.concatenate([top, value - top], 0).astype(bf16)
-
-    for x in range(planes + 1):
-        for index, y in enumerate(core):
-            second_force(second_m, x, y, x * len(core) + index)
+        return s - d + shift_up(s + d)
+
+    inner_columns, outer_columns, _, _ = core_columns(planes, rows)
+    for index, (x, y) in enumerate(outer_columns):
+        keep_split(second_m, index, second_force(x, y), cases)
     for index, (x, y) in enumerate(columns):
-        second_force(second_r, x, y, index)
+        keep_split(second_r, index, second_force(x, y), cases)
 
     two = 2 * cases
     gram = products(right[...], both_out[:, : own_count * 3 * LANES]) + gram_m[...]
-    other = products(second_m[...], both_m[...]) + products(second_r[...], both_out[...])
+    other = products(second_m[...], both_m[:, len(inner_columns) * 3 * LANES :]) + other_m[...]
+    other = other + products(second_r[...], both_out[...])
     row = lax.broadcasted_iota(jnp.int32, (cases, cases), 0)
     column = lax.broadcasted_iota(jnp.int32, (cases, cases), 1)
     load_load, load_image = gram[:cases, :cases], gram[cases:, :cases]
@@ -761,17 +779,14 @@
             sums[column, k * cases : (k + 1) * cases, :] = part + moved
             diffs[column, k * cases : (k + 1) * cases, :] = moved - part
 
-    core = core_rows(rows)
-    for x in range(planes + 1):
-        value = combined(both_m, x * len(core), len(core))
-        for index, y in enumerate(core):
-            keep(value, index, x * nodes_y + y)
+    inner_columns, outer_columns, _, _ = core_columns(planes, rows)
     columns, _ = rim_columns(planes, rows)
-    for start in range(0, len(columns), 6):
-        some = columns[start : start + 6]
-        value = combined(both_r, start, len(some))
-        for index, (x, y) in enumerate(some):
-            keep(value, index, x * nodes_y + y)
+    for ref, columns in ((both_m, inner_columns + outer_columns), (both_r, columns)):
+        for start in range(0, len(columns), 6):
+            some = columns[start : start + 6]
+            value = combined(ref, start, len(some))
+            for index, (x, y) in enumerate(some):
+                keep(value, index, x * nodes_y + y)
 
     find = whole(sums, diffs, nodes_y)
     tiles = cases // 8
@@ -968,13 +983,15 @@
         + [columns(3 * (rows - 1))] * 2
         + [columns((planes + 1) * core)] * 2
         + [fields(4, (planes + 1) * core), jax.ShapeDtypeStruct((2 * cases, 2 * cases), f32)]
+        + [jax.ShapeDtypeStruct((cases, 2 * cases), f32)]
         + [columns((planes + 1) * core)] * 2,
         in_specs=[VMEM] * 9,
-        out_specs=[VMEM] * 11,
+        out_specs=[VMEM] * 12,
         scratch_shapes=[
             pltpu.VMEM((planes + 4, up8(rows), LANES), f32),
             pltpu.VMEM((planes + 3, up8(rows), LANES), f32),
             scratch(fields(4, planes * core)),
+            scratch(fields(2, (planes + 1) * (core - 2))),
         ],
         compiler_params=PARAMS,
         name="middle",
@@ -987,7 +1004,7 @@
             fields(4, len(rim)),
             jax.ShapeDtypeStruct((devices, 5 * cases // 24, 2, LANES), f32),
         ],
-        in_specs=[VMEM] * 25,
+        in_specs=[VMEM] * 26,
         out_specs=[VMEM] * 2,
         scratch_shapes=[
             pltpu.VMEM((planes + 4, up8(rows + 4), LANES), f32),
@@ -998,7 +1015,7 @@
             *[scratch(columns((planes + 1) * 4))] * 2,
             *[scratch(columns((planes + 1) * 3))] * 4,
             scratch(fields(4, rim_own)),
-            scratch(fields(2, (planes + 1) * core)),
+            scratch(fields(2, (planes + 1) * 2)),
             scratch(fields(2, len(rim))),
             pltpu.VMEM((cases, LANES), f32),
             pltpu.VMEM((5 * cases // 12, LANES), f32),

time: 59.4 us -> 59.1 us (level)
  blocking collectives: 25.2 us -> 24.5 us
    all_to_all x1, blocking collectives: 14.7 us -> 14.1 us  [local(): system = lax.all_to_all(system, ('gx', 'gy'), 0, 0)]
    pallas_call x1, Pallas kernels: 2.56 us -> 3.23 us  [local(): pl.pallas_call(functools.partial(middle_kernel, sizes), out_shape=[column...]
  transfers between devices with their start and end apart: 10 -> 10, of which waited for: 4 -> 4; matrix products, arithmetic and copies ran while one was open for 0% -> 0% of each run, Pallas kernels for 8% -> 9%
where the time goes in v18:
time: 59.1 us; the launch traced here: 58.7 us
  blocking collectives  24.5 us (41%)
  starting transfers between devices  15.5 us (26%)
  Pallas kernels  12.5 us (21%)
  waiting for transfers between devices  4.24 us (7%)
  local copies, waits for them, and re-layouts  1.07 us (2%)
  other arithmetic  0.72 us (1%)
    all_to_all x1, blocking collectives, local(): system = lax.all_to_all(system, ('gx', 'gy'), 0, 0)  14.1 us
    all_to_all x1, blocking collectives, gathered(): mine = lax.all_to_all(copies, ('gx', 'gy'), 0, 0, axis_index_groups=groups)  10.5 us
    ppermute x2, starting transfers between devices, moved(): return lax.ppermute(value, axis, pairs)  6.77 us
    ppermute x5, starting transfers between devices, swapped(): return lax.ppermute(value, 'gx', links(0, 1) + links(1, -1))  6.71 us
    ppermute x5, waiting for transfers between devices, swapped(): return lax.ppermute(value, 'gx', links(0, 1) + links(1, -1))  4.22 us
    pallas_call x1, Pallas kernels, local(): pl.pallas_call(functools.partial(main_kernel, sizes), out_shape=[fields(4...  3.37 us
    pallas_call x1, Pallas kernels, local(): pl.pallas_call(functools.partial(middle_kernel, sizes), out_shape=[column...  3.23 us
    pallas_call x1, Pallas kernels, local(): pl.pallas_call(functools.partial(solve_kernel, sizes), out_shape=jax.Shap...  3.11 us
  transfers between devices with their start and end apart: 10, of which 4 were waited for; matrix products, arithmetic and copies ran while one was open for 0% of the time, Pallas kernels for 9%

profile of v18, /device:TPU:0, one launch (start us, length us, event | category | flops | bytes accessed | tf_op | source)
XLA Modules:
  0.0 58.7 jit_solution(5441877736784233866)
XLA Ops:
  0.0 0.7 %negate_select_fusion.codes = f32[2,8,128]{2,1,0:T(8,128)S(1)} fusion(s32[2,8,128]{2,1,0:T(8,128)} %levels.1, s32[2,8,128]{2,1,0:T(8,128)} %param.5), kind=kLoop, calls=%fused_computation | loop fusion | flops 16384 | bytes 24576 | tf_op jit(solution)/shard_map/jit(_where)/select_n | solution.py:881
  0.7 0.0 copy-start
  0.7 1.1 %copy-done = f32[3,24,2,8,128]{4,3,2,1,0:T(8,128)S(1)} copy-done((f32[3,24,2,8,128]{4,3,2,1,0:T(8,128)S(1)}, f32[3,24,2,8,128]{4,3,2,1,0:T(8,128)}, u32[]{:S(2)}) %copy-start) | copy-done | bytes 589848
  1.8 0.1 pack.1
  1.9 0.5 collective-permute-start
  2.4 0.7 %collective-permute-start.3 = (f32[592,128]{1,0:T(8,128)S(1)}, f32[592,128]{1,0:T(8,128)S(1)}, u32[]{:S(2)}, u32[]{:S(2)}) collective-permute-start(f32[592,128]{1,0:T(8,128)S(1)} %get-tuple-element.38), channel_id=1, source_target_pairs={{4,8},{12,16},{20,24},{8,4},{16,12},{24,20},{5,9},{13,17},{21,25},... | collective-permute-start | bytes 909320 | tf_op jit(solution)/shard_map/ppermute | solution.py:913
  3.1 1.0 %collective-permute-done.pair = f32[1168,128]{1,0:T(8,128)S(1)} collective-permute-done((f32[1168,128]{1,0:T(8,128)S(1)}, f32[1168,128]{1,0:T(8,128)S(1)}, u32[]{:S(2)}, u32[]{:S(2)}) %collective-permute-start) | collective-permute-done | bytes 598048 | tf_op jit(solution)/shard_map/ppermute | solution.py:910
  4.1 1.3 %collective-permute-start.2 = (f32[296,128]{1,0:T(8,128)S(1)}, f32[296,128]{1,0:T(8,128)S(1)}, u32[]{:S(2)}, u32[]{:S(2)}) collective-permute-start(f32[296,128]{1,0:T(8,128)S(1)} %get-tuple-element.37), channel_id=1, source_target_pairs={{1,0},{2,1},{3,2},{5,4},{6,5},{7,6},{9,8},{10,9},{11,10},{13,12},{... | collective-permute-start | bytes 454664 | tf_op jit(solution)/shard_map/ppermute | solution.py:904
  5.4 5.5 %collective-permute-start.1 = (f32[152,128]{1,0:T(8,128)S(1)}, f32[152,128]{1,0:T(8,128)S(1)}, u32[]{:S(2)}, u32[]{:S(2)}) collective-permute-start(f32[152,128]{1,0:T(8,128)S(1)} %get-tuple-element.36), channel_id=1, source_target_pairs={{0,1},{1,2},{2,3},{4,5},{5,6},{6,7},{8,9},{9,10},{10,11},{12,13},{... | collective-permute-start | bytes 233480 | tf_op jit(solution)/shard_map/ppermute | solution.py:904
  10.9 1.5 %collective-permute-start.4 = (f32[2,8,128]{2,1,0:T(8,128)S(1)}, f32[2,8,128]{2,1,0:T(8,128)S(1)}, u32[]{:S(2)}, u32[]{:S(2)}) collective-permute-start(f32[2,8,128]{2,1,0:T(8,128)S(1)} %negate_select_fusion.codes), channel_id=1, source_target_pairs={{0,4},{8,12},{16,20},{24,28},{4,0},{12,8},{20,16},{28,24},{1,5},{9... | collective-permute-start | bytes 24584 | tf_op jit(solution)/shard_map/ppermute | solution.py:910
  12.4 0.8 %collective-permute-done.4.begun = f32[2,8,128]{2,1,0:T(8,128)S(1)} collective-permute-done((f32[2,8,128]{2,1,0:T(8,128)S(1)}, f32[2,8,128]{2,1,0:T(8,128)S(1)}, u32[]{:S(2)}, u32[]{:S(2)}) %collective-permute-start.4) | collective-permute-done | bytes 8224 | tf_op jit(solution)/shard_map/ppermute | solution.py:910
  13.2 0.7 %collective-permute-start.5 = (f32[576,128]{1,0:T(8,128)S(1)}, f32[576,128]{1,0:T(8,128)S(1)}, u32[]{:S(2)}, u32[]{:S(2)}) collective-permute-start(f32[576,128]{1,0:T(8,128)S(1)} %second.1), channel_id=1, source_target_pairs={{8,4},{16,12},{24,20},{9,5},{17,13},{25,21},{10,6},{18,14},{26,22}... | collective-permute-start | bytes 884744 | tf_op jit(solution)/shard_map/ppermute | solution.py:935
  13.9 0.0 collective-permute-done.3.edge
  13.9 0.0 collective-permute-done.1.ym
  13.9 0.0 collective-permute-done.2.yp
  14.0 0.7 %collective-permute-start.8 = (f32[448,128]{1,0:T(8,128)S(1)}, f32[448,128]{1,0:T(8,128)S(1)}, u32[]{:S(2)}, u32[]{:S(2)}) collective-permute-start(f32[448,128]{1,0:T(8,128)S(1)} %corners.1), channel_id=1, source_target_pairs={{4,8},{12,16},{20,24},{8,4},{16,12},{24,20},{5,9},{13,17},{21,25},... | collective-permute-start | bytes 688136 | tf_op jit(solution)/shard_map/ppermute | solution.py:913
  14.7 4.6 %collective-permute-start.7 = (f32[296,128]{1,0:T(8,128)S(1)}, f32[296,128]{1,0:T(8,128)S(1)}, u32[]{:S(2)}, u32[]{:S(2)}) collective-permute-start(f32[296,128]{1,0:T(8,128)S(1)} %collective-permute-done.2.yp), channel_id=1, source_target_pairs={{0,4},{8,12},{16,20},{24,28},{4,0},{12,8},{20,16},{28,24},{1,5},{9... | collective-permute-start | bytes 454664 | tf_op jit(solution)/shard_map/ppermute | solution.py:910
  19.3 0.1 collective-permute-start.6
  19.4 1.2 %collective-permute-done.6.ym_pair = f32[152,128]{1,0:T(8,128)S(1)} collective-permute-done((f32[152,128]{1,0:T(8,128)S(1)}, f32[152,128]{1,0:T(8,128)S(1)}, u32[]{:S(2)}, u32[]{:S(2)}) %collective-permute-start.6) | collective-permute-done | bytes 77856 | tf_op jit(solution)/shard_map/ppermute | solution.py:910
  20.6 0.0 collective-permute-done.7.yp_pair
  20.6 1.8 %early.1 = (f32[33,72,128]{2,1,0:T(8,128)S(1)}, f32[33,72,128]{2,1,0:T(8,128)S(1)}, f32[33,72,128]{2,1,0:T(8,128)S(1)}, f32[27,72,128]{2,1,0:T(8,128)S(1)}, f32[27,72,128]{2,1,0:T(8,128)S(1)}) custom-call(f32[1168,128]{1,0:T(8,128)S(1)} %get-tuple-element.34.own, f32[1168,128]{1,0:T(8,128)S(1)} %collective-permute-done.pair, ...), custom_call_target="tpu_custom_call" | custom-call | flops 29491200 | bytes 8388608 | tf_op jit(solution)/shard_map/early/pallas_call | solution.py:953
  22.4 0.0 collective-permute-done.5.second
  22.4 3.2 %middle.1 = (f32[21,72,128]{2,1,0:T(8,128)S(1)}, f32[21,72,128]{2,1,0:T(8,128)S(1)}, f32[7,72,128]{2,1,0:T(8,128)S(1)}, f32[21,72,128]{2,1,0:T(8,128)S(1)}, f32[...) custom-call(f32[1168,128]{1,0:T(8,128)S(1)} %get-tuple-element.34.ow, ...), custom_call_target="tpu_custom_call" | custom-call | tf_op jit(solution)/shard_map/middle/pallas_call | solution.py:979
  25.6 0.0 collective-permute-done.8.corners
  25.6 3.4 %operator.1 = (bf16[96,4608]{1,0:T(8,128)(2,1)S(1)}, f32[32,5,2,128]{3,2,1,0:T(2,128)S(1)}) custom-call(f32[1168,128]{1,0:T(8,128)S(1)} %get-tuple-element.34.own, f32[1168,128]{1,0:T(8,128)S(1)} %collective-permute-done.pair, f32[592,128]{1,0:T(8,128)S(1)} %collective-permute-done.3.edge, f32[576,128]{1,0:T(8,128)S(1)} %collective-permute-done.5.second, ...), custom_call_target="tpu_custom_call" | custom-call | tf_op jit(solution)/shard_map/operator/pallas_call | solution.py:1001
  29.0 14.1 %all_to_all.10.system = f32[32,5,2,128]{3,2,1,0:T(2,128)S(1)} all-to-all(f32[32,5,2,128]{3,2,1,0:T(2,128)S(1)} %get-tuple-element.59), channel_id=1, replica_groups=mesh['gx'=8,'gy'=4] {'gx','gy'}, dimensions={0} | all-to-all | bytes 327680 | tf_op jit(solution)/shard_map/all_to_all | solution.py:1039
  43.1 0.0 copy-start.1
  43.1 3.1 %solve.1 = f32[16,2,8,128]{3,2,1,0:T(8,128)S(1)} custom-call(f32[32,5,2,128]{3,2,1,0:T(2,128)S(1)} %all_to_all.10.system, bf16[96,5760]{1,0:T(8,128)(2,1)S(1)} %get-tuple-element.54.both_m, bf16[96,4608]{1,0:T(8,128)(2,1)S(1)} %get-tuple-element.60.both_r, f32[2,8,128]{2,1,0:T(8,128)S(1)} %negate_select_fusion.codes), custom_call_target="tpu_custom_call" | custom-call | tf_op jit(solution)/shard_map/solve/pallas_call | solution.py:1041
  46.2 10.5 %all_to_all.11.blocks = f32[16,2,8,128]{3,2,1,0:T(8,128)S(1)} all-to-all(f32[16,2,8,128]{3,2,1,0:T(8,128)S(1)} %solve.1), channel_id=1, replica_groups={{0,1,2,3,8,9,10,11,16,17,18,19,24,25,26,27},{4,5,6,7,12,13,14,15,20,21,..., dimensions={0} | all-to-all | bytes 262144 | tf_op jit(solution)/shard_map/all_to_all | solution.py:1036
  56.7 0.0 collective-permute-start.9
  56.7 0.0 copy-done.1
  56.7 0.1 scale.1
  56.8 1.2 %collective-permute-done.9.blocks_pair = f32[16,2,8,128]{3,2,1,0:T(8,128)S(1)} collective-permute-done((f32[16,2,8,128]{3,2,1,0:T(8,128)S(1)}, f32[16,2,8,128]{3,2,1,0:T(8,128)S(1)}, u32[]{:S(2)}, u32[]{:S(2)}) %collective-permute-start.9) | collective-permute-done | bytes 131104 | tf_op jit(solution)/shard_map/ppermute | solution.py:910
  58.0 0.7 %cone.1 = f32[2,8,128]{2,1,0:T(8,128)} custom-call(f32[16,2,8,128]{3,2,1,0:T(8,128)S(1)} %all_to_all.11.blocks, f32[16,2,8,128]{3,2,1,0:T(8,128)S(1)} %collective-permute-done.9.blocks_pair, f32[2,8,128]{2,1,0:T(8,128)S(1)} %scale.1), custom_call_target="tpu_custom_call" | custom-call | tf_op jit(solution)/shard_map/cone/pallas_call | solution.py:1060
  (3 shorter events, 0.1 us)
Async XLA Ops:
  0.7 1.1 %copy-start = (f32[3,24,2,8,128]{4,3,2,1,0:T(8,128)S(1)}, f32[3,24,2,8,128]{4,3,2,1,0:T(8,128)}, u32[]{:S(2)}) copy-start(f32[3,24,2,8,128]{4,3,2,1,0:T(8,128)} %forces.1) | copy-start | bytes 1769476
  1.9 2.2 %collective-permute-start = (f32[1168,128]{1,0:T(8,128)S(1)}, f32[1168,128]{1,0:T(8,128)S(1)}, u32[]{:S(2)}, u32[]{:S(2)}) collective-permute-start(f32[1168,128]{1,0:T(8,128)S(1)} %get-tuple-element.34.own), channel_id=1, source_target_pairs={{0,4},{8,12},{16,20},{24,28},{4,0},{12,8},{20,16},{28,24},{1,5},{9... | collective-permute-start | bytes 1794056 | tf_op jit(solution)/shard_map/ppermute | solution.py:910
  2.4 11.5 %collective-permute-start.3 = (f32[592,128]{1,0:T(8,128)S(1)}, f32[592,128]{1,0:T(8,128)S(1)}, u32[]{:S(2)}, u32[]{:S(2)}) collective-permute-start(f32[592,128]{1,0:T(8,128)S(1)} %get-tuple-element.38), channel_id=1, source_target_pairs={{4,8},{12,16},{20,24},{8,4},{16,12},{24,20},{5,9},{13,17},{21,25},... | collective-permute-start | bytes 909320 | tf_op jit(solution)/shard_map/ppermute | solution.py:913
  4.1 9.8 %collective-permute-start.2 = (f32[296,128]{1,0:T(8,128)S(1)}, f32[296,128]{1,0:T(8,128)S(1)}, u32[]{:S(2)}, u32[]{:S(2)}) collective-permute-start(f32[296,128]{1,0:T(8,128)S(1)} %get-tuple-element.37), channel_id=1, source_target_pairs={{1,0},{2,1},{3,2},{5,4},{6,5},{7,6},{9,8},{10,9},{11,10},{13,12},{... | collective-permute-start | bytes 454664 | tf_op jit(solution)/shard_map/ppermute | solution.py:904
  5.4 8.5 %collective-permute-start.1 = (f32[152,128]{1,0:T(8,128)S(1)}, f32[152,128]{1,0:T(8,128)S(1)}, u32[]{:S(2)}, u32[]{:S(2)}) collective-permute-start(f32[152,128]{1,0:T(8,128)S(1)} %get-tuple-element.36), channel_id=1, source_target_pairs={{0,1},{1,2},{2,3},{4,5},{5,6},{6,7},{8,9},{9,10},{10,11},{12,13},{... | collective-permute-start | bytes 233480 | tf_op jit(solution)/shard_map/ppermute | solution.py:904
  10.9 2.3 %collective-permute-start.4 = (f32[2,8,128]{2,1,0:T(8,128)S(1)}, f32[2,8,128]{2,1,0:T(8,128)S(1)}, u32[]{:S(2)}, u32[]{:S(2)}) collective-permute-start(f32[2,8,128]{2,1,0:T(8,128)S(1)} %negate_select_fusion.codes), channel_id=1, source_target_pairs={{0,4},{8,12},{16,20},{24,28},{4,0},{12,8},{20,16},{28,24},{1,5},{9... | collective-permute-start | bytes 24584 | tf_op jit(solution)/shard_map/ppermute | solution.py:910
  13.2 9.2 %collective-permute-start.5 = (f32[576,128]{1,0:T(8,128)S(1)}, f32[576,128]{1,0:T(8,128)S(1)}, u32[]{:S(2)}, u32[]{:S(2)}) collective-permute-start(f32[576,128]{1,0:T(8,128)S(1)} %second.1), channel_id=1, source_target_pairs={{8,4},{16,12},{24,20},{9,5},{17,13},{25,21},{10,6},{18,14},{26,22}... | collective-permute-start | bytes 884744 | tf_op jit(solution)/shard_map/ppermute | solution.py:935
  14.0 11.7 %collective-permute-start.8 = (f32[448,128]{1,0:T(8,128)S(1)}, f32[448,128]{1,0:T(8,128)S(1)}, u32[]{:S(2)}, u32[]{:S(2)}) collective-permute-start(f32[448,128]{1,0:T(8,128)S(1)} %corners.1), channel_id=1, source_target_pairs={{4,8},{12,16},{20,24},{8,4},{16,12},{24,20},{5,9},{13,17},{21,25},... | collective-permute-start | bytes 688136 | tf_op jit(solution)/shard_map/ppermute | solution.py:913
  14.7 5.9 %collective-permute-start.7 = (f32[296,128]{1,0:T(8,128)S(1)}, f32[296,128]{1,0:T(8,128)S(1)}, u32[]{:S(2)}, u32[]{:S(2)}) collective-permute-start(f32[296,128]{1,0:T(8,128)S(1)} %collective-permute-done.2.yp), channel_id=1, source_target_pairs={{0,4},{8,12},{16,20},{24,28},{4,0},{12,8},{20,16},{28,24},{1,5},{9... | collective-permute-start | bytes 454664 | tf_op jit(solution)/shard_map/ppermute | solution.py:910
  19.3 1.3 %collective-permute-start.6 = (f32[152,128]{1,0:T(8,128)S(1)}, f32[152,128]{1,0:T(8,128)S(1)}, u32[]{:S(2)}, u32[]{:S(2)}) collective-permute-start(f32[152,128]{1,0:T(8,128)S(1)} %collective-permute-done.1.ym), channel_id=1, source_target_pairs={{0,4},{8,12},{16,20},{24,28},{4,0},{12,8},{20,16},{28,24},{1,5},{9... | collective-permute-start | bytes 233480 | tf_op jit(solution)/shard_map/ppermute | solution.py:910
  43.1 13.6 %copy-start.1 = (s32[2,8,128]{2,1,0:T(8,128)S(1)}, s32[2,8,128]{2,1,0:T(8,128)}, u32[]{:S(2)}) copy-start(s32[2,8,128]{2,1,0:T(8,128)} %levels.1) | copy-start | bytes 24580
  56.7 1.3 %collective-permute-start.9 = (f32[16,2,8,128]{3,2,1,0:T(8,128)S(1)}, f32[16,2,8,128]{3,2,1,0:T(8,128)S(1)}, u32[]{:S(2)}, u32[]{:S(2)}) collective-permute-start(f32[16,2,8,128]{3,2,1,0:T(8,128)S(1)} %all_to_all.11.blocks), channel_id=1, source_target_pairs={{0,4},{8,12},{16,20},{24,28},{4,0},{12,8},{20,16},{28,24},{1,5},{9... | collective-permute-start | bytes 393224 | tf_op jit(solution)/shard_map/ppermute | solution.py:910

commit v19 on v18

--- a/solution.py
+++ b/solution.py
@@ -419,21 +419,24 @@
         ref[2 * cases : 4 * cases, lane] = rest
 
 
-def keep_split(ref, place, value, cases):
+def keep_split(ref, line, place, value, cases):
     for k in range(3):
         part = value[k * cases : (k + 1) * cases]
         high = part.astype(bf16).astype(f32)
-        ref[:, (place * 3 + k) * LANES : (place * 3 + k + 1) * LANES] = jnp.concatenate(
-            [high, part - high], 0
-        ).astype(bf16)
-
-
-def products(first, second):
+        lane = slice((place * 3 + k) * LANES, (place * 3 + k + 1) * LANES)
+        both = jnp.concatenate([high, part - high], 0).astype(bf16)
+        ref[line : line + 2 * cases, lane] = both
+
+
+def folded(value):
+    half = value.shape[0] // 2
+    return value[:half] + value[half:]
+
+
+def products(first, second, cases):
     contract = (((1,), (1,)), ((), ()))
     out = lax.dot_general(first, second, contract, preferred_element_type=f32)
-    left, right = out.shape[0] // 2, out.shape[1] // 2
-    out = out[:, :right] + out[:, right:]
-    return out[:left] + out[left:]
+    return out[:, : 2 * cases] + out[:, 2 * cases :]
 
 
 def folds(cases):
@@ -527,12 +530,10 @@
     for index, (x, y) in enumerate(inner_columns + outer_columns):
         force = image(x, y, index)
         if x < planes:
-            place = index if index < count else inner_own + index - count
-            keep_pair(right, place, inside(own, x, y, rows, block), force, cases)
-    width = 3 * LANES
-    gram = products(right[:, : inner_own * width], both_out[:, : inner_own * width])
-    outer_part = both_out[:, count * width : (count + outer_own) * width]
-    gram_out[...] = gram + products(right[:, inner_own * width :], outer_part)
+            ref, place = (again, index) if index < count else (right, index - count)
+            keep_pair(ref, place, inside(own, x, y, rows, block), force, cases)
+    width, two = 3 * LANES, 2 * cases
+    again[: 2 * two, inner_own * width :] = jnp.zeros((2 * two, (count - inner_own) * width), bf16)
 
     find = whole(w_sums, w_diffs, len(core))
     kept = range(len(core))
@@ -542,8 +543,11 @@
     for index, (x, y) in enumerate(inner_columns):
         column = x * len(core) + y - core[0]
         s, d = acc2_s[column], acc2_d[column]
-        keep_split(again, index, s - d + shift_up(s + d), cases)
-    other_out[...] = products(again[...], both_out[:, : count * width])
+        keep_split(again, 2 * two, index, s - d + shift_up(s + d), cases)
+    product = products(again[...], both_out[:, : count * width], cases)
+    outer_part = both_out[:, count * width : (count + outer_own) * width]
+    gram_out[...] = folded(product[: 2 * two]) + folded(products(right[...], outer_part, cases))
+    other_out[...] = folded(product[2 * two :])
 
 
 def main_kernel(
@@ -552,7 +556,7 @@
     sums_m, diffs_m, middle_m, acc_sm, acc_dm, w_sm, w_dm, both_m, gram_m,
     other_m, acc2_sm, acc2_dm, both_out, system_out, stiff_ref, inverse,
     middle, sums, diffs, acc_s0, acc_d0, acc_s1, acc_d1, w_sums, w_diffs,
-    acc2_s0, acc2_d0, acc2_s1, acc2_d1, right, second_m, second_r, table, dense,
+    acc2_s0, acc2_d0, acc2_s1, acc2_d1, right, second_m, table, dense,
 ):
     planes, rows, cases = sizes
     block = 3 * cases
@@ -667,15 +671,18 @@
         return s - d + shift_up(s + d)
 
     inner_columns, outer_columns, _, _ = core_columns(planes, rows)
+    two = 2 * cases
     for index, (x, y) in enumerate(outer_columns):
-        keep_split(second_m, index, second_force(x, y), cases)
+        keep_split(second_m, 0, index, second_force(x, y), cases)
     for index, (x, y) in enumerate(columns):
-        keep_split(second_r, index, second_force(x, y), cases)
-
-    two = 2 * cases
-    gram = products(right[...], both_out[:, : own_count * 3 * LANES]) + gram_m[...]
-    other = products(second_m[...], both_m[:, len(inner_columns) * 3 * LANES :]) + other_m[...]
-    other = other + products(second_r[...], both_out[...])
+        keep_split(right, 2 * two, index, second_force(x, y), cases)
+    lane = own_count * 3 * LANES
+    right[: 2 * two, lane:] = jnp.zeros((2 * two, right.shape[1] - lane), bf16)
+
+    product = products(right[...], both_out[...], cases)
+    more = products(second_m[...], both_m[:, len(inner_columns) * 3 * LANES :], cases)
+    gram = folded(product[: 2 * two]) + gram_m[...]
+    other = folded(product[2 * two :]) + folded(more) + other_m[...]
     row = lax.broadcasted_iota(jnp.int32, (cases, cases), 0)
     column = lax.broadcasted_iota(jnp.int32, (cases, cases), 1)
     load_load, load_image = gram[:cases, :cases], gram[cases:, :cases]
@@ -990,14 +997,14 @@
         scratch_shapes=[
             pltpu.VMEM((planes + 4, up8(rows), LANES), f32),
             pltpu.VMEM((planes + 3, up8(rows), LANES), f32),
-            scratch(fields(4, planes * core)),
-            scratch(fields(2, (planes + 1) * (core - 2))),
+            scratch(fields(4, planes * 2)),
+            scratch(fields(6, (planes + 1) * (core - 2))),
         ],
         compiler_params=PARAMS,
         name="middle",
     )(own, pair, edge, second, *early)
 
-    rim, rim_own = rim_columns(planes, rows)
+    rim, _ = rim_columns(planes, rows)
     both, system = pl.pallas_call(
         functools.partial(main_kernel, sizes),
         out_shape=[
@@ -1014,9 +1021,8 @@
             *[scratch(columns(6))] * 4,
             *[scratch(columns((planes + 1) * 4))] * 2,
             *[scratch(columns((planes + 1) * 3))] * 4,
-            scratch(fields(4, rim_own)),
+            scratch(fields(6, len(rim))),
             scratch(fields(2, (planes + 1) * 2)),
-            scratch(fields(2, len(rim))),
             pltpu.VMEM((cases, LANES), f32),
             pltpu.VMEM((5 * cases // 12, LANES), f32),
         ],

time: 59.1 us -> 59 us (level)
  no operation moved by 1% of the time
where the time goes in v19:
time: 59 us; the launch traced here: 58.7 us
  blocking collectives  24.5 us (42%)
  starting transfers between devices  15.5 us (26%)
  Pallas kernels  12.6 us (21%)
  waiting for transfers between devices  4.23 us (7%)
  local copies, waits for them, and re-layouts  1.07 us (2%)
  other arithmetic  0.72 us (1%)
    all_to_all x1, blocking collectives, local(): system = lax.all_to_all(system, ('gx', 'gy'), 0, 0)  14 us
    all_to_all x1, blocking collectives, gathered(): mine = lax.all_to_all(copies, ('gx', 'gy'), 0, 0, axis_index_groups=groups)  10.5 us
    ppermute x2, starting transfers between devices, moved(): return lax.ppermute(value, axis, pairs)  6.77 us
    ppermute x5, starting transfers between devices, swapped(): return lax.ppermute(value, 'gx', links(0, 1) + links(1, -1))  6.71 us
    ppermute x5, waiting for transfers between devices, swapped(): return lax.ppermute(value, 'gx', links(0, 1) + links(1, -1))  4.22 us
    pallas_call x1, Pallas kernels, local(): pl.pallas_call(functools.partial(middle_kernel, sizes), out_shape=[column...  3.31 us
    pallas_call x1, Pallas kernels, local(): pl.pallas_call(functools.partial(main_kernel, sizes), out_shape=[fields(4...  3.29 us
    pallas_call x1, Pallas kernels, local(): pl.pallas_call(functools.partial(solve_kernel, sizes), out_shape=jax.Shap...  3.11 us
  transfers between devices with their start and end apart: 10, of which 4 were waited for; matrix products, arithmetic and copies ran while one was open for 0% of the time, Pallas kernels for 9%

profile of v19, /device:TPU:0, one launch (start us, length us, event | category | flops | bytes accessed | tf_op | source)
XLA Modules:
  0.0 58.7 jit_solution(8047986109448929817)
XLA Ops:
  0.0 0.7 %negate_select_fusion.codes = f32[2,8,128]{2,1,0:T(8,128)S(1)} fusion(s32[2,8,128]{2,1,0:T(8,128)} %levels.1, s32[2,8,128]{2,1,0:T(8,128)} %param.5), kind=kLoop, calls=%fused_computation | loop fusion | flops 16384 | bytes 24576 | tf_op jit(solution)/shard_map/jit(_where)/select_n | solution.py:888
  0.7 0.0 copy-start
  0.7 1.1 %copy-done = f32[3,24,2,8,128]{4,3,2,1,0:T(8,128)S(1)} copy-done((f32[3,24,2,8,128]{4,3,2,1,0:T(8,128)S(1)}, f32[3,24,2,8,128]{4,3,2,1,0:T(8,128)}, u32[]{:S(2)}) %copy-start) | copy-done | bytes 589848
  1.8 0.1 pack.1
  1.9 0.5 collective-permute-start
  2.4 0.7 %collective-permute-start.3 = (f32[592,128]{1,0:T(8,128)S(1)}, f32[592,128]{1,0:T(8,128)S(1)}, u32[]{:S(2)}, u32[]{:S(2)}) collective-permute-start(f32[592,128]{1,0:T(8,128)S(1)} %get-tuple-element.38), channel_id=1, source_target_pairs={{4,8},{12,16},{20,24},{8,4},{16,12},{24,20},{5,9},{13,17},{21,25},... | collective-permute-start | bytes 909320 | tf_op jit(solution)/shard_map/ppermute | solution.py:920
  3.1 1.0 %collective-permute-done.pair = f32[1168,128]{1,0:T(8,128)S(1)} collective-permute-done((f32[1168,128]{1,0:T(8,128)S(1)}, f32[1168,128]{1,0:T(8,128)S(1)}, u32[]{:S(2)}, u32[]{:S(2)}) %collective-permute-start) | collective-permute-done | bytes 598048 | tf_op jit(solution)/shard_map/ppermute | solution.py:917
  4.1 1.3 %collective-permute-start.2 = (f32[296,128]{1,0:T(8,128)S(1)}, f32[296,128]{1,0:T(8,128)S(1)}, u32[]{:S(2)}, u32[]{:S(2)}) collective-permute-start(f32[296,128]{1,0:T(8,128)S(1)} %get-tuple-element.37), channel_id=1, source_target_pairs={{1,0},{2,1},{3,2},{5,4},{6,5},{7,6},{9,8},{10,9},{11,10},{13,12},{... | collective-permute-start | bytes 454664 | tf_op jit(solution)/shard_map/ppermute | solution.py:911
  5.4 5.5 %collective-permute-start.1 = (f32[152,128]{1,0:T(8,128)S(1)}, f32[152,128]{1,0:T(8,128)S(1)}, u32[]{:S(2)}, u32[]{:S(2)}) collective-permute-start(f32[152,128]{1,0:T(8,128)S(1)} %get-tuple-element.36), channel_id=1, source_target_pairs={{0,1},{1,2},{2,3},{4,5},{5,6},{6,7},{8,9},{9,10},{10,11},{12,13},{... | collective-permute-start | bytes 233480 | tf_op jit(solution)/shard_map/ppermute | solution.py:911
  10.9 1.5 %collective-permute-start.4 = (f32[2,8,128]{2,1,0:T(8,128)S(1)}, f32[2,8,128]{2,1,0:T(8,128)S(1)}, u32[]{:S(2)}, u32[]{:S(2)}) collective-permute-start(f32[2,8,128]{2,1,0:T(8,128)S(1)} %negate_select_fusion.codes), channel_id=1, source_target_pairs={{0,4},{8,12},{16,20},{24,28},{4,0},{12,8},{20,16},{28,24},{1,5},{9... | collective-permute-start | bytes 24584 | tf_op jit(solution)/shard_map/ppermute | solution.py:917
  12.4 0.8 %collective-permute-done.4.begun = f32[2,8,128]{2,1,0:T(8,128)S(1)} collective-permute-done((f32[2,8,128]{2,1,0:T(8,128)S(1)}, f32[2,8,128]{2,1,0:T(8,128)S(1)}, u32[]{:S(2)}, u32[]{:S(2)}) %collective-permute-start.4) | collective-permute-done | bytes 8224 | tf_op jit(solution)/shard_map/ppermute | solution.py:917
  13.2 0.7 %collective-permute-start.5 = (f32[576,128]{1,0:T(8,128)S(1)}, f32[576,128]{1,0:T(8,128)S(1)}, u32[]{:S(2)}, u32[]{:S(2)}) collective-permute-start(f32[576,128]{1,0:T(8,128)S(1)} %second.1), channel_id=1, source_target_pairs={{8,4},{16,12},{24,20},{9,5},{17,13},{25,21},{10,6},{18,14},{26,22}... | collective-permute-start | bytes 884744 | tf_op jit(solution)/shard_map/ppermute | solution.py:942
  13.9 0.0 collective-permute-done.3.edge
  13.9 0.0 collective-permute-done.1.ym
  13.9 0.0 collective-permute-done.2.yp
  14.0 0.7 %collective-permute-start.8 = (f32[448,128]{1,0:T(8,128)S(1)}, f32[448,128]{1,0:T(8,128)S(1)}, u32[]{:S(2)}, u32[]{:S(2)}) collective-permute-start(f32[448,128]{1,0:T(8,128)S(1)} %corners.1), channel_id=1, source_target_pairs={{4,8},{12,16},{20,24},{8,4},{16,12},{24,20},{5,9},{13,17},{21,25},... | collective-permute-start | bytes 688136 | tf_op jit(solution)/shard_map/ppermute | solution.py:920
  14.7 4.6 %collective-permute-start.7 = (f32[296,128]{1,0:T(8,128)S(1)}, f32[296,128]{1,0:T(8,128)S(1)}, u32[]{:S(2)}, u32[]{:S(2)}) collective-permute-start(f32[296,128]{1,0:T(8,128)S(1)} %collective-permute-done.2.yp), channel_id=1, source_target_pairs={{0,4},{8,12},{16,20},{24,28},{4,0},{12,8},{20,16},{28,24},{1,5},{9... | collective-permute-start | bytes 454664 | tf_op jit(solution)/shard_map/ppermute | solution.py:917
  19.3 0.1 collective-permute-start.6
  19.4 1.2 %collective-permute-done.6.ym_pair = f32[152,128]{1,0:T(8,128)S(1)} collective-permute-done((f32[152,128]{1,0:T(8,128)S(1)}, f32[152,128]{1,0:T(8,128)S(1)}, u32[]{:S(2)}, u32[]{:S(2)}) %collective-permute-start.6) | collective-permute-done | bytes 77856 | tf_op jit(solution)/shard_map/ppermute | solution.py:917
  20.6 0.0 collective-permute-done.7.yp_pair
  20.6 1.8 %early.1 = (f32[33,72,128]{2,1,0:T(8,128)S(1)}, f32[33,72,128]{2,1,0:T(8,128)S(1)}, f32[33,72,128]{2,1,0:T(8,128)S(1)}, f32[27,72,128]{2,1,0:T(8,128)S(1)}, f32[27,72,128]{2,1,0:T(8,128)S(1)}) custom-call(f32[1168,128]{1,0:T(8,128)S(1)} %get-tuple-element.34.own, f32[1168,128]{1,0:T(8,128)S(1)} %collective-permute-done.pair, ...), custom_call_target="tpu_custom_call" | custom-call | flops 29491200 | bytes 8388608 | tf_op jit(solution)/shard_map/early/pallas_call | solution.py:960
  22.4 0.0 collective-permute-done.5.second
  22.4 3.3 %middle.1 = (f32[21,72,128]{2,1,0:T(8,128)S(1)}, f32[21,72,128]{2,1,0:T(8,128)S(1)}, f32[7,72,128]{2,1,0:T(8,128)S(1)}, f32[21,72,128]{2,1,0:T(8,128)S(1)}, f32[...) custom-call(f32[1168,128]{1,0:T(8,128)S(1)} %get-tuple-element.34.ow, ...), custom_call_target="tpu_custom_call" | custom-call | tf_op jit(solution)/shard_map/middle/pallas_call | solution.py:986
  25.7 0.0 collective-permute-done.8.corners
  25.7 3.3 %operator.1 = (bf16[96,4608]{1,0:T(8,128)(2,1)S(1)}, f32[32,5,2,128]{3,2,1,0:T(2,128)S(1)}) custom-call(f32[1168,128]{1,0:T(8,128)S(1)} %get-tuple-element.34.own, f32[1168,128]{1,0:T(8,128)S(1)} %collective-permute-done.pair, f32[592,128]{1,0:T(8,128)S(1)} %collective-permute-done.3.edge, f32[576,128]{1,0:T(8,128)S(1)} %collective-permute-done.5.second, ...), custom_call_target="tpu_custom_call" | custom-call | tf_op jit(solution)/shard_map/operator/pallas_call | solution.py:1008
  29.0 14.0 %all_to_all.10.system = f32[32,5,2,128]{3,2,1,0:T(2,128)S(1)} all-to-all(f32[32,5,2,128]{3,2,1,0:T(2,128)S(1)} %get-tuple-element.59), channel_id=1, replica_groups=mesh['gx'=8,'gy'=4] {'gx','gy'}, dimensions={0} | all-to-all | bytes 327680 | tf_op jit(solution)/shard_map/all_to_all | solution.py:1045
  43.0 0.0 copy-start.1
  43.0 3.1 %solve.1 = f32[16,2,8,128]{3,2,1,0:T(8,128)S(1)} custom-call(f32[32,5,2,128]{3,2,1,0:T(2,128)S(1)} %all_to_all.10.system, bf16[96,5760]{1,0:T(8,128)(2,1)S(1)} %get-tuple-element.54.both_m, bf16[96,4608]{1,0:T(8,128)(2,1)S(1)} %get-tuple-element.60.both_r, f32[2,8,128]{2,1,0:T(8,128)S(1)} %negate_select_fusion.codes), custom_call_target="tpu_custom_call" | custom-call | tf_op jit(solution)/shard_map/solve/pallas_call | solution.py:1047
  46.1 10.5 %all_to_all.11.blocks = f32[16,2,8,128]{3,2,1,0:T(8,128)S(1)} all-to-all(f32[16,2,8,128]{3,2,1,0:T(8,128)S(1)} %solve.1), channel_id=1, replica_groups={{0,1,2,3,8,9,10,11,16,17,18,19,24,25,26,27},{4,5,6,7,12,13,14,15,20,21,..., dimensions={0} | all-to-all | bytes 262144 | tf_op jit(solution)/shard_map/all_to_all | solution.py:1042
  56.6 0.0 collective-permute-start.9
  56.6 0.0 copy-done.1
  56.6 0.1 scale.1
  56.7 1.2 %collective-permute-done.9.blocks_pair = f32[16,2,8,128]{3,2,1,0:T(8,128)S(1)} collective-permute-done((f32[16,2,8,128]{3,2,1,0:T(8,128)S(1)}, f32[16,2,8,128]{3,2,1,0:T(8,128)S(1)}, u32[]{:S(2)}, u32[]{:S(2)}) %collective-permute-start.9) | collective-permute-done | bytes 131104 | tf_op jit(solution)/shard_map/ppermute | solution.py:917
  58.0 0.7 %cone.1 = f32[2,8,128]{2,1,0:T(8,128)} custom-call(f32[16,2,8,128]{3,2,1,0:T(8,128)S(1)} %all_to_all.11.blocks, f32[16,2,8,128]{3,2,1,0:T(8,128)S(1)} %collective-permute-done.9.blocks_pair, f32[2,8,128]{2,1,0:T(8,128)S(1)} %scale.1), custom_call_target="tpu_custom_call" | custom-call | tf_op jit(solution)/shard_map/cone/pallas_call | solution.py:1066
  (3 shorter events, 0.1 us)
Async XLA Ops:
  0.7 1.1 %copy-start = (f32[3,24,2,8,128]{4,3,2,1,0:T(8,128)S(1)}, f32[3,24,2,8,128]{4,3,2,1,0:T(8,128)}, u32[]{:S(2)}) copy-start(f32[3,24,2,8,128]{4,3,2,1,0:T(8,128)} %forces.1) | copy-start | bytes 1769476
  1.9 2.2 %collective-permute-start = (f32[1168,128]{1,0:T(8,128)S(1)}, f32[1168,128]{1,0:T(8,128)S(1)}, u32[]{:S(2)}, u32[]{:S(2)}) collective-permute-start(f32[1168,128]{1,0:T(8,128)S(1)} %get-tuple-element.34.own), channel_id=1, source_target_pairs={{0,4},{8,12},{16,20},{24,28},{4,0},{12,8},{20,16},{28,24},{1,5},{9... | collective-permute-start | bytes 1794056 | tf_op jit(solution)/shard_map/ppermute | solution.py:917
  2.4 11.5 %collective-permute-start.3 = (f32[592,128]{1,0:T(8,128)S(1)}, f32[592,128]{1,0:T(8,128)S(1)}, u32[]{:S(2)}, u32[]{:S(2)}) collective-permute-start(f32[592,128]{1,0:T(8,128)S(1)} %get-tuple-element.38), channel_id=1, source_target_pairs={{4,8},{12,16},{20,24},{8,4},{16,12},{24,20},{5,9},{13,17},{21,25},... | collective-permute-start | bytes 909320 | tf_op jit(solution)/shard_map/ppermute | solution.py:920
  4.1 9.8 %collective-permute-start.2 = (f32[296,128]{1,0:T(8,128)S(1)}, f32[296,128]{1,0:T(8,128)S(1)}, u32[]{:S(2)}, u32[]{:S(2)}) collective-permute-start(f32[296,128]{1,0:T(8,128)S(1)} %get-tuple-element.37), channel_id=1, source_target_pairs={{1,0},{2,1},{3,2},{5,4},{6,5},{7,6},{9,8},{10,9},{11,10},{13,12},{... | collective-permute-start | bytes 454664 | tf_op jit(solution)/shard_map/ppermute | solution.py:911
  5.4 8.5 %collective-permute-start.1 = (f32[152,128]{1,0:T(8,128)S(1)}, f32[152,128]{1,0:T(8,128)S(1)}, u32[]{:S(2)}, u32[]{:S(2)}) collective-permute-start(f32[152,128]{1,0:T(8,128)S(1)} %get-tuple-element.36), channel_id=1, source_target_pairs={{0,1},{1,2},{2,3},{4,5},{5,6},{6,7},{8,9},{9,10},{10,11},{12,13},{... | collective-permute-start | bytes 233480 | tf_op jit(solution)/shard_map/ppermute | solution.py:911
  10.9 2.3 %collective-permute-start.4 = (f32[2,8,128]{2,1,0:T(8,128)S(1)}, f32[2,8,128]{2,1,0:T(8,128)S(1)}, u32[]{:S(2)}, u32[]{:S(2)}) collective-permute-start(f32[2,8,128]{2,1,0:T(8,128)S(1)} %negate_select_fusion.codes), channel_id=1, source_target_pairs={{0,4},{8,12},{16,20},{24,28},{4,0},{12,8},{20,16},{28,24},{1,5},{9... | collective-permute-start | bytes 24584 | tf_op jit(solution)/shard_map/ppermute | solution.py:917
  13.2 9.2 %collective-permute-start.5 = (f32[576,128]{1,0:T(8,128)S(1)}, f32[576,128]{1,0:T(8,128)S(1)}, u32[]{:S(2)}, u32[]{:S(2)}) collective-permute-start(f32[576,128]{1,0:T(8,128)S(1)} %second.1), channel_id=1, source_target_pairs={{8,4},{16,12},{24,20},{9,5},{17,13},{25,21},{10,6},{18,14},{26,22}... | collective-permute-start | bytes 884744 | tf_op jit(solution)/shard_map/ppermute | solution.py:942
  14.0 11.7 %collective-permute-start.8 = (f32[448,128]{1,0:T(8,128)S(1)}, f32[448,128]{1,0:T(8,128)S(1)}, u32[]{:S(2)}, u32[]{:S(2)}) collective-permute-start(f32[448,128]{1,0:T(8,128)S(1)} %corners.1), channel_id=1, source_target_pairs={{4,8},{12,16},{20,24},{8,4},{16,12},{24,20},{5,9},{13,17},{21,25},... | collective-permute-start | bytes 688136 | tf_op jit(solution)/shard_map/ppermute | solution.py:920
  14.7 5.9 %collective-permute-start.7 = (f32[296,128]{1,0:T(8,128)S(1)}, f32[296,128]{1,0:T(8,128)S(1)}, u32[]{:S(2)}, u32[]{:S(2)}) collective-permute-start(f32[296,128]{1,0:T(8,128)S(1)} %collective-permute-done.2.yp), channel_id=1, source_target_pairs={{0,4},{8,12},{16,20},{24,28},{4,0},{12,8},{20,16},{28,24},{1,5},{9... | collective-permute-start | bytes 454664 | tf_op jit(solution)/shard_map/ppermute | solution.py:917
  19.3 1.3 %collective-permute-start.6 = (f32[152,128]{1,0:T(8,128)S(1)}, f32[152,128]{1,0:T(8,128)S(1)}, u32[]{:S(2)}, u32[]{:S(2)}) collective-permute-start(f32[152,128]{1,0:T(8,128)S(1)} %collective-permute-done.1.ym), channel_id=1, source_target_pairs={{0,4},{8,12},{16,20},{24,28},{4,0},{12,8},{20,16},{28,24},{1,5},{9... | collective-permute-start | bytes 233480 | tf_op jit(solution)/shard_map/ppermute | solution.py:917
  43.0 13.6 %copy-start.1 = (s32[2,8,128]{2,1,0:T(8,128)S(1)}, s32[2,8,128]{2,1,0:T(8,128)}, u32[]{:S(2)}) copy-start(s32[2,8,128]{2,1,0:T(8,128)} %levels.1) | copy-start | bytes 24580
  56.6 1.3 %collective-permute-start.9 = (f32[16,2,8,128]{3,2,1,0:T(8,128)S(1)}, f32[16,2,8,128]{3,2,1,0:T(8,128)S(1)}, u32[]{:S(2)}, u32[]{:S(2)}) collective-permute-start(f32[16,2,8,128]{3,2,1,0:T(8,128)S(1)} %all_to_all.11.blocks), channel_id=1, source_target_pairs={{0,4},{8,12},{16,20},{24,28},{4,0},{12,8},{20,16},{28,24},{1,5},{9... | collective-permute-start | bytes 393224 | tf_op jit(solution)/shard_map/ppermute | solution.py:917

commit v20 on v19

--- a/solution.py
+++ b/solution.py
@@ -280,17 +280,21 @@
 
 
 def beyond(refs, slot, y, rows, block):
-    below, above = refs
+    below, above, base = refs
     if y < 0:
         return lines(below, slot * block, block)
-    return lines(above, (slot * 2 + y - rows) * block, block)
+    return lines(above, base + (slot * 2 + y - rows) * block, block)
 
 
 def beyond_codes(refs, slots, slot, y, block):
-    below, above = refs
+    below, above, base = refs
     if y < 0:
         return lines(below, slots * block + slot * 2, 2)
-    return lines(above, slots * 2 * block + slot * 2, 2)
+    return lines(above, base + slots * 2 * block + slot * 2, 2)
+
+
+def pair_base(planes, block):
+    return 2 * block + 8 if planes == 2 else 0
 
 
 def corner(ref, slot, y, rows, block):
@@ -330,7 +334,7 @@
     block = 3 * cases
     ys = rows + 3
     even = lax.axis_index("gx") % 2 == 0
-    y_own, y_pair = (ym, yp), (ym_pair, yp_pair)
+    y_own, y_pair = (ym, yp, 0), (ym_pair, yp_pair, pair_base(planes, block))
 
     def both_ways(w, read):
         low = read(True, w + 1) if w + 1 < planes else read(False, w + 1 - planes)
@@ -564,7 +568,7 @@
     core, rim = core_rows(rows), rim_rows(rows)
     columns, own_count = rim_columns(planes, rows)
     even = lax.axis_index("gx") % 2 == 0
-    y_own, y_pair = (ym, yp), (ym_pair, yp_pair)
+    y_own, y_pair = (ym, yp, 0), (ym_pair, yp_pair, pair_base(planes, block))
 
     def codes(x, y):
         def read(mine, plane):
@@ -940,18 +944,20 @@
         name="second",
     )(swapped(codes), own)
     second = lax.ppermute(second, "gx", links(2, -1))
-    pair_yp, pair_ym = swapped(from_yp), swapped(from_ym)
     from_ym, from_yp, edge = lax.optimization_barrier((from_ym, from_yp, edge))
-    corners = across(
-        pl.pallas_call(
-            functools.partial(corner_kernel, sizes),
-            out_shape=jax.ShapeDtypeStruct((6 * block + 16, LANES), f32),
-            in_specs=[VMEM] * 2,
-            out_specs=VMEM,
-            compiler_params=PARAMS,
-            name="corners",
-        )(from_ym, from_yp)
-    )
+    corners = pl.pallas_call(
+        functools.partial(corner_kernel, sizes),
+        out_shape=jax.ShapeDtypeStruct((6 * block + 16, LANES), f32),
+        in_specs=[VMEM] * 2,
+        out_specs=VMEM,
+        compiler_params=PARAMS,
+        name="corners",
+    )(from_ym, from_yp)
+    if planes == 2:
+        pair_ym = pair_yp = swapped(corners)
+    else:
+        pair_yp, pair_ym = swapped(from_yp), swapped(from_ym)
+    corners = across(corners)
 
     devices = count_x * count_y
     nodes = (planes + 1) * (rows + 1)

time: 59 us -> 59.1 us (level)
  blocking collectives: 24.5 us -> 29 us
  starting transfers between devices: 15.5 us -> 11.8 us
  waiting for transfers between devices: 4.23 us -> 3.48 us
    all_to_all x1, blocking collectives: 14 us -> 18.5 us  [local(): system = lax.all_to_all(system, ('gx', 'gy'), 0, 0)]
    ppermute x5 -> x4, starting transfers between devices: 6.71 us -> 3.02 us  [swapped(): return lax.ppermute(value, 'gx', links(0, 1) + links(1, -1))]
    ppermute x5 -> x4, waiting for transfers between devices: 4.22 us -> 3.47 us  [swapped(): return lax.ppermute(value, 'gx', links(0, 1) + links(1, -1))]
  transfers between devices with their start and end apart: 10 -> 9, of which waited for: 4 -> 4; matrix products, arithmetic and copies ran while one was open for 0% -> 0% of each run, Pallas kernels for 9% -> 9%
where the time goes in v20:
time: 59.1 us; the launch traced here: 58.8 us
  blocking collectives  29 us (49%)
  Pallas kernels  12.6 us (21%)
  starting transfers between devices  11.8 us (20%)
  waiting for transfers between devices  3.48 us (6%)
  local copies, waits for them, and re-layouts  1.07 us (2%)
  other arithmetic  0.72 us (1%)
    all_to_all x1, blocking collectives, local(): system = lax.all_to_all(system, ('gx', 'gy'), 0, 0)  18.5 us
    all_to_all x1, blocking collectives, gathered(): mine = lax.all_to_all(copies, ('gx', 'gy'), 0, 0, axis_index_groups=groups)  10.5 us
    ppermute x2, starting transfers between devices, moved(): return lax.ppermute(value, axis, pairs)  6.77 us
    ppermute x4, waiting for transfers between devices, swapped(): return lax.ppermute(value, 'gx', links(0, 1) + links(1, -1))  3.47 us
    pallas_call x1, Pallas kernels, local(): pl.pallas_call(functools.partial(middle_kernel, sizes), out_shape=[column...  3.32 us
    pallas_call x1, Pallas kernels, local(): pl.pallas_call(functools.partial(main_kernel, sizes), out_shape=[fields(4...  3.3 us
    pallas_call x1, Pallas kernels, local(): pl.pallas_call(functools.partial(solve_kernel, sizes), out_shape=jax.Shap...  3.12 us
    ppermute x4, starting transfers between devices, swapped(): return lax.ppermute(value, 'gx', links(0, 1) + links(1, -1))  3.02 us
  transfers between devices with their start and end apart: 9, of which 4 were waited for; matrix products, arithmetic and copies ran while one was open for 0% of the time, Pallas kernels for 9%

profile of v20, /device:TPU:0, one launch (start us, length us, event | category | flops | bytes accessed | tf_op | source)
XLA Modules:
  0.0 58.8 jit_solution(2435225553746050293)
XLA Ops:
  0.0 0.7 %negate_select_fusion.codes = f32[2,8,128]{2,1,0:T(8,128)S(1)} fusion(s32[2,8,128]{2,1,0:T(8,128)} %levels.1, s32[2,8,128]{2,1,0:T(8,128)} %param.5), kind=kLoop, calls=%fused_computation | loop fusion | flops 16384 | bytes 24576 | tf_op jit(solution)/shard_map/jit(_where)/select_n | solution.py:892
  0.7 0.0 copy-start
  0.7 1.1 %copy-done = f32[3,24,2,8,128]{4,3,2,1,0:T(8,128)S(1)} copy-done((f32[3,24,2,8,128]{4,3,2,1,0:T(8,128)S(1)}, f32[3,24,2,8,128]{4,3,2,1,0:T(8,128)}, u32[]{:S(2)}) %copy-start) | copy-done | bytes 589848
  1.8 0.1 pack.1
  1.9 0.5 collective-permute-start
  2.4 0.7 %collective-permute-start.3 = (f32[592,128]{1,0:T(8,128)S(1)}, f32[592,128]{1,0:T(8,128)S(1)}, u32[]{:S(2)}, u32[]{:S(2)}) collective-permute-start(f32[592,128]{1,0:T(8,128)S(1)} %get-tuple-element.38), channel_id=1, source_target_pairs={{4,8},{12,16},{20,24},{8,4},{16,12},{24,20},{5,9},{13,17},{21,25},... | collective-permute-start | bytes 909320 | tf_op jit(solution)/shard_map/ppermute | solution.py:924
  3.1 1.0 %collective-permute-done.pair = f32[1168,128]{1,0:T(8,128)S(1)} collective-permute-done((f32[1168,128]{1,0:T(8,128)S(1)}, f32[1168,128]{1,0:T(8,128)S(1)}, u32[]{:S(2)}, u32[]{:S(2)}) %collective-permute-start) | collective-permute-done | bytes 598048 | tf_op jit(solution)/shard_map/ppermute | solution.py:921
  4.1 1.3 %collective-permute-start.2 = (f32[296,128]{1,0:T(8,128)S(1)}, f32[296,128]{1,0:T(8,128)S(1)}, u32[]{:S(2)}, u32[]{:S(2)}) collective-permute-start(f32[296,128]{1,0:T(8,128)S(1)} %get-tuple-element.37), channel_id=1, source_target_pairs={{1,0},{2,1},{3,2},{5,4},{6,5},{7,6},{9,8},{10,9},{11,10},{13,12},{... | collective-permute-start | bytes 454664 | tf_op jit(solution)/shard_map/ppermute | solution.py:915
  5.4 5.5 %collective-permute-start.1 = (f32[152,128]{1,0:T(8,128)S(1)}, f32[152,128]{1,0:T(8,128)S(1)}, u32[]{:S(2)}, u32[]{:S(2)}) collective-permute-start(f32[152,128]{1,0:T(8,128)S(1)} %get-tuple-element.36), channel_id=1, source_target_pairs={{0,1},{1,2},{2,3},{4,5},{5,6},{6,7},{8,9},{9,10},{10,11},{12,13},{... | collective-permute-start | bytes 233480 | tf_op jit(solution)/shard_map/ppermute | solution.py:915
  10.9 1.5 %collective-permute-start.4 = (f32[2,8,128]{2,1,0:T(8,128)S(1)}, f32[2,8,128]{2,1,0:T(8,128)S(1)}, u32[]{:S(2)}, u32[]{:S(2)}) collective-permute-start(f32[2,8,128]{2,1,0:T(8,128)S(1)} %negate_select_fusion.codes), channel_id=1, source_target_pairs={{0,4},{8,12},{16,20},{24,28},{4,0},{12,8},{20,16},{28,24},{1,5},{9... | collective-permute-start | bytes 24584 | tf_op jit(solution)/shard_map/ppermute | solution.py:921
  12.4 0.8 %collective-permute-done.4.begun = f32[2,8,128]{2,1,0:T(8,128)S(1)} collective-permute-done((f32[2,8,128]{2,1,0:T(8,128)S(1)}, f32[2,8,128]{2,1,0:T(8,128)S(1)}, u32[]{:S(2)}, u32[]{:S(2)}) %collective-permute-start.4) | collective-permute-done | bytes 8224 | tf_op jit(solution)/shard_map/ppermute | solution.py:921
  13.2 0.7 %collective-permute-start.5 = (f32[576,128]{1,0:T(8,128)S(1)}, f32[576,128]{1,0:T(8,128)S(1)}, u32[]{:S(2)}, u32[]{:S(2)}) collective-permute-start(f32[576,128]{1,0:T(8,128)S(1)} %second.1), channel_id=1, source_target_pairs={{8,4},{16,12},{24,20},{9,5},{17,13},{25,21},{10,6},{18,14},{26,22}... | collective-permute-start | bytes 884744 | tf_op jit(solution)/shard_map/ppermute | solution.py:946
  13.9 0.0 collective-permute-done.3.edge
  13.9 0.0 collective-permute-done.1.ym
  13.9 0.0 collective-permute-done.2.yp
  14.0 1.0 %collective-permute-start.6 = (f32[448,128]{1,0:T(8,128)S(1)}, f32[448,128]{1,0:T(8,128)S(1)}, u32[]{:S(2)}, u32[]{:S(2)}) collective-permute-start(f32[448,128]{1,0:T(8,128)S(1)} %corners.1), channel_id=1, source_target_pairs={{0,4},{8,12},{16,20},{24,28},{4,0},{12,8},{20,16},{28,24},{1,5},{9... | collective-permute-start | bytes 688136 | tf_op jit(solution)/shard_map/ppermute | solution.py:921
  15.0 0.7 %collective-permute-start.7 = (f32[448,128]{1,0:T(8,128)S(1)}, f32[448,128]{1,0:T(8,128)S(1)}, u32[]{:S(2)}, u32[]{:S(2)}) collective-permute-start(f32[448,128]{1,0:T(8,128)S(1)} %corners.1), channel_id=1, source_target_pairs={{4,8},{12,16},{20,24},{8,4},{16,12},{24,20},{5,9},{13,17},{21,25},... | collective-permute-start | bytes 688136 | tf_op jit(solution)/shard_map/ppermute | solution.py:924
  15.7 0.4 collective-permute-done.6.ym_pair.yp_pair
  16.1 1.8 %early.1 = (f32[33,72,128]{2,1,0:T(8,128)S(1)}, f32[33,72,128]{2,1,0:T(8,128)S(1)}, f32[33,72,128]{2,1,0:T(8,128)S(1)}, f32[27,72,128]{2,1,0:T(8,128)S(1)}, f32[27,72,128]{2,1,0:T(8,128)S(1)}) custom-call(f32[1168,128]{1,0:T(8,128)S(1)} %get-tuple-element.34.own, f32[1168,128]{1,0:T(8,128)S(1)} %collective-permute-done.pair, ...), custom_call_target="tpu_custom_call" | custom-call | flops 29491200 | bytes 8388608 | tf_op jit(solution)/shard_map/early/pallas_call | solution.py:966
  17.9 0.0 collective-permute-done.5.second
  17.9 3.3 %middle.1 = (f32[21,72,128]{2,1,0:T(8,128)S(1)}, f32[21,72,128]{2,1,0:T(8,128)S(1)}, f32[7,72,128]{2,1,0:T(8,128)S(1)}, f32[21,72,128]{2,1,0:T(8,128)S(1)}, f32[...) custom-call(f32[1168,128]{1,0:T(8,128)S(1)} %get-tuple-element.34.ow, ...), custom_call_target="tpu_custom_call" | custom-call | tf_op jit(solution)/shard_map/middle/pallas_call | solution.py:992
  21.3 0.0 collective-permute-done.7.corners
  21.3 3.3 %operator.1 = (bf16[96,4608]{1,0:T(8,128)(2,1)S(1)}, f32[32,5,2,128]{3,2,1,0:T(2,128)S(1)}) custom-call(f32[1168,128]{1,0:T(8,128)S(1)} %get-tuple-element.34.own, f32[1168,128]{1,0:T(8,128)S(1)} %collective-permute-done.pair, f32[592,128]{1,0:T(8,128)S(1)} %collective-permute-done.3.edge, f32[576,128]{1,0:T(8,128)S(1)} %collective-permute-done.5.second, ...), custom_call_target="tpu_custom_call" | custom-call | tf_op jit(solution)/shard_map/operator/pallas_call | solution.py:1014
  24.6 18.5 %all_to_all.10.system = f32[32,5,2,128]{3,2,1,0:T(2,128)S(1)} all-to-all(f32[32,5,2,128]{3,2,1,0:T(2,128)S(1)} %get-tuple-element.59), channel_id=1, replica_groups=mesh['gx'=8,'gy'=4] {'gx','gy'}, dimensions={0} | all-to-all | bytes 327680 | tf_op jit(solution)/shard_map/all_to_all | solution.py:1051
  43.1 0.0 copy-start.1
  43.1 3.1 %solve.1 = f32[16,2,8,128]{3,2,1,0:T(8,128)S(1)} custom-call(f32[32,5,2,128]{3,2,1,0:T(2,128)S(1)} %all_to_all.10.system, bf16[96,5760]{1,0:T(8,128)(2,1)S(1)} %get-tuple-element.54.both_m, bf16[96,4608]{1,0:T(8,128)(2,1)S(1)} %get-tuple-element.60.both_r, f32[2,8,128]{2,1,0:T(8,128)S(1)} %negate_select_fusion.codes), custom_call_target="tpu_custom_call" | custom-call | tf_op jit(solution)/shard_map/solve/pallas_call | solution.py:1053
  46.2 10.5 %all_to_all.11.blocks = f32[16,2,8,128]{3,2,1,0:T(8,128)S(1)} all-to-all(f32[16,2,8,128]{3,2,1,0:T(8,128)S(1)} %solve.1), channel_id=1, replica_groups={{0,1,2,3,8,9,10,11,16,17,18,19,24,25,26,27},{4,5,6,7,12,13,14,15,20,21,..., dimensions={0} | all-to-all | bytes 262144 | tf_op jit(solution)/shard_map/all_to_all | solution.py:1048
  56.7 0.0 collective-permute-start.8
  56.7 0.0 copy-done.1
  56.7 0.1 scale.1
  56.8 1.2 %collective-permute-done.8.blocks_pair = f32[16,2,8,128]{3,2,1,0:T(8,128)S(1)} collective-permute-done((f32[16,2,8,128]{3,2,1,0:T(8,128)S(1)}, f32[16,2,8,128]{3,2,1,0:T(8,128)S(1)}, u32[]{:S(2)}, u32[]{:S(2)}) %collective-permute-start.8) | collective-permute-done | bytes 131104 | tf_op jit(solution)/shard_map/ppermute | solution.py:921
  58.0 0.7 %cone.1 = f32[2,8,128]{2,1,0:T(8,128)} custom-call(f32[16,2,8,128]{3,2,1,0:T(8,128)S(1)} %all_to_all.11.blocks, f32[16,2,8,128]{3,2,1,0:T(8,128)S(1)} %collective-permute-done.8.blocks_pair, f32[2,8,128]{2,1,0:T(8,128)S(1)} %scale.1), custom_call_target="tpu_custom_call" | custom-call | tf_op jit(solution)/shard_map/cone/pallas_call | solution.py:1072
  (3 shorter events, 0.1 us)
Async XLA Ops:
  0.7 1.1 %copy-start = (f32[3,24,2,8,128]{4,3,2,1,0:T(8,128)S(1)}, f32[3,24,2,8,128]{4,3,2,1,0:T(8,128)}, u32[]{:S(2)}) copy-start(f32[3,24,2,8,128]{4,3,2,1,0:T(8,128)} %forces.1) | copy-start | bytes 1769476
  1.9 2.2 %collective-permute-start = (f32[1168,128]{1,0:T(8,128)S(1)}, f32[1168,128]{1,0:T(8,128)S(1)}, u32[]{:S(2)}, u32[]{:S(2)}) collective-permute-start(f32[1168,128]{1,0:T(8,128)S(1)} %get-tuple-element.34.own), channel_id=1, source_target_pairs={{0,4},{8,12},{16,20},{24,28},{4,0},{12,8},{20,16},{28,24},{1,5},{9... | collective-permute-start | bytes 1794056 | tf_op jit(solution)/shard_map/ppermute | solution.py:921
  2.4 11.5 %collective-permute-start.3 = (f32[592,128]{1,0:T(8,128)S(1)}, f32[592,128]{1,0:T(8,128)S(1)}, u32[]{:S(2)}, u32[]{:S(2)}) collective-permute-start(f32[592,128]{1,0:T(8,128)S(1)} %get-tuple-element.38), channel_id=1, source_target_pairs={{4,8},{12,16},{20,24},{8,4},{16,12},{24,20},{5,9},{13,17},{21,25},... | collective-permute-start | bytes 909320 | tf_op jit(solution)/shard_map/ppermute | solution.py:924
  4.1 9.8 %collective-permute-start.2 = (f32[296,128]{1,0:T(8,128)S(1)}, f32[296,128]{1,0:T(8,128)S(1)}, u32[]{:S(2)}, u32[]{:S(2)}) collective-permute-start(f32[296,128]{1,0:T(8,128)S(1)} %get-tuple-element.37), channel_id=1, source_target_pairs={{1,0},{2,1},{3,2},{5,4},{6,5},{7,6},{9,8},{10,9},{11,10},{13,12},{... | collective-permute-start | bytes 454664 | tf_op jit(solution)/shard_map/ppermute | solution.py:915
  5.4 8.5 %collective-permute-start.1 = (f32[152,128]{1,0:T(8,128)S(1)}, f32[152,128]{1,0:T(8,128)S(1)}, u32[]{:S(2)}, u32[]{:S(2)}) collective-permute-start(f32[152,128]{1,0:T(8,128)S(1)} %get-tuple-element.36), channel_id=1, source_target_pairs={{0,1},{1,2},{2,3},{4,5},{5,6},{6,7},{8,9},{9,10},{10,11},{12,13},{... | collective-permute-start | bytes 233480 | tf_op jit(solution)/shard_map/ppermute | solution.py:915
  10.9 2.3 %collective-permute-start.4 = (f32[2,8,128]{2,1,0:T(8,128)S(1)}, f32[2,8,128]{2,1,0:T(8,128)S(1)}, u32[]{:S(2)}, u32[]{:S(2)}) collective-permute-start(f32[2,8,128]{2,1,0:T(8,128)S(1)} %negate_select_fusion.codes), channel_id=1, source_target_pairs={{0,4},{8,12},{16,20},{24,28},{4,0},{12,8},{20,16},{28,24},{1,5},{9... | collective-permute-start | bytes 24584 | tf_op jit(solution)/shard_map/ppermute | solution.py:921
  13.2 4.7 %collective-permute-start.5 = (f32[576,128]{1,0:T(8,128)S(1)}, f32[576,128]{1,0:T(8,128)S(1)}, u32[]{:S(2)}, u32[]{:S(2)}) collective-permute-start(f32[576,128]{1,0:T(8,128)S(1)} %second.1), channel_id=1, source_target_pairs={{8,4},{16,12},{24,20},{9,5},{17,13},{25,21},{10,6},{18,14},{26,22}... | collective-permute-start | bytes 884744 | tf_op jit(solution)/shard_map/ppermute | solution.py:946
  14.0 2.1 %collective-permute-start.6 = (f32[448,128]{1,0:T(8,128)S(1)}, f32[448,128]{1,0:T(8,128)S(1)}, u32[]{:S(2)}, u32[]{:S(2)}) collective-permute-start(f32[448,128]{1,0:T(8,128)S(1)} %corners.1), channel_id=1, source_target_pairs={{0,4},{8,12},{16,20},{24,28},{4,0},{12,8},{20,16},{28,24},{1,5},{9... | collective-permute-start | bytes 688136 | tf_op jit(solution)/shard_map/ppermute | solution.py:921
  15.0 6.3 %collective-permute-start.7 = (f32[448,128]{1,0:T(8,128)S(1)}, f32[448,128]{1,0:T(8,128)S(1)}, u32[]{:S(2)}, u32[]{:S(2)}) collective-permute-start(f32[448,128]{1,0:T(8,128)S(1)} %corners.1), channel_id=1, source_target_pairs={{4,8},{12,16},{20,24},{8,4},{16,12},{24,20},{5,9},{13,17},{21,25},... | collective-permute-start | bytes 688136 | tf_op jit(solution)/shard_map/ppermute | solution.py:924
  43.1 13.6 %copy-start.1 = (s32[2,8,128]{2,1,0:T(8,128)S(1)}, s32[2,8,128]{2,1,0:T(8,128)}, u32[]{:S(2)}) copy-start(s32[2,8,128]{2,1,0:T(8,128)} %levels.1) | copy-start | bytes 24580
  56.7 1.3 %collective-permute-start.8 = (f32[16,2,8,128]{3,2,1,0:T(8,128)S(1)}, f32[16,2,8,128]{3,2,1,0:T(8,128)S(1)}, u32[]{:S(2)}, u32[]{:S(2)}) collective-permute-start(f32[16,2,8,128]{3,2,1,0:T(8,128)S(1)} %all_to_all.11.blocks), channel_id=1, source_target_pairs={{0,4},{8,12},{16,20},{24,28},{4,0},{12,8},{20,16},{28,24},{1,5},{9... | collective-permute-start | bytes 393224 | tf_op jit(solution)/shard_map/ppermute | solution.py:921

commit v21 on v20

--- a/solution.py
+++ b/solution.py
@@ -738,7 +738,7 @@
         full[index * cases : (index + 1) * cases, cases:two] = right
     table = full[...]
     lane = lax.broadcasted_iota(jnp.int32, (1, LANES), 1)
-    gone, wide = 0, 8
+    gone, wide = 0, 16
     for pivot in range(0, two, wide):
         drop = pivot // 8 * 8 - gone
         table = table[drop:]

time: 59.1 us -> 60.4 us (1.022)
  Pallas kernels: 12.6 us -> 13.8 us
    pallas_call x1, Pallas kernels: 3.12 us -> 4.34 us  [local(): pl.pallas_call(functools.partial(solve_kernel, sizes), out_shape=jax.Shap...]
where the time goes in v21:
time: 60.4 us; the launch traced here: 60 us
  blocking collectives  29 us (48%)
  Pallas kernels  13.8 us (23%)
  starting transfers between devices  11.8 us (20%)
  waiting for transfers between devices  3.48 us (6%)
  local copies, waits for them, and re-layouts  1.07 us (2%)
  other arithmetic  0.72 us (1%)
    all_to_all x1, blocking collectives, local(): system = lax.all_to_all(system, ('gx', 'gy'), 0, 0)  18.5 us
    all_to_all x1, blocking collectives, gathered(): mine = lax.all_to_all(copies, ('gx', 'gy'), 0, 0, axis_index_groups=groups)  10.5 us
    ppermute x2, starting transfers between devices, moved(): return lax.ppermute(value, axis, pairs)  6.77 us
    pallas_call x1, Pallas kernels, local(): pl.pallas_call(functools.partial(solve_kernel, sizes), out_shape=jax.Shap...  4.34 us
    ppermute x4, waiting for transfers between devices, swapped(): return lax.ppermute(value, 'gx', links(0, 1) + links(1, -1))  3.47 us
    pallas_call x1, Pallas kernels, local(): pl.pallas_call(functools.partial(middle_kernel, sizes), out_shape=[column...  3.32 us
    pallas_call x1, Pallas kernels, local(): pl.pallas_call(functools.partial(main_kernel, sizes), out_shape=[fields(4...  3.3 us
    ppermute x4, starting transfers between devices, swapped(): return lax.ppermute(value, 'gx', links(0, 1) + links(1, -1))  3.02 us
  transfers between devices with their start and end apart: 9, of which 4 were waited for; matrix products, arithmetic and copies ran while one was open for 0% of the time, Pallas kernels for 9%

profile of v21, /device:TPU:0, one launch (start us, length us, event | category | flops | bytes accessed | tf_op | source)
XLA Modules:
  0.0 60.0 jit_solution(3000534988043128012)
XLA Ops:
  0.0 0.7 %negate_select_fusion.codes = f32[2,8,128]{2,1,0:T(8,128)S(1)} fusion(s32[2,8,128]{2,1,0:T(8,128)} %levels.1, s32[2,8,128]{2,1,0:T(8,128)} %param.5), kind=kLoop, calls=%fused_computation | loop fusion | flops 16384 | bytes 24576 | tf_op jit(solution)/shard_map/jit(_where)/select_n | solution.py:892
  0.7 0.0 copy-start
  0.7 1.1 %copy-done = f32[3,24,2,8,128]{4,3,2,1,0:T(8,128)S(1)} copy-done((f32[3,24,2,8,128]{4,3,2,1,0:T(8,128)S(1)}, f32[3,24,2,8,128]{4,3,2,1,0:T(8,128)}, u32[]{:S(2)}) %copy-start) | copy-done | bytes 589848
  1.8 0.1 pack.1
  1.9 0.5 collective-permute-start
  2.4 0.7 %collective-permute-start.3 = (f32[592,128]{1,0:T(8,128)S(1)}, f32[592,128]{1,0:T(8,128)S(1)}, u32[]{:S(2)}, u32[]{:S(2)}) collective-permute-start(f32[592,128]{1,0:T(8,128)S(1)} %get-tuple-element.38), channel_id=1, source_target_pairs={{4,8},{12,16},{20,24},{8,4},{16,12},{24,20},{5,9},{13,17},{21,25},... | collective-permute-start | bytes 909320 | tf_op jit(solution)/shard_map/ppermute | solution.py:924
  3.1 1.0 %collective-permute-done.pair = f32[1168,128]{1,0:T(8,128)S(1)} collective-permute-done((f32[1168,128]{1,0:T(8,128)S(1)}, f32[1168,128]{1,0:T(8,128)S(1)}, u32[]{:S(2)}, u32[]{:S(2)}) %collective-permute-start) | collective-permute-done | bytes 598048 | tf_op jit(solution)/shard_map/ppermute | solution.py:921
  4.1 1.3 %collective-permute-start.2 = (f32[296,128]{1,0:T(8,128)S(1)}, f32[296,128]{1,0:T(8,128)S(1)}, u32[]{:S(2)}, u32[]{:S(2)}) collective-permute-start(f32[296,128]{1,0:T(8,128)S(1)} %get-tuple-element.37), channel_id=1, source_target_pairs={{1,0},{2,1},{3,2},{5,4},{6,5},{7,6},{9,8},{10,9},{11,10},{13,12},{... | collective-permute-start | bytes 454664 | tf_op jit(solution)/shard_map/ppermute | solution.py:915
  5.4 5.5 %collective-permute-start.1 = (f32[152,128]{1,0:T(8,128)S(1)}, f32[152,128]{1,0:T(8,128)S(1)}, u32[]{:S(2)}, u32[]{:S(2)}) collective-permute-start(f32[152,128]{1,0:T(8,128)S(1)} %get-tuple-element.36), channel_id=1, source_target_pairs={{0,1},{1,2},{2,3},{4,5},{5,6},{6,7},{8,9},{9,10},{10,11},{12,13},{... | collective-permute-start | bytes 233480 | tf_op jit(solution)/shard_map/ppermute | solution.py:915
  10.9 1.5 %collective-permute-start.4 = (f32[2,8,128]{2,1,0:T(8,128)S(1)}, f32[2,8,128]{2,1,0:T(8,128)S(1)}, u32[]{:S(2)}, u32[]{:S(2)}) collective-permute-start(f32[2,8,128]{2,1,0:T(8,128)S(1)} %negate_select_fusion.codes), channel_id=1, source_target_pairs={{0,4},{8,12},{16,20},{24,28},{4,0},{12,8},{20,16},{28,24},{1,5},{9... | collective-permute-start | bytes 24584 | tf_op jit(solution)/shard_map/ppermute | solution.py:921
  12.4 0.8 %collective-permute-done.4.begun = f32[2,8,128]{2,1,0:T(8,128)S(1)} collective-permute-done((f32[2,8,128]{2,1,0:T(8,128)S(1)}, f32[2,8,128]{2,1,0:T(8,128)S(1)}, u32[]{:S(2)}, u32[]{:S(2)}) %collective-permute-start.4) | collective-permute-done | bytes 8224 | tf_op jit(solution)/shard_map/ppermute | solution.py:921
  13.2 0.7 %collective-permute-start.5 = (f32[576,128]{1,0:T(8,128)S(1)}, f32[576,128]{1,0:T(8,128)S(1)}, u32[]{:S(2)}, u32[]{:S(2)}) collective-permute-start(f32[576,128]{1,0:T(8,128)S(1)} %second.1), channel_id=1, source_target_pairs={{8,4},{16,12},{24,20},{9,5},{17,13},{25,21},{10,6},{18,14},{26,22}... | collective-permute-start | bytes 884744 | tf_op jit(solution)/shard_map/ppermute | solution.py:946
  13.9 0.0 collective-permute-done.3.edge
  13.9 0.0 collective-permute-done.1.ym
  13.9 0.0 collective-permute-done.2.yp
  14.0 1.0 %collective-permute-start.6 = (f32[448,128]{1,0:T(8,128)S(1)}, f32[448,128]{1,0:T(8,128)S(1)}, u32[]{:S(2)}, u32[]{:S(2)}) collective-permute-start(f32[448,128]{1,0:T(8,128)S(1)} %corners.1), channel_id=1, source_target_pairs={{0,4},{8,12},{16,20},{24,28},{4,0},{12,8},{20,16},{28,24},{1,5},{9... | collective-permute-start | bytes 688136 | tf_op jit(solution)/shard_map/ppermute | solution.py:921
  15.0 0.7 %collective-permute-start.7 = (f32[448,128]{1,0:T(8,128)S(1)}, f32[448,128]{1,0:T(8,128)S(1)}, u32[]{:S(2)}, u32[]{:S(2)}) collective-permute-start(f32[448,128]{1,0:T(8,128)S(1)} %corners.1), channel_id=1, source_target_pairs={{4,8},{12,16},{20,24},{8,4},{16,12},{24,20},{5,9},{13,17},{21,25},... | collective-permute-start | bytes 688136 | tf_op jit(solution)/shard_map/ppermute | solution.py:924
  15.7 0.4 collective-permute-done.6.ym_pair.yp_pair
  16.1 1.8 %early.1 = (f32[33,72,128]{2,1,0:T(8,128)S(1)}, f32[33,72,128]{2,1,0:T(8,128)S(1)}, f32[33,72,128]{2,1,0:T(8,128)S(1)}, f32[27,72,128]{2,1,0:T(8,128)S(1)}, f32[27,72,128]{2,1,0:T(8,128)S(1)}) custom-call(f32[1168,128]{1,0:T(8,128)S(1)} %get-tuple-element.34.own, f32[1168,128]{1,0:T(8,128)S(1)} %collective-permute-done.pair, ...), custom_call_target="tpu_custom_call" | custom-call | flops 29491200 | bytes 8388608 | tf_op jit(solution)/shard_map/early/pallas_call | solution.py:966
  17.9 0.0 collective-permute-done.5.second
  17.9 3.3 %middle.1 = (f32[21,72,128]{2,1,0:T(8,128)S(1)}, f32[21,72,128]{2,1,0:T(8,128)S(1)}, f32[7,72,128]{2,1,0:T(8,128)S(1)}, f32[21,72,128]{2,1,0:T(8,128)S(1)}, f32[...) custom-call(f32[1168,128]{1,0:T(8,128)S(1)} %get-tuple-element.34.ow, ...), custom_call_target="tpu_custom_call" | custom-call | tf_op jit(solution)/shard_map/middle/pallas_call | solution.py:992
  21.3 0.0 collective-permute-done.7.corners
  21.3 3.3 %operator.1 = (bf16[96,4608]{1,0:T(8,128)(2,1)S(1)}, f32[32,5,2,128]{3,2,1,0:T(2,128)S(1)}) custom-call(f32[1168,128]{1,0:T(8,128)S(1)} %get-tuple-element.34.own, f32[1168,128]{1,0:T(8,128)S(1)} %collective-permute-done.pair, f32[592,128]{1,0:T(8,128)S(1)} %collective-permute-done.3.edge, f32[576,128]{1,0:T(8,128)S(1)} %collective-permute-done.5.second, ...), custom_call_target="tpu_custom_call" | custom-call | tf_op jit(solution)/shard_map/operator/pallas_call | solution.py:1014
  24.6 18.5 %all_to_all.10.system = f32[32,5,2,128]{3,2,1,0:T(2,128)S(1)} all-to-all(f32[32,5,2,128]{3,2,1,0:T(2,128)S(1)} %get-tuple-element.59), channel_id=1, replica_groups=mesh['gx'=8,'gy'=4] {'gx','gy'}, dimensions={0} | all-to-all | bytes 327680 | tf_op jit(solution)/shard_map/all_to_all | solution.py:1051
  43.1 0.0 copy-start.1
  43.1 4.3 %solve.1 = f32[16,2,8,128]{3,2,1,0:T(8,128)S(1)} custom-call(f32[32,5,2,128]{3,2,1,0:T(2,128)S(1)} %all_to_all.10.system, bf16[96,5760]{1,0:T(8,128)(2,1)S(1)} %get-tuple-element.54.both_m, bf16[96,4608]{1,0:T(8,128)(2,1)S(1)} %get-tuple-element.60.both_r, f32[2,8,128]{2,1,0:T(8,128)S(1)} %negate_select_fusion.codes), custom_call_target="tpu_custom_call" | custom-call | tf_op jit(solution)/shard_map/solve/pallas_call | solution.py:1053
  47.4 10.5 %all_to_all.11.blocks = f32[16,2,8,128]{3,2,1,0:T(8,128)S(1)} all-to-all(f32[16,2,8,128]{3,2,1,0:T(8,128)S(1)} %solve.1), channel_id=1, replica_groups={{0,1,2,3,8,9,10,11,16,17,18,19,24,25,26,27},{4,5,6,7,12,13,14,15,20,21,..., dimensions={0} | all-to-all | bytes 262144 | tf_op jit(solution)/shard_map/all_to_all | solution.py:1048
  57.9 0.0 collective-permute-start.8
  57.9 0.0 copy-done.1
  57.9 0.1 scale.1
  58.0 1.2 %collective-permute-done.8.blocks_pair = f32[16,2,8,128]{3,2,1,0:T(8,128)S(1)} collective-permute-done((f32[16,2,8,128]{3,2,1,0:T(8,128)S(1)}, f32[16,2,8,128]{3,2,1,0:T(8,128)S(1)}, u32[]{:S(2)}, u32[]{:S(2)}) %collective-permute-start.8) | collective-permute-done | bytes 131104 | tf_op jit(solution)/shard_map/ppermute | solution.py:921
  59.3 0.7 %cone.1 = f32[2,8,128]{2,1,0:T(8,128)} custom-call(f32[16,2,8,128]{3,2,1,0:T(8,128)S(1)} %all_to_all.11.blocks, f32[16,2,8,128]{3,2,1,0:T(8,128)S(1)} %collective-permute-done.8.blocks_pair, f32[2,8,128]{2,1,0:T(8,128)S(1)} %scale.1), custom_call_target="tpu_custom_call" | custom-call | tf_op jit(solution)/shard_map/cone/pallas_call | solution.py:1072
  (3 shorter events, 0.1 us)
Async XLA Ops:
  0.7 1.1 %copy-start = (f32[3,24,2,8,128]{4,3,2,1,0:T(8,128)S(1)}, f32[3,24,2,8,128]{4,3,2,1,0:T(8,128)}, u32[]{:S(2)}) copy-start(f32[3,24,2,8,128]{4,3,2,1,0:T(8,128)} %forces.1) | copy-start | bytes 1769476
  1.9 2.2 %collective-permute-start = (f32[1168,128]{1,0:T(8,128)S(1)}, f32[1168,128]{1,0:T(8,128)S(1)}, u32[]{:S(2)}, u32[]{:S(2)}) collective-permute-start(f32[1168,128]{1,0:T(8,128)S(1)} %get-tuple-element.34.own), channel_id=1, source_target_pairs={{0,4},{8,12},{16,20},{24,28},{4,0},{12,8},{20,16},{28,24},{1,5},{9... | collective-permute-start | bytes 1794056 | tf_op jit(solution)/shard_map/ppermute | solution.py:921
  2.4 11.5 %collective-permute-start.3 = (f32[592,128]{1,0:T(8,128)S(1)}, f32[592,128]{1,0:T(8,128)S(1)}, u32[]{:S(2)}, u32[]{:S(2)}) collective-permute-start(f32[592,128]{1,0:T(8,128)S(1)} %get-tuple-element.38), channel_id=1, source_target_pairs={{4,8},{12,16},{20,24},{8,4},{16,12},{24,20},{5,9},{13,17},{21,25},... | collective-permute-start | bytes 909320 | tf_op jit(solution)/shard_map/ppermute | solution.py:924
  4.1 9.8 %collective-permute-start.2 = (f32[296,128]{1,0:T(8,128)S(1)}, f32[296,128]{1,0:T(8,128)S(1)}, u32[]{:S(2)}, u32[]{:S(2)}) collective-permute-start(f32[296,128]{1,0:T(8,128)S(1)} %get-tuple-element.37), channel_id=1, source_target_pairs={{1,0},{2,1},{3,2},{5,4},{6,5},{7,6},{9,8},{10,9},{11,10},{13,12},{... | collective-permute-start | bytes 454664 | tf_op jit(solution)/shard_map/ppermute | solution.py:915
  5.4 8.5 %collective-permute-start.1 = (f32[152,128]{1,0:T(8,128)S(1)}, f32[152,128]{1,0:T(8,128)S(1)}, u32[]{:S(2)}, u32[]{:S(2)}) collective-permute-start(f32[152,128]{1,0:T(8,128)S(1)} %get-tuple-element.36), channel_id=1, source_target_pairs={{0,1},{1,2},{2,3},{4,5},{5,6},{6,7},{8,9},{9,10},{10,11},{12,13},{... | collective-permute-start | bytes 233480 | tf_op jit(solution)/shard_map/ppermute | solution.py:915
  10.9 2.3 %collective-permute-start.4 = (f32[2,8,128]{2,1,0:T(8,128)S(1)}, f32[2,8,128]{2,1,0:T(8,128)S(1)}, u32[]{:S(2)}, u32[]{:S(2)}) collective-permute-start(f32[2,8,128]{2,1,0:T(8,128)S(1)} %negate_select_fusion.codes), channel_id=1, source_target_pairs={{0,4},{8,12},{16,20},{24,28},{4,0},{12,8},{20,16},{28,24},{1,5},{9... | collective-permute-start | bytes 24584 | tf_op jit(solution)/shard_map/ppermute | solution.py:921
  13.2 4.7 %collective-permute-start.5 = (f32[576,128]{1,0:T(8,128)S(1)}, f32[576,128]{1,0:T(8,128)S(1)}, u32[]{:S(2)}, u32[]{:S(2)}) collective-permute-start(f32[576,128]{1,0:T(8,128)S(1)} %second.1), channel_id=1, source_target_pairs={{8,4},{16,12},{24,20},{9,5},{17,13},{25,21},{10,6},{18,14},{26,22}... | collective-permute-start | bytes 884744 | tf_op jit(solution)/shard_map/ppermute | solution.py:946
  14.0 2.1 %collective-permute-start.6 = (f32[448,128]{1,0:T(8,128)S(1)}, f32[448,128]{1,0:T(8,128)S(1)}, u32[]{:S(2)}, u32[]{:S(2)}) collective-permute-start(f32[448,128]{1,0:T(8,128)S(1)} %corners.1), channel_id=1, source_target_pairs={{0,4},{8,12},{16,20},{24,28},{4,0},{12,8},{20,16},{28,24},{1,5},{9... | collective-permute-start | bytes 688136 | tf_op jit(solution)/shard_map/ppermute | solution.py:921
  15.0 6.3 %collective-permute-start.7 = (f32[448,128]{1,0:T(8,128)S(1)}, f32[448,128]{1,0:T(8,128)S(1)}, u32[]{:S(2)}, u32[]{:S(2)}) collective-permute-start(f32[448,128]{1,0:T(8,128)S(1)} %corners.1), channel_id=1, source_target_pairs={{4,8},{12,16},{20,24},{8,4},{16,12},{24,20},{5,9},{13,17},{21,25},... | collective-permute-start | bytes 688136 | tf_op jit(solution)/shard_map/ppermute | solution.py:924
  43.1 14.8 %copy-start.1 = (s32[2,8,128]{2,1,0:T(8,128)S(1)}, s32[2,8,128]{2,1,0:T(8,128)}, u32[]{:S(2)}) copy-start(s32[2,8,128]{2,1,0:T(8,128)} %levels.1) | copy-start | bytes 24580
  57.9 1.3 %collective-permute-start.8 = (f32[16,2,8,128]{3,2,1,0:T(8,128)S(1)}, f32[16,2,8,128]{3,2,1,0:T(8,128)S(1)}, u32[]{:S(2)}, u32[]{:S(2)}) collective-permute-start(f32[16,2,8,128]{3,2,1,0:T(8,128)S(1)} %all_to_all.11.blocks), channel_id=1, source_target_pairs={{0,4},{8,12},{16,20},{24,28},{4,0},{12,8},{20,16},{28,24},{1,5},{9... | collective-permute-start | bytes 393224 | tf_op jit(solution)/shard_map/ppermute | solution.py:921

commit v22 on v20

--- a/solution.py
+++ b/solution.py
@@ -252,7 +252,7 @@
     fill(own, base, sizes, yp, every_x, (rows - 1,), every_x, (rows - 2, rows - 1))
 
 
-def corner_kernel(sizes, ym, yp, out):
+def corner_kernel(sizes, ym, yp, out, copy):
     planes, rows, cases = sizes
     block = 3 * cases
     even = lax.axis_index("gx") % 2 == 0
@@ -269,6 +269,8 @@
             line += count
         out[line : line + 4, :] = jnp.zeros((4, LANES), f32)
         line += 4
+    copy[...] = lines(out, 0, line)
+    out[line:, :] = jnp.zeros((out.shape[0] - line, LANES), f32)
 
 
 def lines(ref, start, count):
@@ -945,16 +947,19 @@
     )(swapped(codes), own)
     second = lax.ppermute(second, "gx", links(2, -1))
     from_ym, from_yp, edge = lax.optimization_barrier((from_ym, from_yp, edge))
-    corners = pl.pallas_call(
+    corners, copy = pl.pallas_call(
         functools.partial(corner_kernel, sizes),
-        out_shape=jax.ShapeDtypeStruct((6 * block + 16, LANES), f32),
+        out_shape=[
+            jax.ShapeDtypeStruct((6 * block + 32, LANES), f32),
+            jax.ShapeDtypeStruct((6 * block + 16, LANES), f32),
+        ],
         in_specs=[VMEM] * 2,
-        out_specs=VMEM,
+        out_specs=[VMEM] * 2,
         compiler_params=PARAMS,
         name="corners",
     )(from_ym, from_yp)
     if planes == 2:
-        pair_ym = pair_yp = swapped(corners)
+        pair_ym = pair_yp = swapped(copy)
     else:
         pair_yp, pair_ym = swapped(from_yp), swapped(from_ym)
     corners = across(corners)

time: 59.1 us -> 59.2 us (level)
  blocking collectives: 29 us -> 24.8 us
  starting transfers between devices: 11.8 us -> 15.4 us
  waiting for transfers between devices: 3.48 us -> 4.15 us
    all_to_all x1, blocking collectives: 18.5 us -> 14.4 us  [local(): system = lax.all_to_all(system, ('gx', 'gy'), 0, 0)]
    ppermute x4, starting transfers between devices: 3.02 us -> 6.63 us  [swapped(): return lax.ppermute(value, 'gx', links(0, 1) + links(1, -1))]
    ppermute x4, waiting for transfers between devices: 3.47 us -> 4.14 us  [swapped(): return lax.ppermute(value, 'gx', links(0, 1) + links(1, -1))]
where the time goes in v22:
time: 59.2 us; the launch traced here: 58.9 us
  blocking collectives  24.8 us (42%)
  starting transfers between devices  15.4 us (26%)
  Pallas kernels  12.5 us (21%)
  waiting for transfers between devices  4.15 us (7%)
  local copies, waits for them, and re-layouts  1.07 us (2%)
  other arithmetic  0.72 us (1%)
    all_to_all x1, blocking collectives, local(): system = lax.all_to_all(system, ('gx', 'gy'), 0, 0)  14.4 us
    all_to_all x1, blocking collectives, gathered(): mine = lax.all_to_all(copies, ('gx', 'gy'), 0, 0, axis_index_groups=groups)  10.5 us
    ppermute x2, starting transfers between devices, moved(): return lax.ppermute(value, axis, pairs)  6.77 us
    ppermute x4, starting transfers between devices, swapped(): return lax.ppermute(value, 'gx', links(0, 1) + links(1, -1))  6.63 us
    ppermute x4, waiting for transfers between devices, swapped(): return lax.ppermute(value, 'gx', links(0, 1) + links(1, -1))  4.14 us
    pallas_call x1, Pallas kernels, local(): pl.pallas_call(functools.partial(middle_kernel, sizes), out_shape=[column...  3.29 us
    pallas_call x1, Pallas kernels, local(): pl.pallas_call(functools.partial(main_kernel, sizes), out_shape=[fields(4...  3.29 us
    pallas_call x1, Pallas kernels, local(): pl.pallas_call(functools.partial(solve_kernel, sizes), out_shape=jax.Shap...  3.11 us
  transfers between devices with their start and end apart: 9, of which 4 were waited for; matrix products, arithmetic and copies ran while one was open for 0% of the time, Pallas kernels for 9%

profile of v22, /device:TPU:0, one launch (start us, length us, event | category | flops | bytes accessed | tf_op | source)
XLA Modules:
  0.0 58.9 jit_solution(2611434723405478607)
XLA Ops:
  0.0 0.7 %negate_select_fusion.codes = f32[2,8,128]{2,1,0:T(8,128)S(1)} fusion(s32[2,8,128]{2,1,0:T(8,128)} %levels.1, s32[2,8,128]{2,1,0:T(8,128)} %param.5), kind=kLoop, calls=%fused_computation | loop fusion | flops 16384 | bytes 24576 | tf_op jit(solution)/shard_map/jit(_where)/select_n | solution.py:894
  0.7 0.0 copy-start
  0.7 1.1 %copy-done = f32[3,24,2,8,128]{4,3,2,1,0:T(8,128)S(1)} copy-done((f32[3,24,2,8,128]{4,3,2,1,0:T(8,128)S(1)}, f32[3,24,2,8,128]{4,3,2,1,0:T(8,128)}, u32[]{:S(2)}) %copy-start) | copy-done | bytes 589848
  1.8 0.1 pack.1
  1.9 0.5 collective-permute-start
  2.4 0.7 %collective-permute-start.3 = (f32[592,128]{1,0:T(8,128)S(1)}, f32[592,128]{1,0:T(8,128)S(1)}, u32[]{:S(2)}, u32[]{:S(2)}) collective-permute-start(f32[592,128]{1,0:T(8,128)S(1)} %get-tuple-element.40), channel_id=1, source_target_pairs={{4,8},{12,16},{20,24},{8,4},{16,12},{24,20},{5,9},{13,17},{21,25},... | collective-permute-start | bytes 909320 | tf_op jit(solution)/shard_map/ppermute | solution.py:926
  3.1 1.0 %collective-permute-done.pair = f32[1168,128]{1,0:T(8,128)S(1)} collective-permute-done((f32[1168,128]{1,0:T(8,128)S(1)}, f32[1168,128]{1,0:T(8,128)S(1)}, u32[]{:S(2)}, u32[]{:S(2)}) %collective-permute-start) | collective-permute-done | bytes 598048 | tf_op jit(solution)/shard_map/ppermute | solution.py:923
  4.1 1.3 %collective-permute-start.2 = (f32[296,128]{1,0:T(8,128)S(1)}, f32[296,128]{1,0:T(8,128)S(1)}, u32[]{:S(2)}, u32[]{:S(2)}) collective-permute-start(f32[296,128]{1,0:T(8,128)S(1)} %get-tuple-element.39), channel_id=1, source_target_pairs={{1,0},{2,1},{3,2},{5,4},{6,5},{7,6},{9,8},{10,9},{11,10},{13,12},{... | collective-permute-start | bytes 454664 | tf_op jit(solution)/shard_map/ppermute | solution.py:917
  5.4 5.5 %collective-permute-start.1 = (f32[152,128]{1,0:T(8,128)S(1)}, f32[152,128]{1,0:T(8,128)S(1)}, u32[]{:S(2)}, u32[]{:S(2)}) collective-permute-start(f32[152,128]{1,0:T(8,128)S(1)} %get-tuple-element.38), channel_id=1, source_target_pairs={{0,1},{1,2},{2,3},{4,5},{5,6},{6,7},{8,9},{9,10},{10,11},{12,13},{... | collective-permute-start | bytes 233480 | tf_op jit(solution)/shard_map/ppermute | solution.py:917
  10.9 1.5 %collective-permute-start.4 = (f32[2,8,128]{2,1,0:T(8,128)S(1)}, f32[2,8,128]{2,1,0:T(8,128)S(1)}, u32[]{:S(2)}, u32[]{:S(2)}) collective-permute-start(f32[2,8,128]{2,1,0:T(8,128)S(1)} %negate_select_fusion.codes), channel_id=1, source_target_pairs={{0,4},{8,12},{16,20},{24,28},{4,0},{12,8},{20,16},{28,24},{1,5},{9... | collective-permute-start | bytes 24584 | tf_op jit(solution)/shard_map/ppermute | solution.py:923
  12.4 0.8 %collective-permute-done.4.begun = f32[2,8,128]{2,1,0:T(8,128)S(1)} collective-permute-done((f32[2,8,128]{2,1,0:T(8,128)S(1)}, f32[2,8,128]{2,1,0:T(8,128)S(1)}, u32[]{:S(2)}, u32[]{:S(2)}) %collective-permute-start.4) | collective-permute-done | bytes 8224 | tf_op jit(solution)/shard_map/ppermute | solution.py:923
  13.2 0.7 %collective-permute-start.5 = (f32[576,128]{1,0:T(8,128)S(1)}, f32[576,128]{1,0:T(8,128)S(1)}, u32[]{:S(2)}, u32[]{:S(2)}) collective-permute-start(f32[576,128]{1,0:T(8,128)S(1)} %second.1), channel_id=1, source_target_pairs={{8,4},{16,12},{24,20},{9,5},{17,13},{25,21},{10,6},{18,14},{26,22}... | collective-permute-start | bytes 884744 | tf_op jit(solution)/shard_map/ppermute | solution.py:948
  13.9 0.0 collective-permute-done.3.edge
  13.9 0.0 collective-permute-done.1.ym
  13.9 0.0 collective-permute-done.2.yp
  14.0 0.7 %collective-permute-start.7 = (f32[464,128]{1,0:T(8,128)S(1)}, f32[464,128]{1,0:T(8,128)S(1)}, u32[]{:S(2)}, u32[]{:S(2)}) collective-permute-start(f32[464,128]{1,0:T(8,128)S(1)} %get-tuple-element.45), channel_id=1, source_target_pairs={{4,8},{12,16},{20,24},{8,4},{16,12},{24,20},{5,9},{13,17},{21,25},... | collective-permute-start | bytes 712712 | tf_op jit(solution)/shard_map/ppermute | solution.py:926
  14.7 4.6 %collective-permute-start.6 = (f32[448,128]{1,0:T(8,128)S(1)}, f32[448,128]{1,0:T(8,128)S(1)}, u32[]{:S(2)}, u32[]{:S(2)}) collective-permute-start(f32[448,128]{1,0:T(8,128)S(1)} %get-tuple-element.44), channel_id=1, source_target_pairs={{0,4},{8,12},{16,20},{24,28},{4,0},{12,8},{20,16},{28,24},{1,5},{9... | collective-permute-start | bytes 688136 | tf_op jit(solution)/shard_map/ppermute | solution.py:923
  19.3 1.1 %collective-permute-done.6.ym_pair.yp_pair = f32[448,128]{1,0:T(8,128)S(1)} collective-permute-done((f32[448,128]{1,0:T(8,128)S(1)}, f32[448,128]{1,0:T(8,128)S(1)}, u32[]{:S(2)}, u32[]{:S(2)}) %collective-permute-start.6) | collective-permute-done | bytes 229408 | tf_op jit(solution)/shard_map/ppermute | solution.py:923
  20.4 1.8 %early.1 = (f32[33,72,128]{2,1,0:T(8,128)S(1)}, f32[33,72,128]{2,1,0:T(8,128)S(1)}, f32[33,72,128]{2,1,0:T(8,128)S(1)}, f32[27,72,128]{2,1,0:T(8,128)S(1)}, f32[27,72,128]{2,1,0:T(8,128)S(1)}) custom-call(f32[1168,128]{1,0:T(8,128)S(1)} %get-tuple-element.36.own, f32[1168,128]{1,0:T(8,128)S(1)} %collective-permute-done.pair, ...), custom_call_target="tpu_custom_call" | custom-call | flops 29491200 | bytes 8388608 | tf_op jit(solution)/shard_map/early/pallas_call | solution.py:971
  22.2 0.0 collective-permute-done.5.second
  22.2 3.3 %middle.1 = (f32[21,72,128]{2,1,0:T(8,128)S(1)}, f32[21,72,128]{2,1,0:T(8,128)S(1)}, f32[7,72,128]{2,1,0:T(8,128)S(1)}, f32[21,72,128]{2,1,0:T(8,128)S(1)}, f32[...) custom-call(f32[1168,128]{1,0:T(8,128)S(1)} %get-tuple-element.36.ow, ...), custom_call_target="tpu_custom_call" | custom-call | tf_op jit(solution)/shard_map/middle/pallas_call | solution.py:997
  25.5 0.0 collective-permute-done.7.corners
  25.6 3.3 %operator.1 = (bf16[96,4608]{1,0:T(8,128)(2,1)S(1)}, f32[32,5,2,128]{3,2,1,0:T(2,128)S(1)}) custom-call(f32[1168,128]{1,0:T(8,128)S(1)} %get-tuple-element.36.own, f32[1168,128]{1,0:T(8,128)S(1)} %collective-permute-done.pair, f32[592,128]{1,0:T(8,128)S(1)} %collective-permute-done.3.edge, f32[576,128]{1,0:T(8,128)S(1)} %collective-permute-done.5.second, ...), custom_call_target="tpu_custom_call" | custom-call | tf_op jit(solution)/shard_map/operator/pallas_call | solution.py:1019
  28.9 14.4 %all_to_all.10.system = f32[32,5,2,128]{3,2,1,0:T(2,128)S(1)} all-to-all(f32[32,5,2,128]{3,2,1,0:T(2,128)S(1)} %get-tuple-element.63), channel_id=1, replica_groups=mesh['gx'=8,'gy'=4] {'gx','gy'}, dimensions={0} | all-to-all | bytes 327680 | tf_op jit(solution)/shard_map/all_to_all | solution.py:1056
  43.2 0.0 copy-start.1
  43.2 3.1 %solve.1 = f32[16,2,8,128]{3,2,1,0:T(8,128)S(1)} custom-call(f32[32,5,2,128]{3,2,1,0:T(2,128)S(1)} %all_to_all.10.system, bf16[96,5760]{1,0:T(8,128)(2,1)S(1)} %get-tuple-element.58.both_m, bf16[96,4608]{1,0:T(8,128)(2,1)S(1)} %get-tuple-element.64.both_r, f32[2,8,128]{2,1,0:T(8,128)S(1)} %negate_select_fusion.codes), custom_call_target="tpu_custom_call" | custom-call | tf_op jit(solution)/shard_map/solve/pallas_call | solution.py:1058
  46.3 10.5 %all_to_all.11.blocks = f32[16,2,8,128]{3,2,1,0:T(8,128)S(1)} all-to-all(f32[16,2,8,128]{3,2,1,0:T(8,128)S(1)} %solve.1), channel_id=1, replica_groups={{0,1,2,3,8,9,10,11,16,17,18,19,24,25,26,27},{4,5,6,7,12,13,14,15,20,21,..., dimensions={0} | all-to-all | bytes 262144 | tf_op jit(solution)/shard_map/all_to_all | solution.py:1053
  56.8 0.0 collective-permute-start.8
  56.8 0.0 copy-done.1
  56.8 0.1 scale.1
  56.9 1.2 %collective-permute-done.8.blocks_pair = f32[16,2,8,128]{3,2,1,0:T(8,128)S(1)} collective-permute-done((f32[16,2,8,128]{3,2,1,0:T(8,128)S(1)}, f32[16,2,8,128]{3,2,1,0:T(8,128)S(1)}, u32[]{:S(2)}, u32[]{:S(2)}) %collective-permute-start.8) | collective-permute-done | bytes 131104 | tf_op jit(solution)/shard_map/ppermute | solution.py:923
  58.1 0.7 %cone.1 = f32[2,8,128]{2,1,0:T(8,128)} custom-call(f32[16,2,8,128]{3,2,1,0:T(8,128)S(1)} %all_to_all.11.blocks, f32[16,2,8,128]{3,2,1,0:T(8,128)S(1)} %collective-permute-done.8.blocks_pair, f32[2,8,128]{2,1,0:T(8,128)S(1)} %scale.1), custom_call_target="tpu_custom_call" | custom-call | tf_op jit(solution)/shard_map/cone/pallas_call | solution.py:1077
  (3 shorter events, 0.1 us)
Async XLA Ops:
  0.7 1.1 %copy-start = (f32[3,24,2,8,128]{4,3,2,1,0:T(8,128)S(1)}, f32[3,24,2,8,128]{4,3,2,1,0:T(8,128)}, u32[]{:S(2)}) copy-start(f32[3,24,2,8,128]{4,3,2,1,0:T(8,128)} %forces.1) | copy-start | bytes 1769476
  1.9 2.2 %collective-permute-start = (f32[1168,128]{1,0:T(8,128)S(1)}, f32[1168,128]{1,0:T(8,128)S(1)}, u32[]{:S(2)}, u32[]{:S(2)}) collective-permute-start(f32[1168,128]{1,0:T(8,128)S(1)} %get-tuple-element.36.own), channel_id=1, source_target_pairs={{0,4},{8,12},{16,20},{24,28},{4,0},{12,8},{20,16},{28,24},{1,5},{9... | collective-permute-start | bytes 1794056 | tf_op jit(solution)/shard_map/ppermute | solution.py:923
  2.4 11.5 %collective-permute-start.3 = (f32[592,128]{1,0:T(8,128)S(1)}, f32[592,128]{1,0:T(8,128)S(1)}, u32[]{:S(2)}, u32[]{:S(2)}) collective-permute-start(f32[592,128]{1,0:T(8,128)S(1)} %get-tuple-element.40), channel_id=1, source_target_pairs={{4,8},{12,16},{20,24},{8,4},{16,12},{24,20},{5,9},{13,17},{21,25},... | collective-permute-start | bytes 909320 | tf_op jit(solution)/shard_map/ppermute | solution.py:926
  4.1 9.8 %collective-permute-start.2 = (f32[296,128]{1,0:T(8,128)S(1)}, f32[296,128]{1,0:T(8,128)S(1)}, u32[]{:S(2)}, u32[]{:S(2)}) collective-permute-start(f32[296,128]{1,0:T(8,128)S(1)} %get-tuple-element.39), channel_id=1, source_target_pairs={{1,0},{2,1},{3,2},{5,4},{6,5},{7,6},{9,8},{10,9},{11,10},{13,12},{... | collective-permute-start | bytes 454664 | tf_op jit(solution)/shard_map/ppermute | solution.py:917
  5.4 8.5 %collective-permute-start.1 = (f32[152,128]{1,0:T(8,128)S(1)}, f32[152,128]{1,0:T(8,128)S(1)}, u32[]{:S(2)}, u32[]{:S(2)}) collective-permute-start(f32[152,128]{1,0:T(8,128)S(1)} %get-tuple-element.38), channel_id=1, source_target_pairs={{0,1},{1,2},{2,3},{4,5},{5,6},{6,7},{8,9},{9,10},{10,11},{12,13},{... | collective-permute-start | bytes 233480 | tf_op jit(solution)/shard_map/ppermute | solution.py:917
  10.9 2.3 %collective-permute-start.4 = (f32[2,8,128]{2,1,0:T(8,128)S(1)}, f32[2,8,128]{2,1,0:T(8,128)S(1)}, u32[]{:S(2)}, u32[]{:S(2)}) collective-permute-start(f32[2,8,128]{2,1,0:T(8,128)S(1)} %negate_select_fusion.codes), channel_id=1, source_target_pairs={{0,4},{8,12},{16,20},{24,28},{4,0},{12,8},{20,16},{28,24},{1,5},{9... | collective-permute-start | bytes 24584 | tf_op jit(solution)/shard_map/ppermute | solution.py:923
  13.2 9.0 %collective-permute-start.5 = (f32[576,128]{1,0:T(8,128)S(1)}, f32[576,128]{1,0:T(8,128)S(1)}, u32[]{:S(2)}, u32[]{:S(2)}) collective-permute-start(f32[576,128]{1,0:T(8,128)S(1)} %second.1), channel_id=1, source_target_pairs={{8,4},{16,12},{24,20},{9,5},{17,13},{25,21},{10,6},{18,14},{26,22}... | collective-permute-start | bytes 884744 | tf_op jit(solution)/shard_map/ppermute | solution.py:948
  14.0 11.6 %collective-permute-start.7 = (f32[464,128]{1,0:T(8,128)S(1)}, f32[464,128]{1,0:T(8,128)S(1)}, u32[]{:S(2)}, u32[]{:S(2)}) collective-permute-start(f32[464,128]{1,0:T(8,128)S(1)} %get-tuple-element.45), channel_id=1, source_target_pairs={{4,8},{12,16},{20,24},{8,4},{16,12},{24,20},{5,9},{13,17},{21,25},... | collective-permute-start | bytes 712712 | tf_op jit(solution)/shard_map/ppermute | solution.py:926
  14.7 5.7 %collective-permute-start.6 = (f32[448,128]{1,0:T(8,128)S(1)}, f32[448,128]{1,0:T(8,128)S(1)}, u32[]{:S(2)}, u32[]{:S(2)}) collective-permute-start(f32[448,128]{1,0:T(8,128)S(1)} %get-tuple-element.44), channel_id=1, source_target_pairs={{0,4},{8,12},{16,20},{24,28},{4,0},{12,8},{20,16},{28,24},{1,5},{9... | collective-permute-start | bytes 688136 | tf_op jit(solution)/shard_map/ppermute | solution.py:923
  43.2 13.6 %copy-start.1 = (s32[2,8,128]{2,1,0:T(8,128)S(1)}, s32[2,8,128]{2,1,0:T(8,128)}, u32[]{:S(2)}) copy-start(s32[2,8,128]{2,1,0:T(8,128)} %levels.1) | copy-start | bytes 24580
  56.8 1.3 %collective-permute-start.8 = (f32[16,2,8,128]{3,2,1,0:T(8,128)S(1)}, f32[16,2,8,128]{3,2,1,0:T(8,128)S(1)}, u32[]{:S(2)}, u32[]{:S(2)}) collective-permute-start(f32[16,2,8,128]{3,2,1,0:T(8,128)S(1)} %all_to_all.11.blocks), channel_id=1, source_target_pairs={{0,4},{8,12},{16,20},{24,28},{4,0},{12,8},{20,16},{28,24},{1,5},{9... | collective-permute-start | bytes 393224 | tf_op jit(solution)/shard_map/ppermute | solution.py:923
